TPU v7x, 256 devices: a whole 4x4x8 slice. The times are simulated.
256 devices in a mesh: row: 32 (over x, z), head: 8 (over y, core).
Axes of the slice: x: 4, y: 4, z: 8, core: 2. Of those that a mesh axis runs over, the one named last changes fastest.
Arguments:
- q_nope: bfloat16 [4, 64, 128, 128], P(None, 'row', 'head'), may hold values from -9 to 9
- q_rope: bfloat16 [4, 64, 8192], P(None, 'row', 'head'), may hold values from -18 to 18
- new_latent: bfloat16 [4, 64, 512], P(None, 'row'), may hold values from -6 to 6
- new_rope: bfloat16 [4, 64, 64], P(None, 'row'), may hold values from -6 to 6
- latent_pages: bfloat16 [2560, 64, 512], P('row'), may hold values from -6 to 6
- rope_pages: bfloat16 [2560, 4096], P('row'), may hold values from -6 to 6
- dest_rows: int32 [2560], P('row'), may hold values from 0 to 63, as said below
- dest_slots: int32 [2560], P('row'), may hold values from 0 to 39
- page_table: int32 [64, 40], P('row'), may hold values from 0 to 39, each once within a row
- lengths: int32 [64], P('row'), may hold values from 1 to 2560, as said below
- w_uk: bfloat16 [128, 128, 512], P('head'), may hold values from -0.5 to 0.5
- w_uv: bfloat16 [128, 512, 128], P('head'), may hold values from -1 to 1
- w_o: bfloat16 [16384, 7168], P('head', 'row'), may hold values from -0.046875 to 0.046875
Outputs:
- mixed_out: bfloat16 [4, 64, 7168], P(None, 'row', 'head')
Inputs may be any that keep to these rules, and one draw needn't show every extreme that they name: `dest_rows`: together with dest_slots, each page of a device is named a row and a page slot of that row; every slot of every row is named exactly once over all pages. From the pages of one index of row at most 5 go to the rows of any one index of row, exactly 5 for some pairs; every index of row receives 80 pages. `page_table`: each row of the table is a permutation of the slots. `lengths`: some row holds 2560 tokens.
All inputs are finite; a program needn't handle non-finite values.
Results may differ from a plain program's by a relative error of at most 0.008.
Values may be sent and summed in bfloat16 or wider, within the bound.
No kernel may reach another device: no remote copies, remote signals or barrier semaphores. Data moves between devices by JAX's collectives and lax.ppermute only.
A program may use at most 128 MiB of HBM per device.

v0:
```python
import jax
import jax.numpy as jnp
from jax import lax
from jax.sharding import PartitionSpec as P


def token_positions(page_table, page_len):
    pages_row = page_table.shape[1]
    slot_ids = jnp.arange(pages_row, dtype=jnp.int32)
    holds = (page_table[:, :, None] == slot_ids[None, None, :]).astype(jnp.int32)
    logical = jnp.sum(holds * slot_ids[None, :, None], axis=1)
    within = jnp.arange(page_len, dtype=jnp.int32)
    return (logical[:, :, None] * page_len + within[None, None, :]).reshape(
        page_table.shape[0], pages_row * page_len
    )


def attend(
    q_nope, q_rope, new_latent, new_rope, cache_lat, cache_rope, usable, first_step, w_uk, w_uv
):
    step_count, row_count, heads, _ = q_nope.shape
    rope_w = new_rope.shape[-1]
    score_scale = 1.0 / (q_nope.shape[-1] + rope_w) ** 0.5
    absorbed = jnp.einsum(
        "srhn,hnl->srhl", q_nope, w_uk, preferred_element_type=jnp.float32
    ).astype(jnp.bfloat16)
    rope_q = q_rope.reshape(step_count, row_count, heads, rope_w)
    cache_scores = (
        jnp.einsum("srhl,rkl->srhk", absorbed, cache_lat, preferred_element_type=jnp.float32)
        + jnp.einsum("srhe,rke->srhk", rope_q, cache_rope, preferred_element_type=jnp.float32)
    ) * score_scale
    cache_scores = jnp.where(usable[None, :, None, :], cache_scores, -1e30)
    fresh_scores = (
        jnp.einsum("srhl,url->srhu", absorbed, new_latent, preferred_element_type=jnp.float32)
        + jnp.einsum("srhe,ure->srhu", rope_q, new_rope, preferred_element_type=jnp.float32)
    ) * score_scale
    step_ids = first_step + jnp.arange(step_count, dtype=jnp.int32)
    allowed = jnp.arange(new_latent.shape[0], dtype=jnp.int32)[None, :] <= step_ids[:, None]
    fresh_scores = jnp.where(allowed[:, None, None, :], fresh_scores, -1e30)
    highest = jnp.maximum(jnp.max(cache_scores, axis=-1), jnp.max(fresh_scores, axis=-1))
    cache_exp = jnp.exp(cache_scores - highest[..., None])
    fresh_exp = jnp.exp(fresh_scores - highest[..., None])
    denominator = jnp.sum(cache_exp, axis=-1) + jnp.sum(fresh_exp, axis=-1)
    cache_weights = (cache_exp / denominator[..., None]).astype(jnp.bfloat16)
    fresh_weights = (fresh_exp / denominator[..., None]).astype(jnp.bfloat16)
    latent_out = (
        jnp.einsum("srhk,rkl->srhl", cache_weights, cache_lat, preferred_element_type=jnp.float32)
        + jnp.einsum(
            "srhu,url->srhl", fresh_weights, new_latent, preferred_element_type=jnp.float32
        )
    ).astype(jnp.bfloat16)
    head_out = jnp.einsum(
        "srhl,hlv->srhv", latent_out, w_uv, preferred_element_type=jnp.float32
    ).astype(jnp.bfloat16)
    return head_out.reshape(step_count, row_count, heads * w_uv.shape[-1])


def project(head_out, w_o):
    partial_out = jnp.einsum(
        "srf,fc->src",
        lax.all_gather(head_out, "row", axis=1, tiled=True),
        w_o,
        preferred_element_type=jnp.float32,
    )
    regrouped = lax.all_to_all(partial_out, "row", split_axis=1, concat_axis=2, tiled=True)
    return lax.psum_scatter(regrouped, "head", scatter_dimension=2, tiled=True).astype(jnp.bfloat16)


def on_device(
    q_nope,
    q_rope,
    new_latent,
    new_rope,
    latent_pages,
    rope_pages,
    dest_rows,
    dest_slots,
    page_table,
    lengths,
    w_uk,
    w_uv,
    w_o,
):
    row_count = lax.axis_size("row")
    rows_dev, pages_row = page_table.shape
    page_count, page_len, latent_w = latent_pages.shape
    rope_w = new_rope.shape[-1]
    page_bound = 2 * (page_count // row_count) + min(page_count % row_count, 1)
    target_dev = dest_rows // rows_dev
    local_slot = dest_rows % rows_dev * pages_row + dest_slots
    owners = (target_dev[:, None] == jnp.arange(row_count, dtype=jnp.int32)[None, :]).astype(
        jnp.int32
    )
    send_rank = jnp.sum((jnp.cumsum(owners, axis=0) - owners) * owners, axis=1)
    slot_labels = (
        jnp.full((row_count, page_bound), rows_dev * pages_row, jnp.int32)
        .at[target_dev, send_rank]
        .set(local_slot)
    )
    send_latent = (
        jnp.zeros((row_count, page_bound, page_len, latent_w), latent_pages.dtype)
        .at[target_dev, send_rank]
        .set(latent_pages)
    )
    send_rope = (
        jnp.zeros((row_count, page_bound, page_len * rope_w), rope_pages.dtype)
        .at[target_dev, send_rank]
        .set(rope_pages)
    )
    got_latent, got_rope, got_labels = (
        lax.all_to_all(send_latent, "row", split_axis=0, concat_axis=0, tiled=True),
        lax.all_to_all(send_rope, "row", split_axis=0, concat_axis=0, tiled=True),
        lax.all_to_all(slot_labels, "row", split_axis=0, concat_axis=0, tiled=True),
    )
    flat_labels = got_labels.reshape(-1)
    cache_lat = (
        jnp.zeros((rows_dev * pages_row, page_len, latent_w), latent_pages.dtype)
        .at[flat_labels]
        .set(got_latent.reshape(-1, page_len, latent_w), mode="drop")
    )
    cache_lat = cache_lat.reshape(rows_dev, pages_row * page_len, latent_w)
    cache_rope = (
        jnp.zeros((rows_dev * pages_row, page_len * rope_w), rope_pages.dtype)
        .at[flat_labels]
        .set(got_rope.reshape(-1, page_len * rope_w), mode="drop")
    )
    cache_rope = cache_rope.reshape(rows_dev, pages_row * page_len, rope_w)
    usable = token_positions(page_table, page_len) < lengths[:, None]
    step_count = q_nope.shape[0]
    outputs = []
    for step_index in range(step_count):
        head_out = attend(
            q_nope[step_index : step_index + 1],
            q_rope[step_index : step_index + 1],
            new_latent,
            new_rope,
            cache_lat,
            cache_rope,
            usable,
            step_index,
            w_uk,
            w_uv,
        )
        outputs.append(project(head_out, w_o))
    mixed_out = jnp.concatenate(outputs, axis=0)
    return mixed_out


def solution(mesh):
    placed = (
        P(None, "row", "head", None),
        P(None, "row", "head"),
        P(None, "row", None),
        P(None, "row", None),
        P("row", None, None),
        P("row", None),
        P("row"),
        P("row"),
        P("row", None),
        P("row"),
        P("head", None, None),
        P("head", None, None),
        P("head", "row"),
    )
    return jax.shard_map(
        on_device, mesh=mesh, in_specs=placed, out_specs=P(None, "row", "head"), check_vma=False
    )
```

profile of v0, /device:TPU:1, one launch (start us, length us, event | category | flops | bytes accessed | tf_op | source)
XLA Modules:
  0.0 745.7 jit_solution(11361533569849963729)
XLA Ops:
  6.5 0.8 fusion.105
  7.8 4.2 scatter_fusion
  12.7 11.9 %all-to-all-start = ((s32[32,1,5]{2,1,0:T(1,128)}), s32[32,1,5]{2,1,0:T(1,128)S(1)}, u32[]{:S(2)}, u32[]{:S(2)}) async-start(s32[32,1,5]{2,1,0:T(1,128)} %copy.172), calls=%async_computation | async-start | bytes 32768 | tf_op jit(solution)/shard_map/all_to_all | solution.py:113
  24.7 16.6 %scatter_fusion.3 = bf16[32,5,4096]{2,0,1:T(8,128)(2,1)S(1)} fusion(bf16[32,5,4096]{2,0,1:T(8,128)(2,1)S(1)} %broadcast_in_dim.121, s32[80]{0:T(128)S(1)} %fusion.107, bf16[80,4096]{1,0:T(8,128)(2,1)} %param.18), kind=kCustom, calls=%fused_computation.3 | custom fusion | bytes 1966720 | tf_op jit(solution)/shard_map/scatter | solution.py:108
  41.3 2.1 copy.175
  43.4 9.4 %all-to-all-start.2 = ((bf16[32,5,4096]{2,1,0:T(8,128)(2,1)}), bf16[32,5,4096]{2,1,0:T(8,128)(2,1)}, u32[]{:S(2)}, u32[]{:S(2)}) async-start(bf16[32,5,4096]{2,1,0:T(8,128)(2,1)} %copy.175), calls=%async_computation.2 | async-start | bytes 4194304 | tf_op jit(solution)/shard_map/all_to_all | solution.py:112
  52.7 5.2 broadcast_in_dim.118
  57.9 15.7 %scatter_fusion.1 = bf16[32,5,64,512]{3,2,1,0:T(8,128)(2,1)} fusion(bf16[32,5,64,512]{3,2,1,0:T(8,128)(2,1)} %broadcast_in_dim.118, s32[80]{0:T(128)S(1)} %fusion.107, bf16[80,64,512]{2,1,0:T(8,128)(2,1)} %param.17), kind=kCustom, calls=%fused_computation.1 | custom fusion | bytes 15729280 | tf_op jit(solution)/shard_map/scatter | solution.py:103
  73.6 27.9 %all-to-all-done.2 = bf16[32,5,4096]{2,1,0:T(8,128)(2,1)} async-done(((bf16[32,5,4096]{2,1,0:T(8,128)(2,1)}), bf16[32,5,4096]{2,1,0:T(8,128)(2,1)}, u32[]{:S(2)}, u32[]{:S(2)}) %all-to-all-start.2) | async-done | bytes 1310752 | tf_op jit(solution)/shard_map/all_to_all | solution.py:112
  101.4 7.1 all-to-all-start.1
  109.9 1.3 fusion.125
  111.7 1.2 fusion.123
  113.4 1.3 fusion.121
  117.4 1.8 reshape.538
  119.2 2.7 scatter_custom_fusion.4
  121.9 1.4 reshape.477
  123.3 222.1 %all-to-all-done.1 = bf16[32,5,64,512]{3,2,1,0:T(8,128)(2,1)} async-done(((bf16[32,5,64,512]{3,2,1,0:T(8,128)(2,1)}), bf16[32,5,64,512]{3,2,1,0:T(8,128)(2,1)}, u32[]{:S(2)}, u32[]{:S(2)}) %all-to-all-start.1) | async-done | bytes 10485792 | tf_op jit(solution)/shard_map/all_to_all | solution.py:111
  345.3 3.0 broadcast_in_dim.115
  348.4 28.1 %scatter_fusion.2 = bf16[80,64,512]{2,1,0:T(8,128)(2,1)} fusion(bf16[80,64,512]{2,1,0:T(8,128)(2,1)} %broadcast_in_dim.115, s32[160]{0:T(256)S(1)} %bitcast.330, bf16[160,64,512]{2,1,0:T(8,128)(2,1)} %bitcast.5), kind=kCustom, calls=%fused_computation.2 | custom fusion | bytes 31457920 | tf_op jit(solution)/shard_map/scatter | solution.py:119
  376.4 4.1 fusion.85
  380.5 2.2 fusion.82
  382.7 2.2 fusion.79
  385.0 2.2 fusion.76
  388.2 0.8 fusion.23
  390.2 42.6 %all_gather.12 = bf16[1,64,2048]{2,0,1:T(2,128)(2,1)S(1)} all-gather(bf16[1,2,2048]{2,0,1:T(2,128)(2,1)S(1)} %copy.182), channel_id=1, replica_groups=mesh['row'=32,'head'=8] {'row'}, dimensions={1}, use_global_device_ids=true | all-gather | bytes 270336 | tf_op jit(solution)/shard_map/all_gather | solution.py:61
  433.9 8.6 %all-to-all-start.3 = ((f32[1,64,224]{2,0,1:T(1,128)}), f32[1,64,224]{2,0,1:T(1,128)}, u32[]{:S(2)}, u32[]{:S(2)}) async-start(f32[1,64,224]{2,0,1:T(1,128)} %copy.183), calls=%async_computation.3 | async-start | bytes 131072 | tf_op jit(solution)/shard_map/all_to_all | solution.py:65
  442.5 1.5 fusion.122
  444.5 3.5 fusion.22
  448.5 38.9 %all_gather.13 = bf16[1,64,2048]{2,0,1:T(2,128)(2,1)S(1)} all-gather(bf16[1,2,2048]{2,0,1:T(2,128)(2,1)S(1)} %copy.193), channel_id=1, replica_groups=mesh['row'=32,'head'=8] {'row'}, dimensions={1}, use_global_device_ids=true | all-gather | bytes 270336 | tf_op jit(solution)/shard_map/all_gather | solution.py:61
  488.4 0.8 fusion.21
  491.3 1.4 fusion.20
  493.9 35.8 %all_gather.14 = bf16[1,64,2048]{2,0,1:T(2,128)(2,1)S(1)} all-gather(bf16[1,2,2048]{2,0,1:T(2,128)(2,1)S(1)} %copy.204), channel_id=1, replica_groups=mesh['row'=32,'head'=8] {'row'}, dimensions={1}, use_global_device_ids=true | all-gather | bytes 270336 | tf_op jit(solution)/shard_map/all_gather | solution.py:61
  529.7 6.9 all-to-all-start.4
  536.7 3.2 copy.230
  541.0 4.5 all-to-all-done.4
  545.5 4.7 all-to-all-start.5
  550.2 3.2 copy.231
  554.6 39.2 %all_gather.15 = bf16[1,64,2048]{2,0,1:T(2,128)(2,1)S(1)} all-gather(bf16[1,2,2048]{2,0,1:T(2,128)(2,1)S(1)} %copy.215), channel_id=1, replica_groups=mesh['row'=32,'head'=8] {'row'}, dimensions={1}, use_global_device_ids=true | all-gather | bytes 270336 | tf_op jit(solution)/shard_map/all_gather | solution.py:61
  593.8 2.5 copy.232
  596.9 15.4 %all_to_all.91 = f32[1,64,224]{2,0,1:T(1,128)S(1)} all-to-all(f32[1,64,224]{2,0,1:T(1,128)S(1)} %copy.216), channel_id=1, replica_groups=mesh['row'=32,'head'=8] {'row'}, dimensions={1} | all-to-all | bytes 114688 | tf_op jit(solution)/shard_map/all_to_all | solution.py:65
  612.3 2.5 copy.233
  614.9 1.3 copy.223
  616.2 39.3 %reduce-scatter.15.cloned.1.call-done = f32[896,2]{1,0:T(8,128)} async-done(((f32[7168,2]{1,0:T(8,128)}), f32[896,2]{1,0:T(8,128)}) %reduce-scatter.15.cloned.1.call-update) | async-done | bytes 7184
  655.6 1.2 copy.225
  656.8 39.9 %reduce-scatter.17.cloned.1.call-done = f32[896,2]{1,0:T(8,128)} async-done(((f32[7168,2]{1,0:T(8,128)}), f32[896,2]{1,0:T(8,128)}) %reduce-scatter.17.cloned.1.call-update) | async-done | bytes 7184
  696.7 1.2 copy.227
  697.8 39.5 %reduce-scatter.19.cloned.1.call-done = f32[896,2]{1,0:T(8,128)} async-done(((f32[7168,2]{1,0:T(8,128)}), f32[896,2]{1,0:T(8,128)}) %reduce-scatter.19.cloned.1.call-update) | async-done | bytes 7184
  737.3 1.2 copy.229
  (160 shorter events, 18.0 us)
Async XLA Ops:
  6.5 102.8 %copy-start = (bf16[16,128,512]{2,1,0:T(8,128)(2,1)S(1)}, bf16[16,128,512]{2,1,0:T(8,128)(2,1)}, u32[]{:S(2)}) copy-start(bf16[16,128,512]{2,1,0:T(8,128)(2,1)} %param.23) | copy-start | bytes 6291460
  12.7 30.7 %all-to-all-start = ((s32[32,1,5]{2,1,0:T(1,128)}), s32[32,1,5]{2,1,0:T(1,128)S(1)}, u32[]{:S(2)}, u32[]{:S(2)}) async-start(s32[32,1,5]{2,1,0:T(1,128)} %copy.172), calls=%async_computation | async-start | bytes 32768 | tf_op jit(solution)/shard_map/all_to_all | solution.py:113
  43.4 14.5 %copy-start.11 = (s32[32,1,5]{2,1,0:T(1,128)}, s32[32,1,5]{2,1,0:T(1,128)S(1)}, u32[]{:S(2)}) copy-start(s32[32,1,5]{2,1,0:T(1,128)S(1)} %all-to-all-done) | copy-start | bytes 1924
  43.4 58.0 %all-to-all-start.2 = ((bf16[32,5,4096]{2,1,0:T(8,128)(2,1)}), bf16[32,5,4096]{2,1,0:T(8,128)(2,1)}, u32[]{:S(2)}, u32[]{:S(2)}) async-start(bf16[32,5,4096]{2,1,0:T(8,128)(2,1)} %copy.175), calls=%async_computation.2 | async-start | bytes 4194304 | tf_op jit(solution)/shard_map/all_to_all | solution.py:112
  73.6 35.0 %copy-start.25 = (bf16[4,2,1024]{2,1,0:T(2,128)(2,1)S(1)}, bf16[4,2,1024]{2,1,0:T(2,128)(2,1)}, u32[]{:S(2)}) copy-start(bf16[4,2,1024]{2,1,0:T(2,128)(2,1)} %param.14) | copy-start | bytes 49156
  73.6 35.1 %copy-start.30 = (s32[2,40]{1,0:T(2,128)S(1)}, s32[2,40]{1,0:T(2,128)}, u32[]{:S(2)}) copy-start(s32[2,40]{1,0:T(2,128)} %param.21) | copy-start | bytes 964
  73.6 35.8 %copy-start.21 = (bf16[4,2,16,128]{3,2,1,0:T(8,128)(2,1)S(1)}, bf16[4,2,16,128]{3,2,1,0:T(8,128)(2,1)}, u32[]{:S(2)}) copy-start(bf16[4,2,16,128]{3,2,1,0:T(8,128)(2,1)} %param.13) | copy-start | bytes 98308
  101.4 243.9 %all-to-all-start.1 = ((bf16[32,5,64,512]{3,2,1,0:T(8,128)(2,1)}), bf16[32,5,64,512]{3,2,1,0:T(8,128)(2,1)}, u32[]{:S(2)}, u32[]{:S(2)}) async-start(bf16[32,5,64,512]{3,2,1,0:T(8,128)(2,1)} %scatter_fusion.1), calls=%async_computation.1 | async-start | bytes 20971520 | tf_op jit(solution)/shard_map/all_to_all | solution.py:111
  108.5 1.2 copy-start.9
  108.5 1.3 copy-start.32
  108.7 2.9 copy-start.19
  109.1 2.5 copy-start.17
  109.2 4.2 copy-start.15
  109.3 5.9 copy-start.13
  112.9 3.1 copy-start.31
  112.9 3.7 copy-start.12
  376.4 4.1 copy-start.2
  384.9 2.2 copy-start.20
  385.0 2.7 copy-start.29
  387.1 0.8 copy-start.24
  387.1 0.8 copy-start.10
  388.2 1.6 copy-start.3
  389.8 43.0 %copy-start.4 = (bf16[2048,224]{0,1:T(8,128)(2,1)S(1)}, bf16[2048,224]{0,1:T(8,128)(2,1)}, u32[]{:S(2)}) copy-start(bf16[2048,224]{0,1:T(8,128)(2,1)} %param.25) | copy-start | bytes 2752516
  389.8 52.8 %copy-start.18 = (bf16[2,16,64]{2,1,0:T(8,128)(2,1)S(1)}, bf16[2,16,64]{2,1,0:T(8,128)(2,1)}, u32[]{:S(2)}) copy-start(bf16[2,16,64]{2,1,0:T(8,128)(2,1)} %copy-done.17) | copy-start | bytes 12292
  390.2 53.9 %copy-start.28 = (f32[2,16]{1,0:T(2,128)S(1)}, f32[2,16]{1,0:T(2,128)}, u32[]{:S(2)}) copy-start(f32[2,16]{1,0:T(2,128)} %get-tuple-element.25) | copy-start | bytes 388
  390.2 54.1 %copy-start.23 = (f32[1,2,16,4]{2,3,1,0:T(4,128)S(1)}, f32[1,2,16,4]{2,3,1,0:T(4,128)}, u32[]{:S(2)}) copy-start(f32[1,2,16,4]{2,3,1,0:T(4,128)} %get-tuple-element.26) | copy-start | bytes 1540
  433.9 95.8 %all-to-all-start.3 = ((f32[1,64,224]{2,0,1:T(1,128)}), f32[1,64,224]{2,0,1:T(1,128)}, u32[]{:S(2)}, u32[]{:S(2)}) async-start(f32[1,64,224]{2,0,1:T(1,128)} %copy.183), calls=%async_computation.3 | async-start | bytes 131072 | tf_op jit(solution)/shard_map/all_to_all | solution.py:65
  444.3 44.1 %slice-start = ((s8[5242880]{0:T(1024)(128)(4,1)}), s8[4194304]{0:T(1024)(128)(4,1)S(1)}, s32[]{:S(2)}) async-start(s8[5242880]{0:T(1024)(128)(4,1)} %bitcast.314), calls=%async_computation.15 | async-start | bytes 8388608
  444.5 43.9 %slice-start.1 = ((s8[5242880]{0:T(1024)(128)(4,1)}), s8[1048576]{0:T(1024)(128)(4,1)S(1)}, s32[]{:S(2)}) async-start(s8[5242880]{0:T(1024)(128)(4,1)} %bitcast.314), calls=%async_computation.16 | async-start | bytes 2097152
  448.0 39.4 %copy-start.7 = (f32[2,2560,16]{1,2,0:T(8,128)S(1)}, f32[2,2560,16]{1,2,0:T(8,128)}, u32[]{:S(2)}) copy-start(f32[2,2560,16]{1,2,0:T(8,128)} %fusion.79) | copy-start | bytes 983044
  448.0 39.4 %copy-start.16 = (bf16[2,16,64]{2,1,0:T(8,128)(2,1)S(1)}, bf16[2,16,64]{2,1,0:T(8,128)(2,1)}, u32[]{:S(2)}) copy-start(bf16[2,16,64]{2,1,0:T(8,128)(2,1)} %copy-done.15) | copy-start | bytes 12292
  448.0 39.9 %copy-start.27 = (f32[2,16]{1,0:T(2,128)S(1)}, f32[2,16]{1,0:T(2,128)}, u32[]{:S(2)}) copy-start(f32[2,16]{1,0:T(2,128)} %get-tuple-element.21) | copy-start | bytes 388
  448.0 40.1 %copy-start.22 = (f32[1,2,16,4]{2,3,1,0:T(4,128)S(1)}, f32[1,2,16,4]{2,3,1,0:T(4,128)}, u32[]{:S(2)}) copy-start(f32[1,2,16,4]{2,3,1,0:T(4,128)} %get-tuple-element.22) | copy-start | bytes 1540
  489.3 1.0 copy-start.6
  489.3 1.0 copy-start.14
  489.3 1.5 copy-start.26
  491.3 1.4 copy-start.5
  529.7 15.8 %all-to-all-start.4 = ((f32[1,64,224]{2,0,1:T(1,128)}), f32[1,64,224]{2,0,1:T(1,128)}, u32[]{:S(2)}, u32[]{:S(2)}) async-start(f32[1,64,224]{2,0,1:T(1,128)} %copy.194), calls=%async_computation.4 | async-start | bytes 131072 | tf_op jit(solution)/shard_map/all_to_all | solution.py:65
  536.6 78.3 %reduce-scatter.13.cloned.1.call-start = ((), (), s32[]{:S(2)}) async-start(), calls=%async_computation.11 | async-start | bytes 4128768
  545.5 48.3 %all-to-all-start.5 = ((f32[1,64,224]{2,0,1:T(1,128)}), f32[1,64,224]{2,0,1:T(1,128)S(1)}, u32[]{:S(2)}, u32[]{:S(2)}) async-start(f32[1,64,224]{2,0,1:T(1,128)} %copy.205), calls=%async_computation.5 | async-start | bytes 131072 | tf_op jit(solution)/shard_map/all_to_all | solution.py:65
  550.1 105.4 %reduce-scatter.15.cloned.1.call-start = ((), (), s32[]{:S(2)}) async-start(), calls=%async_computation.12 | async-start | bytes 4128768
  553.4 0.8 copy-start.8
  553.5 143.2 %reduce-scatter.17.cloned.1.call-start = ((), (), s32[]{:S(2)}) async-start(), calls=%async_computation.13 | async-start | bytes 4128768
  596.3 141.0 %reduce-scatter.19.cloned.1.call-start = ((), (), s32[]{:S(2)}) async-start(), calls=%async_computation.14 | async-start | bytes 4128768
  614.8 124.4 %copy-start.1 = (bf16[16,128,512]{2,1,0:T(8,128)(2,1)S(1)}, bf16[16,128,512]{2,1,0:T(8,128)(2,1)}, u32[]{:S(2)}) copy-start(bf16[16,128,512]{2,1,0:T(8,128)(2,1)} %param.23) | copy-start | bytes 6291460
Sparse Core Ops, SparseCore 0:
  540.0 74.8 reduce-scatter.12
  617.5 38.0 reduce-scatter.14
  658.1 38.4 reduce-scatter.16
  699.1 38.2 reduce-scatter.18
where the time goes:
time: 749 us; the launch traced here: 746 us
  waiting for transfers between devices  373 us (50%)
  blocking collectives  172 us (23%)
  local copies, waits for them, and re-layouts  103 us (14%)
  starting transfers between devices  48.7 us (7%)
  matrix products  31 us (4%)
  between operations  13.6 us (2%)
    all_to_all x1, waiting for transfers between devices, on_device(): lax.all_to_all(send_latent, 'row', split_axis=0, concat_axis=0, tiled=True)  222 us
    all_gather x4, blocking collectives, project(): lax.all_gather(head_out, 'row', axis=1, tiled=True)  157 us
    unnamed x8, waiting for transfers between devices  119 us
    scatter x1, local copies, waits for them, and re-layouts, on_device(): cache_lat = jnp.zeros((rows_dev * pages_row, page_len, latent_w), latent_...  28.1 us
    all_to_all x1, waiting for transfers between devices, on_device(): lax.all_to_all(send_rope, 'row', split_axis=0, concat_axis=0, tiled=True)  27.9 us
    all_to_all x3, starting transfers between devices, project(): lax.all_to_all(partial_out, 'row', split_axis=1, concat_axis=2, tiled=True)  20.2 us
    scatter x2, local copies, waits for them, and re-layouts, on_device(): send_rope = jnp.zeros((row_count, page_bound, page_len * rope_w), rope_pa...  18.7 us
    unnamed x78, local copies, waits for them, and re-layouts  18.5 us
  transfers between devices with their start and end apart: 10, of which 7 were waited for; matrix products, arithmetic and copies ran while one was open for 11% of the time, Pallas kernels for 0%

commit v1 on v0

v1 whole, which is shorter than its diff:
```python
import functools

import jax
import jax.numpy as jnp
from jax import lax
from jax.experimental import pallas as pl
from jax.experimental.pallas import tpu as pltpu
from jax.sharding import PartitionSpec as P

NX = 4
NZ = 8
TAIL = 128
INFO = 16
NEG = -1e30
LOG2E = 1.4426950408889634
LN2 = 0.6931471805599453

VMEM = pl.BlockSpec(memory_space=pltpu.VMEM)
SMEM = pl.BlockSpec(memory_space=pltpu.SMEM)


def call(body, out_shape, ins, scratch=(), flops=0, nbytes=0, mem=48, out_spec=VMEM):
    return pl.pallas_call(
        body,
        out_shape=out_shape,
        in_specs=[SMEM if a.dtype == jnp.int32 and a.ndim == 1 else VMEM for a in ins],
        out_specs=jax.tree.map(lambda _: out_spec, out_shape),
        scratch_shapes=list(scratch),
        compiler_params=pltpu.CompilerParams(vmem_limit_bytes=mem * 2**20),
        cost_estimate=pl.CostEstimate(flops=flops, bytes_accessed=nbytes, transcendentals=0),
    )(*ins)


def dot(a, b):
    return lax.dot_general(a, b, (((1,), (0,)), ((), ())), preferred_element_type=jnp.float32)


def dot_t(a, b):
    return lax.dot_general(a, b, (((1,), (1,)), ((), ())), preferred_element_type=jnp.float32)


def iota(shape, dim):
    return lax.broadcasted_iota(jnp.int32, shape, dim)


def pack_kernel(piece, per_pair, lat_ref, tail_ref, lane_ref, col_ref, out_ref, buf_ref, sem_ref):
    tokens, lat_w = lat_ref.shape
    pages = col_ref.shape[0]
    chunks, chunk, _ = buf_ref.shape
    dest = lane_ref[...]
    page_of = iota((1, tokens), 1) // piece
    same = (col_ref[...] == dest) & (iota((pages, tokens), 0) < page_of)
    rank = jnp.sum(same.astype(jnp.int32), axis=0, keepdims=True)
    place = (dest * per_pair + rank) * piece + iota((1, tokens), 1) % piece
    lat = lat_ref[...]
    tail = tail_ref[...]
    copies = []
    for i in range(chunks):
        pick = jnp.where(iota((chunk, tokens), 0) + i * chunk == place, 1.0, 0.0)
        pick = pick.astype(jnp.bfloat16)
        buf_ref[i, :, :lat_w] = dot(pick, lat).astype(jnp.bfloat16)
        buf_ref[i, :, lat_w:] = dot(pick, tail).astype(jnp.bfloat16)
        copy = pltpu.make_async_copy(
            buf_ref.at[i], out_ref.at[pl.ds(i * chunk, chunk)], sem_ref.at[i]
        )
        copy.start()
        copies.append(copy)
    for copy in copies:
        copy.wait()


def split3(x):
    hi = x.astype(jnp.bfloat16)
    rest = x - hi.astype(jnp.float32)
    mid = rest.astype(jnp.bfloat16)
    low = (rest - mid.astype(jnp.float32)).astype(jnp.bfloat16)
    return hi.astype(jnp.float32), mid.astype(jnp.float32), low.astype(jnp.float32)


def query_kernel(
    scale, rows, qn_ref, qtail_ref, w_ref, fresh_ref, fresh_t_ref, q_ref, part_ref, lse_ref, acc_ref
):
    heads, width, _ = qn_ref.shape
    lat_w = w_ref.shape[2]
    for head in range(heads):
        acc_ref[head * width : (head + 1) * width, :] = dot(qn_ref[head], w_ref[head])
    q_ref[:lat_w, :] = acc_ref[...].T.astype(jnp.bfloat16)
    q_ref[lat_w:, :] = qtail_ref[...].astype(jnp.float32).T.astype(jnp.bfloat16)
    scores = dot(fresh_ref[...], q_ref[...]) * scale
    shape = scores.shape
    token = iota(shape, 0)
    query = iota(shape, 1) % width
    allowed = (query % rows == token % rows) & (token // rows <= query // rows)
    scores = jnp.where(allowed, scores, NEG)
    high = jnp.max(scores, axis=0, keepdims=True)
    weights = jnp.exp(scores - high)
    total = jnp.sum(weights, axis=0, keepdims=True)
    part_ref[...] = dot(fresh_t_ref[...], weights.astype(jnp.bfloat16)) * (1.0 / total)
    lse_ref[...] = jnp.broadcast_to(high + jnp.log(total), lse_ref.shape)


def attend_kernel(scale, piece, rope_w, pages_row, place_ref, key_ref, limit_ref, *refs):
    q_refs, out_ref = refs[:-1], refs[-1]
    count = len(q_refs)
    tokens = key_ref.shape[0]
    lat_w = key_ref.shape[1] - TAIL
    tail = key_ref[:, lat_w:].astype(jnp.float32)
    lane = iota((tokens, TAIL), 1)
    label = jnp.sum(jnp.where(lane == rope_w, tail, 0.0), axis=1, keepdims=True).astype(jnp.int32)
    limit = jnp.sum(jnp.where(label == lane + 1, limit_ref[...], 0), axis=1, keepdims=True)
    usable = iota((tokens, 1), 0) % piece < limit
    second = label > pages_row
    first_bias = jnp.where(usable & ~second, 0.0, NEG)
    second_bias = jnp.where(usable & second, 0.0, NEG)
    tail = jnp.where(lane == rope_w, first_bias, tail)
    tail = jnp.where(lane == rope_w + 1, second_bias, tail)
    lat = key_ref[:, :lat_w]
    key = jnp.concatenate([lat, tail.astype(jnp.bfloat16)], axis=1)
    lat_t = lat.T
    head = place_ref[1]
    queries = q_refs[0].shape[1]
    for k in range(0, count, 2):
        query = jnp.concatenate([q_refs[k][...], q_refs[k + 1][...]], axis=1)
        scores = dot(key, query)
        high = jnp.max(scores, axis=0, keepdims=True)
        weights = jnp.exp2((scores - high) * (scale * LOG2E))
        total = jnp.sum(weights, axis=0, keepdims=True)
        part = dot(lat_t, weights.astype(jnp.bfloat16)) * (1.0 / total)
        part = part.astype(jnp.bfloat16)
        hi, mid, low = split3(high * scale + jnp.log(total))
        mark = iota((INFO, 2 * queries), 0)
        info = jnp.where(mark == 0, hi, jnp.where(mark == 1, mid, jnp.where(mark == 2, low, 0.0)))
        info = info.astype(jnp.bfloat16)
        for half in range(2):
            owner = (head - (k + half) + count) % count
            lanes = slice(half * queries, (half + 1) * queries)
            out_ref[owner, :lat_w, :] = part[:, lanes]
            out_ref[owner, lat_w:, :] = info[:, lanes]


def merge_kernel(width, fresh_ref, fresh_lse_ref, w_ref, part_ref, out_ref, lat_ref):
    heads, lat_w, value_w = w_ref.shape
    count = part_ref.shape[0]
    lses = [fresh_lse_ref[:1, :]]
    for k in range(count):
        info = part_ref[k, lat_w:, :].astype(jnp.float32)
        lses.append(jnp.sum(info, axis=0, keepdims=True))
    high = functools.reduce(jnp.maximum, lses)
    shares = [jnp.exp(lse - high) for lse in lses]
    inverse = 1.0 / functools.reduce(jnp.add, shares)
    total = fresh_ref[...] * (shares[0] * inverse)
    for k in range(count):
        total = total + part_ref[k, :lat_w, :].astype(jnp.float32) * (shares[k + 1] * inverse)
    lat_ref[...] = total.T
    for head in range(heads):
        rows = lat_ref[head * width : (head + 1) * width, :].astype(jnp.bfloat16)
        value = dot(rows, w_ref[head]).astype(jnp.bfloat16)
        for copy in range(out_ref.shape[0]):
            out_ref[copy, :, head * value_w : (head + 1) * value_w] = value


def project_kernel(width, place_ref, x_ref, *refs):
    ws, out_ref = refs[:-1], refs[-1]
    per_core = out_ref.shape[1]
    cores = out_ref.shape[0] // NX
    x = x_ref[...]
    here = place_ref[0] // NZ
    for k in range(NX):
        block = dot_t(x, ws[k][...])
        owner = (here - k + NX) % NX
        for core in range(cores):
            for i in range(per_core):
                first = (core * per_core + i) * width
                out_ref[owner * cores + core, i] = block[first : first + width]


def sum_kernel(place_ref, in_ref, *outs):
    count = len(outs)
    for j in range(count):
        i = (place_ref[0] + j) % count
        parts = [in_ref[k, i] for k in range(in_ref.shape[0])]
        outs[j][...] = functools.reduce(jnp.add, parts).astype(outs[j].dtype)


def shift(x, axis, n, k):
    if k % n == 0:
        return x
    return lax.ppermute(x, axis, [(i, (i + k) % n) for i in range(n)])


def shift_x(x, k):
    if k % NX == 0:
        return x
    return lax.ppermute(
        x,
        "row",
        [(a * NZ + b, (a + k) % NX * NZ + b) for a in range(NX) for b in range(NZ)],
    )


def on_device(
    q_nope,
    q_rope,
    new_latent,
    new_rope,
    latent_pages,
    rope_pages,
    dest_rows,
    dest_slots,
    page_table,
    lengths,
    w_uk,
    w_uv,
    w_o,
):
    bf16, f32 = jnp.bfloat16, jnp.float32
    n_row = lax.axis_size("row")
    n_head = lax.axis_size("head")
    row, head = lax.axis_index("row"), lax.axis_index("head")
    rows_dev, pages_row = page_table.shape
    pages, page_len, lat_w = latent_pages.shape
    rope_w = new_rope.shape[-1]
    steps, _, heads, nope_w = q_nope.shape
    value_w = w_uv.shape[-1]
    piece = page_len // n_head
    per_pair = 2 * (pages // n_row) + min(pages % n_row, 1)
    scale = 1.0 / (nope_w + rope_w) ** 0.5
    width = steps * rows_dev
    queries = heads * width
    tokens = pages * piece
    slots = n_row * per_pair * piece

    lat = lax.dynamic_slice_in_dim(latent_pages, head * piece, piece, axis=1)
    lat, rope_pages = lax.optimization_barrier((lat, rope_pages))
    lat = lat.reshape(tokens, lat_w)
    rope = lax.dynamic_slice_in_dim(rope_pages, head * piece * rope_w, piece * rope_w, axis=1)
    label = dest_rows % rows_dev * pages_row + dest_slots + 1
    label = jnp.repeat(label, piece)[:, None].astype(bf16)
    tail = jnp.concatenate(
        [rope.reshape(tokens, rope_w), label, jnp.zeros((tokens, TAIL - rope_w - 1), bf16)], axis=1
    )
    dest = dest_rows // rows_dev
    dest_lane = jnp.repeat(dest, piece)[None, :]
    send = call(
        functools.partial(pack_kernel, piece, per_pair),
        jax.ShapeDtypeStruct((slots, lat_w + TAIL), bf16),
        [lat, tail, dest_lane, dest[:, None]],
        scratch=[
            pltpu.VMEM((4, slots // 4, lat_w + TAIL), bf16),
            pltpu.SemaphoreType.DMA((4,)),
        ],
        flops=2 * slots * tokens * (lat_w + TAIL),
        nbytes=2 * (slots + tokens) * (lat_w + TAIL),
        out_spec=pl.BlockSpec(memory_space=pltpu.HBM),
    )
    send = send.reshape(n_row, per_pair * piece, lat_w + TAIL)
    got = lax.all_to_all(send, "row", split_axis=0, concat_axis=0, tiled=True)
    got = got.reshape(slots, lat_w + TAIL)

    place = jnp.stack([row, head]).astype(jnp.int32)
    qn = jnp.transpose(q_nope.reshape(width, heads, nope_w), (1, 0, 2))
    qr = jnp.transpose(q_rope.reshape(width, heads, rope_w), (1, 0, 2)).reshape(queries, rope_w)
    row_lane = jnp.arange(TAIL - rope_w, dtype=jnp.int32)[None, :]
    row_mark = (jnp.arange(queries, dtype=jnp.int32)[:, None] % rows_dev == row_lane).astype(bf16)
    q_tail = jnp.concatenate([qr, row_mark], axis=1)
    fresh = jnp.concatenate(
        [
            new_latent.reshape(width, lat_w),
            new_rope.reshape(width, rope_w),
            jnp.zeros((width, TAIL - rope_w), bf16),
        ],
        axis=1,
    )
    fresh = jnp.concatenate([fresh, jnp.zeros((-width % 16, lat_w + TAIL), bf16)], axis=0)
    query, fresh_part, fresh_lse = call(
        functools.partial(query_kernel, scale, rows_dev),
        (
            jax.ShapeDtypeStruct((lat_w + TAIL, queries), bf16),
            jax.ShapeDtypeStruct((lat_w, queries), f32),
            jax.ShapeDtypeStruct((8, queries), f32),
        ),
        [qn, q_tail, w_uk, fresh, fresh[:, :lat_w].T],
        scratch=[pltpu.VMEM((queries, lat_w), f32)],
        flops=2 * queries * nope_w * lat_w,
        nbytes=2 * heads * nope_w * lat_w,
    )
    all_queries = [shift(query, "head", n_head, k) for k in range(n_head)]
    w_cols = [shift_x(w_o.T, k) for k in range(NX)]

    slot_ids = jnp.arange(pages_row, dtype=jnp.int32)
    holds = (page_table[:, :, None] == slot_ids[None, None, :]).astype(jnp.int32)
    logical = jnp.sum(holds * slot_ids[None, :, None], axis=1)
    limit = lengths[:, None] - logical * page_len - head * piece
    limit = jnp.pad(limit.reshape(1, rows_dev * pages_row), ((0, 0), (0, TAIL - rows_dev * pages_row)))

    parts = call(
        functools.partial(attend_kernel, scale, piece, rope_w, pages_row),
        jax.ShapeDtypeStruct((n_head, lat_w + INFO, queries), bf16),
        [place, got, limit] + all_queries,
        flops=2 * n_head * queries * slots * (2 * lat_w + TAIL),
        nbytes=2 * (slots + 2 * n_head * queries) * (lat_w + TAIL),
    )
    parts = lax.all_to_all(parts, "head", split_axis=0, concat_axis=0, tiled=True)
    head_out = call(
        functools.partial(merge_kernel, width),
        jax.ShapeDtypeStruct((NZ, width, heads * value_w), bf16),
        [fresh_part, fresh_lse, w_uv, parts],
        scratch=[pltpu.VMEM((queries, lat_w), f32)],
        flops=2 * queries * lat_w * value_w,
        nbytes=2 * heads * lat_w * value_w,
    )

    rings = [[a * NZ + b for b in range(NZ)] for a in range(NX)]
    ring = lax.all_to_all(
        head_out, "row", split_axis=0, concat_axis=0, axis_index_groups=rings, tiled=True
    )
    cols = w_o.shape[1]
    cores = n_head // NX
    per_core = NZ // cores
    sums = call(
        functools.partial(project_kernel, width),
        jax.ShapeDtypeStruct((n_head, per_core, width, cols), f32),
        [place, ring.reshape(NZ * width, heads * value_w)] + w_cols,
        flops=2 * NX * NZ * width * w_o.size,
        nbytes=2 * NX * w_o.size,
    )
    sums = lax.all_to_all(sums, "head", split_axis=0, concat_axis=0, tiled=True)
    pieces = call(
        sum_kernel,
        tuple(jax.ShapeDtypeStruct((width, cols), bf16) for _ in range(per_core)),
        [place, sums],
    )
    moved = []
    for j in range(per_core):
        pairs = []
        for r in range(n_row):
            for h in range(n_head):
                ring_at, (a, i) = r // NZ, divmod(r % NZ, per_core)
                y, c = divmod(h, cores)
                to_row = ring_at * NZ + c * per_core + (i + j) % per_core
                pairs.append((r * n_head + h, to_row * n_head + y * cores + a))
        moved.append(lax.ppermute(pieces[j], ("row", "head"), pairs))
    blocks = []
    for i in range(per_core):
        turn = (row - i) % per_core
        block = moved[0]
        for j in range(1, per_core):
            block = jnp.where(turn == j, moved[j], block)
        blocks.append(block)
    out = jnp.concatenate(blocks, axis=1)
    return out.reshape(steps, rows_dev, per_core * cols)


def solution(mesh):
    placed = (
        P(None, "row", "head", None),
        P(None, "row", "head"),
        P(None, "row", None),
        P(None, "row", None),
        P("row", None, None),
        P("row", None),
        P("row"),
        P("row"),
        P("row", None),
        P("row"),
        P("head", None, None),
        P("head", None, None),
        P("head", "row"),
    )
    return jax.shard_map(
        on_device, mesh=mesh, in_specs=placed, out_specs=P(None, "row", "head"), check_vma=False
    )
```

time: 749 us -> 153 us (0.20)
  waiting for transfers between devices: 373 us -> 66.5 us
  blocking collectives: 172 us -> 11.9 us
  local copies, waits for them, and re-layouts: 103 us -> 5.99 us
  matrix products: 31 us -> 0 us
  Pallas kernels: 0 us -> 19.4 us
  between operations: 13.6 us -> 0.36 us
    all_to_all x6 -> x3, waiting for transfers between devices: 254 us -> 28.9 us  [the longest x1 16.2 us: on_device(): got = lax.all_to_all(send, 'row', split_axis=0, concat_axis=0, tiled=True)]
    all_gather x4 -> x0, blocking collectives: 157 us -> none  [project(): lax.all_gather(head_out, 'row', axis=1, tiled=True)]
    unnamed x8 -> x0, waiting for transfers between devices: 119 us -> none
    scatter x6 -> x0, local copies, waits for them, and re-layouts: 69.3 us -> none  [the longest x1 28.1 us: on_device(): cache_lat = jnp.zeros((rows_dev * pages_row, page_len, latent_w), latent_...]
    ppermute x0 -> x14, waiting for transfers between devices: none -> 37.6 us  [the longest x3 21 us: shift_x(): lax.ppermute(x, 'row', [(a * NZ + b, (a + k) % NX * NZ + b) for a in rang...]
    dot_general x36 -> x0, matrix products: 31 us -> none  [the longest x4 10.7 us: attend(): jnp.einsum('srhl,rkl->srhk', absorbed, cache_lat, preferred_element_type=...]
    all_to_all x6 -> x3, starting transfers between devices: 48.5 us -> 23.8 us  [the longest x1 12.1 us: on_device(): got = lax.all_to_all(send, 'row', split_axis=0, concat_axis=0, tiled=True)]
    ppermute x0 -> x14, starting transfers between devices: none -> 22.9 us  [the longest x4 11.7 us: on_device(): moved.append(lax.ppermute(pieces[j], ('row', 'head'), pairs))]
  transfers between devices with their start and end apart: 10 -> 17, of which waited for: 7 -> 10; matrix products, arithmetic and copies ran while one was open for 11% -> 1% of each run, Pallas kernels for 0% -> 1%
where the time goes in v1:
time: 153 us; the launch traced here: 152 us
  waiting for transfers between devices  66.5 us (43%)
  starting transfers between devices  46.7 us (31%)
  Pallas kernels  19.4 us (13%)
  blocking collectives  11.9 us (8%)
  local copies, waits for them, and re-layouts  5.99 us (4%)
    ppermute x3, waiting for transfers between devices, shift_x(): lax.ppermute(x, 'row', [(a * NZ + b, (a + k) % NX * NZ + b) for a in rang...  21 us
    pallas_call x6, Pallas kernels, call(): pl.pallas_call(body, out_shape=out_shape, in_specs=[SMEM if a.dtype == jn...  19.4 us
    all_to_all x1, waiting for transfers between devices, on_device(): got = lax.all_to_all(send, 'row', split_axis=0, concat_axis=0, tiled=True)  16.2 us
    all_to_all x1, waiting for transfers between devices, on_device(): lax.all_to_all(parts, 'head', split_axis=0, concat_axis=0, tiled=True)  12.8 us
    all_to_all x1, starting transfers between devices, on_device(): got = lax.all_to_all(send, 'row', split_axis=0, concat_axis=0, tiled=True)  12.1 us
    all_to_all x1, blocking collectives, on_device(): sums = lax.all_to_all(sums, 'head', split_axis=0, concat_axis=0, tiled=True)  11.9 us
    ppermute x4, starting transfers between devices, on_device(): moved.append(lax.ppermute(pieces[j], ('row', 'head'), pairs))  11.7 us
    ppermute x7, waiting for transfers between devices, shift(): return lax.ppermute(x, axis, [(i, (i + k) % n) for i in range(n)])  11.6 us
  transfers between devices with their start and end apart: 17, of which 10 were waited for; matrix products, arithmetic and copies ran while one was open for 1% of the time, Pallas kernels for 1%

profile of v1, /device:TPU:1, one launch (start us, length us, event | category | flops | bytes accessed | tf_op | source)
XLA Modules:
  0.0 152.2 jit_solution(15087151204229250597)
XLA Ops:
  0.0 1.2 constant_dynamic-slice_fusion.1
  1.2 0.7 and_select_fusion
  2.0 0.2 convert_element_type.22
  2.2 0.1 reshape.100
  2.4 0.1 broadcast_in_dim_reshape.4.lane_ref
  2.5 0.1 copy.38.col_ref
  2.7 0.1 maximum_maximum_fusion.tail_ref
  2.8 3.3 %shard_map.128 = bf16[1280,640]{1,0:T(8,128)(2,1)S(1)} custom-call(bf16[640,512]{1,0:T(8,128)(2,1)S(1)} %bitcast.25, bf16[640,128]{1,0:T(8,128)(2,1)S(1)} %maximum_maximum_fusion.tail_ref, s32[1,640]{1,0:T(1,128)S(1)} %broadcast_in_dim_reshape.4.lane_ref, s32[80,1]{1,0:T(8,128)S(1)} %copy.38.col_ref), custom_call_target="tpu_custom_call" | custom-call | flops 1048576000 | bytes 2457600 | tf_op jit(solution)/shard_map/pallas_call | solution.py:23
  6.2 1.2 copy-done.3
  7.3 12.1 %all-to-all-start = ((bf16[32,40,640]{2,1,0:T(8,128)(2,1)}), bf16[32,40,640]{2,1,0:T(8,128)(2,1)}, u32[]{:S(2)}, u32[]{:S(2)}) async-start(bf16[32,40,640]{2,1,0:T(8,128)(2,1)} %bitcast.19), calls=%async_computation | async-start | bytes 3276800 | tf_op jit(solution)/shard_map/all_to_all | solution.py:257
  19.6 0.1 reshape.95
  19.8 0.2 copy.35
  20.0 0.1 copy.40
  20.1 0.1 fusion
  20.2 0.1 pad_maximum_fusion.qtail_ref
  20.3 0.8 shard_map.127
  21.2 2.1 %collective-permute-start = (bf16[640,128]{1,0:T(8,128)(2,1)S(1)}, bf16[640,128]{1,0:T(8,128)(2,1)S(1)}, u32[]{:S(2)}, u32[]{:S(2)}) collective-permute-start(bf16[640,128]{1,0:T(8,128)(2,1)S(1)} %get-tuple-element.18.refs_0_), channel_id=1, source_target_pairs={{0,1},{1,2},{2,3},{3,4},{4,5},{5,6},{6,7},{7,0},{8,9},{9,10},{10,1... | collective-permute-start | bytes 491528 | tf_op jit(solution)/shard_map/ppermute | solution.py:188
  23.3 1.3 collective-permute-start.1
  24.6 1.7 %collective-permute-start.2 = (bf16[640,128]{1,0:T(8,128)(2,1)S(1)}, bf16[640,128]{1,0:T(8,128)(2,1)S(1)}, u32[]{:S(2)}, u32[]{:S(2)}) collective-permute-start(bf16[640,128]{1,0:T(8,128)(2,1)S(1)} %get-tuple-element.18.refs_0_), channel_id=1, source_target_pairs={{0,3},{1,4},{2,5},{3,6},{4,7},{5,0},{6,1},{7,2},{8,11},{9,12},{10,... | collective-permute-start | bytes 491528 | tf_op jit(solution)/shard_map/ppermute | solution.py:188
  26.3 0.4 collective-permute-start.3
  26.7 1.9 %collective-permute-start.4 = (bf16[640,128]{1,0:T(8,128)(2,1)S(1)}, bf16[640,128]{1,0:T(8,128)(2,1)S(1)}, u32[]{:S(2)}, u32[]{:S(2)}) collective-permute-start(bf16[640,128]{1,0:T(8,128)(2,1)S(1)} %get-tuple-element.18.refs_0_), channel_id=1, source_target_pairs={{0,5},{1,6},{2,7},{3,0},{4,1},{5,2},{6,3},{7,4},{8,13},{9,14},{10,... | collective-permute-start | bytes 491528 | tf_op jit(solution)/shard_map/ppermute | solution.py:188
  28.6 0.1 select_reduce_fusion
  28.7 1.1 collective-permute-start.5
  29.8 2.7 %collective-permute-done.1.refs_2_ = bf16[640,128]{1,0:T(8,128)(2,1)S(1)} collective-permute-done((bf16[640,128]{1,0:T(8,128)(2,1)S(1)}, bf16[640,128]{1,0:T(8,128)(2,1)S(1)}, u32[]{:S(2)}, u32[]{:S(2)}) %collective-permute-start.1) | collective-permute-done | bytes 163872 | tf_op jit(solution)/shard_map/ppermute | solution.py:188
  32.7 1.1 collective-permute-done.2.refs_3_
  33.8 6.9 %collective-permute-done.3.refs_4_ = bf16[640,128]{1,0:T(8,128)(2,1)S(1)} collective-permute-done((bf16[640,128]{1,0:T(8,128)(2,1)S(1)}, bf16[640,128]{1,0:T(8,128)(2,1)S(1)}, u32[]{:S(2)}, u32[]{:S(2)}) %collective-permute-start.3) | collective-permute-done | bytes 163872 | tf_op jit(solution)/shard_map/ppermute | solution.py:188
  40.7 0.6 collective-permute-done.4.refs_5_
  41.3 0.3 collective-permute-done.6.refs_7_
  41.6 16.2 %all-to-all-done = bf16[32,40,640]{2,1,0:T(8,128)(2,1)} async-done(((bf16[32,40,640]{2,1,0:T(8,128)(2,1)}), bf16[32,40,640]{2,1,0:T(8,128)(2,1)}, u32[]{:S(2)}, u32[]{:S(2)}) %all-to-all-start) | async-done | bytes 1638432 | tf_op jit(solution)/shard_map/all_to_all | solution.py:257
  57.8 10.3 %shard_map.129 = bf16[8,528,128]{2,1,0:T(8,128)(2,1)} custom-call(s32[2]{0:T(128)S(1)} %pad_add_fusion.place_ref, bf16[1280,640]{1,0:T(8,128)(2,1)} %bitcast.11.key_ref, s32[1,128]{1,0:T(1,128)S(1)} %pad.5.limit_ref, bf16[640,128]{1,0:T(8,128)(2,1)S(1)} %get-tuple-element.18.refs_0_, bf16[640,128]{1,0:T(8,128)(2,1)S(1)} %collective-permute-done.refs_1_, ...), custom_call_target="tpu_custom_call" | custom-call | flops 3019898880 | bytes 4259840 | tf_op jit(solution)/shard_map/pallas_call | solution.py:23
  68.1 7.9 %all-to-all-start.1 = ((bf16[8,528,128]{2,1,0:T(8,128)(2,1)}), bf16[8,528,128]{2,1,0:T(8,128)(2,1)S(1)}, u32[]{:S(2)}, u32[]{:S(2)}) async-start(bf16[8,528,128]{2,1,0:T(8,128)(2,1)} %shard_map.129), calls=%async_computation.1 | async-start | bytes 2162688 | tf_op jit(solution)/shard_map/all_to_all | solution.py:303
  76.0 1.7 %collective-permute-start.8 = (bf16[224,2048]{1,0:T(8,128)(2,1)S(1)}, bf16[224,2048]{1,0:T(8,128)(2,1)}, u32[]{:S(2)}, u32[]{:S(2)}) collective-permute-start(bf16[224,2048]{1,0:T(8,128)(2,1)S(1)} %bitcast.22), channel_id=1, source_target_pairs={{0,128},{8,136},{16,144},{24,152},{32,160},{40,168},{48,176},{56,1... | collective-permute-start | bytes 2752520 | tf_op jit(solution)/shard_map/ppermute | solution.py:194
  77.7 1.0 collective-permute-start.9
  78.7 12.8 %all-to-all-done.1.part_ref = bf16[8,528,128]{2,1,0:T(8,128)(2,1)S(1)} async-done(((bf16[8,528,128]{2,1,0:T(8,128)(2,1)}), bf16[8,528,128]{2,1,0:T(8,128)(2,1)S(1)}, u32[]{:S(2)}, u32[]{:S(2)}) %all-to-all-start.1) | async-done | bytes 1081376 | tf_op jit(solution)/shard_map/all_to_all | solution.py:303
  91.4 1.6 %copy-done.2 = bf16[16,512,128]{2,1,0:T(8,128)(2,1)S(1)} copy-done((bf16[16,512,128]{2,1,0:T(8,128)(2,1)S(1)}, bf16[16,512,128]{2,1,0:T(8,128)(2,1)}, u32[]{:S(2)}) %copy-start.2) | copy-done | bytes 2097176
  93.0 1.4 shard_map.130
  94.4 3.8 %all-to-all-start.2 = ((bf16[8,8,2048]{2,1,0:T(8,128)(2,1)}), bf16[8,8,2048]{2,1,0:T(8,128)(2,1)S(1)}, u32[]{:S(2)}, u32[]{:S(2)}) async-start(bf16[8,8,2048]{2,1,0:T(8,128)(2,1)} %shard_map.130), calls=%async_computation.2 | async-start | bytes 524288 | tf_op jit(solution)/shard_map/all_to_all | solution.py:314
  98.2 20.7 %collective-permute-done.7.refs_1_ = bf16[224,2048]{1,0:T(8,128)(2,1)} collective-permute-done((bf16[224,2048]{1,0:T(8,128)(2,1)S(1)}, bf16[224,2048]{1,0:T(8,128)(2,1)}, u32[]{:S(2)}, u32[]{:S(2)}) %collective-permute-start.7) | collective-permute-done | bytes 917536 | tf_op jit(solution)/shard_map/ppermute | solution.py:194
  118.9 0.3 collective-permute-done.9.refs_3_
  119.2 3.0 %shard_map.131 = f32[8,4,8,224]{3,2,1,0:T(8,128)S(1)} custom-call(s32[2]{0:T(128)S(1)} %pad_add_fusion.place_ref, bf16[64,2048]{1,0:T(8,128)(2,1)S(1)} %bitcast.20, bf16[224,2048]{1,0:T(8,128)(2,1)S(1)} %bitcast.24, bf16[224,2048]{1,0:T(8,128)(2,1)} %collective-permute-done.7.refs_1_, bf16[224,2048]{1,0:T(8,128)(2,1)} %collective-permute-done.8.refs_2_, ...), custom_call_target="tpu_custom_call" | custom-call | flops 234881024 | bytes 3670016 | tf_op jit(solution)/shard_map/pallas_call | solution.py:23
  122.2 11.9 %all_to_all.20.in_ref = f32[8,4,8,224]{3,2,1,0:T(8,128)S(1)} all-to-all(f32[8,4,8,224]{3,2,1,0:T(8,128)S(1)} %shard_map.131), channel_id=1, replica_groups=mesh['row'=32,'head'=8] {'head'}, dimensions={0} | all-to-all | bytes 458752 | tf_op jit(solution)/shard_map/all_to_all | solution.py:327
  134.1 0.6 shard_map.132
  134.7 1.6 %collective-permute-start.10 = (bf16[8,224]{1,0:T(8,128)(2,1)S(1)}, bf16[8,224]{1,0:T(8,128)(2,1)S(1)}, u32[]{:S(2)}, u32[]{:S(2)}) collective-permute-start(bf16[8,224]{1,0:T(8,128)(2,1)S(1)} %get-tuple-element.19), channel_id=1, source_target_pairs={{0,24},{1,56},{2,26},{3,58},{4,28},{5,60},{6,30},{7,62},{8,0},{9,3... | collective-permute-start | bytes 10760 | tf_op jit(solution)/shard_map/ppermute | solution.py:342
  136.3 3.1 %collective-permute-start.11 = (bf16[8,224]{1,0:T(8,128)(2,1)S(1)}, bf16[8,224]{1,0:T(8,128)(2,1)S(1)}, u32[]{:S(2)}, u32[]{:S(2)}) collective-permute-start(bf16[8,224]{1,0:T(8,128)(2,1)S(1)} %get-tuple-element.20), channel_id=1, source_target_pairs={{0,16},{1,48},{2,18},{3,50},{4,20},{5,52},{6,22},{7,54},{8,24},{9,... | collective-permute-start | bytes 10760 | tf_op jit(solution)/shard_map/ppermute | solution.py:342
  139.4 3.2 %collective-permute-start.12 = (bf16[8,224]{1,0:T(8,128)(2,1)S(1)}, bf16[8,224]{1,0:T(8,128)(2,1)S(1)}, u32[]{:S(2)}, u32[]{:S(2)}) collective-permute-start(bf16[8,224]{1,0:T(8,128)(2,1)S(1)} %get-tuple-element.21), channel_id=1, source_target_pairs={{0,8},{1,40},{2,10},{3,42},{4,12},{5,44},{6,14},{7,46},{8,16},{9,4... | collective-permute-start | bytes 10760 | tf_op jit(solution)/shard_map/ppermute | solution.py:342
  142.6 3.7 %collective-permute-start.13 = (bf16[8,224]{1,0:T(8,128)(2,1)S(1)}, bf16[8,224]{1,0:T(8,128)(2,1)S(1)}, u32[]{:S(2)}, u32[]{:S(2)}) collective-permute-start(bf16[8,224]{1,0:T(8,128)(2,1)S(1)} %get-tuple-element.22), channel_id=1, source_target_pairs={{0,0},{1,32},{2,2},{3,34},{4,4},{5,36},{6,6},{7,38},{8,8},{9,40},{... | collective-permute-start | bytes 10760 | tf_op jit(solution)/shard_map/ppermute | solution.py:342
  146.5 5.0 %collective-permute-done.13 = bf16[8,224]{1,0:T(8,128)(2,1)S(1)} collective-permute-done((bf16[8,224]{1,0:T(8,128)(2,1)S(1)}, bf16[8,224]{1,0:T(8,128)(2,1)S(1)}, u32[]{:S(2)}, u32[]{:S(2)}) %collective-permute-start.13) | collective-permute-done | bytes 3616 | tf_op jit(solution)/shard_map/ppermute | solution.py:342
  151.5 0.6 reshape.104
  (49 shorter events, 0.8 us)
Async XLA Ops:
  0.0 2.1 %copy-start = (bf16[80,4096]{1,0:T(8,128)(2,1)S(1)}, bf16[80,4096]{1,0:T(8,128)(2,1)}, u32[]{:S(2)}) copy-start(bf16[80,4096]{1,0:T(8,128)(2,1)} %param.18) | copy-start | bytes 1966084
  6.1 1.2 copy-start.3
  7.3 12.2 %copy-start.5 = (bf16[4,2,16,128]{3,2,1,0:T(8,128)(2,1)S(1)}, bf16[4,2,16,128]{3,2,1,0:T(8,128)(2,1)}, u32[]{:S(2)}) copy-start(bf16[4,2,16,128]{3,2,1,0:T(8,128)(2,1)} %param.13) | copy-start | bytes 98308
  7.3 12.2 %copy-start.6 = (bf16[4,2,1024]{2,1,0:T(2,128)(2,1)S(1)}, bf16[4,2,1024]{2,1,0:T(2,128)(2,1)}, u32[]{:S(2)}) copy-start(bf16[4,2,1024]{2,1,0:T(2,128)(2,1)} %param.14) | copy-start | bytes 49156
  7.3 12.3 %copy-start.7 = (bf16[4,2,512]{2,1,0:T(2,128)(2,1)S(1)}, bf16[4,2,512]{2,1,0:T(2,128)(2,1)}, u32[]{:S(2)}) copy-start(bf16[4,2,512]{2,1,0:T(2,128)(2,1)} %param.15) | copy-start | bytes 24580
  7.3 12.5 %copy-start.8 = (bf16[4,2,64]{2,1,0:T(2,128)(2,1)S(1)}, bf16[4,2,64]{2,1,0:T(2,128)(2,1)}, u32[]{:S(2)}) copy-start(bf16[4,2,64]{2,1,0:T(2,128)(2,1)} %param.16) | copy-start | bytes 3076
  7.3 13.0 %copy-start.1 = (bf16[16,128,512]{2,1,0:T(8,128)(2,1)S(1)}, bf16[16,128,512]{2,1,0:T(8,128)(2,1)}, u32[]{:S(2)}) copy-start(bf16[16,128,512]{2,1,0:T(8,128)(2,1)} %w_ref.2) | copy-start | bytes 6291460
  7.3 50.4 %all-to-all-start = ((bf16[32,40,640]{2,1,0:T(8,128)(2,1)}), bf16[32,40,640]{2,1,0:T(8,128)(2,1)}, u32[]{:S(2)}, u32[]{:S(2)}) async-start(bf16[32,40,640]{2,1,0:T(8,128)(2,1)} %bitcast.19), calls=%async_computation | async-start | bytes 3276800 | tf_op jit(solution)/shard_map/all_to_all | solution.py:257
  19.5 9.1 %copy-start.9 = (s32[2,40]{1,0:T(2,128)S(1)}, s32[2,40]{1,0:T(2,128)}, u32[]{:S(2)}) copy-start(s32[2,40]{1,0:T(2,128)} %param.21) | copy-start | bytes 964
  19.5 13.0 %copy-start.10 = (s32[2]{0:T(128)S(1)}, s32[2]{0:T(128)}, u32[]{:S(2)}) copy-start(s32[2]{0:T(128)} %param.22) | copy-start | bytes 28
  21.2 7.5 %collective-permute-start = (bf16[640,128]{1,0:T(8,128)(2,1)S(1)}, bf16[640,128]{1,0:T(8,128)(2,1)S(1)}, u32[]{:S(2)}, u32[]{:S(2)}) collective-permute-start(bf16[640,128]{1,0:T(8,128)(2,1)S(1)} %get-tuple-element.18.refs_0_), channel_id=1, source_target_pairs={{0,1},{1,2},{2,3},{3,4},{4,5},{5,6},{6,7},{7,0},{8,9},{9,10},{10,1... | collective-permute-start | bytes 491528 | tf_op jit(solution)/shard_map/ppermute | solution.py:188
  23.3 9.1 %collective-permute-start.1 = (bf16[640,128]{1,0:T(8,128)(2,1)S(1)}, bf16[640,128]{1,0:T(8,128)(2,1)S(1)}, u32[]{:S(2)}, u32[]{:S(2)}) collective-permute-start(bf16[640,128]{1,0:T(8,128)(2,1)S(1)} %get-tuple-element.18.refs_0_), channel_id=1, source_target_pairs={{0,2},{1,3},{2,4},{3,5},{4,6},{5,7},{6,0},{7,1},{8,10},{9,11},{10,... | collective-permute-start | bytes 491528 | tf_op jit(solution)/shard_map/ppermute | solution.py:188
  24.6 9.2 %collective-permute-start.2 = (bf16[640,128]{1,0:T(8,128)(2,1)S(1)}, bf16[640,128]{1,0:T(8,128)(2,1)S(1)}, u32[]{:S(2)}, u32[]{:S(2)}) collective-permute-start(bf16[640,128]{1,0:T(8,128)(2,1)S(1)} %get-tuple-element.18.refs_0_), channel_id=1, source_target_pairs={{0,3},{1,4},{2,5},{3,6},{4,7},{5,0},{6,1},{7,2},{8,11},{9,12},{10,... | collective-permute-start | bytes 491528 | tf_op jit(solution)/shard_map/ppermute | solution.py:188
  26.3 14.4 %collective-permute-start.3 = (bf16[640,128]{1,0:T(8,128)(2,1)S(1)}, bf16[640,128]{1,0:T(8,128)(2,1)S(1)}, u32[]{:S(2)}, u32[]{:S(2)}) collective-permute-start(bf16[640,128]{1,0:T(8,128)(2,1)S(1)} %get-tuple-element.18.refs_0_), channel_id=1, source_target_pairs={{0,4},{1,5},{2,6},{3,7},{4,0},{5,1},{6,2},{7,3},{8,12},{9,13},{10,... | collective-permute-start | bytes 491528 | tf_op jit(solution)/shard_map/ppermute | solution.py:188
  26.7 14.7 %collective-permute-start.4 = (bf16[640,128]{1,0:T(8,128)(2,1)S(1)}, bf16[640,128]{1,0:T(8,128)(2,1)S(1)}, u32[]{:S(2)}, u32[]{:S(2)}) collective-permute-start(bf16[640,128]{1,0:T(8,128)(2,1)S(1)} %get-tuple-element.18.refs_0_), channel_id=1, source_target_pairs={{0,5},{1,6},{2,7},{3,0},{4,1},{5,2},{6,3},{7,4},{8,13},{9,14},{10,... | collective-permute-start | bytes 491528 | tf_op jit(solution)/shard_map/ppermute | solution.py:188
  28.7 12.6 %collective-permute-start.5 = (bf16[640,128]{1,0:T(8,128)(2,1)S(1)}, bf16[640,128]{1,0:T(8,128)(2,1)S(1)}, u32[]{:S(2)}, u32[]{:S(2)}) collective-permute-start(bf16[640,128]{1,0:T(8,128)(2,1)S(1)} %get-tuple-element.18.refs_0_), channel_id=1, source_target_pairs={{0,6},{1,7},{2,0},{3,1},{4,2},{5,3},{6,4},{7,5},{8,14},{9,15},{10,... | collective-permute-start | bytes 491528 | tf_op jit(solution)/shard_map/ppermute | solution.py:188
  32.5 9.2 %collective-permute-start.6 = (bf16[640,128]{1,0:T(8,128)(2,1)S(1)}, bf16[640,128]{1,0:T(8,128)(2,1)S(1)}, u32[]{:S(2)}, u32[]{:S(2)}) collective-permute-start(bf16[640,128]{1,0:T(8,128)(2,1)S(1)} %get-tuple-element.18.refs_0_), channel_id=1, source_target_pairs={{0,7},{1,0},{2,1},{3,2},{4,3},{5,4},{6,5},{7,6},{8,15},{9,8},{10,9... | collective-permute-start | bytes 491528 | tf_op jit(solution)/shard_map/ppermute | solution.py:188
  68.1 7.9 %copy-start.4 = (bf16[2048,224]{0,1:T(8,128)(2,1)S(1)}, bf16[2048,224]{0,1:T(8,128)(2,1)}, u32[]{:S(2)}) copy-start(bf16[2048,224]{0,1:T(8,128)(2,1)} %param.25) | copy-start | bytes 2752516
  68.1 23.4 %all-to-all-start.1 = ((bf16[8,528,128]{2,1,0:T(8,128)(2,1)}), bf16[8,528,128]{2,1,0:T(8,128)(2,1)S(1)}, u32[]{:S(2)}, u32[]{:S(2)}) async-start(bf16[8,528,128]{2,1,0:T(8,128)(2,1)} %shard_map.129), calls=%async_computation.1 | async-start | bytes 2162688 | tf_op jit(solution)/shard_map/all_to_all | solution.py:303
  76.0 42.9 %collective-permute-start.7 = (bf16[224,2048]{1,0:T(8,128)(2,1)S(1)}, bf16[224,2048]{1,0:T(8,128)(2,1)}, u32[]{:S(2)}, u32[]{:S(2)}) collective-permute-start(bf16[224,2048]{1,0:T(8,128)(2,1)S(1)} %bitcast.21), channel_id=1, source_target_pairs={{0,64},{8,72},{16,80},{24,88},{32,96},{40,104},{48,112},{56,120},{... | collective-permute-start | bytes 2752520 | tf_op jit(solution)/shard_map/ppermute | solution.py:194
  76.0 42.9 %collective-permute-start.8 = (bf16[224,2048]{1,0:T(8,128)(2,1)S(1)}, bf16[224,2048]{1,0:T(8,128)(2,1)}, u32[]{:S(2)}, u32[]{:S(2)}) collective-permute-start(bf16[224,2048]{1,0:T(8,128)(2,1)S(1)} %bitcast.22), channel_id=1, source_target_pairs={{0,128},{8,136},{16,144},{24,152},{32,160},{40,168},{48,176},{56,1... | collective-permute-start | bytes 2752520 | tf_op jit(solution)/shard_map/ppermute | solution.py:194
  77.7 41.5 %collective-permute-start.9 = (bf16[224,2048]{1,0:T(8,128)(2,1)S(1)}, bf16[224,2048]{1,0:T(8,128)(2,1)}, u32[]{:S(2)}, u32[]{:S(2)}) collective-permute-start(bf16[224,2048]{1,0:T(8,128)(2,1)S(1)} %bitcast.23), channel_id=1, source_target_pairs={{0,192},{8,200},{16,208},{24,216},{32,224},{40,232},{48,240},{56,2... | collective-permute-start | bytes 2752520 | tf_op jit(solution)/shard_map/ppermute | solution.py:194
  91.4 1.6 %copy-start.2 = (bf16[16,512,128]{2,1,0:T(8,128)(2,1)S(1)}, bf16[16,512,128]{2,1,0:T(8,128)(2,1)}, u32[]{:S(2)}) copy-start(bf16[16,512,128]{2,1,0:T(8,128)(2,1)} %w_ref.3) | copy-start | bytes 6291460
  94.4 24.8 %all-to-all-start.2 = ((bf16[8,8,2048]{2,1,0:T(8,128)(2,1)}), bf16[8,8,2048]{2,1,0:T(8,128)(2,1)S(1)}, u32[]{:S(2)}, u32[]{:S(2)}) async-start(bf16[8,8,2048]{2,1,0:T(8,128)(2,1)} %shard_map.130), calls=%async_computation.2 | async-start | bytes 524288 | tf_op jit(solution)/shard_map/all_to_all | solution.py:314
  134.7 11.8 %collective-permute-start.10 = (bf16[8,224]{1,0:T(8,128)(2,1)S(1)}, bf16[8,224]{1,0:T(8,128)(2,1)S(1)}, u32[]{:S(2)}, u32[]{:S(2)}) collective-permute-start(bf16[8,224]{1,0:T(8,128)(2,1)S(1)} %get-tuple-element.19), channel_id=1, source_target_pairs={{0,24},{1,56},{2,26},{3,58},{4,28},{5,60},{6,30},{7,62},{8,0},{9,3... | collective-permute-start | bytes 10760 | tf_op jit(solution)/shard_map/ppermute | solution.py:342
  136.3 10.2 %collective-permute-start.11 = (bf16[8,224]{1,0:T(8,128)(2,1)S(1)}, bf16[8,224]{1,0:T(8,128)(2,1)S(1)}, u32[]{:S(2)}, u32[]{:S(2)}) collective-permute-start(bf16[8,224]{1,0:T(8,128)(2,1)S(1)} %get-tuple-element.20), channel_id=1, source_target_pairs={{0,16},{1,48},{2,18},{3,50},{4,20},{5,52},{6,22},{7,54},{8,24},{9,... | collective-permute-start | bytes 10760 | tf_op jit(solution)/shard_map/ppermute | solution.py:342
  139.4 7.1 %collective-permute-start.12 = (bf16[8,224]{1,0:T(8,128)(2,1)S(1)}, bf16[8,224]{1,0:T(8,128)(2,1)S(1)}, u32[]{:S(2)}, u32[]{:S(2)}) collective-permute-start(bf16[8,224]{1,0:T(8,128)(2,1)S(1)} %get-tuple-element.21), channel_id=1, source_target_pairs={{0,8},{1,40},{2,10},{3,42},{4,12},{5,44},{6,14},{7,46},{8,16},{9,4... | collective-permute-start | bytes 10760 | tf_op jit(solution)/shard_map/ppermute | solution.py:342
  142.6 8.8 %collective-permute-start.13 = (bf16[8,224]{1,0:T(8,128)(2,1)S(1)}, bf16[8,224]{1,0:T(8,128)(2,1)S(1)}, u32[]{:S(2)}, u32[]{:S(2)}) collective-permute-start(bf16[8,224]{1,0:T(8,128)(2,1)S(1)} %get-tuple-element.22), channel_id=1, source_target_pairs={{0,0},{1,32},{2,2},{3,34},{4,4},{5,36},{6,6},{7,38},{8,8},{9,40},{... | collective-permute-start | bytes 10760 | tf_op jit(solution)/shard_map/ppermute | solution.py:342

commit v2 on v1

--- a/solution.py
+++ b/solution.py
@@ -17,13 +17,19 @@
 
 VMEM = pl.BlockSpec(memory_space=pltpu.VMEM)
 SMEM = pl.BlockSpec(memory_space=pltpu.SMEM)
-
-
-def call(body, out_shape, ins, scratch=(), flops=0, nbytes=0, mem=48, out_spec=VMEM):
+HBM = pl.BlockSpec(memory_space=pltpu.HBM)
+
+
+def call(
+    body, out_shape, ins, scratch=(), flops=0, nbytes=0, mem=48, out_spec=VMEM, in_hbm=()
+):
     return pl.pallas_call(
         body,
         out_shape=out_shape,
-        in_specs=[SMEM if a.dtype == jnp.int32 and a.ndim == 1 else VMEM for a in ins],
+        in_specs=[
+            HBM if i in in_hbm else SMEM if a.dtype == jnp.int32 and a.ndim == 1 else VMEM
+            for i, a in enumerate(ins)
+        ],
         out_specs=jax.tree.map(lambda _: out_spec, out_shape),
         scratch_shapes=list(scratch),
         compiler_params=pltpu.CompilerParams(vmem_limit_bytes=mem * 2**20),
@@ -43,26 +49,85 @@
     return lax.broadcasted_iota(jnp.int32, shape, dim)
 
 
-def pack_kernel(piece, per_pair, lat_ref, tail_ref, lane_ref, col_ref, out_ref, buf_ref, sem_ref):
-    tokens, lat_w = lat_ref.shape
-    pages = col_ref.shape[0]
-    chunks, chunk, _ = buf_ref.shape
-    dest = lane_ref[...]
-    page_of = iota((1, tokens), 1) // piece
-    same = (col_ref[...] == dest) & (iota((pages, tokens), 0) < page_of)
-    rank = jnp.sum(same.astype(jnp.int32), axis=0, keepdims=True)
-    place = (dest * per_pair + rank) * piece + iota((1, tokens), 1) % piece
-    lat = lat_ref[...]
-    tail = tail_ref[...]
+def ones_where(mask):
+    return jnp.where(mask, 1.0, 0.0).astype(jnp.bfloat16)
+
+
+def pack_kernel(
+    rows_dev,
+    pages_row,
+    per_pair,
+    place_ref,
+    rows_ref,
+    slots_ref,
+    lat_hbm,
+    rope_hbm,
+    out_hbm,
+    lat_buf,
+    rope_buf,
+    buf_ref,
+    in_sem,
+    out_sem,
+):
+    pages, both, lat_w = lat_buf.shape
+    piece = both // 2
+    count, block, _ = buf_ref.shape
+    chunks = out_sem.shape[0]
+    cuts = lat_w // TAIL
+    rope_rows = rope_buf.shape[1] // TAIL
+    lat_rows = per_pair * cuts * piece
+    head = place_ref[1]
+    first = pl.multiple_of(head // 2 * both, both)
+    lat_copy = pltpu.make_async_copy(lat_hbm.at[:, pl.ds(first, both), :], lat_buf, in_sem.at[0])
+    lat_copy.start()
+    lane0 = pl.multiple_of(head * rope_buf.shape[1], rope_buf.shape[1])
+    rope_copy = pltpu.make_async_copy(
+        rope_hbm.at[:, pl.ds(lane0, rope_buf.shape[1])], rope_buf, in_sem.at[1]
+    )
+    rope_copy.start()
+
+    dest = rows_ref[...] // rows_dev
+    label = (rows_ref[...] % rows_dev * pages_row + slots_ref[...] + 1).astype(jnp.float32)
+    owned = jnp.where(iota((count, pages), 0) == dest, 1.0, 0.0)
+    before = ones_where(iota((pages, pages), 0) < iota((pages, pages), 1))
+    rank = jnp.sum(owned * dot(owned.astype(jnp.bfloat16), before), axis=0, keepdims=True)
+    rank = rank.astype(jnp.int32)
+    at_slot = (dest * per_pair + rank).astype(jnp.float32).astype(jnp.bfloat16)
+    spread = ones_where(iota((pages, pages * piece), 0) == iota((pages, pages * piece), 1) // piece)
+    at_slot = dot(jnp.broadcast_to(at_slot, (8, pages)), spread)[:1].astype(jnp.int32)
+    place = at_slot * piece + iota((1, pages * piece), 1) % piece
+
+    label_lane = iota((TAIL, pages), 0)
+    named = ones_where((label_lane // piece == rank) & (label_lane < per_pair * piece))
+    labels = dot_t((owned * label).astype(jnp.bfloat16), named).astype(jnp.bfloat16)
+    rest = block - lat_rows
+    row = iota((count * rest, 1), 0)
+    tail = dot(
+        ones_where(row == iota((1, count), 1) * rest + per_pair * rope_rows), labels
+    )
+    rope_copy.wait()
+    for j in range(rope_rows):
+        pick = ones_where(row == dest * rest + rank * rope_rows + j)
+        tail = tail + dot(pick, rope_buf[:, j * TAIL : (j + 1) * TAIL])
+    buf_ref[:, lat_rows:, :] = tail.reshape(count, rest, TAIL).astype(jnp.bfloat16)
+
+    lat_copy.wait()
+    lat = lat_buf[...].astype(jnp.float32).reshape(pages, 2, piece, lat_w)
+    lat = jnp.where(head % 2 == 1, lat[:, 1], lat[:, 0]).reshape(pages * piece, lat_w)
+    lat = lat.astype(jnp.bfloat16)
+    step = count // chunks
     copies = []
     for i in range(chunks):
-        pick = jnp.where(iota((chunk, tokens), 0) + i * chunk == place, 1.0, 0.0)
-        pick = pick.astype(jnp.bfloat16)
-        buf_ref[i, :, :lat_w] = dot(pick, lat).astype(jnp.bfloat16)
-        buf_ref[i, :, lat_w:] = dot(pick, tail).astype(jnp.bfloat16)
-        copy = pltpu.make_async_copy(
-            buf_ref.at[i], out_ref.at[pl.ds(i * chunk, chunk)], sem_ref.at[i]
-        )
+        rows = step * per_pair * piece
+        value = dot(ones_where(iota((rows, 1), 0) + i * rows == place), lat)
+        value = [
+            value[:, c * TAIL : (c + 1) * TAIL].reshape(step * per_pair, 1, piece, TAIL)
+            for c in range(cuts)
+        ]
+        value = jnp.concatenate(value, axis=1).reshape(step, lat_rows, TAIL)
+        here = pl.ds(i * step, step)
+        buf_ref[here, :lat_rows, :] = value.astype(jnp.bfloat16)
+        copy = pltpu.make_async_copy(buf_ref.at[here], out_hbm.at[here], out_sem.at[i])
         copy.start()
         copies.append(copy)
     for copy in copies:
@@ -82,15 +147,19 @@
 ):
     heads, width, _ = qn_ref.shape
     lat_w = w_ref.shape[2]
+    steps = width // rows
     for head in range(heads):
-        acc_ref[head * width : (head + 1) * width, :] = dot(qn_ref[head], w_ref[head])
+        absorbed = dot(qn_ref[head], w_ref[head])
+        for row in range(rows):
+            at = (row * heads + head) * steps
+            acc_ref[at : at + steps, :] = absorbed[row * steps : (row + 1) * steps]
     q_ref[:lat_w, :] = acc_ref[...].T.astype(jnp.bfloat16)
     q_ref[lat_w:, :] = qtail_ref[...].astype(jnp.float32).T.astype(jnp.bfloat16)
     scores = dot(fresh_ref[...], q_ref[...]) * scale
     shape = scores.shape
     token = iota(shape, 0)
-    query = iota(shape, 1) % width
-    allowed = (query % rows == token % rows) & (token // rows <= query // rows)
+    query = iota(shape, 1)
+    allowed = (query // (heads * steps) == token % rows) & (token // rows <= query % steps)
     scores = jnp.where(allowed, scores, NEG)
     high = jnp.max(scores, axis=0, keepdims=True)
     weights = jnp.exp(scores - high)
@@ -99,47 +168,89 @@
     lse_ref[...] = jnp.broadcast_to(high + jnp.log(total), lse_ref.shape)
 
 
-def attend_kernel(scale, piece, rope_w, pages_row, place_ref, key_ref, limit_ref, *refs):
-    q_refs, out_ref = refs[:-1], refs[-1]
-    count = len(q_refs)
-    tokens = key_ref.shape[0]
-    lat_w = key_ref.shape[1] - TAIL
-    tail = key_ref[:, lat_w:].astype(jnp.float32)
-    lane = iota((tokens, TAIL), 1)
-    label = jnp.sum(jnp.where(lane == rope_w, tail, 0.0), axis=1, keepdims=True).astype(jnp.int32)
-    limit = jnp.sum(jnp.where(label == lane + 1, limit_ref[...], 0), axis=1, keepdims=True)
-    usable = iota((tokens, 1), 0) % piece < limit
-    second = label > pages_row
-    first_bias = jnp.where(usable & ~second, 0.0, NEG)
-    second_bias = jnp.where(usable & second, 0.0, NEG)
-    tail = jnp.where(lane == rope_w, first_bias, tail)
-    tail = jnp.where(lane == rope_w + 1, second_bias, tail)
-    lat = key_ref[:, :lat_w]
-    key = jnp.concatenate([lat, tail.astype(jnp.bfloat16)], axis=1)
-    lat_t = lat.T
-    head = place_ref[1]
-    queries = q_refs[0].shape[1]
-    for k in range(0, count, 2):
-        query = jnp.concatenate([q_refs[k][...], q_refs[k + 1][...]], axis=1)
-        scores = dot(key, query)
+def attend_kernel(
+    scale, piece, per_pair, rope_w, pages_row, place_ref, key_ref, bias_ref, q_ref, out_ref
+):
+    count, block, _ = key_ref.shape
+    n_head, _, queries = out_ref.shape
+    rows = q_ref.shape[0]
+    cuts = (q_ref.shape[1] - TAIL) // TAIL
+    lat_w = cuts * TAIL
+    pair_tokens = per_pair * piece
+    lat_rows = pair_tokens * cuts
+    rest = block - lat_rows
+    rope_rows = piece * rope_w // TAIL
+    per_row = pages_row * piece
+    half = per_row // 2
+
+    lat = key_ref[:, :lat_rows, :].astype(jnp.float32)
+    lat = lat.reshape(count * per_pair, cuts, piece, TAIL)
+    lat = [lat[:, c].reshape(count * pair_tokens, TAIL) for c in range(cuts)]
+    lat = jnp.concatenate(lat, axis=1).astype(jnp.bfloat16)
+    tail = key_ref[:, lat_rows:, :].astype(jnp.float32)
+    marked = iota(tail.shape, 1) == per_pair * rope_rows
+    labels = jnp.sum(jnp.where(marked, tail, 0.0), axis=1).astype(jnp.bfloat16)
+
+    def slot_of(columns, group, lane):
+        spread = ones_where(iota((TAIL, columns), 0) == lane)
+        wide = dot(labels, spread)
+        own = iota((count, columns), 0) == iota((1, columns), 1) // group
+        return jnp.sum(jnp.where(own, wide, 0.0), axis=0, keepdims=True).astype(jnp.int32) - 1
+
+    columns = count * pair_tokens
+    inner = iota((1, columns), 1) % pair_tokens
+    slot = slot_of(columns, pair_tokens, inner)
+    token = inner % piece
+    row = (slot >= pages_row).astype(jnp.int32)
+    target = row * (per_row - pages_row * (piece // 2)) + token % 2 * half
+    target = target + slot * (piece // 2) + token // 2
+    target = jnp.where(slot >= 0, target, -1)
+    key = dot(ones_where(iota((rows * per_row, 1), 0) == target), lat).astype(jnp.bfloat16)
+
+    columns = count * rest
+    inner = iota((1, columns), 1) % rest
+    lane = jnp.where(inner < per_pair * rope_rows, inner // rope_rows * piece, TAIL)
+    slot = slot_of(columns, rest, lane)
+    target = jnp.where(slot >= 0, slot * rope_rows + inner % rope_rows, -1)
+    tail = tail.reshape(columns, TAIL).astype(jnp.bfloat16)
+    rope = dot(ones_where(iota((rows * half, 1), 0) == target), tail)
+
+    mark = iota((half, TAIL), 1)
+    parts = []
+    for b in range(rows):
+        rope_b = rope[b * half : (b + 1) * half]
+        rope_b = jnp.concatenate([rope_b, pltpu.roll(rope_b, TAIL - rope_w, 1)], axis=0)
+        lane = iota(rope_b.shape, 1)
+        bias = bias_ref[b * per_row : (b + 1) * per_row]
+        rope_b = jnp.where(lane < rope_w, rope_b, jnp.where(lane == rope_w, bias, 0.0))
+        key_b = key[b * per_row : (b + 1) * per_row]
+        scores = dot(jnp.concatenate([key_b, rope_b.astype(jnp.bfloat16)], axis=1), q_ref[b])
         high = jnp.max(scores, axis=0, keepdims=True)
         weights = jnp.exp2((scores - high) * (scale * LOG2E))
         total = jnp.sum(weights, axis=0, keepdims=True)
-        part = dot(lat_t, weights.astype(jnp.bfloat16)) * (1.0 / total)
-        part = part.astype(jnp.bfloat16)
+        part = dot(key_b.T, weights.astype(jnp.bfloat16)) * (1.0 / total)
         hi, mid, low = split3(high * scale + jnp.log(total))
-        mark = iota((INFO, 2 * queries), 0)
+        mark = iota((INFO, part.shape[1]), 0)
         info = jnp.where(mark == 0, hi, jnp.where(mark == 1, mid, jnp.where(mark == 2, low, 0.0)))
-        info = info.astype(jnp.bfloat16)
-        for half in range(2):
-            owner = (head - (k + half) + count) % count
-            lanes = slice(half * queries, (half + 1) * queries)
-            out_ref[owner, :lat_w, :] = part[:, lanes]
-            out_ref[owner, lat_w:, :] = info[:, lanes]
-
-
-def merge_kernel(width, fresh_ref, fresh_lse_ref, w_ref, part_ref, out_ref, lat_ref):
+        parts.append(jnp.concatenate([part, info], axis=0))
+    head = place_ref[1]
+    left = iota((lat_w + INFO, queries), 1) < queries // 2
+    for k in range(0, n_head, 2):
+        lanes = slice(k * queries // 2, (k + 2) * queries // 2)
+        one, two = parts[0][:, lanes], parts[1][:, lanes]
+        ready = (
+            jnp.where(left, one, pltpu.roll(two, queries // 2, 1)),
+            jnp.where(left, pltpu.roll(one, queries // 2, 1), two),
+        )
+        for i in range(2):
+            owner = (head - (k + i) + n_head) % n_head
+            out_ref[owner] = ready[i].astype(jnp.bfloat16)
+
+
+def merge_kernel(rows_dev, fresh_ref, fresh_lse_ref, w_ref, part_ref, out_ref, lat_ref):
     heads, lat_w, value_w = w_ref.shape
+    width = out_ref.shape[1]
+    steps = width // rows_dev
     count = part_ref.shape[0]
     lses = [fresh_lse_ref[:1, :]]
     for k in range(count):
@@ -151,7 +262,10 @@
     total = fresh_ref[...] * (shares[0] * inverse)
     for k in range(count):
         total = total + part_ref[k, :lat_w, :].astype(jnp.float32) * (shares[k + 1] * inverse)
-    lat_ref[...] = total.T
+    shape = (heads * width, heads * width)
+    to, at = iota(shape, 0), iota(shape, 1)
+    wanted = (to % rows_dev * heads + to // width) * steps + to % width // rows_dev
+    lat_ref[...] = dot_t(ones_where(at == wanted), total.astype(jnp.bfloat16))
     for head in range(heads):
         rows = lat_ref[head * width : (head + 1) * width, :].astype(jnp.bfloat16)
         value = dot(rows, w_ref[head]).astype(jnp.bfloat16)
@@ -163,10 +277,21 @@
     ws, out_ref = refs[:-1], refs[-1]
     per_core = out_ref.shape[1]
     cores = out_ref.shape[0] // NX
-    x = x_ref[...]
+    depth = x_ref.shape[1] // 2
     here = place_ref[0] // NZ
-    for k in range(NX):
-        block = dot_t(x, ws[k][...])
+    own, near, far, opposite_a, opposite_b = ws
+    blocks = [
+        (0, lambda: dot_t(x_ref[...], own[...])),
+        (1, lambda: dot_t(x_ref[...], near[...])),
+        (3, lambda: dot_t(x_ref[...], far[...])),
+        (
+            2,
+            lambda: dot_t(x_ref[:, :depth], opposite_a[...])
+            + dot_t(x_ref[:, depth:], opposite_b[...]),
+        ),
+    ]
+    for k, make in blocks:
+        block = make()
         owner = (here - k + NX) % NX
         for core in range(cores):
             for i in range(per_core):
@@ -230,39 +355,36 @@
     tokens = pages * piece
     slots = n_row * per_pair * piece
 
-    lat = lax.dynamic_slice_in_dim(latent_pages, head * piece, piece, axis=1)
-    lat, rope_pages = lax.optimization_barrier((lat, rope_pages))
-    lat = lat.reshape(tokens, lat_w)
-    rope = lax.dynamic_slice_in_dim(rope_pages, head * piece * rope_w, piece * rope_w, axis=1)
-    label = dest_rows % rows_dev * pages_row + dest_slots + 1
-    label = jnp.repeat(label, piece)[:, None].astype(bf16)
-    tail = jnp.concatenate(
-        [rope.reshape(tokens, rope_w), label, jnp.zeros((tokens, TAIL - rope_w - 1), bf16)], axis=1
-    )
-    dest = dest_rows // rows_dev
-    dest_lane = jnp.repeat(dest, piece)[None, :]
+    place = jnp.stack([row, head]).astype(jnp.int32)
+    lat_rows = per_pair * piece * lat_w // TAIL
+    rope_rows = per_pair * piece * rope_w // TAIL
+    block = lat_rows + (rope_rows + 8) // 8 * 8
     send = call(
-        functools.partial(pack_kernel, piece, per_pair),
-        jax.ShapeDtypeStruct((slots, lat_w + TAIL), bf16),
-        [lat, tail, dest_lane, dest[:, None]],
+        functools.partial(pack_kernel, rows_dev, pages_row, per_pair),
+        jax.ShapeDtypeStruct((n_row, block, TAIL), bf16),
+        [place, dest_rows[None, :], dest_slots[None, :], latent_pages, rope_pages],
         scratch=[
-            pltpu.VMEM((4, slots // 4, lat_w + TAIL), bf16),
+            pltpu.VMEM((pages, 2 * piece, lat_w), bf16),
+            pltpu.VMEM((pages, piece * rope_w), bf16),
+            pltpu.VMEM((n_row, block, TAIL), bf16),
+            pltpu.SemaphoreType.DMA((2,)),
             pltpu.SemaphoreType.DMA((4,)),
         ],
-        flops=2 * slots * tokens * (lat_w + TAIL),
-        nbytes=2 * (slots + tokens) * (lat_w + TAIL),
-        out_spec=pl.BlockSpec(memory_space=pltpu.HBM),
-    )
-    send = send.reshape(n_row, per_pair * piece, lat_w + TAIL)
+        flops=2 * slots * tokens * lat_w,
+        nbytes=2 * (slots + 2 * tokens) * lat_w,
+        mem=60,
+        out_spec=HBM,
+        in_hbm=(3, 4),
+    )
     got = lax.all_to_all(send, "row", split_axis=0, concat_axis=0, tiled=True)
-    got = got.reshape(slots, lat_w + TAIL)
-
-    place = jnp.stack([row, head]).astype(jnp.int32)
-    qn = jnp.transpose(q_nope.reshape(width, heads, nope_w), (1, 0, 2))
-    qr = jnp.transpose(q_rope.reshape(width, heads, rope_w), (1, 0, 2)).reshape(queries, rope_w)
-    row_lane = jnp.arange(TAIL - rope_w, dtype=jnp.int32)[None, :]
-    row_mark = (jnp.arange(queries, dtype=jnp.int32)[:, None] % rows_dev == row_lane).astype(bf16)
-    q_tail = jnp.concatenate([qr, row_mark], axis=1)
+
+    qn = jnp.transpose(q_nope, (2, 1, 0, 3)).reshape(heads, width, nope_w)
+    qr = q_rope.reshape(steps, rows_dev, heads, rope_w)
+    qr = jnp.transpose(qr, (1, 2, 0, 3)).reshape(queries, rope_w)
+    one_lane = jnp.arange(TAIL - rope_w, dtype=jnp.int32)[None, :] == 0
+    q_tail = jnp.concatenate(
+        [qr, jnp.broadcast_to(one_lane, (queries, TAIL - rope_w)).astype(bf16)], axis=1
+    )
     fresh = jnp.concatenate(
         [
             new_latent.reshape(width, lat_w),
@@ -285,24 +407,44 @@
         nbytes=2 * heads * nope_w * lat_w,
     )
     all_queries = [shift(query, "head", n_head, k) for k in range(n_head)]
-    w_cols = [shift_x(w_o.T, k) for k in range(NX)]
+    per_row = queries // rows_dev
+    all_queries = jnp.stack(
+        [
+            jnp.concatenate([q[:, b * per_row : (b + 1) * per_row] for q in all_queries], axis=1)
+            for b in range(rows_dev)
+        ]
+    )
+
+    w_t = w_o.T
+    w_near, w_far = shift_x(w_t, 1), shift_x(w_t, -1)
+    depth = w_t.shape[1] // 2
 
     slot_ids = jnp.arange(pages_row, dtype=jnp.int32)
     holds = (page_table[:, :, None] == slot_ids[None, None, :]).astype(jnp.int32)
     logical = jnp.sum(holds * slot_ids[None, :, None], axis=1)
     limit = lengths[:, None] - logical * page_len - head * piece
-    limit = jnp.pad(limit.reshape(1, rows_dev * pages_row), ((0, 0), (0, TAIL - rows_dev * pages_row)))
-
+    within = jnp.arange(piece, dtype=jnp.int32).reshape(piece // 2, 2).T
+    usable = within[None, :, None, :] < limit[:, None, :, None]
+    bias = jnp.where(usable, 0.0, NEG).astype(f32).reshape(rows_dev * pages_row * piece, 1)
+
+    got, w_near, w_far = lax.optimization_barrier((got, w_near, w_far))
+    w_cols = [
+        w_t,
+        w_near,
+        w_far,
+        shift_x(w_near[:, :depth], 1),
+        shift_x(w_far[:, depth:], -1),
+    ]
     parts = call(
-        functools.partial(attend_kernel, scale, piece, rope_w, pages_row),
+        functools.partial(attend_kernel, scale, piece, per_pair, rope_w, pages_row),
         jax.ShapeDtypeStruct((n_head, lat_w + INFO, queries), bf16),
-        [place, got, limit] + all_queries,
-        flops=2 * n_head * queries * slots * (2 * lat_w + TAIL),
+        [place, got, bias, all_queries],
+        flops=2 * n_head * queries * tokens * (2 * lat_w + TAIL) // 2 + 2 * slots * tokens * lat_w,
         nbytes=2 * (slots + 2 * n_head * queries) * (lat_w + TAIL),
     )
     parts = lax.all_to_all(parts, "head", split_axis=0, concat_axis=0, tiled=True)
     head_out = call(
-        functools.partial(merge_kernel, width),
+        functools.partial(merge_kernel, rows_dev),
         jax.ShapeDtypeStruct((NZ, width, heads * value_w), bf16),
         [fresh_part, fresh_lse, w_uv, parts],
         scratch=[pltpu.VMEM((queries, lat_w), f32)],

time: 153 us -> 144 us (0.941)
  waiting for transfers between devices: 66.5 us -> 46.3 us
  local copies, waits for them, and re-layouts: 5.99 us -> 19.3 us
  Pallas kernels: 19.4 us -> 15.2 us
    all_to_all x1, waiting for transfers between devices: 16.2 us -> 0.01 us  [on_device(): got = lax.all_to_all(send, 'row', split_axis=0, concat_axis=0, tiled=True)]
    all_to_all x1, waiting for transfers between devices: 0.01 us -> 10.2 us  [on_device(): lax.all_to_all(head_out, 'row', split_axis=0, concat_axis=0, axis_index_g...]
    slice x0 -> x10, local copies, waits for them, and re-layouts: none -> 8.57 us  [the longest x8 4.85 us: on_device(): q[:, b * per_row:(b + 1) * per_row]]
    ppermute x7, waiting for transfers between devices: 11.6 us -> 4.91 us  [shift(): return lax.ppermute(x, axis, [(i, (i + k) % n) for i in range(n)])]
    concatenate x1 -> x3, local copies, waits for them, and re-layouts: 0.08 us -> 4.45 us  [the longest x2 4.38 us: on_device(): jnp.concatenate([q[:, b * per_row:(b + 1) * per_row] for q in all_queries...]
    pallas_call x6, Pallas kernels: 19.4 us -> 15.2 us  [call(): pl.pallas_call(body, out_shape=out_shape, in_specs=[HBM if i in in_hbm el...]
    ppermute x3 -> x4, waiting for transfers between devices: 21 us -> 17.4 us  [shift_x(): lax.ppermute(x, 'row', [(a * NZ + b, (a + k) % NX * NZ + b) for a in rang...]
    all_to_all x1, waiting for transfers between devices: 12.8 us -> 9.35 us  [on_device(): lax.all_to_all(parts, 'head', split_axis=0, concat_axis=0, tiled=True)]
  transfers between devices with their start and end apart: 17 -> 18, of which waited for: 10 -> 6; matrix products, arithmetic and copies ran while one was open for 1% -> 11% of each run, Pallas kernels for 1% -> 2%
where the time goes in v2:
time: 144 us; the launch traced here: 143 us
  starting transfers between devices  47.9 us (33%)
  waiting for transfers between devices  46.3 us (32%)
  local copies, waits for them, and re-layouts  19.3 us (13%)
  Pallas kernels  15.2 us (11%)
  blocking collectives  11.5 us (8%)
  other arithmetic  2.39 us (2%)
    ppermute x4, waiting for transfers between devices, shift_x(): lax.ppermute(x, 'row', [(a * NZ + b, (a + k) % NX * NZ + b) for a in rang...  17.4 us
    pallas_call x6, Pallas kernels, call(): pl.pallas_call(body, out_shape=out_shape, in_specs=[HBM if i in in_hbm el...  15.2 us
    all_to_all x1, starting transfers between devices, on_device(): got = lax.all_to_all(send, 'row', split_axis=0, concat_axis=0, tiled=True)  12.1 us
    ppermute x7, starting transfers between devices, shift(): return lax.ppermute(x, axis, [(i, (i + k) % n) for i in range(n)])  11.6 us
    all_to_all x1, blocking collectives, on_device(): sums = lax.all_to_all(sums, 'head', split_axis=0, concat_axis=0, tiled=True)  11.5 us
    all_to_all x1, waiting for transfers between devices, on_device(): lax.all_to_all(head_out, 'row', split_axis=0, concat_axis=0, axis_index_g...  10.2 us
    ppermute x4, starting transfers between devices, on_device(): moved.append(lax.ppermute(pieces[j], ('row', 'head'), pairs))  10.1 us
    all_to_all x1, waiting for transfers between devices, on_device(): lax.all_to_all(parts, 'head', split_axis=0, concat_axis=0, tiled=True)  9.35 us
  transfers between devices with their start and end apart: 18, of which 6 were waited for; matrix products, arithmetic and copies ran while one was open for 11% of the time, Pallas kernels for 2%

profile of v2, /device:TPU:1, one launch (start us, length us, event | category | flops | bytes accessed | tf_op | source)
XLA Modules:
  0.0 143.1 jit_solution(1162450549380373915)
XLA Ops:
  0.0 0.6 pad_add_fusion.place_ref
  0.6 4.8 %shard_map.128 = bf16[32,184,128]{2,1,0:T(8,128)(2,1)} custom-call(s32[2]{0:T(128)} %pad_add_fusion.place_ref, s32[1,80]{1,0:T(1,128)} %bitcast.25, s32[1,80]{1,0:T(1,128)} %bitcast.26, bf16[80,64,512]{2,1,0:T(8,128)(2,1)} %lat_hbm.1, bf16[80,4096]{1,0:T(8,128)(2,1)} %rope_hbm.1), custom_call_target="tpu_custom_call" | custom-call | flops 838860800 | bytes 2621440 | tf_op jit(solution)/shard_map/pallas_call | solution.py:26
  5.5 12.1 %all-to-all-start = ((bf16[32,184,128]{2,1,0:T(8,128)(2,1)}), bf16[32,184,128]{2,1,0:T(8,128)(2,1)}, u32[]{:S(2)}, u32[]{:S(2)}) async-start(bf16[32,184,128]{2,1,0:T(8,128)(2,1)} %shard_map.128), calls=%async_computation | async-start | bytes 3014656 | tf_op jit(solution)/shard_map/all_to_all | solution.py:379
  17.8 0.2 copy.32
  18.4 0.9 shard_map.127
  19.3 0.7 copy-done.7
  20.0 1.0 collective-permute-start.8
  20.9 2.7 %collective-permute-start.7 = (bf16[640,128]{1,0:T(8,128)(2,1)S(1)}, bf16[640,128]{1,0:T(8,128)(2,1)S(1)}, u32[]{:S(2)}, u32[]{:S(2)}) collective-permute-start(bf16[640,128]{1,0:T(8,128)(2,1)S(1)} %get-tuple-element.18), channel_id=1, source_target_pairs={{0,6},{1,7},{2,0},{3,1},{4,2},{5,3},{6,4},{7,5},{8,14},{9,15},{10,... | collective-permute-start | bytes 491528 | tf_op jit(solution)/shard_map/ppermute | solution.py:313
  23.6 0.6 collective-permute-start.6
  24.3 2.2 %collective-permute-start.5 = (bf16[640,128]{1,0:T(8,128)(2,1)S(1)}, bf16[640,128]{1,0:T(8,128)(2,1)S(1)}, u32[]{:S(2)}, u32[]{:S(2)}) collective-permute-start(bf16[640,128]{1,0:T(8,128)(2,1)S(1)} %get-tuple-element.18), channel_id=1, source_target_pairs={{0,4},{1,5},{2,6},{3,7},{4,0},{5,1},{6,2},{7,3},{8,12},{9,13},{10,... | collective-permute-start | bytes 491528 | tf_op jit(solution)/shard_map/ppermute | solution.py:313
  26.5 1.0 collective-permute-start.4
  28.1 0.8 collective-permute-start.3
  29.0 3.3 %collective-permute-start.2 = (bf16[640,128]{1,0:T(8,128)(2,1)S(1)}, bf16[640,128]{1,0:T(8,128)(2,1)S(1)}, u32[]{:S(2)}, u32[]{:S(2)}) collective-permute-start(bf16[640,128]{1,0:T(8,128)(2,1)S(1)} %get-tuple-element.18), channel_id=1, source_target_pairs={{0,1},{1,2},{2,3},{3,4},{4,5},{5,6},{6,7},{7,0},{8,9},{9,10},{10,1... | collective-permute-start | bytes 491528 | tf_op jit(solution)/shard_map/ppermute | solution.py:313
  32.2 0.7 fusion.1
  32.9 4.9 %collective-permute-done.6 = bf16[640,128]{1,0:T(8,128)(2,1)S(1)} collective-permute-done((bf16[640,128]{1,0:T(8,128)(2,1)S(1)}, bf16[640,128]{1,0:T(8,128)(2,1)S(1)}, u32[]{:S(2)}, u32[]{:S(2)}) %collective-permute-start.6) | collective-permute-done | bytes 163872 | tf_op jit(solution)/shard_map/ppermute | solution.py:313
  37.8 1.2 collective-permute-start
  39.0 0.8 fusion.2
  39.8 1.5 %collective-permute-start.1 = (bf16[224,2048]{1,0:T(8,128)(2,1)}, bf16[224,2048]{1,0:T(8,128)(2,1)S(1)}, u32[]{:S(2)}, u32[]{:S(2)}) collective-permute-start(bf16[224,2048]{1,0:T(8,128)(2,1)} %bitcast.10.refs_0_), channel_id=1, source_target_pairs={{0,192},{8,200},{16,208},{24,216},{32,224},{40,232},{48,240},{56,2... | collective-permute-start | bytes 2752520 | tf_op jit(solution)/shard_map/ppermute | solution.py:319
  41.3 0.8 fusion.3
  42.1 0.8 fusion.4
  42.9 0.8 fusion.5
  43.7 0.8 fusion.6
  44.4 2.3 %concatenate.21 = bf16[640,512]{1,0:T(8,128)(2,1)} concatenate(bf16[640,64]{1,0:T(8,128)(2,1)S(1)} %get-tuple-element.39, bf16[640,64]{1,0:T(8,128)(2,1)} %get-tuple-element.37, bf16[640,64]{1,0:T(8,128)(2,1)} %get-tuple-element.35, bf16[640,64]{1,0:T(8,128)(2,1)} %get-tuple-element.33, bf16[640,64]{1,0:T(8,128)(2,1)} %get-tuple-element.31, bf16[640,64]{1,0:T(8,128)(2,1)} %get-tuple-element.29, ...), dimensions={1} | concatenate | bytes 1310720 | tf_op jit(solution)/shard_map/concatenate | solution.py:413
  46.7 2.1 %concatenate.22 = bf16[640,512]{1,0:T(8,128)(2,1)} concatenate(bf16[640,64]{1,0:T(8,128)(2,1)S(1)} %get-tuple-element.40, bf16[640,64]{1,0:T(8,128)(2,1)} %get-tuple-element.38, bf16[640,64]{1,0:T(8,128)(2,1)} %get-tuple-element.36, bf16[640,64]{1,0:T(8,128)(2,1)S(1)} %copy-done.12, bf16[640,64]{1,0:T(8,128)(2,1)S(1)} %copy-done.11, bf16[640,64]{1,0:T(8,128)(2,1)S(1)} %copy-done.10, ...), dimensions={1} | concatenate | bytes 1310720 | tf_op jit(solution)/shard_map/concatenate | solution.py:413
  48.8 1.4 pad_maximum_fusion.q_ref
  50.3 16.6 %collective-permute-done.refs_1_ = bf16[224,2048]{1,0:T(8,128)(2,1)S(1)} collective-permute-done((bf16[224,2048]{1,0:T(8,128)(2,1)}, bf16[224,2048]{1,0:T(8,128)(2,1)S(1)}, u32[]{:S(2)}, u32[]{:S(2)}) %collective-permute-start) | collective-permute-done | bytes 917536 | tf_op jit(solution)/shard_map/ppermute | solution.py:319
  66.9 0.8 collective-permute-done.1.refs_2_
  67.8 0.8 copy-done.4
  68.7 4.7 %shard_map.129 = bf16[8,528,128]{2,1,0:T(8,128)(2,1)S(1)} custom-call(s32[2]{0:T(128)S(1)} %copy-done.9, bf16[32,184,128]{2,1,0:T(8,128)(2,1)} %all-to-all-done.key_ref, f32[640,1]{1,0:T(8,128)S(1)} %select_n.137.bias_ref, bf16[2,640,512]{2,1,0:T(8,128)(2,1)S(1)} %pad_maximum_fusion.q_ref), custom_call_target="tpu_custom_call" | custom-call | flops 1593835520 | bytes 4259840 | tf_op jit(solution)/shard_map/pallas_call | solution.py:26
  73.4 1.0 copy-done.6
  74.3 4.9 %all-to-all-start.1 = ((bf16[8,528,128]{2,1,0:T(8,128)(2,1)}), bf16[8,528,128]{2,1,0:T(8,128)(2,1)S(1)}, u32[]{:S(2)}, u32[]{:S(2)}) async-start(bf16[8,528,128]{2,1,0:T(8,128)(2,1)} %copy-done.6), calls=%async_computation.1 | async-start | bytes 2162688 | tf_op jit(solution)/shard_map/all_to_all | solution.py:445
  79.2 1.9 %slice.75 = bf16[224,1024]{1,0:T(8,128)(2,1)} slice(bf16[224,2048]{1,0:T(8,128)(2,1)} %copy-done.4), slice={[0:224], [1024:2048]} | slice | bytes 917504 | tf_op jit(solution)/shard_map/slice | solution.py:436
  81.1 2.4 %collective-permute-start.10 = (bf16[224,1024]{1,0:T(8,128)(2,1)}, bf16[224,1024]{1,0:T(8,128)(2,1)}, u32[]{:S(2)}, u32[]{:S(2)}) collective-permute-start(bf16[224,1024]{1,0:T(8,128)(2,1)} %slice.75), channel_id=1, source_target_pairs={{0,192},{8,200},{16,208},{24,216},{32,224},{40,232},{48,240},{56,2... | collective-permute-start | bytes 1376264 | tf_op jit(solution)/shard_map/ppermute | solution.py:319
  83.5 1.8 %slice.74 = bf16[224,1024]{1,0:T(8,128)(2,1)} slice(bf16[224,2048]{1,0:T(8,128)(2,1)} %copy-done.2), slice={[0:224], [0:1024]} | slice | bytes 917504 | tf_op jit(solution)/shard_map/slice | solution.py:435
  85.3 9.4 %all-to-all-done.1.part_ref = bf16[8,528,128]{2,1,0:T(8,128)(2,1)S(1)} async-done(((bf16[8,528,128]{2,1,0:T(8,128)(2,1)}), bf16[8,528,128]{2,1,0:T(8,128)(2,1)S(1)}, u32[]{:S(2)}, u32[]{:S(2)}) %all-to-all-start.1) | async-done | bytes 1081376 | tf_op jit(solution)/shard_map/all_to_all | solution.py:445
  94.7 1.5 %shard_map.130 = bf16[8,8,2048]{2,1,0:T(8,128)(2,1)} custom-call(f32[512,128]{1,0:T(8,128)S(1)} %copy-done.8, f32[8,128]{1,0:T(8,128)S(1)} %get-tuple-element.16.fresh_lse_ref, bf16[16,512,128]{2,1,0:T(8,128)(2,1)S(1)} %copy-done.1, bf16[8,528,128]{2,1,0:T(8,128)(2,1)S(1)} %all-to-all-done.1.part_ref), custom_call_target="tpu_custom_call" | custom-call | flops 16777216 | bytes 2097152 | tf_op jit(solution)/shard_map/pallas_call | solution.py:26
  96.2 4.2 %all-to-all-start.2 = ((bf16[8,8,2048]{2,1,0:T(8,128)(2,1)}), bf16[8,8,2048]{2,1,0:T(8,128)(2,1)S(1)}, u32[]{:S(2)}, u32[]{:S(2)}) async-start(bf16[8,8,2048]{2,1,0:T(8,128)(2,1)} %shard_map.130), calls=%async_computation.2 | async-start | bytes 524288 | tf_op jit(solution)/shard_map/all_to_all | solution.py:456
  100.3 10.2 %all-to-all-done.2 = bf16[8,8,2048]{2,1,0:T(8,128)(2,1)S(1)} async-done(((bf16[8,8,2048]{2,1,0:T(8,128)(2,1)}), bf16[8,8,2048]{2,1,0:T(8,128)(2,1)S(1)}, u32[]{:S(2)}, u32[]{:S(2)}) %all-to-all-start.2) | async-done | bytes 262176 | tf_op jit(solution)/shard_map/all_to_all | solution.py:456
  110.5 1.2 copy-done.3
  111.7 1.2 copy-done.5
  112.9 2.7 %shard_map.131 = f32[8,4,8,224]{3,2,1,0:T(8,128)S(1)} custom-call(s32[2]{0:T(128)S(1)} %copy-done.9, bf16[64,2048]{1,0:T(8,128)(2,1)S(1)} %bitcast.18, bf16[224,2048]{1,0:T(8,128)(2,1)} %bitcast.10.refs_0_, bf16[224,2048]{1,0:T(8,128)(2,1)S(1)} %copy-done.3, bf16[224,2048]{1,0:T(8,128)(2,1)S(1)} %copy-done.5, ...), custom_call_target="tpu_custom_call" | custom-call | flops 234881024 | bytes 3670016 | tf_op jit(solution)/shard_map/pallas_call | solution.py:26
  115.6 11.5 %all_to_all.20.in_ref = f32[8,4,8,224]{3,2,1,0:T(8,128)S(1)} all-to-all(f32[8,4,8,224]{3,2,1,0:T(8,128)S(1)} %shard_map.131), channel_id=1, replica_groups=mesh['row'=32,'head'=8] {'head'}, dimensions={0} | all-to-all | bytes 458752 | tf_op jit(solution)/shard_map/all_to_all | solution.py:469
  127.1 0.6 shard_map.132
  127.8 3.8 %collective-permute-start.12 = (bf16[8,224]{1,0:T(8,128)(2,1)S(1)}, bf16[8,224]{1,0:T(8,128)(2,1)S(1)}, u32[]{:S(2)}, u32[]{:S(2)}) collective-permute-start(bf16[8,224]{1,0:T(8,128)(2,1)S(1)} %get-tuple-element.22), channel_id=1, source_target_pairs={{0,16},{1,48},{2,18},{3,50},{4,20},{5,52},{6,22},{7,54},{8,24},{9,... | collective-permute-start | bytes 10760 | tf_op jit(solution)/shard_map/ppermute | solution.py:484
  131.6 1.9 %collective-permute-start.13 = (bf16[8,224]{1,0:T(8,128)(2,1)S(1)}, bf16[8,224]{1,0:T(8,128)(2,1)S(1)}, u32[]{:S(2)}, u32[]{:S(2)}) collective-permute-start(bf16[8,224]{1,0:T(8,128)(2,1)S(1)} %get-tuple-element.23), channel_id=1, source_target_pairs={{0,8},{1,40},{2,10},{3,42},{4,12},{5,44},{6,14},{7,46},{8,16},{9,4... | collective-permute-start | bytes 10760 | tf_op jit(solution)/shard_map/ppermute | solution.py:484
  133.5 4.3 %collective-permute-start.14 = (bf16[8,224]{1,0:T(8,128)(2,1)S(1)}, bf16[8,224]{1,0:T(8,128)(2,1)S(1)}, u32[]{:S(2)}, u32[]{:S(2)}) collective-permute-start(bf16[8,224]{1,0:T(8,128)(2,1)S(1)} %get-tuple-element.24), channel_id=1, source_target_pairs={{0,0},{1,32},{2,2},{3,34},{4,4},{5,36},{6,6},{7,38},{8,8},{9,40},{... | collective-permute-start | bytes 10760 | tf_op jit(solution)/shard_map/ppermute | solution.py:484
  137.9 4.4 %collective-permute-done.14 = bf16[8,224]{1,0:T(8,128)(2,1)S(1)} collective-permute-done((bf16[8,224]{1,0:T(8,128)(2,1)S(1)}, bf16[8,224]{1,0:T(8,128)(2,1)S(1)}, u32[]{:S(2)}, u32[]{:S(2)}) %collective-permute-start.14) | collective-permute-done | bytes 3616 | tf_op jit(solution)/shard_map/ppermute | solution.py:484
  142.5 0.6 reshape.99
  (69 shorter events, 1.5 us)
Async XLA Ops:
  5.5 12.2 %copy-start.15 = (bf16[4,2,512]{2,1,0:T(2,128)(2,1)S(1)}, bf16[4,2,512]{2,1,0:T(2,128)(2,1)}, u32[]{:S(2)}) copy-start(bf16[4,2,512]{2,1,0:T(2,128)(2,1)} %param.15) | copy-start | bytes 24580
  5.5 12.3 %copy-start.16 = (bf16[4,2,64]{2,1,0:T(2,128)(2,1)S(1)}, bf16[4,2,64]{2,1,0:T(2,128)(2,1)}, u32[]{:S(2)}) copy-start(bf16[4,2,64]{2,1,0:T(2,128)(2,1)} %param.16) | copy-start | bytes 3076
  5.5 12.6 %copy-start.14 = (bf16[4,2,1024]{2,1,0:T(2,128)(2,1)S(1)}, bf16[4,2,1024]{2,1,0:T(2,128)(2,1)}, u32[]{:S(2)}) copy-start(bf16[4,2,1024]{2,1,0:T(2,128)(2,1)} %param.14) | copy-start | bytes 49156
  5.5 12.8 %copy-start.13 = (bf16[4,2,16,128]{3,2,1,0:T(8,128)(2,1)S(1)}, bf16[4,2,16,128]{3,2,1,0:T(8,128)(2,1)}, u32[]{:S(2)}) copy-start(bf16[4,2,16,128]{3,2,1,0:T(8,128)(2,1)} %param.13) | copy-start | bytes 98308
  5.5 12.9 %copy-start = (bf16[16,128,512]{2,1,0:T(8,128)(2,1)S(1)}, bf16[16,128,512]{2,1,0:T(8,128)(2,1)}, u32[]{:S(2)}) copy-start(bf16[16,128,512]{2,1,0:T(8,128)(2,1)} %w_ref.2) | copy-start | bytes 6291460
  5.5 62.2 %all-to-all-start = ((bf16[32,184,128]{2,1,0:T(8,128)(2,1)}), bf16[32,184,128]{2,1,0:T(8,128)(2,1)}, u32[]{:S(2)}, u32[]{:S(2)}) async-start(bf16[32,184,128]{2,1,0:T(8,128)(2,1)} %shard_map.128), calls=%async_computation | async-start | bytes 3014656 | tf_op jit(solution)/shard_map/all_to_all | solution.py:379
  18.1 9.5 %copy-start.17 = (s32[2,40]{1,0:T(2,128)S(1)}, s32[2,40]{1,0:T(2,128)}, u32[]{:S(2)}) copy-start(s32[2,40]{1,0:T(2,128)} %param.21) | copy-start | bytes 964
  18.1 9.5 %copy-start.18 = (s32[2]{0:T(128)S(1)}, s32[2]{0:T(128)}, u32[]{:S(2)}) copy-start(s32[2]{0:T(128)} %param.22) | copy-start | bytes 28
  19.2 0.7 copy-start.7
  20.0 8.1 %collective-permute-start.8 = (bf16[640,128]{1,0:T(8,128)(2,1)S(1)}, bf16[640,128]{1,0:T(8,128)(2,1)S(1)}, u32[]{:S(2)}, u32[]{:S(2)}) collective-permute-start(bf16[640,128]{1,0:T(8,128)(2,1)S(1)} %get-tuple-element.18), channel_id=1, source_target_pairs={{0,7},{1,0},{2,1},{3,2},{4,3},{5,4},{6,5},{7,6},{8,15},{9,8},{10,9... | collective-permute-start | bytes 491528 | tf_op jit(solution)/shard_map/ppermute | solution.py:313
  20.9 8.0 %collective-permute-start.7 = (bf16[640,128]{1,0:T(8,128)(2,1)S(1)}, bf16[640,128]{1,0:T(8,128)(2,1)S(1)}, u32[]{:S(2)}, u32[]{:S(2)}) collective-permute-start(bf16[640,128]{1,0:T(8,128)(2,1)S(1)} %get-tuple-element.18), channel_id=1, source_target_pairs={{0,6},{1,7},{2,0},{3,1},{4,2},{5,3},{6,4},{7,5},{8,14},{9,15},{10,... | collective-permute-start | bytes 491528 | tf_op jit(solution)/shard_map/ppermute | solution.py:313
  23.6 14.2 %collective-permute-start.6 = (bf16[640,128]{1,0:T(8,128)(2,1)S(1)}, bf16[640,128]{1,0:T(8,128)(2,1)S(1)}, u32[]{:S(2)}, u32[]{:S(2)}) collective-permute-start(bf16[640,128]{1,0:T(8,128)(2,1)S(1)} %get-tuple-element.18), channel_id=1, source_target_pairs={{0,5},{1,6},{2,7},{3,0},{4,1},{5,2},{6,3},{7,4},{8,13},{9,14},{10,... | collective-permute-start | bytes 491528 | tf_op jit(solution)/shard_map/ppermute | solution.py:313
  24.3 15.5 %collective-permute-start.5 = (bf16[640,128]{1,0:T(8,128)(2,1)S(1)}, bf16[640,128]{1,0:T(8,128)(2,1)S(1)}, u32[]{:S(2)}, u32[]{:S(2)}) collective-permute-start(bf16[640,128]{1,0:T(8,128)(2,1)S(1)} %get-tuple-element.18), channel_id=1, source_target_pairs={{0,4},{1,5},{2,6},{3,7},{4,0},{5,1},{6,2},{7,3},{8,12},{9,13},{10,... | collective-permute-start | bytes 491528 | tf_op jit(solution)/shard_map/ppermute | solution.py:313
  26.5 15.6 %collective-permute-start.4 = (bf16[640,128]{1,0:T(8,128)(2,1)S(1)}, bf16[640,128]{1,0:T(8,128)(2,1)S(1)}, u32[]{:S(2)}, u32[]{:S(2)}) collective-permute-start(bf16[640,128]{1,0:T(8,128)(2,1)S(1)} %get-tuple-element.18), channel_id=1, source_target_pairs={{0,3},{1,4},{2,5},{3,6},{4,7},{5,0},{6,1},{7,2},{8,11},{9,12},{10,... | collective-permute-start | bytes 491528 | tf_op jit(solution)/shard_map/ppermute | solution.py:313
  28.1 14.8 %collective-permute-start.3 = (bf16[640,128]{1,0:T(8,128)(2,1)S(1)}, bf16[640,128]{1,0:T(8,128)(2,1)S(1)}, u32[]{:S(2)}, u32[]{:S(2)}) collective-permute-start(bf16[640,128]{1,0:T(8,128)(2,1)S(1)} %get-tuple-element.18), channel_id=1, source_target_pairs={{0,2},{1,3},{2,4},{3,5},{4,6},{5,7},{6,0},{7,1},{8,10},{9,11},{10,... | collective-permute-start | bytes 491528 | tf_op jit(solution)/shard_map/ppermute | solution.py:313
  29.0 14.7 %collective-permute-start.2 = (bf16[640,128]{1,0:T(8,128)(2,1)S(1)}, bf16[640,128]{1,0:T(8,128)(2,1)S(1)}, u32[]{:S(2)}, u32[]{:S(2)}) collective-permute-start(bf16[640,128]{1,0:T(8,128)(2,1)S(1)} %get-tuple-element.18), channel_id=1, source_target_pairs={{0,1},{1,2},{2,3},{3,4},{4,5},{5,6},{6,7},{7,0},{8,9},{9,10},{10,1... | collective-permute-start | bytes 491528 | tf_op jit(solution)/shard_map/ppermute | solution.py:313
  37.8 29.1 %collective-permute-start = (bf16[224,2048]{1,0:T(8,128)(2,1)}, bf16[224,2048]{1,0:T(8,128)(2,1)S(1)}, u32[]{:S(2)}, u32[]{:S(2)}) collective-permute-start(bf16[224,2048]{1,0:T(8,128)(2,1)} %bitcast.10.refs_0_), channel_id=1, source_target_pairs={{0,64},{8,72},{16,80},{24,88},{32,96},{40,104},{48,112},{56,120},{... | collective-permute-start | bytes 2752520 | tf_op jit(solution)/shard_map/ppermute | solution.py:319
  39.8 27.9 %collective-permute-start.1 = (bf16[224,2048]{1,0:T(8,128)(2,1)}, bf16[224,2048]{1,0:T(8,128)(2,1)S(1)}, u32[]{:S(2)}, u32[]{:S(2)}) collective-permute-start(bf16[224,2048]{1,0:T(8,128)(2,1)} %bitcast.10.refs_0_), channel_id=1, source_target_pairs={{0,192},{8,200},{16,208},{24,216},{32,224},{40,232},{48,240},{56,2... | collective-permute-start | bytes 2752520 | tf_op jit(solution)/shard_map/ppermute | solution.py:319
  43.7 3.1 %copy-start.10 = (bf16[640,64]{1,0:T(8,128)(2,1)S(1)}, bf16[640,64]{1,0:T(8,128)(2,1)}, u32[]{:S(2)}) copy-start(bf16[640,64]{1,0:T(8,128)(2,1)} %get-tuple-element.30) | copy-start | bytes 245764
  43.7 3.1 %copy-start.11 = (bf16[640,64]{1,0:T(8,128)(2,1)S(1)}, bf16[640,64]{1,0:T(8,128)(2,1)}, u32[]{:S(2)}) copy-start(bf16[640,64]{1,0:T(8,128)(2,1)} %get-tuple-element.32) | copy-start | bytes 245764
  43.7 3.1 %copy-start.12 = (bf16[640,64]{1,0:T(8,128)(2,1)S(1)}, bf16[640,64]{1,0:T(8,128)(2,1)}, u32[]{:S(2)}) copy-start(bf16[640,64]{1,0:T(8,128)(2,1)} %get-tuple-element.34) | copy-start | bytes 245764
  48.8 19.8 %copy-start.9 = (s32[2]{0:T(128)S(1)}, s32[2]{0:T(128)}, u32[]{:S(2)}) copy-start(s32[2]{0:T(128)} %pad_add_fusion.place_ref) | copy-start | bytes 28
  66.9 0.9 copy-start.2
  67.7 1.0 copy-start.4
  73.4 1.0 copy-start.6
  74.3 20.3 %copy-start.1 = (bf16[16,512,128]{2,1,0:T(8,128)(2,1)S(1)}, bf16[16,512,128]{2,1,0:T(8,128)(2,1)}, u32[]{:S(2)}) copy-start(bf16[16,512,128]{2,1,0:T(8,128)(2,1)} %w_ref.3) | copy-start | bytes 6291460
  74.3 20.3 %all-to-all-start.1 = ((bf16[8,528,128]{2,1,0:T(8,128)(2,1)}), bf16[8,528,128]{2,1,0:T(8,128)(2,1)S(1)}, u32[]{:S(2)}, u32[]{:S(2)}) async-start(bf16[8,528,128]{2,1,0:T(8,128)(2,1)} %copy-done.6), calls=%async_computation.1 | async-start | bytes 2162688 | tf_op jit(solution)/shard_map/all_to_all | solution.py:445
  79.2 15.5 %copy-start.8 = (f32[512,128]{1,0:T(8,128)S(1)}, f32[512,128]{1,0:T(8,128)}, u32[]{:S(2)}) copy-start(f32[512,128]{1,0:T(8,128)} %copy-done.7) | copy-start | bytes 786436
  81.1 19.2 %collective-permute-start.10 = (bf16[224,1024]{1,0:T(8,128)(2,1)}, bf16[224,1024]{1,0:T(8,128)(2,1)}, u32[]{:S(2)}, u32[]{:S(2)}) collective-permute-start(bf16[224,1024]{1,0:T(8,128)(2,1)} %slice.75), channel_id=1, source_target_pairs={{0,192},{8,200},{16,208},{24,216},{32,224},{40,232},{48,240},{56,2... | collective-permute-start | bytes 1376264 | tf_op jit(solution)/shard_map/ppermute | solution.py:319
  85.3 15.0 %collective-permute-start.9 = (bf16[224,1024]{1,0:T(8,128)(2,1)}, bf16[224,1024]{1,0:T(8,128)(2,1)}, u32[]{:S(2)}, u32[]{:S(2)}) collective-permute-start(bf16[224,1024]{1,0:T(8,128)(2,1)} %slice.74), channel_id=1, source_target_pairs={{0,64},{8,72},{16,80},{24,88},{32,96},{40,104},{48,112},{56,120},{... | collective-permute-start | bytes 1376264 | tf_op jit(solution)/shard_map/ppermute | solution.py:319
  96.2 14.4 %all-to-all-start.2 = ((bf16[8,8,2048]{2,1,0:T(8,128)(2,1)}), bf16[8,8,2048]{2,1,0:T(8,128)(2,1)S(1)}, u32[]{:S(2)}, u32[]{:S(2)}) async-start(bf16[8,8,2048]{2,1,0:T(8,128)(2,1)} %shard_map.130), calls=%async_computation.2 | async-start | bytes 524288 | tf_op jit(solution)/shard_map/all_to_all | solution.py:456
  110.5 1.2 copy-start.3
  111.7 1.2 copy-start.5
  127.7 10.2 %collective-permute-start.11 = (bf16[8,224]{1,0:T(8,128)(2,1)S(1)}, bf16[8,224]{1,0:T(8,128)(2,1)S(1)}, u32[]{:S(2)}, u32[]{:S(2)}) collective-permute-start(bf16[8,224]{1,0:T(8,128)(2,1)S(1)} %get-tuple-element.21), channel_id=1, source_target_pairs={{0,24},{1,56},{2,26},{3,58},{4,28},{5,60},{6,30},{7,62},{8,0},{9,3... | collective-permute-start | bytes 10760 | tf_op jit(solution)/shard_map/ppermute | solution.py:484
  127.8 10.1 %collective-permute-start.12 = (bf16[8,224]{1,0:T(8,128)(2,1)S(1)}, bf16[8,224]{1,0:T(8,128)(2,1)S(1)}, u32[]{:S(2)}, u32[]{:S(2)}) collective-permute-start(bf16[8,224]{1,0:T(8,128)(2,1)S(1)} %get-tuple-element.22), channel_id=1, source_target_pairs={{0,16},{1,48},{2,18},{3,50},{4,20},{5,52},{6,22},{7,54},{8,24},{9,... | collective-permute-start | bytes 10760 | tf_op jit(solution)/shard_map/ppermute | solution.py:484
  131.6 6.3 %collective-permute-start.13 = (bf16[8,224]{1,0:T(8,128)(2,1)S(1)}, bf16[8,224]{1,0:T(8,128)(2,1)S(1)}, u32[]{:S(2)}, u32[]{:S(2)}) collective-permute-start(bf16[8,224]{1,0:T(8,128)(2,1)S(1)} %get-tuple-element.23), channel_id=1, source_target_pairs={{0,8},{1,40},{2,10},{3,42},{4,12},{5,44},{6,14},{7,46},{8,16},{9,4... | collective-permute-start | bytes 10760 | tf_op jit(solution)/shard_map/ppermute | solution.py:484
  133.5 8.8 %collective-permute-start.14 = (bf16[8,224]{1,0:T(8,128)(2,1)S(1)}, bf16[8,224]{1,0:T(8,128)(2,1)S(1)}, u32[]{:S(2)}, u32[]{:S(2)}) collective-permute-start(bf16[8,224]{1,0:T(8,128)(2,1)S(1)} %get-tuple-element.24), channel_id=1, source_target_pairs={{0,0},{1,32},{2,2},{3,34},{4,4},{5,36},{6,6},{7,38},{8,8},{9,40},{... | collective-permute-start | bytes 10760 | tf_op jit(solution)/shard_map/ppermute | solution.py:484

commit v3 on v2

--- a/solution.py
+++ b/solution.py
@@ -21,7 +21,7 @@
 
 
 def call(
-    body, out_shape, ins, scratch=(), flops=0, nbytes=0, mem=48, out_spec=VMEM, in_hbm=()
+    body, out_shape, ins, scratch=(), flops=0, nbytes=0, mem=24, out_spec=VMEM, in_hbm=()
 ):
     return pl.pallas_call(
         body,
@@ -57,7 +57,6 @@
     rows_dev,
     pages_row,
     per_pair,
-    place_ref,
     rows_ref,
     slots_ref,
     lat_hbm,
@@ -76,7 +75,7 @@
     cuts = lat_w // TAIL
     rope_rows = rope_buf.shape[1] // TAIL
     lat_rows = per_pair * cuts * piece
-    head = place_ref[1]
+    head = lax.axis_index("head")
     first = pl.multiple_of(head // 2 * both, both)
     lat_copy = pltpu.make_async_copy(lat_hbm.at[:, pl.ds(first, both), :], lat_buf, in_sem.at[0])
     lat_copy.start()
@@ -143,7 +142,7 @@
 
 
 def query_kernel(
-    scale, rows, qn_ref, qtail_ref, w_ref, fresh_ref, fresh_t_ref, q_ref, part_ref, lse_ref, acc_ref
+    scale, rows, qn_ref, qtail_ref, w_ref, fresh_ref, fresh_t_ref, q_ref, swap_ref, part_ref, lse_ref, acc_ref
 ):
     heads, width, _ = qn_ref.shape
     lat_w = w_ref.shape[2]
@@ -153,8 +152,13 @@
         for row in range(rows):
             at = (row * heads + head) * steps
             acc_ref[at : at + steps, :] = absorbed[row * steps : (row + 1) * steps]
-    q_ref[:lat_w, :] = acc_ref[...].T.astype(jnp.bfloat16)
-    q_ref[lat_w:, :] = qtail_ref[...].astype(jnp.float32).T.astype(jnp.bfloat16)
+    half = rows * heads * steps // 2
+    absorbed = acc_ref[...].T
+    tail = qtail_ref[...].astype(jnp.float32).T
+    q_ref[:lat_w, :] = absorbed.astype(jnp.bfloat16)
+    q_ref[lat_w:, :] = tail.astype(jnp.bfloat16)
+    swap_ref[:lat_w, :] = pltpu.roll(absorbed, half, 1).astype(jnp.bfloat16)
+    swap_ref[lat_w:, :] = pltpu.roll(tail, half, 1).astype(jnp.bfloat16)
     scores = dot(fresh_ref[...], q_ref[...]) * scale
     shape = scores.shape
     token = iota(shape, 0)
@@ -169,12 +173,13 @@
 
 
 def attend_kernel(
-    scale, piece, per_pair, rope_w, pages_row, place_ref, key_ref, bias_ref, q_ref, out_ref
+    scale, piece, per_pair, rope_w, pages_row, key_ref, bias_ref, *refs
 ):
+    q_refs, out_ref = refs[:-1], refs[-1]
     count, block, _ = key_ref.shape
     n_head, _, queries = out_ref.shape
-    rows = q_ref.shape[0]
-    cuts = (q_ref.shape[1] - TAIL) // TAIL
+    rows = 2
+    cuts = (q_refs[0].shape[0] - TAIL) // TAIL
     lat_w = cuts * TAIL
     pair_tokens = per_pair * piece
     lat_rows = pair_tokens * cuts
@@ -215,7 +220,12 @@
     tail = tail.reshape(columns, TAIL).astype(jnp.bfloat16)
     rope = dot(ones_where(iota((rows * half, 1), 0) == target), tail)
 
-    mark = iota((half, TAIL), 1)
+    left = iota((lat_w + TAIL, queries), 1) < queries // 2
+    asked = [[], []]
+    for k in range(0, n_head, 2):
+        one, two = q_refs[k][...].astype(jnp.float32), q_refs[k + 1][...].astype(jnp.float32)
+        asked[0].append(jnp.where(left, one, two).astype(jnp.bfloat16))
+        asked[1].append(jnp.where(left, two, one).astype(jnp.bfloat16))
     parts = []
     for b in range(rows):
         rope_b = rope[b * half : (b + 1) * half]
@@ -224,7 +234,8 @@
         bias = bias_ref[b * per_row : (b + 1) * per_row]
         rope_b = jnp.where(lane < rope_w, rope_b, jnp.where(lane == rope_w, bias, 0.0))
         key_b = key[b * per_row : (b + 1) * per_row]
-        scores = dot(jnp.concatenate([key_b, rope_b.astype(jnp.bfloat16)], axis=1), q_ref[b])
+        query = jnp.concatenate(asked[b], axis=1)
+        scores = dot(jnp.concatenate([key_b, rope_b.astype(jnp.bfloat16)], axis=1), query)
         high = jnp.max(scores, axis=0, keepdims=True)
         weights = jnp.exp2((scores - high) * (scale * LOG2E))
         total = jnp.sum(weights, axis=0, keepdims=True)
@@ -233,15 +244,12 @@
         mark = iota((INFO, part.shape[1]), 0)
         info = jnp.where(mark == 0, hi, jnp.where(mark == 1, mid, jnp.where(mark == 2, low, 0.0)))
         parts.append(jnp.concatenate([part, info], axis=0))
-    head = place_ref[1]
+    head = lax.axis_index("head")
     left = iota((lat_w + INFO, queries), 1) < queries // 2
     for k in range(0, n_head, 2):
         lanes = slice(k * queries // 2, (k + 2) * queries // 2)
         one, two = parts[0][:, lanes], parts[1][:, lanes]
-        ready = (
-            jnp.where(left, one, pltpu.roll(two, queries // 2, 1)),
-            jnp.where(left, pltpu.roll(one, queries // 2, 1), two),
-        )
+        ready = (jnp.where(left, one, two), jnp.where(left, two, one))
         for i in range(2):
             owner = (head - (k + i) + n_head) % n_head
             out_ref[owner] = ready[i].astype(jnp.bfloat16)
@@ -252,16 +260,25 @@
     width = out_ref.shape[1]
     steps = width // rows_dev
     count = part_ref.shape[0]
-    lses = [fresh_lse_ref[:1, :]]
+    odd = lax.axis_index("head") % 2
+    half = part_ref.shape[2] // 2
+    lses = [fresh_lse_ref[...]]
     for k in range(count):
-        info = part_ref[k, lat_w:, :].astype(jnp.float32)
-        lses.append(jnp.sum(info, axis=0, keepdims=True))
+        info = jnp.sum(part_ref[k, lat_w:, :].astype(jnp.float32), axis=0, keepdims=True)
+        info = jnp.broadcast_to(info, lses[0].shape)
+        lses.append(jnp.where(odd != k % 2, pltpu.roll(info, half, 1), info))
     high = functools.reduce(jnp.maximum, lses)
     shares = [jnp.exp(lse - high) for lse in lses]
     inverse = 1.0 / functools.reduce(jnp.add, shares)
-    total = fresh_ref[...] * (shares[0] * inverse)
+    total = fresh_ref[...] * (shares[0] * inverse)[:1]
+    sums = [0.0, 0.0]
     for k in range(count):
-        total = total + part_ref[k, :lat_w, :].astype(jnp.float32) * (shares[k + 1] * inverse)
+        share = shares[k + 1] * inverse
+        share = jnp.where(odd != k % 2, pltpu.roll(share, half, 1), share)[:1]
+        sums[k % 2] = sums[k % 2] + part_ref[k, :lat_w, :].astype(jnp.float32) * share
+    same = jnp.where(odd == 1, sums[1], sums[0])
+    other = jnp.where(odd == 1, sums[0], sums[1])
+    total = total + same + pltpu.roll(other, half, 1)
     shape = (heads * width, heads * width)
     to, at = iota(shape, 0), iota(shape, 1)
     wanted = (to % rows_dev * heads + to // width) * steps + to % width // rows_dev
@@ -273,36 +290,22 @@
             out_ref[copy, :, head * value_w : (head + 1) * value_w] = value
 
 
-def project_kernel(width, place_ref, x_ref, *refs):
-    ws, out_ref = refs[:-1], refs[-1]
+def project_kernel(width, x_ref, w_ref, out_ref):
     per_core = out_ref.shape[1]
     cores = out_ref.shape[0] // NX
-    depth = x_ref.shape[1] // 2
-    here = place_ref[0] // NZ
-    own, near, far, opposite_a, opposite_b = ws
-    blocks = [
-        (0, lambda: dot_t(x_ref[...], own[...])),
-        (1, lambda: dot_t(x_ref[...], near[...])),
-        (3, lambda: dot_t(x_ref[...], far[...])),
-        (
-            2,
-            lambda: dot_t(x_ref[:, :depth], opposite_a[...])
-            + dot_t(x_ref[:, depth:], opposite_b[...]),
-        ),
-    ]
-    for k, make in blocks:
-        block = make()
-        owner = (here - k + NX) % NX
+    x = x_ref[...]
+    for k in range(NX):
+        block = dot_t(x, w_ref[k])
         for core in range(cores):
             for i in range(per_core):
                 first = (core * per_core + i) * width
-                out_ref[owner * cores + core, i] = block[first : first + width]
-
-
-def sum_kernel(place_ref, in_ref, *outs):
+                out_ref[k * cores + core, i] = block[first : first + width]
+
+
+def sum_kernel(in_ref, *outs):
     count = len(outs)
     for j in range(count):
-        i = (place_ref[0] + j) % count
+        i = (lax.axis_index("row") + j) % count
         parts = [in_ref[k, i] for k in range(in_ref.shape[0])]
         outs[j][...] = functools.reduce(jnp.add, parts).astype(outs[j].dtype)
 
@@ -311,16 +314,6 @@
     if k % n == 0:
         return x
     return lax.ppermute(x, axis, [(i, (i + k) % n) for i in range(n)])
-
-
-def shift_x(x, k):
-    if k % NX == 0:
-        return x
-    return lax.ppermute(
-        x,
-        "row",
-        [(a * NZ + b, (a + k) % NX * NZ + b) for a in range(NX) for b in range(NZ)],
-    )
 
 
 def on_device(
@@ -355,14 +348,13 @@
     tokens = pages * piece
     slots = n_row * per_pair * piece
 
-    place = jnp.stack([row, head]).astype(jnp.int32)
     lat_rows = per_pair * piece * lat_w // TAIL
     rope_rows = per_pair * piece * rope_w // TAIL
     block = lat_rows + (rope_rows + 8) // 8 * 8
     send = call(
         functools.partial(pack_kernel, rows_dev, pages_row, per_pair),
         jax.ShapeDtypeStruct((n_row, block, TAIL), bf16),
-        [place, dest_rows[None, :], dest_slots[None, :], latent_pages, rope_pages],
+        [dest_rows[None, :], dest_slots[None, :], latent_pages, rope_pages],
         scratch=[
             pltpu.VMEM((pages, 2 * piece, lat_w), bf16),
             pltpu.VMEM((pages, piece * rope_w), bf16),
@@ -374,7 +366,7 @@
         nbytes=2 * (slots + 2 * tokens) * lat_w,
         mem=60,
         out_spec=HBM,
-        in_hbm=(3, 4),
+        in_hbm=(2, 3),
     )
     got = lax.all_to_all(send, "row", split_axis=0, concat_axis=0, tiled=True)
 
@@ -394,9 +386,10 @@
         axis=1,
     )
     fresh = jnp.concatenate([fresh, jnp.zeros((-width % 16, lat_w + TAIL), bf16)], axis=0)
-    query, fresh_part, fresh_lse = call(
+    query, swapped, fresh_part, fresh_lse = call(
         functools.partial(query_kernel, scale, rows_dev),
         (
+            jax.ShapeDtypeStruct((lat_w + TAIL, queries), bf16),
             jax.ShapeDtypeStruct((lat_w + TAIL, queries), bf16),
             jax.ShapeDtypeStruct((lat_w, queries), f32),
             jax.ShapeDtypeStruct((8, queries), f32),
@@ -406,18 +399,10 @@
         flops=2 * queries * nope_w * lat_w,
         nbytes=2 * heads * nope_w * lat_w,
     )
-    all_queries = [shift(query, "head", n_head, k) for k in range(n_head)]
-    per_row = queries // rows_dev
-    all_queries = jnp.stack(
-        [
-            jnp.concatenate([q[:, b * per_row : (b + 1) * per_row] for q in all_queries], axis=1)
-            for b in range(rows_dev)
-        ]
-    )
-
-    w_t = w_o.T
-    w_near, w_far = shift_x(w_t, 1), shift_x(w_t, -1)
-    depth = w_t.shape[1] // 2
+    all_queries = [shift((query, swapped)[k % 2], "head", n_head, k) for k in range(n_head)]
+
+    w_rings = [[a * NZ + b for a in range(NX)] for b in range(NZ)]
+    w_cols = lax.all_gather(w_o.T, "row", axis_index_groups=w_rings)
 
     slot_ids = jnp.arange(pages_row, dtype=jnp.int32)
     holds = (page_table[:, :, None] == slot_ids[None, None, :]).astype(jnp.int32)
@@ -427,18 +412,10 @@
     usable = within[None, :, None, :] < limit[:, None, :, None]
     bias = jnp.where(usable, 0.0, NEG).astype(f32).reshape(rows_dev * pages_row * piece, 1)
 
-    got, w_near, w_far = lax.optimization_barrier((got, w_near, w_far))
-    w_cols = [
-        w_t,
-        w_near,
-        w_far,
-        shift_x(w_near[:, :depth], 1),
-        shift_x(w_far[:, depth:], -1),
-    ]
     parts = call(
         functools.partial(attend_kernel, scale, piece, per_pair, rope_w, pages_row),
         jax.ShapeDtypeStruct((n_head, lat_w + INFO, queries), bf16),
-        [place, got, bias, all_queries],
+        [got, bias] + all_queries,
         flops=2 * n_head * queries * tokens * (2 * lat_w + TAIL) // 2 + 2 * slots * tokens * lat_w,
         nbytes=2 * (slots + 2 * n_head * queries) * (lat_w + TAIL),
     )
@@ -462,7 +439,7 @@
     sums = call(
         functools.partial(project_kernel, width),
         jax.ShapeDtypeStruct((n_head, per_core, width, cols), f32),
-        [place, ring.reshape(NZ * width, heads * value_w)] + w_cols,
+        [ring.reshape(NZ * width, heads * value_w), w_cols],
         flops=2 * NX * NZ * width * w_o.size,
         nbytes=2 * NX * w_o.size,
     )
@@ -470,7 +447,7 @@
     pieces = call(
         sum_kernel,
         tuple(jax.ShapeDtypeStruct((width, cols), bf16) for _ in range(per_core)),
-        [place, sums],
+        [sums],
     )
     moved = []
     for j in range(per_core):

time: 144 us -> 142 us (0.986)
  blocking collectives: 11.5 us -> 38.1 us
  local copies, waits for them, and re-layouts: 19.3 us -> 3.48 us
  between operations: 0.41 us -> 13.7 us
  waiting for transfers between devices: 46.3 us -> 35.4 us
  starting transfers between devices: 47.9 us -> 37.3 us
  other arithmetic: 2.39 us -> 0.36 us
  Pallas kernels: 15.2 us -> 13.3 us
    all_to_all x1 -> x2, blocking collectives: 11.5 us -> 38.1 us  [the longest x1 24 us: on_device(): lax.all_to_all(parts, 'head', split_axis=0, concat_axis=0, tiled=True)]
    ppermute x4 -> x0, waiting for transfers between devices: 17.4 us -> none  [shift_x(): lax.ppermute(x, 'row', [(a * NZ + b, (a + k) % NX * NZ + b) for a in rang...]
    all_to_all x2 -> x1, waiting for transfers between devices: 19.5 us -> 6.52 us  [on_device(): sums = lax.all_to_all(sums, 'head', split_axis=0, concat_axis=0, tiled=True)]
    all_to_all x1, waiting for transfers between devices: 0.01 us -> 12.9 us  [on_device(): got = lax.all_to_all(send, 'row', split_axis=0, concat_axis=0, tiled=True)]
    slice x10 -> x0, local copies, waits for them, and re-layouts: 8.57 us -> none  [the longest x8 4.85 us: on_device(): q[:, b * per_row:(b + 1) * per_row]]
    ppermute x7, waiting for transfers between devices: 4.91 us -> 10.7 us  [shift(): return lax.ppermute(x, axis, [(i, (i + k) % n) for i in range(n)])]
    ppermute x4 -> x0, starting transfers between devices: 5.05 us -> none  [shift_x(): lax.ppermute(x, 'row', [(a * NZ + b, (a + k) % NX * NZ + b) for a in rang...]
    concatenate x2 -> x0, local copies, waits for them, and re-layouts: 4.38 us -> none  [on_device(): jnp.concatenate([q[:, b * per_row:(b + 1) * per_row] for q in all_queries...]
  transfers between devices with their start and end apart: 18 -> 14, of which waited for: 6 -> 7; matrix products, arithmetic and copies ran while one was open for 11% -> 1% of each run, Pallas kernels for 2% -> 8%
where the time goes in v3:
time: 142 us
  blocking collectives  38.1 us (27%)
  starting transfers between devices  37.3 us (26%)
  waiting for transfers between devices  35.4 us (25%)
  between operations  13.7 us (10%)
  Pallas kernels  13.3 us (9%)
  local copies, waits for them, and re-layouts  3.48 us (2%)
    all_to_all x1, blocking collectives, on_device(): lax.all_to_all(parts, 'head', split_axis=0, concat_axis=0, tiled=True)  24 us
    all_to_all x1, blocking collectives, on_device(): lax.all_to_all(head_out, 'row', split_axis=0, concat_axis=0, axis_index_g...  14.1 us
    pallas_call x6, Pallas kernels, call(): pl.pallas_call(body, out_shape=out_shape, in_specs=[HBM if i in in_hbm el...  13.3 us
    all_to_all x1, waiting for transfers between devices, on_device(): got = lax.all_to_all(send, 'row', split_axis=0, concat_axis=0, tiled=True)  12.9 us
    all_to_all x1, starting transfers between devices, on_device(): got = lax.all_to_all(send, 'row', split_axis=0, concat_axis=0, tiled=True)  12.1 us
    ppermute x7, waiting for transfers between devices, shift(): return lax.ppermute(x, axis, [(i, (i + k) % n) for i in range(n)])  10.7 us
    ppermute x4, starting transfers between devices, on_device(): moved.append(lax.ppermute(pieces[j], ('row', 'head'), pairs))  9.96 us
    ppermute x7, starting transfers between devices, shift(): return lax.ppermute(x, axis, [(i, (i + k) % n) for i in range(n)])  9.68 us
  transfers between devices with their start and end apart: 14, of which 7 were waited for; matrix products, arithmetic and copies ran while one was open for 1% of the time, Pallas kernels for 8%

profile of v3, /device:TPU:1, one launch (start us, length us, event | category | flops | bytes accessed | tf_op | source)
XLA Modules:
  0.0 141.7 jit_solution(3140562987117048034)
XLA Ops:
  6.5 0.7 all-gather.3.cloned.1.call-update
  7.3 4.8 %shard_map.128 = bf16[32,184,128]{2,1,0:T(8,128)(2,1)} custom-call(s32[1,80]{1,0:T(1,128)} %bitcast.22, s32[1,80]{1,0:T(1,128)} %bitcast.23, bf16[80,64,512]{2,1,0:T(8,128)(2,1)} %lat_hbm.1, bf16[80,4096]{1,0:T(8,128)(2,1)} %rope_hbm.1), custom_call_target="tpu_custom_call" | custom-call | flops 838860800 | bytes 2621440 | tf_op jit(solution)/shard_map/pallas_call | solution.py:26
  12.1 0.0 copy-start.3
  12.1 0.0 copy-start.4
  12.1 0.0 copy-start.5
  12.1 0.0 copy-start.6
  12.1 0.0 copy-start.1
  12.2 12.1 %all-to-all-start = ((bf16[32,184,128]{2,1,0:T(8,128)(2,1)}), bf16[32,184,128]{2,1,0:T(8,128)(2,1)}, u32[]{:S(2)}, u32[]{:S(2)}) async-start(bf16[32,184,128]{2,1,0:T(8,128)(2,1)} %shard_map.128), calls=%async_computation | async-start | bytes 3014656 | tf_op jit(solution)/shard_map/all_to_all | solution.py:371
  24.3 0.0 copy-start.7
  24.3 0.0 copy-start.8
  24.4 0.1 reshape.91
  24.5 0.1 pad.9.clone
  24.6 0.1 pad.7.clone
  24.7 0.2 copy.32
  24.9 0.1 copy.35
  25.1 0.9 shard_map.127
  25.9 2.1 %collective-permute-start = (bf16[640,128]{1,0:T(8,128)(2,1)S(1)}, bf16[640,128]{1,0:T(8,128)(2,1)S(1)}, u32[]{:S(2)}, u32[]{:S(2)}) collective-permute-start(bf16[640,128]{1,0:T(8,128)(2,1)S(1)} %get-tuple-element.16), channel_id=1, source_target_pairs={{0,1},{1,2},{2,3},{3,4},{4,5},{5,6},{6,7},{7,0},{8,9},{9,10},{10,1... | collective-permute-start | bytes 491528 | tf_op jit(solution)/shard_map/ppermute | solution.py:316
  28.1 1.7 %collective-permute-start.2 = (bf16[640,128]{1,0:T(8,128)(2,1)S(1)}, bf16[640,128]{1,0:T(8,128)(2,1)S(1)}, u32[]{:S(2)}, u32[]{:S(2)}) collective-permute-start(bf16[640,128]{1,0:T(8,128)(2,1)S(1)} %get-tuple-element.16), channel_id=1, source_target_pairs={{0,3},{1,4},{2,5},{3,6},{4,7},{5,0},{6,1},{7,2},{8,11},{9,12},{10,... | collective-permute-start | bytes 491528 | tf_op jit(solution)/shard_map/ppermute | solution.py:316
  29.8 0.4 collective-permute-start.1
  30.2 1.6 %collective-permute-start.3 = (bf16[640,128]{1,0:T(8,128)(2,1)S(1)}, bf16[640,128]{1,0:T(8,128)(2,1)S(1)}, u32[]{:S(2)}, u32[]{:S(2)}) collective-permute-start(bf16[640,128]{1,0:T(8,128)(2,1)S(1)} %get-tuple-element.15.refs_0_), channel_id=1, source_target_pairs={{0,4},{1,5},{2,6},{3,7},{4,0},{5,1},{6,2},{7,3},{8,12},{9,13},{10,... | collective-permute-start | bytes 491528 | tf_op jit(solution)/shard_map/ppermute | solution.py:316
  31.7 1.8 %collective-permute-start.4 = (bf16[640,128]{1,0:T(8,128)(2,1)S(1)}, bf16[640,128]{1,0:T(8,128)(2,1)S(1)}, u32[]{:S(2)}, u32[]{:S(2)}) collective-permute-start(bf16[640,128]{1,0:T(8,128)(2,1)S(1)} %get-tuple-element.16), channel_id=1, source_target_pairs={{0,5},{1,6},{2,7},{3,0},{4,1},{5,2},{6,3},{7,4},{8,13},{9,14},{10,... | collective-permute-start | bytes 491528 | tf_op jit(solution)/shard_map/ppermute | solution.py:316
  33.6 0.1 select_reduce_fusion
  33.7 0.1 subtract_subtract_fusion
  33.7 1.0 collective-permute-start.5
  34.7 4.4 %collective-permute-done.1.refs_2_ = bf16[640,128]{1,0:T(8,128)(2,1)S(1)} collective-permute-done((bf16[640,128]{1,0:T(8,128)(2,1)S(1)}, bf16[640,128]{1,0:T(8,128)(2,1)S(1)}, u32[]{:S(2)}, u32[]{:S(2)}) %collective-permute-start.1) | collective-permute-done | bytes 163872 | tf_op jit(solution)/shard_map/ppermute | solution.py:316
  39.1 1.1 collective-permute-start.6
  40.2 0.1 compare_select_fusion
  40.2 0.1 select_n.137.bias_ref
  40.4 5.2 %collective-permute-done.3.refs_4_ = bf16[640,128]{1,0:T(8,128)(2,1)S(1)} collective-permute-done((bf16[640,128]{1,0:T(8,128)(2,1)S(1)}, bf16[640,128]{1,0:T(8,128)(2,1)S(1)}, u32[]{:S(2)}, u32[]{:S(2)}) %collective-permute-start.3) | collective-permute-done | bytes 163872 | tf_op jit(solution)/shard_map/ppermute | solution.py:316
  45.6 0.4 collective-permute-done.4.refs_5_
  46.1 0.6 collective-permute-done.6.refs_7_
  46.7 12.9 %all-to-all-done.key_ref = bf16[32,184,128]{2,1,0:T(8,128)(2,1)} async-done(((bf16[32,184,128]{2,1,0:T(8,128)(2,1)}), bf16[32,184,128]{2,1,0:T(8,128)(2,1)}, u32[]{:S(2)}, u32[]{:S(2)}) %all-to-all-start) | async-done | bytes 1507360 | tf_op jit(solution)/shard_map/all_to_all | solution.py:371
  59.6 4.7 %shard_map.129 = bf16[8,528,128]{2,1,0:T(8,128)(2,1)S(1)} custom-call(bf16[32,184,128]{2,1,0:T(8,128)(2,1)} %all-to-all-done.key_ref, f32[640,1]{1,0:T(8,128)S(1)} %select_n.137.bias_ref, bf16[640,128]{1,0:T(8,128)(2,1)S(1)} %get-tuple-element.15.refs_0_, bf16[640,128]{1,0:T(8,128)(2,1)S(1)} %collective-permute-done.refs_1_, ...), custom_call_target="tpu_custom_call" | custom-call | flops 1593835520 | bytes 4259840 | tf_op jit(solution)/shard_map/pallas_call | solution.py:26
  64.3 0.0 copy-start.2
  64.4 24.0 %all_to_all.20.part_ref = bf16[8,528,128]{2,1,0:T(8,128)(2,1)S(1)} all-to-all(bf16[8,528,128]{2,1,0:T(8,128)(2,1)S(1)} %shard_map.129), channel_id=1, replica_groups=mesh['row'=32,'head'=8] {'head'}, dimensions={0} | all-to-all | bytes 2162688 | tf_op jit(solution)/shard_map/all_to_all | solution.py:422
  88.4 0.9 shard_map.130
  89.3 14.1 %all_to_all.21 = bf16[8,8,2048]{2,1,0:T(8,128)(2,1)S(1)} all-to-all(bf16[8,8,2048]{2,1,0:T(8,128)(2,1)S(1)} %shard_map.130), channel_id=1, replica_groups={{0,8,16,24,32,40,48,56},{64,72,80,88,96,104,112,120},{128,136,144,152,1..., dimensions={0} | all-to-all | bytes 524288 | tf_op jit(solution)/shard_map/all_to_all | solution.py:433
  103.4 2.0 %copy-done = bf16[896,2048]{1,0:T(8,128)(2,1)S(1)} copy-done((bf16[896,2048]{1,0:T(8,128)(2,1)S(1)}, bf16[896,2048]{1,0:T(8,128)(2,1)}, u32[]{:S(2)}) %copy-start) | copy-done | bytes 3670040
  105.5 2.0 %shard_map.131 = f32[8,4,8,224]{3,2,1,0:T(8,128)} custom-call(bf16[64,2048]{1,0:T(8,128)(2,1)S(1)} %bitcast.16, bf16[4,224,2048]{2,1,0:T(8,128)(2,1)S(1)} %bitcast.15), custom_call_target="tpu_custom_call" | custom-call | flops 234881024 | bytes 3670016 | tf_op jit(solution)/shard_map/pallas_call | solution.py:26
  107.4 5.6 %all-to-all-start.3 = ((f32[8,4,8,224]{3,2,1,0:T(8,128)}), f32[8,4,8,224]{3,2,1,0:T(8,128)S(1)}, u32[]{:S(2)}, u32[]{:S(2)}) async-start(f32[8,4,8,224]{3,2,1,0:T(8,128)} %shard_map.131), calls=%async_computation.3 | async-start | bytes 524288 | tf_op jit(solution)/shard_map/all_to_all | solution.py:446
  113.0 6.5 %all-to-all-done.3.in_ref = f32[8,4,8,224]{3,2,1,0:T(8,128)S(1)} async-done(((f32[8,4,8,224]{3,2,1,0:T(8,128)}), f32[8,4,8,224]{3,2,1,0:T(8,128)S(1)}, u32[]{:S(2)}, u32[]{:S(2)}) %all-to-all-start.3) | async-done | bytes 229408 | tf_op jit(solution)/shard_map/all_to_all | solution.py:446
  119.5 0.1 collective-permute-start.7
  119.6 3.8 %collective-permute-start.8 = (bf16[8,224]{1,0:T(8,128)(2,1)S(1)}, bf16[8,224]{1,0:T(8,128)(2,1)S(1)}, u32[]{:S(2)}, u32[]{:S(2)}) collective-permute-start(bf16[8,224]{1,0:T(8,128)(2,1)S(1)} %get-tuple-element.18), channel_id=1, source_target_pairs={{0,16},{1,48},{2,18},{3,50},{4,20},{5,52},{6,22},{7,54},{8,24},{9,... | collective-permute-start | bytes 10760 | tf_op jit(solution)/shard_map/ppermute | solution.py:461
  123.5 1.9 %collective-permute-start.9 = (bf16[8,224]{1,0:T(8,128)(2,1)S(1)}, bf16[8,224]{1,0:T(8,128)(2,1)S(1)}, u32[]{:S(2)}, u32[]{:S(2)}) collective-permute-start(bf16[8,224]{1,0:T(8,128)(2,1)S(1)} %get-tuple-element.19), channel_id=1, source_target_pairs={{0,8},{1,40},{2,10},{3,42},{4,12},{5,44},{6,14},{7,46},{8,16},{9,4... | collective-permute-start | bytes 10760 | tf_op jit(solution)/shard_map/ppermute | solution.py:461
  125.3 4.2 %collective-permute-start.10 = (bf16[8,224]{1,0:T(8,128)(2,1)S(1)}, bf16[8,224]{1,0:T(8,128)(2,1)S(1)}, u32[]{:S(2)}, u32[]{:S(2)}) collective-permute-start(bf16[8,224]{1,0:T(8,128)(2,1)S(1)} %get-tuple-element.20), channel_id=1, source_target_pairs={{0,0},{1,32},{2,2},{3,34},{4,4},{5,36},{6,6},{7,38},{8,8},{9,40},{... | collective-permute-start | bytes 10760 | tf_op jit(solution)/shard_map/ppermute | solution.py:461
  129.6 4.5 %collective-permute-done.10 = bf16[8,224]{1,0:T(8,128)(2,1)S(1)} collective-permute-done((bf16[8,224]{1,0:T(8,128)(2,1)S(1)}, bf16[8,224]{1,0:T(8,128)(2,1)S(1)}, u32[]{:S(2)}, u32[]{:S(2)}) %collective-permute-start.10) | collective-permute-done | bytes 3616 | tf_op jit(solution)/shard_map/ppermute | solution.py:461
  134.2 0.1 pad_maximum_fusion.1
  134.2 0.6 reshape.99
  (29 shorter events, 0.2 us)
Async XLA Ops:
  6.5 96.9 %all-gather.3.cloned.1.call-start = ((), (), s32[]{:S(2)}) async-start(), calls=%async_computation.4 | async-start | bytes 4587520 | tf_op jit(solution)/shard_map/all_gather | solution.py:405
  12.1 12.2 %copy-start.3 = (bf16[4,2,16,128]{3,2,1,0:T(8,128)(2,1)S(1)}, bf16[4,2,16,128]{3,2,1,0:T(8,128)(2,1)}, u32[]{:S(2)}) copy-start(bf16[4,2,16,128]{3,2,1,0:T(8,128)(2,1)} %param.13) | copy-start | bytes 98308
  12.1 12.2 %copy-start.4 = (bf16[4,2,1024]{2,1,0:T(2,128)(2,1)S(1)}, bf16[4,2,1024]{2,1,0:T(2,128)(2,1)}, u32[]{:S(2)}) copy-start(bf16[4,2,1024]{2,1,0:T(2,128)(2,1)} %param.14) | copy-start | bytes 49156
  12.1 12.4 %copy-start.5 = (bf16[4,2,512]{2,1,0:T(2,128)(2,1)S(1)}, bf16[4,2,512]{2,1,0:T(2,128)(2,1)}, u32[]{:S(2)}) copy-start(bf16[4,2,512]{2,1,0:T(2,128)(2,1)} %param.15) | copy-start | bytes 24580
  12.1 12.5 %copy-start.6 = (bf16[4,2,64]{2,1,0:T(2,128)(2,1)S(1)}, bf16[4,2,64]{2,1,0:T(2,128)(2,1)}, u32[]{:S(2)}) copy-start(bf16[4,2,64]{2,1,0:T(2,128)(2,1)} %param.16) | copy-start | bytes 3076
  12.1 12.9 %copy-start.1 = (bf16[16,128,512]{2,1,0:T(8,128)(2,1)S(1)}, bf16[16,128,512]{2,1,0:T(8,128)(2,1)}, u32[]{:S(2)}) copy-start(bf16[16,128,512]{2,1,0:T(8,128)(2,1)} %w_ref.2) | copy-start | bytes 6291460
  12.2 47.4 %all-to-all-start = ((bf16[32,184,128]{2,1,0:T(8,128)(2,1)}), bf16[32,184,128]{2,1,0:T(8,128)(2,1)}, u32[]{:S(2)}, u32[]{:S(2)}) async-start(bf16[32,184,128]{2,1,0:T(8,128)(2,1)} %shard_map.128), calls=%async_computation | async-start | bytes 3014656 | tf_op jit(solution)/shard_map/all_to_all | solution.py:371
  24.3 9.3 %copy-start.7 = (s32[2,40]{1,0:T(2,128)S(1)}, s32[2,40]{1,0:T(2,128)}, u32[]{:S(2)}) copy-start(s32[2,40]{1,0:T(2,128)} %param.21) | copy-start | bytes 964
  24.3 9.4 %copy-start.8 = (s32[2]{0:T(128)S(1)}, s32[2]{0:T(128)}, u32[]{:S(2)}) copy-start(s32[2]{0:T(128)} %param.22) | copy-start | bytes 28
  25.9 7.8 %collective-permute-start = (bf16[640,128]{1,0:T(8,128)(2,1)S(1)}, bf16[640,128]{1,0:T(8,128)(2,1)S(1)}, u32[]{:S(2)}, u32[]{:S(2)}) collective-permute-start(bf16[640,128]{1,0:T(8,128)(2,1)S(1)} %get-tuple-element.16), channel_id=1, source_target_pairs={{0,1},{1,2},{2,3},{3,4},{4,5},{5,6},{6,7},{7,0},{8,9},{9,10},{10,1... | collective-permute-start | bytes 491528 | tf_op jit(solution)/shard_map/ppermute | solution.py:316
  28.1 12.3 %collective-permute-start.2 = (bf16[640,128]{1,0:T(8,128)(2,1)S(1)}, bf16[640,128]{1,0:T(8,128)(2,1)S(1)}, u32[]{:S(2)}, u32[]{:S(2)}) collective-permute-start(bf16[640,128]{1,0:T(8,128)(2,1)S(1)} %get-tuple-element.16), channel_id=1, source_target_pairs={{0,3},{1,4},{2,5},{3,6},{4,7},{5,0},{6,1},{7,2},{8,11},{9,12},{10,... | collective-permute-start | bytes 491528 | tf_op jit(solution)/shard_map/ppermute | solution.py:316
  29.8 9.3 %collective-permute-start.1 = (bf16[640,128]{1,0:T(8,128)(2,1)S(1)}, bf16[640,128]{1,0:T(8,128)(2,1)S(1)}, u32[]{:S(2)}, u32[]{:S(2)}) collective-permute-start(bf16[640,128]{1,0:T(8,128)(2,1)S(1)} %get-tuple-element.15.refs_0_), channel_id=1, source_target_pairs={{0,2},{1,3},{2,4},{3,5},{4,6},{5,7},{6,0},{7,1},{8,10},{9,11},{10,... | collective-permute-start | bytes 491528 | tf_op jit(solution)/shard_map/ppermute | solution.py:316
  30.2 15.5 %collective-permute-start.3 = (bf16[640,128]{1,0:T(8,128)(2,1)S(1)}, bf16[640,128]{1,0:T(8,128)(2,1)S(1)}, u32[]{:S(2)}, u32[]{:S(2)}) collective-permute-start(bf16[640,128]{1,0:T(8,128)(2,1)S(1)} %get-tuple-element.15.refs_0_), channel_id=1, source_target_pairs={{0,4},{1,5},{2,6},{3,7},{4,0},{5,1},{6,2},{7,3},{8,12},{9,13},{10,... | collective-permute-start | bytes 491528 | tf_op jit(solution)/shard_map/ppermute | solution.py:316
  31.7 14.3 %collective-permute-start.4 = (bf16[640,128]{1,0:T(8,128)(2,1)S(1)}, bf16[640,128]{1,0:T(8,128)(2,1)S(1)}, u32[]{:S(2)}, u32[]{:S(2)}) collective-permute-start(bf16[640,128]{1,0:T(8,128)(2,1)S(1)} %get-tuple-element.16), channel_id=1, source_target_pairs={{0,5},{1,6},{2,7},{3,0},{4,1},{5,2},{6,3},{7,4},{8,13},{9,14},{10,... | collective-permute-start | bytes 491528 | tf_op jit(solution)/shard_map/ppermute | solution.py:316
  33.7 12.4 %collective-permute-start.5 = (bf16[640,128]{1,0:T(8,128)(2,1)S(1)}, bf16[640,128]{1,0:T(8,128)(2,1)S(1)}, u32[]{:S(2)}, u32[]{:S(2)}) collective-permute-start(bf16[640,128]{1,0:T(8,128)(2,1)S(1)} %get-tuple-element.15.refs_0_), channel_id=1, source_target_pairs={{0,6},{1,7},{2,0},{3,1},{4,2},{5,3},{6,4},{7,5},{8,14},{9,15},{10,... | collective-permute-start | bytes 491528 | tf_op jit(solution)/shard_map/ppermute | solution.py:316
  39.1 7.6 %collective-permute-start.6 = (bf16[640,128]{1,0:T(8,128)(2,1)S(1)}, bf16[640,128]{1,0:T(8,128)(2,1)S(1)}, u32[]{:S(2)}, u32[]{:S(2)}) collective-permute-start(bf16[640,128]{1,0:T(8,128)(2,1)S(1)} %get-tuple-element.16), channel_id=1, source_target_pairs={{0,7},{1,0},{2,1},{3,2},{4,3},{5,4},{6,5},{7,6},{8,15},{9,8},{10,9... | collective-permute-start | bytes 491528 | tf_op jit(solution)/shard_map/ppermute | solution.py:316
  64.3 24.1 %copy-start.2 = (bf16[16,512,128]{2,1,0:T(8,128)(2,1)S(1)}, bf16[16,512,128]{2,1,0:T(8,128)(2,1)}, u32[]{:S(2)}) copy-start(bf16[16,512,128]{2,1,0:T(8,128)(2,1)} %w_ref.3) | copy-start | bytes 6291460
  103.4 2.0 %copy-start = (bf16[896,2048]{1,0:T(8,128)(2,1)S(1)}, bf16[896,2048]{1,0:T(8,128)(2,1)}, u32[]{:S(2)}) copy-start(bf16[896,2048]{1,0:T(8,128)(2,1)} %all-gather.3.cloned.1.call-done) | copy-start | bytes 11010052
  107.4 12.1 %all-to-all-start.3 = ((f32[8,4,8,224]{3,2,1,0:T(8,128)}), f32[8,4,8,224]{3,2,1,0:T(8,128)S(1)}, u32[]{:S(2)}, u32[]{:S(2)}) async-start(f32[8,4,8,224]{3,2,1,0:T(8,128)} %shard_map.131), calls=%async_computation.3 | async-start | bytes 524288 | tf_op jit(solution)/shard_map/all_to_all | solution.py:446
  119.5 10.1 %collective-permute-start.7 = (bf16[8,224]{1,0:T(8,128)(2,1)S(1)}, bf16[8,224]{1,0:T(8,128)(2,1)S(1)}, u32[]{:S(2)}, u32[]{:S(2)}) collective-permute-start(bf16[8,224]{1,0:T(8,128)(2,1)S(1)} %get-tuple-element.17), channel_id=1, source_target_pairs={{0,24},{1,56},{2,26},{3,58},{4,28},{5,60},{6,30},{7,62},{8,0},{9,3... | collective-permute-start | bytes 10760 | tf_op jit(solution)/shard_map/ppermute | solution.py:461
  119.6 10.0 %collective-permute-start.8 = (bf16[8,224]{1,0:T(8,128)(2,1)S(1)}, bf16[8,224]{1,0:T(8,128)(2,1)S(1)}, u32[]{:S(2)}, u32[]{:S(2)}) collective-permute-start(bf16[8,224]{1,0:T(8,128)(2,1)S(1)} %get-tuple-element.18), channel_id=1, source_target_pairs={{0,16},{1,48},{2,18},{3,50},{4,20},{5,52},{6,22},{7,54},{8,24},{9,... | collective-permute-start | bytes 10760 | tf_op jit(solution)/shard_map/ppermute | solution.py:461
  123.5 6.1 %collective-permute-start.9 = (bf16[8,224]{1,0:T(8,128)(2,1)S(1)}, bf16[8,224]{1,0:T(8,128)(2,1)S(1)}, u32[]{:S(2)}, u32[]{:S(2)}) collective-permute-start(bf16[8,224]{1,0:T(8,128)(2,1)S(1)} %get-tuple-element.19), channel_id=1, source_target_pairs={{0,8},{1,40},{2,10},{3,42},{4,12},{5,44},{6,14},{7,46},{8,16},{9,4... | collective-permute-start | bytes 10760 | tf_op jit(solution)/shard_map/ppermute | solution.py:461
  125.3 8.8 %collective-permute-start.10 = (bf16[8,224]{1,0:T(8,128)(2,1)S(1)}, bf16[8,224]{1,0:T(8,128)(2,1)S(1)}, u32[]{:S(2)}, u32[]{:S(2)}) collective-permute-start(bf16[8,224]{1,0:T(8,128)(2,1)S(1)} %get-tuple-element.20), channel_id=1, source_target_pairs={{0,0},{1,32},{2,2},{3,34},{4,4},{5,36},{6,6},{7,38},{8,8},{9,40},{... | collective-permute-start | bytes 10760 | tf_op jit(solution)/shard_map/ppermute | solution.py:461
Sparse Core Ops, SparseCore 0:
  9.2 65.2 all-gather.2

commit v4 on v3

--- a/solution.py
+++ b/solution.py
@@ -172,27 +172,18 @@
     lse_ref[...] = jnp.broadcast_to(high + jnp.log(total), lse_ref.shape)
 
 
-def attend_kernel(
-    scale, piece, per_pair, rope_w, pages_row, key_ref, bias_ref, *refs
-):
-    q_refs, out_ref = refs[:-1], refs[-1]
-    count, block, _ = key_ref.shape
-    n_head, _, queries = out_ref.shape
-    rows = 2
-    cuts = (q_refs[0].shape[0] - TAIL) // TAIL
+def gather_kernel(piece, per_pair, rope_w, pages_row, block_ref, bias_ref, key_ref):
+    rows, per_row, key_w = key_ref.shape
+    count, block, _ = block_ref.shape
+    cuts = (key_w - TAIL) // TAIL
     lat_w = cuts * TAIL
     pair_tokens = per_pair * piece
     lat_rows = pair_tokens * cuts
     rest = block - lat_rows
     rope_rows = piece * rope_w // TAIL
-    per_row = pages_row * piece
     half = per_row // 2
 
-    lat = key_ref[:, :lat_rows, :].astype(jnp.float32)
-    lat = lat.reshape(count * per_pair, cuts, piece, TAIL)
-    lat = [lat[:, c].reshape(count * pair_tokens, TAIL) for c in range(cuts)]
-    lat = jnp.concatenate(lat, axis=1).astype(jnp.bfloat16)
-    tail = key_ref[:, lat_rows:, :].astype(jnp.float32)
+    tail = block_ref[:, lat_rows:, :].astype(jnp.float32)
     marked = iota(tail.shape, 1) == per_pair * rope_rows
     labels = jnp.sum(jnp.where(marked, tail, 0.0), axis=1).astype(jnp.bfloat16)
 
@@ -210,7 +201,13 @@
     target = row * (per_row - pages_row * (piece // 2)) + token % 2 * half
     target = target + slot * (piece // 2) + token // 2
     target = jnp.where(slot >= 0, target, -1)
-    key = dot(ones_where(iota((rows * per_row, 1), 0) == target), lat).astype(jnp.bfloat16)
+    lat = block_ref[:, :lat_rows, :].astype(jnp.float32)
+    lat = lat.reshape(count * per_pair, cuts, piece, TAIL)
+    lat = [lat[:, c].reshape(count * pair_tokens, TAIL) for c in range(cuts)]
+    lat = jnp.concatenate(lat, axis=1).astype(jnp.bfloat16)
+    for b in range(rows):
+        pick = ones_where(iota((per_row, 1), 0) + b * per_row == target)
+        key_ref[b, :, :lat_w] = dot(pick, lat).astype(jnp.bfloat16)
 
     columns = count * rest
     inner = iota((1, columns), 1) % rest
@@ -219,66 +216,92 @@
     target = jnp.where(slot >= 0, slot * rope_rows + inner % rope_rows, -1)
     tail = tail.reshape(columns, TAIL).astype(jnp.bfloat16)
     rope = dot(ones_where(iota((rows * half, 1), 0) == target), tail)
-
-    left = iota((lat_w + TAIL, queries), 1) < queries // 2
-    asked = [[], []]
-    for k in range(0, n_head, 2):
-        one, two = q_refs[k][...].astype(jnp.float32), q_refs[k + 1][...].astype(jnp.float32)
-        asked[0].append(jnp.where(left, one, two).astype(jnp.bfloat16))
-        asked[1].append(jnp.where(left, two, one).astype(jnp.bfloat16))
-    parts = []
     for b in range(rows):
         rope_b = rope[b * half : (b + 1) * half]
         rope_b = jnp.concatenate([rope_b, pltpu.roll(rope_b, TAIL - rope_w, 1)], axis=0)
         lane = iota(rope_b.shape, 1)
         bias = bias_ref[b * per_row : (b + 1) * per_row]
         rope_b = jnp.where(lane < rope_w, rope_b, jnp.where(lane == rope_w, bias, 0.0))
-        key_b = key[b * per_row : (b + 1) * per_row]
-        query = jnp.concatenate(asked[b], axis=1)
-        scores = dot(jnp.concatenate([key_b, rope_b.astype(jnp.bfloat16)], axis=1), query)
-        high = jnp.max(scores, axis=0, keepdims=True)
-        weights = jnp.exp2((scores - high) * (scale * LOG2E))
-        total = jnp.sum(weights, axis=0, keepdims=True)
-        part = dot(key_b.T, weights.astype(jnp.bfloat16)) * (1.0 / total)
-        hi, mid, low = split3(high * scale + jnp.log(total))
+        key_ref[b, :, lat_w:] = rope_b.astype(jnp.bfloat16)
+
+
+def attend(scale, key, query, lat_w):
+    scores = dot(key, query)
+    high = jnp.max(scores, axis=0, keepdims=True)
+    weights = jnp.exp2((scores - high) * (scale * LOG2E))
+    total = jnp.sum(weights, axis=0, keepdims=True)
+    return high, total, dot(key[:, :lat_w].T, weights.astype(jnp.bfloat16))
+
+
+def ask(q_refs, b):
+    left = iota(q_refs[0].shape, 1) < q_refs[0].shape[1] // 2
+    tiles = []
+    for k in range(0, len(q_refs), 2):
+        one, two = q_refs[k][...].astype(jnp.float32), q_refs[k + 1][...].astype(jnp.float32)
+        first, second = (one, two) if b == 0 else (two, one)
+        tiles.append(jnp.where(left, first, second).astype(jnp.bfloat16))
+    return jnp.concatenate(tiles, axis=1)
+
+
+def own_kernel(scale, key_ref, *refs):
+    q_refs, (part_ref, stat_ref) = refs[:-2], refs[-2:]
+    for b in range(key_ref.shape[0]):
+        high, total, part = attend(scale, key_ref[b], ask(q_refs, b), part_ref.shape[1])
+        part_ref[b] = part
+        stat_ref[b] = jnp.where(iota(stat_ref.shape[1:], 0) == 0, high, total)
+
+
+def both_kernel(scale, key_ref, own_ref, stat_ref, *refs):
+    count = len(refs) // 2
+    q_refs, out_refs = refs[:count], refs[count:]
+    lat_w = own_ref.shape[1]
+    queries = q_refs[0].shape[1]
+    parts = []
+    for b in range(key_ref.shape[0]):
+        high, total, part = attend(scale, key_ref[b], ask(q_refs, b), lat_w)
+        high_own, total_own = stat_ref[b, 0:1], stat_ref[b, 1:2]
+        top = jnp.maximum(high, high_own)
+        keep = jnp.exp2((high - top) * (scale * LOG2E))
+        keep_own = jnp.exp2((high_own - top) * (scale * LOG2E))
+        total = total * keep + total_own * keep_own
+        inverse = 1.0 / total
+        part = part * (keep * inverse) + own_ref[b] * (keep_own * inverse)
+        hi, mid, low = split3(top * scale + jnp.log(total))
         mark = iota((INFO, part.shape[1]), 0)
         info = jnp.where(mark == 0, hi, jnp.where(mark == 1, mid, jnp.where(mark == 2, low, 0.0)))
         parts.append(jnp.concatenate([part, info], axis=0))
-    head = lax.axis_index("head")
     left = iota((lat_w + INFO, queries), 1) < queries // 2
-    for k in range(0, n_head, 2):
+    for k in range(0, count, 2):
         lanes = slice(k * queries // 2, (k + 2) * queries // 2)
         one, two = parts[0][:, lanes], parts[1][:, lanes]
-        ready = (jnp.where(left, one, two), jnp.where(left, two, one))
-        for i in range(2):
-            owner = (head - (k + i) + n_head) % n_head
-            out_ref[owner] = ready[i].astype(jnp.bfloat16)
-
-
-def merge_kernel(rows_dev, fresh_ref, fresh_lse_ref, w_ref, part_ref, out_ref, lat_ref):
+        out_refs[k][...] = jnp.where(left, one, two).astype(jnp.bfloat16)
+        out_refs[k + 1][...] = jnp.where(left, two, one).astype(jnp.bfloat16)
+
+
+def merge_kernel(rows_dev, fresh_ref, fresh_lse_ref, w_ref, *refs):
+    part_refs, out_ref, lat_ref = refs[:-2], refs[-2], refs[-1]
     heads, lat_w, value_w = w_ref.shape
     width = out_ref.shape[1]
     steps = width // rows_dev
-    count = part_ref.shape[0]
-    odd = lax.axis_index("head") % 2
-    half = part_ref.shape[2] // 2
+    half = fresh_ref.shape[1] // 2
     lses = [fresh_lse_ref[...]]
-    for k in range(count):
-        info = jnp.sum(part_ref[k, lat_w:, :].astype(jnp.float32), axis=0, keepdims=True)
+    for k, part_ref in enumerate(part_refs):
+        info = jnp.sum(part_ref[lat_w:, :].astype(jnp.float32), axis=0, keepdims=True)
         info = jnp.broadcast_to(info, lses[0].shape)
-        lses.append(jnp.where(odd != k % 2, pltpu.roll(info, half, 1), info))
+        lses.append(pltpu.roll(info, half, 1) if k % 2 else info)
     high = functools.reduce(jnp.maximum, lses)
     shares = [jnp.exp(lse - high) for lse in lses]
     inverse = 1.0 / functools.reduce(jnp.add, shares)
     total = fresh_ref[...] * (shares[0] * inverse)[:1]
-    sums = [0.0, 0.0]
-    for k in range(count):
+    swapped = 0.0
+    for k, part_ref in enumerate(part_refs):
         share = shares[k + 1] * inverse
-        share = jnp.where(odd != k % 2, pltpu.roll(share, half, 1), share)[:1]
-        sums[k % 2] = sums[k % 2] + part_ref[k, :lat_w, :].astype(jnp.float32) * share
-    same = jnp.where(odd == 1, sums[1], sums[0])
-    other = jnp.where(odd == 1, sums[0], sums[1])
-    total = total + same + pltpu.roll(other, half, 1)
+        part = part_ref[:lat_w, :].astype(jnp.float32)
+        if k % 2:
+            swapped = swapped + part * pltpu.roll(share, half, 1)[:1]
+        else:
+            total = total + part * share[:1]
+    total = total + pltpu.roll(swapped, half, 1)
     shape = (heads * width, heads * width)
     to, at = iota(shape, 0), iota(shape, 1)
     wanted = (to % rows_dev * heads + to // width) * steps + to % width // rows_dev
@@ -290,16 +313,24 @@
             out_ref[copy, :, head * value_w : (head + 1) * value_w] = value
 
 
-def project_kernel(width, x_ref, w_ref, out_ref):
+def project_kernel(width, x_ref, own_ref, near_ref, far_ref, opp_a_ref, opp_b_ref, out_ref):
     per_core = out_ref.shape[1]
     cores = out_ref.shape[0] // NX
-    x = x_ref[...]
-    for k in range(NX):
-        block = dot_t(x, w_ref[k])
+    here = lax.axis_index("row") // NZ
+    depth = x_ref.shape[1] // 2
+
+    def put(k, block):
+        owner = (here - k + NX) % NX
         for core in range(cores):
             for i in range(per_core):
                 first = (core * per_core + i) * width
-                out_ref[k * cores + core, i] = block[first : first + width]
+                out_ref[owner * cores + core, i] = block[first : first + width]
+
+    put(0, dot_t(x_ref[...], own_ref[...]))
+    put(1, dot_t(x_ref[...], near_ref[...]))
+    put(NX - 1, dot_t(x_ref[...], far_ref[...]))
+    opposite = dot_t(x_ref[:, :depth], opp_a_ref[...]) + dot_t(x_ref[:, depth:], opp_b_ref[...])
+    put(NX // 2, opposite)
 
 
 def sum_kernel(in_ref, *outs):
@@ -310,10 +341,19 @@
         outs[j][...] = functools.reduce(jnp.add, parts).astype(outs[j].dtype)
 
 
-def shift(x, axis, n, k):
-    if k % n == 0:
+def shift_y(x, n_head, k):
+    cores = n_head // NX
+    if k % NX == 0:
         return x
-    return lax.ppermute(x, axis, [(i, (i + k) % n) for i in range(n)])
+    return lax.ppermute(x, "head", [(h, (h + k * cores) % n_head) for h in range(n_head)])
+
+
+def shift_x(x, k):
+    return lax.ppermute(
+        x,
+        "row",
+        [(a * NZ + b, (a + k) % NX * NZ + b) for a in range(NX) for b in range(NZ)],
+    )
 
 
 def on_device(
@@ -399,10 +439,11 @@
         flops=2 * queries * nope_w * lat_w,
         nbytes=2 * heads * nope_w * lat_w,
     )
-    all_queries = [shift((query, swapped)[k % 2], "head", n_head, k) for k in range(n_head)]
-
-    w_rings = [[a * NZ + b for a in range(NX)] for b in range(NZ)]
-    w_cols = lax.all_gather(w_o.T, "row", axis_index_groups=w_rings)
+    all_queries = [shift_y((query, swapped)[k % 2], n_head, k) for k in range(NX)]
+
+    w_t = w_o.T
+    w_near, w_far = shift_x(w_t, 1), shift_x(w_t, -1)
+    depth = w_t.shape[1] // 2
 
     slot_ids = jnp.arange(pages_row, dtype=jnp.int32)
     holds = (page_table[:, :, None] == slot_ids[None, None, :]).astype(jnp.int32)
@@ -412,18 +453,45 @@
     usable = within[None, :, None, :] < limit[:, None, :, None]
     bias = jnp.where(usable, 0.0, NEG).astype(f32).reshape(rows_dev * pages_row * piece, 1)
 
+    got, w_near, w_far = lax.optimization_barrier((got, w_near, w_far))
+    w_cols = [
+        w_t,
+        w_near,
+        w_far,
+        shift_x(w_near[:, :depth], 1),
+        shift_x(w_far[:, depth:], -1),
+    ]
+    key = call(
+        functools.partial(gather_kernel, piece, per_pair, rope_w, pages_row),
+        jax.ShapeDtypeStruct((rows_dev, pages_row * piece, lat_w + TAIL), bf16),
+        [got, bias],
+        flops=2 * slots * tokens * lat_w,
+        nbytes=2 * slots * lat_w,
+    )
+    other = lax.ppermute(key, "head", [(h, h ^ 1) for h in range(n_head)])
+    asked = NX * queries // rows_dev
+    own_part, own_stat = call(
+        functools.partial(own_kernel, scale),
+        (
+            jax.ShapeDtypeStruct((rows_dev, lat_w, asked), f32),
+            jax.ShapeDtypeStruct((rows_dev, 8, asked), f32),
+        ),
+        [key] + all_queries,
+        flops=2 * tokens * asked * (2 * lat_w + TAIL),
+        nbytes=2 * tokens * lat_w,
+    )
     parts = call(
-        functools.partial(attend_kernel, scale, piece, per_pair, rope_w, pages_row),
-        jax.ShapeDtypeStruct((n_head, lat_w + INFO, queries), bf16),
-        [got, bias] + all_queries,
-        flops=2 * n_head * queries * tokens * (2 * lat_w + TAIL) // 2 + 2 * slots * tokens * lat_w,
-        nbytes=2 * (slots + 2 * n_head * queries) * (lat_w + TAIL),
-    )
-    parts = lax.all_to_all(parts, "head", split_axis=0, concat_axis=0, tiled=True)
+        functools.partial(both_kernel, scale),
+        tuple(jax.ShapeDtypeStruct((lat_w + INFO, queries), bf16) for _ in range(NX)),
+        [other, own_part, own_stat] + all_queries,
+        flops=2 * tokens * asked * (2 * lat_w + TAIL),
+        nbytes=2 * tokens * lat_w,
+    )
+    parts = [shift_y(part, n_head, -k) for k, part in enumerate(parts)]
     head_out = call(
         functools.partial(merge_kernel, rows_dev),
         jax.ShapeDtypeStruct((NZ, width, heads * value_w), bf16),
-        [fresh_part, fresh_lse, w_uv, parts],
+        [fresh_part, fresh_lse, w_uv] + parts,
         scratch=[pltpu.VMEM((queries, lat_w), f32)],
         flops=2 * queries * lat_w * value_w,
         nbytes=2 * heads * lat_w * value_w,
@@ -439,7 +507,7 @@
     sums = call(
         functools.partial(project_kernel, width),
         jax.ShapeDtypeStruct((n_head, per_core, width, cols), f32),
-        [ring.reshape(NZ * width, heads * value_w), w_cols],
+        [ring.reshape(NZ * width, heads * value_w)] + w_cols,
         flops=2 * NX * NZ * width * w_o.size,
         nbytes=2 * NX * w_o.size,
     )

time: 142 us -> 141 us (level)
  blocking collectives: 38.1 us -> 0 us
  waiting for transfers between devices: 35.4 us -> 68.3 us
  between operations: 13.7 us -> 0.35 us
  starting transfers between devices: 37.3 us -> 49.5 us
  Pallas kernels: 13.3 us -> 19.6 us
    all_to_all x2 -> x0, blocking collectives: 38.1 us -> none  [the longest x1 24 us: on_device(): lax.all_to_all(parts, 'head', split_axis=0, concat_axis=0, tiled=True)]
    ppermute x7 -> x11, waiting for transfers between devices: 10.7 us -> 47.1 us  [the longest x4 35.5 us: shift_x(): lax.ppermute(x, 'row', [(a * NZ + b, (a + k) % NX * NZ + b) for a in rang...]
    all_to_all x1, waiting for transfers between devices: 12.9 us -> 0.01 us  [on_device(): got = lax.all_to_all(send, 'row', split_axis=0, concat_axis=0, tiled=True)]
    all_to_all x0 -> x1, waiting for transfers between devices: none -> 10.2 us  [on_device(): lax.all_to_all(head_out, 'row', split_axis=0, concat_axis=0, axis_index_g...]
    all_to_all x0 -> x1, starting transfers between devices: none -> 6.39 us  [on_device(): lax.all_to_all(head_out, 'row', split_axis=0, concat_axis=0, axis_index_g...]
    pallas_call x6 -> x8, Pallas kernels: 13.3 us -> 19.6 us  [call(): pl.pallas_call(body, out_shape=out_shape, in_specs=[HBM if i in in_hbm el...]
    ppermute x7 -> x11, starting transfers between devices: 9.68 us -> 15.1 us  [the longest x6 8.18 us: shift_y(): lax.ppermute(x, 'head', [(h, (h + k * cores) % n_head) for h in range(n_h...]
    unnamed x19 -> x17, local copies, waits for them, and re-layouts: 2.2 us -> 0.16 us
  transfers between devices with their start and end apart: 14 -> 18, of which waited for: 7 -> 8; matrix products, arithmetic and copies ran while one was open for 1% -> 2% of each run, Pallas kernels for 8% -> 3%
where the time goes in v4:
time: 141 us
  waiting for transfers between devices  68.3 us (48%)
  starting transfers between devices  49.5 us (35%)
  Pallas kernels  19.6 us (14%)
  local copies, waits for them, and re-layouts  2.52 us (2%)
    ppermute x4, waiting for transfers between devices, shift_x(): lax.ppermute(x, 'row', [(a * NZ + b, (a + k) % NX * NZ + b) for a in rang...  35.5 us
    pallas_call x8, Pallas kernels, call(): pl.pallas_call(body, out_shape=out_shape, in_specs=[HBM if i in in_hbm el...  19.6 us
    all_to_all x1, starting transfers between devices, on_device(): got = lax.all_to_all(send, 'row', split_axis=0, concat_axis=0, tiled=True)  12 us
    ppermute x6, waiting for transfers between devices, shift_y(): lax.ppermute(x, 'head', [(h, (h + k * cores) % n_head) for h in range(n_h...  11.6 us
    all_to_all x1, waiting for transfers between devices, on_device(): lax.all_to_all(head_out, 'row', split_axis=0, concat_axis=0, axis_index_g...  10.2 us
    ppermute x4, starting transfers between devices, on_device(): moved.append(lax.ppermute(pieces[j], ('row', 'head'), pairs))  10.1 us
    ppermute x6, starting transfers between devices, shift_y(): lax.ppermute(x, 'head', [(h, (h + k * cores) % n_head) for h in range(n_h...  8.18 us
    all_to_all x1, waiting for transfers between devices, on_device(): sums = lax.all_to_all(sums, 'head', split_axis=0, concat_axis=0, tiled=True)  6.52 us
  transfers between devices with their start and end apart: 18, of which 8 were waited for; matrix products, arithmetic and copies ran while one was open for 2% of the time, Pallas kernels for 3%

profile of v4, /device:TPU:1, one launch (start us, length us, event | category | flops | bytes accessed | tf_op | source)
XLA Modules:
  0.0 140.5 jit_solution(13273006208712377715)
XLA Ops:
  0.0 4.8 %shard_map.128 = bf16[32,184,128]{2,1,0:T(8,128)(2,1)} custom-call(s32[1,80]{1,0:T(1,128)} %bitcast.19, s32[1,80]{1,0:T(1,128)} %bitcast.20, bf16[80,64,512]{2,1,0:T(8,128)(2,1)} %lat_hbm.1, bf16[80,4096]{1,0:T(8,128)(2,1)} %rope_hbm.1), custom_call_target="tpu_custom_call" | custom-call | flops 838860800 | bytes 2621440 | tf_op jit(solution)/shard_map/pallas_call | solution.py:26
  4.8 0.0 copy-start.6
  4.8 12.0 %all-to-all-start = ((bf16[32,184,128]{2,1,0:T(8,128)(2,1)}), bf16[32,184,128]{2,1,0:T(8,128)(2,1)}, u32[]{:S(2)}, u32[]{:S(2)}) async-start(bf16[32,184,128]{2,1,0:T(8,128)(2,1)} %shard_map.128), calls=%async_computation | async-start | bytes 3014656 | tf_op jit(solution)/shard_map/all_to_all | solution.py:411
  16.9 0.0 copy-start.3
  16.9 0.0 copy-start.4
  16.9 1.2 collective-permute-start
  18.1 1.5 %collective-permute-start.1 = (bf16[224,2048]{1,0:T(8,128)(2,1)}, bf16[224,2048]{1,0:T(8,128)(2,1)}, u32[]{:S(2)}, u32[]{:S(2)}) collective-permute-start(bf16[224,2048]{1,0:T(8,128)(2,1)} %bitcast.8.own_ref), channel_id=1, source_target_pairs={{0,192},{8,200},{16,208},{24,216},{32,224},{40,232},{48,240},{56,2... | collective-permute-start | bytes 2752520 | tf_op jit(solution)/shard_map/ppermute | solution.py:352
  19.7 0.1 select_reduce_fusion
  19.8 0.1 subtract_subtract_fusion
  19.8 0.1 compare_select_fusion
  19.9 0.1 select_n.137.bias_ref
  20.1 35.5 %collective-permute-done.near_ref = bf16[224,2048]{1,0:T(8,128)(2,1)S(1)} collective-permute-done((bf16[224,2048]{1,0:T(8,128)(2,1)}, bf16[224,2048]{1,0:T(8,128)(2,1)S(1)}, u32[]{:S(2)}, u32[]{:S(2)}) %collective-permute-start) | collective-permute-done | bytes 917536 | tf_op jit(solution)/shard_map/ppermute | solution.py:352
  55.5 4.1 %shard_map.129.key_ref = bf16[2,320,640]{2,1,0:T(8,128)(2,1)} custom-call(bf16[32,184,128]{2,1,0:T(8,128)(2,1)} %all-to-all-done.block_ref, f32[640,1]{1,0:T(8,128)S(1)} %select_n.137.bias_ref), custom_call_target="tpu_custom_call" | custom-call | flops 838860800 | bytes 1310720 | tf_op jit(solution)/shard_map/pallas_call | solution.py:26
  59.7 1.4 collective-permute-start.2
  61.1 0.1 reshape.91
  61.2 0.1 pad.9.clone
  61.3 0.1 pad.7.clone
  61.4 0.2 copy.32
  61.6 0.1 copy.35
  61.8 0.9 shard_map.127
  62.6 1.4 collective-permute-start.3
  64.0 2.6 %collective-permute-start.4 = (bf16[640,128]{1,0:T(8,128)(2,1)S(1)}, bf16[640,128]{1,0:T(8,128)(2,1)S(1)}, u32[]{:S(2)}, u32[]{:S(2)}) collective-permute-start(bf16[640,128]{1,0:T(8,128)(2,1)S(1)} %get-tuple-element.25.refs_0_), channel_id=1, source_target_pairs={{0,4},{1,5},{2,6},{3,7},{4,0},{5,1},{6,2},{7,3},{8,12},{9,13},{10,... | collective-permute-start | bytes 491528 | tf_op jit(solution)/shard_map/ppermute | solution.py:348
  66.6 1.1 collective-permute-start.5
  67.7 2.2 %collective-permute-done.3.refs_1_ = bf16[640,128]{1,0:T(8,128)(2,1)S(1)} collective-permute-done((bf16[640,128]{1,0:T(8,128)(2,1)S(1)}, bf16[640,128]{1,0:T(8,128)(2,1)S(1)}, u32[]{:S(2)}, u32[]{:S(2)}) %collective-permute-start.3) | collective-permute-done | bytes 163872 | tf_op jit(solution)/shard_map/ppermute | solution.py:348
  69.9 4.6 %collective-permute-done.4.refs_2_ = bf16[640,128]{1,0:T(8,128)(2,1)S(1)} collective-permute-done((bf16[640,128]{1,0:T(8,128)(2,1)S(1)}, bf16[640,128]{1,0:T(8,128)(2,1)S(1)}, u32[]{:S(2)}, u32[]{:S(2)}) %collective-permute-start.4) | collective-permute-done | bytes 163872 | tf_op jit(solution)/shard_map/ppermute | solution.py:348
  74.5 2.3 %shard_map.130 = (f32[2,512,256]{2,1,0:T(8,128)S(1)}, f32[2,8,256]{2,1,0:T(8,128)S(1)}) custom-call(bf16[2,320,640]{2,1,0:T(8,128)(2,1)} %shard_map.129.key_ref, bf16[640,128]{1,0:T(8,128)(2,1)S(1)} %get-tuple-element.25.refs_0_, bf16[640,128]{1,0:T(8,128)(2,1)S(1)} %collective-permute-done.3.refs_1_, bf16[640,128]{1,0:T(8,128)(2,1)S(1)} %collective-permute-done.4.refs_2_, ...), custom_call_target="tpu_custom_call" | custom-call | flops 377487360 | bytes 655360 | tf_op jit(solution)/shard_map/pallas_call | solution.py:26
  76.8 2.5 %shard_map.131 = (bf16[528,128]{1,0:T(8,128)(2,1)S(1)}, bf16[528,128]{1,0:T(8,128)(2,1)S(1)}, bf16[528,128]{1,0:T(8,128)(2,1)S(1)}, bf16[528,128]{1,0:T(8,128)(2,1)S(1)}) custom-call(bf16[2,320,640]{2,1,0:T(8,128)(2,1)} %collective-permute-done.2.key_ref, f32[2,512,256]{2,1,0:T(8,128)S(1)} %get-tuple-element.27.own_ref, ...), custom_call_target="tpu_custom_call" | custom-call | flops 377487360 | bytes 655360 | tf_op jit(solution)/shard_map/pallas_call | solution.py:26
  79.3 2.3 %collective-permute-start.6 = (bf16[528,128]{1,0:T(8,128)(2,1)S(1)}, bf16[528,128]{1,0:T(8,128)(2,1)S(1)}, u32[]{:S(2)}, u32[]{:S(2)}) collective-permute-start(bf16[528,128]{1,0:T(8,128)(2,1)S(1)} %get-tuple-element.30), channel_id=1, source_target_pairs={{0,6},{1,7},{2,0},{3,1},{4,2},{5,3},{6,4},{7,5},{8,14},{9,15},{10,... | collective-permute-start | bytes 405512 | tf_op jit(solution)/shard_map/ppermute | solution.py:348
  81.6 0.2 collective-permute-start.7
  81.8 0.7 collective-permute-start.8
  82.5 0.6 collective-permute-start.9
  83.1 1.0 slice.11
  84.1 2.2 %collective-permute-start.10 = (bf16[224,1024]{1,0:T(8,128)(2,1)S(1)}, bf16[224,1024]{1,0:T(8,128)(2,1)S(1)}, u32[]{:S(2)}, u32[]{:S(2)}) collective-permute-start(bf16[224,1024]{1,0:T(8,128)(2,1)S(1)} %slice.11), channel_id=1, source_target_pairs={{0,192},{8,200},{16,208},{24,216},{32,224},{40,232},{48,240},{56,2... | collective-permute-start | bytes 1376264 | tf_op jit(solution)/shard_map/ppermute | solution.py:352
  86.3 1.1 collective-permute-done.7.refs_2_
  87.5 3.7 %collective-permute-done.8.refs_3_ = bf16[528,128]{1,0:T(8,128)(2,1)S(1)} collective-permute-done((bf16[528,128]{1,0:T(8,128)(2,1)S(1)}, bf16[528,128]{1,0:T(8,128)(2,1)S(1)}, u32[]{:S(2)}, u32[]{:S(2)}) %collective-permute-start.8) | collective-permute-done | bytes 135200 | tf_op jit(solution)/shard_map/ppermute | solution.py:348
  91.2 1.5 %shard_map.132 = bf16[8,8,2048]{2,1,0:T(8,128)(2,1)} custom-call(f32[512,128]{1,0:T(8,128)S(1)} %get-tuple-element.22.fresh_ref, f32[8,128]{1,0:T(8,128)S(1)} %get-tuple-element.23.fresh_lse_ref, bf16[16,512,128]{2,1,0:T(8,128)(2,1)S(1)} %copy-done, bf16[528,128]{1,0:T(8,128)(2,1)S(1)} %get-tuple-element.29.refs_0_, ...), custom_call_target="tpu_custom_call" | custom-call | flops 16777216 | bytes 2097152 | tf_op jit(solution)/shard_map/pallas_call | solution.py:26
  92.7 6.4 %all-to-all-start.1 = ((bf16[8,8,2048]{2,1,0:T(8,128)(2,1)}), bf16[8,8,2048]{2,1,0:T(8,128)(2,1)S(1)}, u32[]{:S(2)}, u32[]{:S(2)}) async-start(bf16[8,8,2048]{2,1,0:T(8,128)(2,1)} %shard_map.132), calls=%async_computation.1 | async-start | bytes 524288 | tf_op jit(solution)/shard_map/all_to_all | solution.py:501
  99.1 10.2 %all-to-all-done.1 = bf16[8,8,2048]{2,1,0:T(8,128)(2,1)S(1)} async-done(((bf16[8,8,2048]{2,1,0:T(8,128)(2,1)}), bf16[8,8,2048]{2,1,0:T(8,128)(2,1)S(1)}, u32[]{:S(2)}, u32[]{:S(2)}) %all-to-all-start.1) | async-done | bytes 262176 | tf_op jit(solution)/shard_map/all_to_all | solution.py:501
  109.3 3.4 %shard_map.133 = f32[8,4,8,224]{3,2,1,0:T(8,128)} custom-call(bf16[64,2048]{1,0:T(8,128)(2,1)S(1)} %bitcast.14, bf16[224,2048]{1,0:T(8,128)(2,1)} %bitcast.8.own_ref, bf16[224,2048]{1,0:T(8,128)(2,1)S(1)} %collective-permute-done.near_ref, bf16[224,2048]{1,0:T(8,128)(2,1)} %collective-permute-done.1.far_ref, ...), custom_call_target="tpu_custom_call" | custom-call | flops 234881024 | bytes 3670016 | tf_op jit(solution)/shard_map/pallas_call | solution.py:26
  112.7 5.9 %all-to-all-start.2 = ((f32[8,4,8,224]{3,2,1,0:T(8,128)}), f32[8,4,8,224]{3,2,1,0:T(8,128)S(1)}, u32[]{:S(2)}, u32[]{:S(2)}) async-start(f32[8,4,8,224]{3,2,1,0:T(8,128)} %shard_map.133), calls=%async_computation.2 | async-start | bytes 524288 | tf_op jit(solution)/shard_map/all_to_all | solution.py:514
  118.7 6.5 %all-to-all-done.2.in_ref = f32[8,4,8,224]{3,2,1,0:T(8,128)S(1)} async-done(((f32[8,4,8,224]{3,2,1,0:T(8,128)}), f32[8,4,8,224]{3,2,1,0:T(8,128)S(1)}, u32[]{:S(2)}, u32[]{:S(2)}) %all-to-all-start.2) | async-done | bytes 229408 | tf_op jit(solution)/shard_map/all_to_all | solution.py:514
  125.2 0.1 collective-permute-start.11
  125.3 3.8 %collective-permute-start.12 = (bf16[8,224]{1,0:T(8,128)(2,1)S(1)}, bf16[8,224]{1,0:T(8,128)(2,1)S(1)}, u32[]{:S(2)}, u32[]{:S(2)}) collective-permute-start(bf16[8,224]{1,0:T(8,128)(2,1)S(1)} %get-tuple-element.36), channel_id=1, source_target_pairs={{0,16},{1,48},{2,18},{3,50},{4,20},{5,52},{6,22},{7,54},{8,24},{9,... | collective-permute-start | bytes 10760 | tf_op jit(solution)/shard_map/ppermute | solution.py:529
  129.1 1.9 %collective-permute-start.13 = (bf16[8,224]{1,0:T(8,128)(2,1)S(1)}, bf16[8,224]{1,0:T(8,128)(2,1)S(1)}, u32[]{:S(2)}, u32[]{:S(2)}) collective-permute-start(bf16[8,224]{1,0:T(8,128)(2,1)S(1)} %get-tuple-element.37), channel_id=1, source_target_pairs={{0,8},{1,40},{2,10},{3,42},{4,12},{5,44},{6,14},{7,46},{8,16},{9,4... | collective-permute-start | bytes 10760 | tf_op jit(solution)/shard_map/ppermute | solution.py:529
  131.0 4.3 %collective-permute-start.14 = (bf16[8,224]{1,0:T(8,128)(2,1)S(1)}, bf16[8,224]{1,0:T(8,128)(2,1)S(1)}, u32[]{:S(2)}, u32[]{:S(2)}) collective-permute-start(bf16[8,224]{1,0:T(8,128)(2,1)S(1)} %get-tuple-element.38), channel_id=1, source_target_pairs={{0,0},{1,32},{2,2},{3,34},{4,4},{5,36},{6,6},{7,38},{8,8},{9,40},{... | collective-permute-start | bytes 10760 | tf_op jit(solution)/shard_map/ppermute | solution.py:529
  135.4 4.4 %collective-permute-done.14 = bf16[8,224]{1,0:T(8,128)(2,1)S(1)} collective-permute-done((bf16[8,224]{1,0:T(8,128)(2,1)S(1)}, bf16[8,224]{1,0:T(8,128)(2,1)S(1)}, u32[]{:S(2)}, u32[]{:S(2)}) %collective-permute-start.14) | collective-permute-done | bytes 3616 | tf_op jit(solution)/shard_map/ppermute | solution.py:529
  139.8 0.1 pad_maximum_fusion.1
  139.9 0.6 reshape.99
  (36 shorter events, 0.3 us)
Async XLA Ops:
  4.8 14.8 %copy-start.6 = (s32[2,40]{1,0:T(2,128)S(1)}, s32[2,40]{1,0:T(2,128)}, u32[]{:S(2)}) copy-start(s32[2,40]{1,0:T(2,128)} %param.21) | copy-start | bytes 964
  4.8 14.9 %copy-start.7 = (s32[2]{0:T(128)S(1)}, s32[2]{0:T(128)}, u32[]{:S(2)}) copy-start(s32[2]{0:T(128)} %param.22) | copy-start | bytes 28
  4.8 50.7 %all-to-all-start = ((bf16[32,184,128]{2,1,0:T(8,128)(2,1)}), bf16[32,184,128]{2,1,0:T(8,128)(2,1)}, u32[]{:S(2)}, u32[]{:S(2)}) async-start(bf16[32,184,128]{2,1,0:T(8,128)(2,1)} %shard_map.128), calls=%async_computation | async-start | bytes 3014656 | tf_op jit(solution)/shard_map/all_to_all | solution.py:411
  16.9 44.2 %copy-start.2 = (bf16[4,2,16,128]{3,2,1,0:T(8,128)(2,1)S(1)}, bf16[4,2,16,128]{3,2,1,0:T(8,128)(2,1)}, u32[]{:S(2)}) copy-start(bf16[4,2,16,128]{3,2,1,0:T(8,128)(2,1)} %param.13) | copy-start | bytes 98308
  16.9 44.2 %copy-start.3 = (bf16[4,2,1024]{2,1,0:T(2,128)(2,1)S(1)}, bf16[4,2,1024]{2,1,0:T(2,128)(2,1)}, u32[]{:S(2)}) copy-start(bf16[4,2,1024]{2,1,0:T(2,128)(2,1)} %param.14) | copy-start | bytes 49156
  16.9 44.3 %copy-start.4 = (bf16[4,2,512]{2,1,0:T(2,128)(2,1)S(1)}, bf16[4,2,512]{2,1,0:T(2,128)(2,1)}, u32[]{:S(2)}) copy-start(bf16[4,2,512]{2,1,0:T(2,128)(2,1)} %param.15) | copy-start | bytes 24580
  16.9 44.5 %copy-start.5 = (bf16[4,2,64]{2,1,0:T(2,128)(2,1)S(1)}, bf16[4,2,64]{2,1,0:T(2,128)(2,1)}, u32[]{:S(2)}) copy-start(bf16[4,2,64]{2,1,0:T(2,128)(2,1)} %param.16) | copy-start | bytes 3076
  16.9 38.6 %collective-permute-start = (bf16[224,2048]{1,0:T(8,128)(2,1)}, bf16[224,2048]{1,0:T(8,128)(2,1)S(1)}, u32[]{:S(2)}, u32[]{:S(2)}) collective-permute-start(bf16[224,2048]{1,0:T(8,128)(2,1)} %bitcast.8.own_ref), channel_id=1, source_target_pairs={{0,64},{8,72},{16,80},{24,88},{32,96},{40,104},{48,112},{56,120},{... | collective-permute-start | bytes 2752520 | tf_op jit(solution)/shard_map/ppermute | solution.py:352
  18.1 37.4 %collective-permute-start.1 = (bf16[224,2048]{1,0:T(8,128)(2,1)}, bf16[224,2048]{1,0:T(8,128)(2,1)}, u32[]{:S(2)}, u32[]{:S(2)}) collective-permute-start(bf16[224,2048]{1,0:T(8,128)(2,1)} %bitcast.8.own_ref), channel_id=1, source_target_pairs={{0,192},{8,200},{16,208},{24,216},{32,224},{40,232},{48,240},{56,2... | collective-permute-start | bytes 2752520 | tf_op jit(solution)/shard_map/ppermute | solution.py:352
  20.1 41.7 %copy-start.1 = (bf16[16,128,512]{2,1,0:T(8,128)(2,1)S(1)}, bf16[16,128,512]{2,1,0:T(8,128)(2,1)}, u32[]{:S(2)}) copy-start(bf16[16,128,512]{2,1,0:T(8,128)(2,1)} %w_ref.2) | copy-start | bytes 6291460
  59.7 17.2 %collective-permute-start.2 = (bf16[2,320,640]{2,1,0:T(8,128)(2,1)}, bf16[2,320,640]{2,1,0:T(8,128)(2,1)}, u32[]{:S(2)}, u32[]{:S(2)}) collective-permute-start(bf16[2,320,640]{2,1,0:T(8,128)(2,1)} %shard_map.129.key_ref), channel_id=1, source_target_pairs={{0,1},{1,0},{2,3},{3,2},{4,5},{5,4},{6,7},{7,6},{8,9},{9,8},{10,11... | collective-permute-start | bytes 2457608 | tf_op jit(solution)/shard_map/ppermute | solution.py:471
  62.6 7.3 %collective-permute-start.3 = (bf16[640,128]{1,0:T(8,128)(2,1)S(1)}, bf16[640,128]{1,0:T(8,128)(2,1)S(1)}, u32[]{:S(2)}, u32[]{:S(2)}) collective-permute-start(bf16[640,128]{1,0:T(8,128)(2,1)S(1)} %get-tuple-element.26), channel_id=1, source_target_pairs={{0,2},{1,3},{2,4},{3,5},{4,6},{5,7},{6,0},{7,1},{8,10},{9,11},{10,... | collective-permute-start | bytes 491528 | tf_op jit(solution)/shard_map/ppermute | solution.py:348
  64.0 10.5 %collective-permute-start.4 = (bf16[640,128]{1,0:T(8,128)(2,1)S(1)}, bf16[640,128]{1,0:T(8,128)(2,1)S(1)}, u32[]{:S(2)}, u32[]{:S(2)}) collective-permute-start(bf16[640,128]{1,0:T(8,128)(2,1)S(1)} %get-tuple-element.25.refs_0_), channel_id=1, source_target_pairs={{0,4},{1,5},{2,6},{3,7},{4,0},{5,1},{6,2},{7,3},{8,12},{9,13},{10,... | collective-permute-start | bytes 491528 | tf_op jit(solution)/shard_map/ppermute | solution.py:348
  66.6 7.9 %collective-permute-start.5 = (bf16[640,128]{1,0:T(8,128)(2,1)S(1)}, bf16[640,128]{1,0:T(8,128)(2,1)S(1)}, u32[]{:S(2)}, u32[]{:S(2)}) collective-permute-start(bf16[640,128]{1,0:T(8,128)(2,1)S(1)} %get-tuple-element.26), channel_id=1, source_target_pairs={{0,6},{1,7},{2,0},{3,1},{4,2},{5,3},{6,4},{7,5},{8,14},{9,15},{10,... | collective-permute-start | bytes 491528 | tf_op jit(solution)/shard_map/ppermute | solution.py:348
  76.8 14.3 %copy-start = (bf16[16,512,128]{2,1,0:T(8,128)(2,1)S(1)}, bf16[16,512,128]{2,1,0:T(8,128)(2,1)}, u32[]{:S(2)}) copy-start(bf16[16,512,128]{2,1,0:T(8,128)(2,1)} %w_ref.3) | copy-start | bytes 6291460
  79.3 7.0 %collective-permute-start.6 = (bf16[528,128]{1,0:T(8,128)(2,1)S(1)}, bf16[528,128]{1,0:T(8,128)(2,1)S(1)}, u32[]{:S(2)}, u32[]{:S(2)}) collective-permute-start(bf16[528,128]{1,0:T(8,128)(2,1)S(1)} %get-tuple-element.30), channel_id=1, source_target_pairs={{0,6},{1,7},{2,0},{3,1},{4,2},{5,3},{6,4},{7,5},{8,14},{9,15},{10,... | collective-permute-start | bytes 405512 | tf_op jit(solution)/shard_map/ppermute | solution.py:348
  81.6 5.9 %collective-permute-start.7 = (bf16[528,128]{1,0:T(8,128)(2,1)S(1)}, bf16[528,128]{1,0:T(8,128)(2,1)S(1)}, u32[]{:S(2)}, u32[]{:S(2)}) collective-permute-start(bf16[528,128]{1,0:T(8,128)(2,1)S(1)} %get-tuple-element.31), channel_id=1, source_target_pairs={{0,4},{1,5},{2,6},{3,7},{4,0},{5,1},{6,2},{7,3},{8,12},{9,13},{10,... | collective-permute-start | bytes 405512 | tf_op jit(solution)/shard_map/ppermute | solution.py:348
  81.8 9.4 %collective-permute-start.8 = (bf16[528,128]{1,0:T(8,128)(2,1)S(1)}, bf16[528,128]{1,0:T(8,128)(2,1)S(1)}, u32[]{:S(2)}, u32[]{:S(2)}) collective-permute-start(bf16[528,128]{1,0:T(8,128)(2,1)S(1)} %get-tuple-element.32), channel_id=1, source_target_pairs={{0,2},{1,3},{2,4},{3,5},{4,6},{5,7},{6,0},{7,1},{8,10},{9,11},{10,... | collective-permute-start | bytes 405512 | tf_op jit(solution)/shard_map/ppermute | solution.py:348
  82.5 16.6 %collective-permute-start.9 = (bf16[224,1024]{1,0:T(8,128)(2,1)S(1)}, bf16[224,1024]{1,0:T(8,128)(2,1)S(1)}, u32[]{:S(2)}, u32[]{:S(2)}) collective-permute-start(bf16[224,1024]{1,0:T(8,128)(2,1)S(1)} %slice.10), channel_id=1, source_target_pairs={{0,64},{8,72},{16,80},{24,88},{32,96},{40,104},{48,112},{56,120},{... | collective-permute-start | bytes 1376264 | tf_op jit(solution)/shard_map/ppermute | solution.py:352
  84.1 15.0 %collective-permute-start.10 = (bf16[224,1024]{1,0:T(8,128)(2,1)S(1)}, bf16[224,1024]{1,0:T(8,128)(2,1)S(1)}, u32[]{:S(2)}, u32[]{:S(2)}) collective-permute-start(bf16[224,1024]{1,0:T(8,128)(2,1)S(1)} %slice.11), channel_id=1, source_target_pairs={{0,192},{8,200},{16,208},{24,216},{32,224},{40,232},{48,240},{56,2... | collective-permute-start | bytes 1376264 | tf_op jit(solution)/shard_map/ppermute | solution.py:352
  92.7 16.6 %all-to-all-start.1 = ((bf16[8,8,2048]{2,1,0:T(8,128)(2,1)}), bf16[8,8,2048]{2,1,0:T(8,128)(2,1)S(1)}, u32[]{:S(2)}, u32[]{:S(2)}) async-start(bf16[8,8,2048]{2,1,0:T(8,128)(2,1)} %shard_map.132), calls=%async_computation.1 | async-start | bytes 524288 | tf_op jit(solution)/shard_map/all_to_all | solution.py:501
  112.7 12.4 %all-to-all-start.2 = ((f32[8,4,8,224]{3,2,1,0:T(8,128)}), f32[8,4,8,224]{3,2,1,0:T(8,128)S(1)}, u32[]{:S(2)}, u32[]{:S(2)}) async-start(f32[8,4,8,224]{3,2,1,0:T(8,128)} %shard_map.133), calls=%async_computation.2 | async-start | bytes 524288 | tf_op jit(solution)/shard_map/all_to_all | solution.py:514
  125.2 10.2 %collective-permute-start.11 = (bf16[8,224]{1,0:T(8,128)(2,1)S(1)}, bf16[8,224]{1,0:T(8,128)(2,1)S(1)}, u32[]{:S(2)}, u32[]{:S(2)}) collective-permute-start(bf16[8,224]{1,0:T(8,128)(2,1)S(1)} %get-tuple-element.35), channel_id=1, source_target_pairs={{0,24},{1,56},{2,26},{3,58},{4,28},{5,60},{6,30},{7,62},{8,0},{9,3... | collective-permute-start | bytes 10760 | tf_op jit(solution)/shard_map/ppermute | solution.py:529
  125.3 10.1 %collective-permute-start.12 = (bf16[8,224]{1,0:T(8,128)(2,1)S(1)}, bf16[8,224]{1,0:T(8,128)(2,1)S(1)}, u32[]{:S(2)}, u32[]{:S(2)}) collective-permute-start(bf16[8,224]{1,0:T(8,128)(2,1)S(1)} %get-tuple-element.36), channel_id=1, source_target_pairs={{0,16},{1,48},{2,18},{3,50},{4,20},{5,52},{6,22},{7,54},{8,24},{9,... | collective-permute-start | bytes 10760 | tf_op jit(solution)/shard_map/ppermute | solution.py:529
  129.1 6.3 %collective-permute-start.13 = (bf16[8,224]{1,0:T(8,128)(2,1)S(1)}, bf16[8,224]{1,0:T(8,128)(2,1)S(1)}, u32[]{:S(2)}, u32[]{:S(2)}) collective-permute-start(bf16[8,224]{1,0:T(8,128)(2,1)S(1)} %get-tuple-element.37), channel_id=1, source_target_pairs={{0,8},{1,40},{2,10},{3,42},{4,12},{5,44},{6,14},{7,46},{8,16},{9,4... | collective-permute-start | bytes 10760 | tf_op jit(solution)/shard_map/ppermute | solution.py:529
  131.0 8.8 %collective-permute-start.14 = (bf16[8,224]{1,0:T(8,128)(2,1)S(1)}, bf16[8,224]{1,0:T(8,128)(2,1)S(1)}, u32[]{:S(2)}, u32[]{:S(2)}) collective-permute-start(bf16[8,224]{1,0:T(8,128)(2,1)S(1)} %get-tuple-element.38), channel_id=1, source_target_pairs={{0,0},{1,32},{2,2},{3,34},{4,4},{5,36},{6,6},{7,38},{8,8},{9,40},{... | collective-permute-start | bytes 10760 | tf_op jit(solution)/shard_map/ppermute | solution.py:529

commit v5 on v4

--- a/solution.py
+++ b/solution.py
@@ -172,7 +172,21 @@
     lse_ref[...] = jnp.broadcast_to(high + jnp.log(total), lse_ref.shape)
 
 
-def gather_kernel(piece, per_pair, rope_w, pages_row, block_ref, bias_ref, key_ref):
+def gather_kernel(
+    piece,
+    per_pair,
+    rope_w,
+    pages_row,
+    block_hbm,
+    bias_ref,
+    key_hbm,
+    block_ref,
+    lat_ref,
+    tail_ref,
+    key_ref,
+    in_sem,
+    out_sem,
+):
     rows, per_row, key_w = key_ref.shape
     count, block, _ = block_ref.shape
     cuts = (key_w - TAIL) // TAIL
@@ -183,9 +197,31 @@
     rope_rows = piece * rope_w // TAIL
     half = per_row // 2
 
-    tail = block_ref[:, lat_rows:, :].astype(jnp.float32)
-    marked = iota(tail.shape, 1) == per_pair * rope_rows
-    labels = jnp.sum(jnp.where(marked, tail, 0.0), axis=1).astype(jnp.bfloat16)
+    chunks = in_sem.shape[0]
+    step = count // chunks
+    copies = []
+    for i in range(chunks):
+        here = pl.ds(i * step, step)
+        copy = pltpu.make_async_copy(block_hbm.at[here], block_ref.at[here], in_sem.at[i])
+        copy.start()
+        copies.append(copy)
+    labels = []
+    for i, copy in enumerate(copies):
+        copy.wait()
+        here = slice(i * step, (i + 1) * step)
+        tail = block_ref[here, lat_rows:, :].astype(jnp.float32)
+        marked = iota(tail.shape, 1) == per_pair * rope_rows
+        labels.append(jnp.sum(jnp.where(marked, tail, 0.0), axis=1))
+        tail_ref[i * step * rest : (i + 1) * step * rest, :] = tail.reshape(
+            step * rest, TAIL
+        ).astype(jnp.bfloat16)
+        lat = block_ref[here, :lat_rows, :].astype(jnp.float32)
+        lat = lat.reshape(step * per_pair, cuts, piece, TAIL)
+        for c in range(cuts):
+            lat_ref[i * step * pair_tokens : (i + 1) * step * pair_tokens, pl.ds(c * TAIL, TAIL)] = (
+                lat[:, c].reshape(step * pair_tokens, TAIL).astype(jnp.bfloat16)
+            )
+    labels = jnp.concatenate(labels, axis=0).astype(jnp.bfloat16)
 
     def slot_of(columns, group, lane):
         spread = ones_where(iota((TAIL, columns), 0) == lane)
@@ -201,28 +237,27 @@
     target = row * (per_row - pages_row * (piece // 2)) + token % 2 * half
     target = target + slot * (piece // 2) + token // 2
     target = jnp.where(slot >= 0, target, -1)
-    lat = block_ref[:, :lat_rows, :].astype(jnp.float32)
-    lat = lat.reshape(count * per_pair, cuts, piece, TAIL)
-    lat = [lat[:, c].reshape(count * pair_tokens, TAIL) for c in range(cuts)]
-    lat = jnp.concatenate(lat, axis=1).astype(jnp.bfloat16)
-    for b in range(rows):
-        pick = ones_where(iota((per_row, 1), 0) + b * per_row == target)
-        key_ref[b, :, :lat_w] = dot(pick, lat).astype(jnp.bfloat16)
-
     columns = count * rest
     inner = iota((1, columns), 1) % rest
     lane = jnp.where(inner < per_pair * rope_rows, inner // rope_rows * piece, TAIL)
     slot = slot_of(columns, rest, lane)
-    target = jnp.where(slot >= 0, slot * rope_rows + inner % rope_rows, -1)
-    tail = tail.reshape(columns, TAIL).astype(jnp.bfloat16)
-    rope = dot(ones_where(iota((rows * half, 1), 0) == target), tail)
+    rope_target = jnp.where(slot >= 0, slot * rope_rows + inner % rope_rows, -1)
+    copies = []
     for b in range(rows):
-        rope_b = rope[b * half : (b + 1) * half]
+        pick = ones_where(iota((half, 1), 0) + b * half == rope_target)
+        rope_b = dot(pick, tail_ref[...])
         rope_b = jnp.concatenate([rope_b, pltpu.roll(rope_b, TAIL - rope_w, 1)], axis=0)
         lane = iota(rope_b.shape, 1)
         bias = bias_ref[b * per_row : (b + 1) * per_row]
         rope_b = jnp.where(lane < rope_w, rope_b, jnp.where(lane == rope_w, bias, 0.0))
         key_ref[b, :, lat_w:] = rope_b.astype(jnp.bfloat16)
+        pick = ones_where(iota((per_row, 1), 0) + b * per_row == target)
+        key_ref[b, :, :lat_w] = dot(pick, lat_ref[...]).astype(jnp.bfloat16)
+        copy = pltpu.make_async_copy(key_ref.at[b], key_hbm.at[b], out_sem.at[b])
+        copy.start()
+        copies.append(copy)
+    for copy in copies:
+        copy.wait()
 
 
 def attend(scale, key, query, lat_w):
@@ -313,7 +348,13 @@
             out_ref[copy, :, head * value_w : (head + 1) * value_w] = value
 
 
-def project_kernel(width, x_ref, own_ref, near_ref, far_ref, opp_a_ref, opp_b_ref, out_ref):
+def project_kernel(width, x_ref, *refs):
+    w_hbm, out_ref, w_refs, sem_ref = refs[:5], refs[5], refs[6:11], refs[11]
+    copies = [
+        pltpu.make_async_copy(w_hbm[i], w_refs[i], sem_ref.at[i]) for i in range(len(w_refs))
+    ]
+    for copy in copies:
+        copy.start()
     per_core = out_ref.shape[1]
     cores = out_ref.shape[0] // NX
     here = lax.axis_index("row") // NZ
@@ -326,11 +367,13 @@
                 first = (core * per_core + i) * width
                 out_ref[owner * cores + core, i] = block[first : first + width]
 
-    put(0, dot_t(x_ref[...], own_ref[...]))
-    put(1, dot_t(x_ref[...], near_ref[...]))
-    put(NX - 1, dot_t(x_ref[...], far_ref[...]))
-    opposite = dot_t(x_ref[:, :depth], opp_a_ref[...]) + dot_t(x_ref[:, depth:], opp_b_ref[...])
-    put(NX // 2, opposite)
+    for i, k in enumerate((0, 1, NX - 1)):
+        copies[i].wait()
+        put(k, dot_t(x_ref[...], w_refs[i][...]))
+    copies[3].wait()
+    opposite = dot_t(x_ref[:, :depth], w_refs[3][...])
+    copies[4].wait()
+    put(NX // 2, opposite + dot_t(x_ref[:, depth:], w_refs[4][...]))
 
 
 def sum_kernel(in_ref, *outs):
@@ -453,7 +496,7 @@
     usable = within[None, :, None, :] < limit[:, None, :, None]
     bias = jnp.where(usable, 0.0, NEG).astype(f32).reshape(rows_dev * pages_row * piece, 1)
 
-    got, w_near, w_far = lax.optimization_barrier((got, w_near, w_far))
+    got, w_near, w_far, all_queries = lax.optimization_barrier((got, w_near, w_far, all_queries))
     w_cols = [
         w_t,
         w_near,
@@ -465,8 +508,18 @@
         functools.partial(gather_kernel, piece, per_pair, rope_w, pages_row),
         jax.ShapeDtypeStruct((rows_dev, pages_row * piece, lat_w + TAIL), bf16),
         [got, bias],
+        scratch=[
+            pltpu.VMEM(got.shape, bf16),
+            pltpu.VMEM((slots, lat_w), bf16),
+            pltpu.VMEM((n_row * (block - lat_rows), TAIL), bf16),
+            pltpu.VMEM((rows_dev, pages_row * piece, lat_w + TAIL), bf16),
+            pltpu.SemaphoreType.DMA((4,)),
+            pltpu.SemaphoreType.DMA((rows_dev,)),
+        ],
         flops=2 * slots * tokens * lat_w,
         nbytes=2 * slots * lat_w,
+        out_spec=HBM,
+        in_hbm=(0,),
     )
     other = lax.ppermute(key, "head", [(h, h ^ 1) for h in range(n_head)])
     asked = NX * queries // rows_dev
@@ -508,8 +561,10 @@
         functools.partial(project_kernel, width),
         jax.ShapeDtypeStruct((n_head, per_core, width, cols), f32),
         [ring.reshape(NZ * width, heads * value_w)] + w_cols,
+        scratch=[pltpu.VMEM(w.shape, bf16) for w in w_cols] + [pltpu.SemaphoreType.DMA((5,))],
         flops=2 * NX * NZ * width * w_o.size,
         nbytes=2 * NX * w_o.size,
+        in_hbm=(1, 2, 3, 4, 5),
     )
     sums = lax.all_to_all(sums, "head", split_axis=0, concat_axis=0, tiled=True)
     pieces = call(

time: 141 us -> 127 us (0.901)
  waiting for transfers between devices: 68.3 us -> 55.7 us
  Pallas kernels: 19.6 us -> 17.1 us
  local copies, waits for them, and re-layouts: 2.52 us -> 3.99 us
    ppermute x4, waiting for transfers between devices: 35.5 us -> 23.2 us  [shift_x(): lax.ppermute(x, 'row', [(a * NZ + b, (a + k) % NX * NZ + b) for a in rang...]
    pallas_call x8, Pallas kernels: 19.6 us -> 17.1 us  [call(): pl.pallas_call(body, out_shape=out_shape, in_specs=[HBM if i in in_hbm el...]
    ppermute x6, waiting for transfers between devices: 11.6 us -> 9.83 us  [shift_y(): lax.ppermute(x, 'head', [(h, (h + k * cores) % n_head) for h in range(n_h...]
  transfers between devices with their start and end apart: 18 -> 18, of which waited for: 8 -> 9; matrix products, arithmetic and copies ran while one was open for 2% -> 2% of each run, Pallas kernels for 3% -> 3%
where the time goes in v5:
time: 127 us
  waiting for transfers between devices  55.7 us (44%)
  starting transfers between devices  49.1 us (39%)
  Pallas kernels  17.1 us (13%)
  local copies, waits for them, and re-layouts  3.99 us (3%)
    ppermute x4, waiting for transfers between devices, shift_x(): lax.ppermute(x, 'row', [(a * NZ + b, (a + k) % NX * NZ + b) for a in rang...  23.2 us
    pallas_call x8, Pallas kernels, call(): pl.pallas_call(body, out_shape=out_shape, in_specs=[HBM if i in in_hbm el...  17.1 us
    all_to_all x1, starting transfers between devices, on_device(): got = lax.all_to_all(send, 'row', split_axis=0, concat_axis=0, tiled=True)  12.1 us
    all_to_all x1, waiting for transfers between devices, on_device(): lax.all_to_all(head_out, 'row', split_axis=0, concat_axis=0, axis_index_g...  10.7 us
    ppermute x4, starting transfers between devices, on_device(): moved.append(lax.ppermute(pieces[j], ('row', 'head'), pairs))  9.92 us
    ppermute x6, waiting for transfers between devices, shift_y(): lax.ppermute(x, 'head', [(h, (h + k * cores) % n_head) for h in range(n_h...  9.83 us
    ppermute x6, starting transfers between devices, shift_y(): lax.ppermute(x, 'head', [(h, (h + k * cores) % n_head) for h in range(n_h...  8.24 us
    all_to_all x1, waiting for transfers between devices, on_device(): sums = lax.all_to_all(sums, 'head', split_axis=0, concat_axis=0, tiled=True)  6.52 us
  transfers between devices with their start and end apart: 18, of which 9 were waited for; matrix products, arithmetic and copies ran while one was open for 2% of the time, Pallas kernels for 3%

profile of v5, /device:TPU:1, one launch (start us, length us, event | category | flops | bytes accessed | tf_op | source)
XLA Modules:
  0.0 126.6 jit_solution(5867537652614494692)
XLA Ops:
  0.0 4.8 %shard_map.128 = bf16[32,184,128]{2,1,0:T(8,128)(2,1)} custom-call(s32[1,80]{1,0:T(1,128)} %bitcast.22, s32[1,80]{1,0:T(1,128)} %bitcast.23, bf16[80,64,512]{2,1,0:T(8,128)(2,1)} %lat_hbm.1, bf16[80,4096]{1,0:T(8,128)(2,1)} %rope_hbm.1), custom_call_target="tpu_custom_call" | custom-call | flops 838860800 | bytes 2621440 | tf_op jit(solution)/shard_map/pallas_call | solution.py:26
  4.8 0.0 copy-start.8
  4.9 12.1 %all-to-all-start = ((bf16[32,184,128]{2,1,0:T(8,128)(2,1)}), bf16[32,184,128]{2,1,0:T(8,128)(2,1)}, u32[]{:S(2)}, u32[]{:S(2)}) async-start(bf16[32,184,128]{2,1,0:T(8,128)(2,1)} %shard_map.128), calls=%async_computation | async-start | bytes 3014656 | tf_op jit(solution)/shard_map/all_to_all | solution.py:454
  17.0 1.2 collective-permute-start
  18.3 1.5 %collective-permute-start.1 = (bf16[224,2048]{1,0:T(8,128)(2,1)}, bf16[224,2048]{1,0:T(8,128)(2,1)}, u32[]{:S(2)}, u32[]{:S(2)}) collective-permute-start(bf16[224,2048]{1,0:T(8,128)(2,1)} %bitcast.16), channel_id=1, source_target_pairs={{0,192},{8,200},{16,208},{24,216},{32,224},{40,232},{48,240},{56,2... | collective-permute-start | bytes 2752520 | tf_op jit(solution)/shard_map/ppermute | solution.py:395
  19.8 0.1 pad.7.clone
  19.9 0.2 copy.32
  20.1 0.1 copy.35
  20.3 0.1 reshape.91
  20.4 0.1 pad.9.clone
  20.5 0.9 shard_map.127
  21.4 0.7 copy-done.3
  22.1 1.3 %collective-permute-start.2 = (bf16[640,128]{1,0:T(8,128)(2,1)S(1)}, bf16[640,128]{1,0:T(8,128)(2,1)S(1)}, u32[]{:S(2)}, u32[]{:S(2)}) collective-permute-start(bf16[640,128]{1,0:T(8,128)(2,1)S(1)} %get-tuple-element.29), channel_id=1, source_target_pairs={{0,2},{1,3},{2,4},{3,5},{4,6},{5,7},{6,0},{7,1},{8,10},{9,11},{10,... | collective-permute-start | bytes 491528 | tf_op jit(solution)/shard_map/ppermute | solution.py:391
  23.4 1.4 %collective-permute-start.4 = (bf16[640,128]{1,0:T(8,128)(2,1)S(1)}, bf16[640,128]{1,0:T(8,128)(2,1)S(1)}, u32[]{:S(2)}, u32[]{:S(2)}) collective-permute-start(bf16[640,128]{1,0:T(8,128)(2,1)S(1)} %get-tuple-element.29), channel_id=1, source_target_pairs={{0,6},{1,7},{2,0},{3,1},{4,2},{5,3},{6,4},{7,5},{8,14},{9,15},{10,... | collective-permute-start | bytes 491528 | tf_op jit(solution)/shard_map/ppermute | solution.py:391
  24.8 1.6 %collective-permute-start.3 = (bf16[640,128]{1,0:T(8,128)(2,1)S(1)}, bf16[640,128]{1,0:T(8,128)(2,1)S(1)}, u32[]{:S(2)}, u32[]{:S(2)}) collective-permute-start(bf16[640,128]{1,0:T(8,128)(2,1)S(1)} %get-tuple-element.31.refs_0_), channel_id=1, source_target_pairs={{0,4},{1,5},{2,6},{3,7},{4,0},{5,1},{6,2},{7,3},{8,12},{9,13},{10,... | collective-permute-start | bytes 491528 | tf_op jit(solution)/shard_map/ppermute | solution.py:391
  26.5 0.1 select_reduce_fusion
  26.6 0.1 subtract_subtract_fusion
  26.6 0.1 compare_select_fusion
  26.7 0.1 select_n.137.bias_ref
  26.9 1.1 collective-permute-done.2.refs_1_
  27.9 4.5 %collective-permute-done.3.refs_2_ = bf16[640,128]{1,0:T(8,128)(2,1)S(1)} collective-permute-done((bf16[640,128]{1,0:T(8,128)(2,1)S(1)}, bf16[640,128]{1,0:T(8,128)(2,1)S(1)}, u32[]{:S(2)}, u32[]{:S(2)}) %collective-permute-start.3) | collective-permute-done | bytes 163872 | tf_op jit(solution)/shard_map/ppermute | solution.py:391
  32.5 23.2 %collective-permute-done.refs_1_ = bf16[224,2048]{1,0:T(8,128)(2,1)S(1)} collective-permute-done((bf16[224,2048]{1,0:T(8,128)(2,1)}, bf16[224,2048]{1,0:T(8,128)(2,1)S(1)}, u32[]{:S(2)}, u32[]{:S(2)}) %collective-permute-start) | collective-permute-done | bytes 917536 | tf_op jit(solution)/shard_map/ppermute | solution.py:395
  55.7 3.4 %shard_map.129.key_ref = bf16[2,320,640]{2,1,0:T(8,128)(2,1)S(1)} custom-call(bf16[32,184,128]{2,1,0:T(8,128)(2,1)} %all-to-all-done.block_hbm, f32[640,1]{1,0:T(8,128)S(1)} %select_n.137.bias_ref), custom_call_target="tpu_custom_call" | custom-call | flops 838860800 | bytes 1310720 | tf_op jit(solution)/shard_map/pallas_call | solution.py:26
  59.1 1.4 %collective-permute-start.5 = (bf16[2,320,640]{2,1,0:T(8,128)(2,1)S(1)}, bf16[2,320,640]{2,1,0:T(8,128)(2,1)S(1)}, u32[]{:S(2)}, u32[]{:S(2)}) collective-permute-start(bf16[2,320,640]{2,1,0:T(8,128)(2,1)S(1)} %shard_map.129.key_ref), channel_id=1, source_target_pairs={{0,1},{1,0},{2,3},{3,2},{4,5},{5,4},{6,7},{7,6},{8,9},{9,8},{10,11... | collective-permute-start | bytes 2457608 | tf_op jit(solution)/shard_map/ppermute | solution.py:524
  60.5 1.2 shard_map.130
  61.7 0.8 collective-permute-done.5.key_ref
  62.5 1.2 shard_map.131
  63.6 2.8 %collective-permute-start.6 = (bf16[528,128]{1,0:T(8,128)(2,1)S(1)}, bf16[528,128]{1,0:T(8,128)(2,1)S(1)}, u32[]{:S(2)}, u32[]{:S(2)}) collective-permute-start(bf16[528,128]{1,0:T(8,128)(2,1)S(1)} %get-tuple-element.38), channel_id=1, source_target_pairs={{0,6},{1,7},{2,0},{3,1},{4,2},{5,3},{6,4},{7,5},{8,14},{9,15},{10,... | collective-permute-start | bytes 405512 | tf_op jit(solution)/shard_map/ppermute | solution.py:391
  66.5 0.5 collective-permute-start.7
  66.9 0.6 collective-permute-start.8
  67.6 0.6 collective-permute-start.9
  68.2 1.8 %slice.11 = bf16[224,1024]{1,0:T(8,128)(2,1)} slice(bf16[224,2048]{1,0:T(8,128)(2,1)} %collective-permute-done.1.refs_2_), slice={[0:224], [1024:2048]} | slice | bytes 917504 | tf_op jit(solution)/shard_map/slice | solution.py:505
  70.0 2.1 %collective-permute-start.10 = (bf16[224,1024]{1,0:T(8,128)(2,1)}, bf16[224,1024]{1,0:T(8,128)(2,1)S(1)}, u32[]{:S(2)}, u32[]{:S(2)}) collective-permute-start(bf16[224,1024]{1,0:T(8,128)(2,1)} %slice.11), channel_id=1, source_target_pairs={{0,192},{8,200},{16,208},{24,216},{32,224},{40,232},{48,240},{56,2... | collective-permute-start | bytes 1376264 | tf_op jit(solution)/shard_map/ppermute | solution.py:395
  72.1 0.3 collective-permute-done.7.refs_2_
  72.4 3.9 %collective-permute-done.8.refs_3_ = bf16[528,128]{1,0:T(8,128)(2,1)S(1)} collective-permute-done((bf16[528,128]{1,0:T(8,128)(2,1)S(1)}, bf16[528,128]{1,0:T(8,128)(2,1)S(1)}, u32[]{:S(2)}, u32[]{:S(2)}) %collective-permute-start.8) | collective-permute-done | bytes 135200 | tf_op jit(solution)/shard_map/ppermute | solution.py:391
  76.4 1.6 %shard_map.132 = bf16[8,8,2048]{2,1,0:T(8,128)(2,1)} custom-call(f32[512,128]{1,0:T(8,128)S(1)} %copy-done.4, f32[8,128]{1,0:T(8,128)S(1)} %get-tuple-element.27.fresh_lse_ref, bf16[16,512,128]{2,1,0:T(8,128)(2,1)S(1)} %copy-done, bf16[528,128]{1,0:T(8,128)(2,1)S(1)} %get-tuple-element.37.refs_0_, bf16[528,128]{1,0:T(8,128)(2,1)S(1)} %collective-permute-done.6.refs_1_, ...), custom_call_target="tpu_custom_call" | custom-call | flops 16777216 | bytes 2097152 | tf_op jit(solution)/shard_map/pallas_call | solution.py:26
  77.9 6.4 %all-to-all-start.1 = ((bf16[8,8,2048]{2,1,0:T(8,128)(2,1)}), bf16[8,8,2048]{2,1,0:T(8,128)(2,1)S(1)}, u32[]{:S(2)}, u32[]{:S(2)}) async-start(bf16[8,8,2048]{2,1,0:T(8,128)(2,1)} %shard_map.132), calls=%async_computation.1 | async-start | bytes 524288 | tf_op jit(solution)/shard_map/all_to_all | solution.py:554
  84.3 10.7 %all-to-all-done.1 = bf16[8,8,2048]{2,1,0:T(8,128)(2,1)S(1)} async-done(((bf16[8,8,2048]{2,1,0:T(8,128)(2,1)}), bf16[8,8,2048]{2,1,0:T(8,128)(2,1)S(1)}, u32[]{:S(2)}, u32[]{:S(2)}) %all-to-all-start.1) | async-done | bytes 262176 | tf_op jit(solution)/shard_map/all_to_all | solution.py:554
  95.0 4.2 %shard_map.133 = f32[8,4,8,224]{3,2,1,0:T(8,128)} custom-call(bf16[64,2048]{1,0:T(8,128)(2,1)S(1)} %bitcast.14, bf16[224,2048]{1,0:T(8,128)(2,1)S(1)} %bitcast.17, bf16[224,2048]{1,0:T(8,128)(2,1)S(1)} %collective-permute-done.refs_1_, bf16[224,2048]{1,0:T(8,128)(2,1)} %collective-permute-done.1.refs_2_, ...), custom_call_target="tpu_custom_call" | custom-call | flops 234881024 | bytes 3670016 | tf_op jit(solution)/shard_map/pallas_call | solution.py:26
  99.2 5.4 %all-to-all-start.2 = ((f32[8,4,8,224]{3,2,1,0:T(8,128)}), f32[8,4,8,224]{3,2,1,0:T(8,128)S(1)}, u32[]{:S(2)}, u32[]{:S(2)}) async-start(f32[8,4,8,224]{3,2,1,0:T(8,128)} %shard_map.133), calls=%async_computation.2 | async-start | bytes 524288 | tf_op jit(solution)/shard_map/all_to_all | solution.py:569
  104.7 6.5 %all-to-all-done.2.in_ref = f32[8,4,8,224]{3,2,1,0:T(8,128)S(1)} async-done(((f32[8,4,8,224]{3,2,1,0:T(8,128)}), f32[8,4,8,224]{3,2,1,0:T(8,128)S(1)}, u32[]{:S(2)}, u32[]{:S(2)}) %all-to-all-start.2) | async-done | bytes 229408 | tf_op jit(solution)/shard_map/all_to_all | solution.py:569
  111.2 0.1 collective-permute-start.11
  111.3 3.8 %collective-permute-start.12 = (bf16[8,224]{1,0:T(8,128)(2,1)S(1)}, bf16[8,224]{1,0:T(8,128)(2,1)S(1)}, u32[]{:S(2)}, u32[]{:S(2)}) collective-permute-start(bf16[8,224]{1,0:T(8,128)(2,1)S(1)} %get-tuple-element.44), channel_id=1, source_target_pairs={{0,16},{1,48},{2,18},{3,50},{4,20},{5,52},{6,22},{7,54},{8,24},{9,... | collective-permute-start | bytes 10760 | tf_op jit(solution)/shard_map/ppermute | solution.py:584
  115.2 1.9 %collective-permute-start.13 = (bf16[8,224]{1,0:T(8,128)(2,1)S(1)}, bf16[8,224]{1,0:T(8,128)(2,1)S(1)}, u32[]{:S(2)}, u32[]{:S(2)}) collective-permute-start(bf16[8,224]{1,0:T(8,128)(2,1)S(1)} %get-tuple-element.45), channel_id=1, source_target_pairs={{0,8},{1,40},{2,10},{3,42},{4,12},{5,44},{6,14},{7,46},{8,16},{9,4... | collective-permute-start | bytes 10760 | tf_op jit(solution)/shard_map/ppermute | solution.py:584
  117.0 4.1 %collective-permute-start.14 = (bf16[8,224]{1,0:T(8,128)(2,1)S(1)}, bf16[8,224]{1,0:T(8,128)(2,1)S(1)}, u32[]{:S(2)}, u32[]{:S(2)}) collective-permute-start(bf16[8,224]{1,0:T(8,128)(2,1)S(1)} %get-tuple-element.46), channel_id=1, source_target_pairs={{0,0},{1,32},{2,2},{3,34},{4,4},{5,36},{6,6},{7,38},{8,8},{9,40},{... | collective-permute-start | bytes 10760 | tf_op jit(solution)/shard_map/ppermute | solution.py:584
  121.3 4.6 %collective-permute-done.14 = bf16[8,224]{1,0:T(8,128)(2,1)S(1)} collective-permute-done((bf16[8,224]{1,0:T(8,128)(2,1)S(1)}, bf16[8,224]{1,0:T(8,128)(2,1)S(1)}, u32[]{:S(2)}, u32[]{:S(2)}) %collective-permute-start.14) | collective-permute-done | bytes 3616 | tf_op jit(solution)/shard_map/ppermute | solution.py:584
  125.9 0.1 pad_maximum_fusion.1
  126.0 0.6 reshape.99
  (42 shorter events, 0.3 us)
Async XLA Ops:
  4.8 15.0 %copy-start.7 = (bf16[4,2,512]{2,1,0:T(2,128)(2,1)S(1)}, bf16[4,2,512]{2,1,0:T(2,128)(2,1)}, u32[]{:S(2)}) copy-start(bf16[4,2,512]{2,1,0:T(2,128)(2,1)} %param.15) | copy-start | bytes 24580
  4.8 15.1 %copy-start.8 = (bf16[4,2,64]{2,1,0:T(2,128)(2,1)S(1)}, bf16[4,2,64]{2,1,0:T(2,128)(2,1)}, u32[]{:S(2)}) copy-start(bf16[4,2,64]{2,1,0:T(2,128)(2,1)} %param.16) | copy-start | bytes 3076
  4.8 15.4 %copy-start.5 = (bf16[4,2,16,128]{3,2,1,0:T(8,128)(2,1)S(1)}, bf16[4,2,16,128]{3,2,1,0:T(8,128)(2,1)}, u32[]{:S(2)}) copy-start(bf16[4,2,16,128]{3,2,1,0:T(8,128)(2,1)} %param.13) | copy-start | bytes 98308
  4.9 15.4 %copy-start.6 = (bf16[4,2,1024]{2,1,0:T(2,128)(2,1)S(1)}, bf16[4,2,1024]{2,1,0:T(2,128)(2,1)}, u32[]{:S(2)}) copy-start(bf16[4,2,1024]{2,1,0:T(2,128)(2,1)} %param.14) | copy-start | bytes 49156
  4.9 15.6 %copy-start.1 = (bf16[16,128,512]{2,1,0:T(8,128)(2,1)S(1)}, bf16[16,128,512]{2,1,0:T(8,128)(2,1)}, u32[]{:S(2)}) copy-start(bf16[16,128,512]{2,1,0:T(8,128)(2,1)} %w_ref.2) | copy-start | bytes 6291460
  4.9 50.8 %all-to-all-start = ((bf16[32,184,128]{2,1,0:T(8,128)(2,1)}), bf16[32,184,128]{2,1,0:T(8,128)(2,1)}, u32[]{:S(2)}, u32[]{:S(2)}) async-start(bf16[32,184,128]{2,1,0:T(8,128)(2,1)} %shard_map.128), calls=%async_computation | async-start | bytes 3014656 | tf_op jit(solution)/shard_map/all_to_all | solution.py:454
  17.0 9.5 %copy-start.9 = (s32[2,40]{1,0:T(2,128)S(1)}, s32[2,40]{1,0:T(2,128)}, u32[]{:S(2)}) copy-start(s32[2,40]{1,0:T(2,128)} %param.21) | copy-start | bytes 964
  17.0 9.5 %copy-start.10 = (s32[2]{0:T(128)S(1)}, s32[2]{0:T(128)}, u32[]{:S(2)}) copy-start(s32[2]{0:T(128)} %param.22) | copy-start | bytes 28
  17.0 38.7 %collective-permute-start = (bf16[224,2048]{1,0:T(8,128)(2,1)}, bf16[224,2048]{1,0:T(8,128)(2,1)S(1)}, u32[]{:S(2)}, u32[]{:S(2)}) collective-permute-start(bf16[224,2048]{1,0:T(8,128)(2,1)} %bitcast.15), channel_id=1, source_target_pairs={{0,64},{8,72},{16,80},{24,88},{32,96},{40,104},{48,112},{56,120},{... | collective-permute-start | bytes 2752520 | tf_op jit(solution)/shard_map/ppermute | solution.py:395
  18.3 37.4 %collective-permute-start.1 = (bf16[224,2048]{1,0:T(8,128)(2,1)}, bf16[224,2048]{1,0:T(8,128)(2,1)}, u32[]{:S(2)}, u32[]{:S(2)}) collective-permute-start(bf16[224,2048]{1,0:T(8,128)(2,1)} %bitcast.16), channel_id=1, source_target_pairs={{0,192},{8,200},{16,208},{24,216},{32,224},{40,232},{48,240},{56,2... | collective-permute-start | bytes 2752520 | tf_op jit(solution)/shard_map/ppermute | solution.py:395
  21.4 0.7 copy-start.3
  22.1 5.8 %collective-permute-start.2 = (bf16[640,128]{1,0:T(8,128)(2,1)S(1)}, bf16[640,128]{1,0:T(8,128)(2,1)S(1)}, u32[]{:S(2)}, u32[]{:S(2)}) collective-permute-start(bf16[640,128]{1,0:T(8,128)(2,1)S(1)} %get-tuple-element.29), channel_id=1, source_target_pairs={{0,2},{1,3},{2,4},{3,5},{4,6},{5,7},{6,0},{7,1},{8,10},{9,11},{10,... | collective-permute-start | bytes 491528 | tf_op jit(solution)/shard_map/ppermute | solution.py:391
  23.4 9.1 %collective-permute-start.4 = (bf16[640,128]{1,0:T(8,128)(2,1)S(1)}, bf16[640,128]{1,0:T(8,128)(2,1)S(1)}, u32[]{:S(2)}, u32[]{:S(2)}) collective-permute-start(bf16[640,128]{1,0:T(8,128)(2,1)S(1)} %get-tuple-element.29), channel_id=1, source_target_pairs={{0,6},{1,7},{2,0},{3,1},{4,2},{5,3},{6,4},{7,5},{8,14},{9,15},{10,... | collective-permute-start | bytes 491528 | tf_op jit(solution)/shard_map/ppermute | solution.py:391
  24.8 7.6 %collective-permute-start.3 = (bf16[640,128]{1,0:T(8,128)(2,1)S(1)}, bf16[640,128]{1,0:T(8,128)(2,1)S(1)}, u32[]{:S(2)}, u32[]{:S(2)}) collective-permute-start(bf16[640,128]{1,0:T(8,128)(2,1)S(1)} %get-tuple-element.31.refs_0_), channel_id=1, source_target_pairs={{0,4},{1,5},{2,6},{3,7},{4,0},{5,1},{6,2},{7,3},{8,12},{9,13},{10,... | collective-permute-start | bytes 491528 | tf_op jit(solution)/shard_map/ppermute | solution.py:391
  59.1 3.4 %collective-permute-start.5 = (bf16[2,320,640]{2,1,0:T(8,128)(2,1)S(1)}, bf16[2,320,640]{2,1,0:T(8,128)(2,1)S(1)}, u32[]{:S(2)}, u32[]{:S(2)}) collective-permute-start(bf16[2,320,640]{2,1,0:T(8,128)(2,1)S(1)} %shard_map.129.key_ref), channel_id=1, source_target_pairs={{0,1},{1,0},{2,3},{3,2},{4,5},{5,4},{6,7},{7,6},{8,9},{9,8},{10,11... | collective-permute-start | bytes 2457608 | tf_op jit(solution)/shard_map/ppermute | solution.py:524
  62.5 13.9 %copy-start = (bf16[16,512,128]{2,1,0:T(8,128)(2,1)S(1)}, bf16[16,512,128]{2,1,0:T(8,128)(2,1)}, u32[]{:S(2)}) copy-start(bf16[16,512,128]{2,1,0:T(8,128)(2,1)} %w_ref.3) | copy-start | bytes 6291460
  62.5 13.9 %copy-start.4 = (f32[512,128]{1,0:T(8,128)S(1)}, f32[512,128]{1,0:T(8,128)}, u32[]{:S(2)}) copy-start(f32[512,128]{1,0:T(8,128)} %copy-done.3) | copy-start | bytes 786436
  63.6 8.5 %collective-permute-start.6 = (bf16[528,128]{1,0:T(8,128)(2,1)S(1)}, bf16[528,128]{1,0:T(8,128)(2,1)S(1)}, u32[]{:S(2)}, u32[]{:S(2)}) collective-permute-start(bf16[528,128]{1,0:T(8,128)(2,1)S(1)} %get-tuple-element.38), channel_id=1, source_target_pairs={{0,6},{1,7},{2,0},{3,1},{4,2},{5,3},{6,4},{7,5},{8,14},{9,15},{10,... | collective-permute-start | bytes 405512 | tf_op jit(solution)/shard_map/ppermute | solution.py:391
  66.5 6.0 %collective-permute-start.7 = (bf16[528,128]{1,0:T(8,128)(2,1)S(1)}, bf16[528,128]{1,0:T(8,128)(2,1)S(1)}, u32[]{:S(2)}, u32[]{:S(2)}) collective-permute-start(bf16[528,128]{1,0:T(8,128)(2,1)S(1)} %get-tuple-element.39), channel_id=1, source_target_pairs={{0,4},{1,5},{2,6},{3,7},{4,0},{5,1},{6,2},{7,3},{8,12},{9,13},{10,... | collective-permute-start | bytes 405512 | tf_op jit(solution)/shard_map/ppermute | solution.py:391
  66.9 9.4 %collective-permute-start.8 = (bf16[528,128]{1,0:T(8,128)(2,1)S(1)}, bf16[528,128]{1,0:T(8,128)(2,1)S(1)}, u32[]{:S(2)}, u32[]{:S(2)}) collective-permute-start(bf16[528,128]{1,0:T(8,128)(2,1)S(1)} %get-tuple-element.40), channel_id=1, source_target_pairs={{0,2},{1,3},{2,4},{3,5},{4,6},{5,7},{6,0},{7,1},{8,10},{9,11},{10,... | collective-permute-start | bytes 405512 | tf_op jit(solution)/shard_map/ppermute | solution.py:391
  67.5 27.5 %copy-start.2 = (bf16[2048,224]{0,1:T(8,128)(2,1)S(1)}, bf16[2048,224]{0,1:T(8,128)(2,1)}, u32[]{:S(2)}) copy-start(bf16[2048,224]{0,1:T(8,128)(2,1)} %param.25) | copy-start | bytes 2752516
  67.6 16.8 %collective-permute-start.9 = (bf16[224,1024]{1,0:T(8,128)(2,1)S(1)}, bf16[224,1024]{1,0:T(8,128)(2,1)S(1)}, u32[]{:S(2)}, u32[]{:S(2)}) collective-permute-start(bf16[224,1024]{1,0:T(8,128)(2,1)S(1)} %slice.10), channel_id=1, source_target_pairs={{0,64},{8,72},{16,80},{24,88},{32,96},{40,104},{48,112},{56,120},{... | collective-permute-start | bytes 1376264 | tf_op jit(solution)/shard_map/ppermute | solution.py:395
  70.0 14.3 %collective-permute-start.10 = (bf16[224,1024]{1,0:T(8,128)(2,1)}, bf16[224,1024]{1,0:T(8,128)(2,1)S(1)}, u32[]{:S(2)}, u32[]{:S(2)}) collective-permute-start(bf16[224,1024]{1,0:T(8,128)(2,1)} %slice.11), channel_id=1, source_target_pairs={{0,192},{8,200},{16,208},{24,216},{32,224},{40,232},{48,240},{56,2... | collective-permute-start | bytes 1376264 | tf_op jit(solution)/shard_map/ppermute | solution.py:395
  77.9 17.1 %all-to-all-start.1 = ((bf16[8,8,2048]{2,1,0:T(8,128)(2,1)}), bf16[8,8,2048]{2,1,0:T(8,128)(2,1)S(1)}, u32[]{:S(2)}, u32[]{:S(2)}) async-start(bf16[8,8,2048]{2,1,0:T(8,128)(2,1)} %shard_map.132), calls=%async_computation.1 | async-start | bytes 524288 | tf_op jit(solution)/shard_map/all_to_all | solution.py:554
  99.2 12.0 %all-to-all-start.2 = ((f32[8,4,8,224]{3,2,1,0:T(8,128)}), f32[8,4,8,224]{3,2,1,0:T(8,128)S(1)}, u32[]{:S(2)}, u32[]{:S(2)}) async-start(f32[8,4,8,224]{3,2,1,0:T(8,128)} %shard_map.133), calls=%async_computation.2 | async-start | bytes 524288 | tf_op jit(solution)/shard_map/all_to_all | solution.py:569
  111.2 10.0 %collective-permute-start.11 = (bf16[8,224]{1,0:T(8,128)(2,1)S(1)}, bf16[8,224]{1,0:T(8,128)(2,1)S(1)}, u32[]{:S(2)}, u32[]{:S(2)}) collective-permute-start(bf16[8,224]{1,0:T(8,128)(2,1)S(1)} %get-tuple-element.43), channel_id=1, source_target_pairs={{0,24},{1,56},{2,26},{3,58},{4,28},{5,60},{6,30},{7,62},{8,0},{9,3... | collective-permute-start | bytes 10760 | tf_op jit(solution)/shard_map/ppermute | solution.py:584
  111.3 9.9 %collective-permute-start.12 = (bf16[8,224]{1,0:T(8,128)(2,1)S(1)}, bf16[8,224]{1,0:T(8,128)(2,1)S(1)}, u32[]{:S(2)}, u32[]{:S(2)}) collective-permute-start(bf16[8,224]{1,0:T(8,128)(2,1)S(1)} %get-tuple-element.44), channel_id=1, source_target_pairs={{0,16},{1,48},{2,18},{3,50},{4,20},{5,52},{6,22},{7,54},{8,24},{9,... | collective-permute-start | bytes 10760 | tf_op jit(solution)/shard_map/ppermute | solution.py:584
  115.2 6.1 %collective-permute-start.13 = (bf16[8,224]{1,0:T(8,128)(2,1)S(1)}, bf16[8,224]{1,0:T(8,128)(2,1)S(1)}, u32[]{:S(2)}, u32[]{:S(2)}) collective-permute-start(bf16[8,224]{1,0:T(8,128)(2,1)S(1)} %get-tuple-element.45), channel_id=1, source_target_pairs={{0,8},{1,40},{2,10},{3,42},{4,12},{5,44},{6,14},{7,46},{8,16},{9,4... | collective-permute-start | bytes 10760 | tf_op jit(solution)/shard_map/ppermute | solution.py:584
  117.0 8.8 %collective-permute-start.14 = (bf16[8,224]{1,0:T(8,128)(2,1)S(1)}, bf16[8,224]{1,0:T(8,128)(2,1)S(1)}, u32[]{:S(2)}, u32[]{:S(2)}) collective-permute-start(bf16[8,224]{1,0:T(8,128)(2,1)S(1)} %get-tuple-element.46), channel_id=1, source_target_pairs={{0,0},{1,32},{2,2},{3,34},{4,4},{5,36},{6,6},{7,38},{8,8},{9,40},{... | collective-permute-start | bytes 10760 | tf_op jit(solution)/shard_map/ppermute | solution.py:584

commit v6 on v5

--- a/solution.py
+++ b/solution.py
@@ -348,40 +348,44 @@
             out_ref[copy, :, head * value_w : (head + 1) * value_w] = value
 
 
-def project_kernel(width, x_ref, *refs):
-    w_hbm, out_ref, w_refs, sem_ref = refs[:5], refs[5], refs[6:11], refs[11]
+def stage_kernel(own_hbm, near_hbm, far_hbm, opp_a_hbm, opp_b_hbm, out_ref, sem_ref):
+    here = lax.axis_index("row") // NZ
+    depth = opp_a_hbm.shape[1]
+    near, far, opposite = [(here + k) % NX for k in (NX - 1, 1, 2)]
     copies = [
-        pltpu.make_async_copy(w_hbm[i], w_refs[i], sem_ref.at[i]) for i in range(len(w_refs))
+        pltpu.make_async_copy(own_hbm, out_ref.at[here], sem_ref.at[0]),
+        pltpu.make_async_copy(near_hbm, out_ref.at[near], sem_ref.at[1]),
+        pltpu.make_async_copy(far_hbm, out_ref.at[far], sem_ref.at[2]),
+        pltpu.make_async_copy(opp_a_hbm, out_ref.at[opposite, :, :depth], sem_ref.at[3]),
+        pltpu.make_async_copy(opp_b_hbm, out_ref.at[opposite, :, depth:], sem_ref.at[4]),
     ]
     for copy in copies:
         copy.start()
-    per_core = out_ref.shape[1]
-    cores = out_ref.shape[0] // NX
-    here = lax.axis_index("row") // NZ
-    depth = x_ref.shape[1] // 2
-
-    def put(k, block):
-        owner = (here - k + NX) % NX
-        for core in range(cores):
-            for i in range(per_core):
-                first = (core * per_core + i) * width
-                out_ref[owner * cores + core, i] = block[first : first + width]
-
-    for i, k in enumerate((0, 1, NX - 1)):
-        copies[i].wait()
-        put(k, dot_t(x_ref[...], w_refs[i][...]))
-    copies[3].wait()
-    opposite = dot_t(x_ref[:, :depth], w_refs[3][...])
-    copies[4].wait()
-    put(NX // 2, opposite + dot_t(x_ref[:, depth:], w_refs[4][...]))
-
-
-def sum_kernel(in_ref, *outs):
-    count = len(outs)
-    for j in range(count):
-        i = (lax.axis_index("row") + j) % count
-        parts = [in_ref[k, i] for k in range(in_ref.shape[0])]
-        outs[j][...] = functools.reduce(jnp.add, parts).astype(outs[j].dtype)
+    for copy in copies:
+        copy.wait()
+
+
+def project_kernel(width, x_ref, w_ref, out_ref):
+    x = x_ref[...]
+    for k in range(NX):
+        block = dot_t(x, w_ref[k])
+        for z in range(NZ):
+            out_ref[z * NX + k] = block[z * width : (z + 1) * width]
+
+
+def sum_kernel(in_ref, keep_ref, send_ref):
+    core = lax.axis_index("head") % 2
+    per_core = keep_ref.shape[0]
+    for i in range(per_core):
+        for ref, half in ((keep_ref, core), (send_ref, 1 - core)):
+            first = (half * per_core + i) * NX
+            ref[i] = functools.reduce(jnp.add, [in_ref[first + y] for y in range(NX)])
+
+
+def final_kernel(keep_ref, got_ref, out_ref):
+    count, width, _ = keep_ref.shape
+    value = [(keep_ref[i] + got_ref[i]).astype(jnp.bfloat16) for i in range(count)]
+    out_ref[...] = jnp.concatenate(value, axis=1)
 
 
 def shift_y(x, n_head, k):
@@ -556,41 +560,43 @@
     )
     cols = w_o.shape[1]
     cores = n_head // NX
-    per_core = NZ // cores
+    w_ring = call(
+        stage_kernel,
+        jax.ShapeDtypeStruct((NX,) + w_t.shape, bf16),
+        w_cols,
+        scratch=[pltpu.SemaphoreType.DMA((5,))],
+        nbytes=4 * NX * w_o.size,
+        in_hbm=(0, 1, 2, 3, 4),
+    )
     sums = call(
         functools.partial(project_kernel, width),
-        jax.ShapeDtypeStruct((n_head, per_core, width, cols), f32),
-        [ring.reshape(NZ * width, heads * value_w)] + w_cols,
-        scratch=[pltpu.VMEM(w.shape, bf16) for w in w_cols] + [pltpu.SemaphoreType.DMA((5,))],
+        jax.ShapeDtypeStruct((NZ * NX, width, cols), f32),
+        [ring.reshape(NZ * width, heads * value_w), w_ring],
         flops=2 * NX * NZ * width * w_o.size,
         nbytes=2 * NX * w_o.size,
-        in_hbm=(1, 2, 3, 4, 5),
-    )
-    sums = lax.all_to_all(sums, "head", split_axis=0, concat_axis=0, tiled=True)
-    pieces = call(
-        sum_kernel,
-        tuple(jax.ShapeDtypeStruct((width, cols), bf16) for _ in range(per_core)),
-        [sums],
-    )
-    moved = []
-    for j in range(per_core):
-        pairs = []
-        for r in range(n_row):
-            for h in range(n_head):
-                ring_at, (a, i) = r // NZ, divmod(r % NZ, per_core)
-                y, c = divmod(h, cores)
-                to_row = ring_at * NZ + c * per_core + (i + j) % per_core
-                pairs.append((r * n_head + h, to_row * n_head + y * cores + a))
-        moved.append(lax.ppermute(pieces[j], ("row", "head"), pairs))
-    blocks = []
-    for i in range(per_core):
-        turn = (row - i) % per_core
-        block = moved[0]
-        for j in range(1, per_core):
-            block = jnp.where(turn == j, moved[j], block)
-        blocks.append(block)
-    out = jnp.concatenate(blocks, axis=1)
-    return out.reshape(steps, rows_dev, per_core * cols)
+    )
+    planes = [
+        [(x * NZ + z) * n_head + y * cores + core for z in range(NZ) for y in range(NX)]
+        for x in range(NX)
+        for core in range(cores)
+    ]
+    sums = lax.all_to_all(
+        sums,
+        ("row", "head"),
+        split_axis=0,
+        concat_axis=0,
+        axis_index_groups=planes,
+        tiled=True,
+    )
+    half = jax.ShapeDtypeStruct((NZ // cores, width, cols), f32)
+    keep, give = call(sum_kernel, (half, half), [sums])
+    taken = lax.ppermute(give, "head", [(h, h ^ 1) for h in range(n_head)])
+    out = call(
+        final_kernel,
+        jax.ShapeDtypeStruct((width, NZ // cores * cols), bf16),
+        [keep, taken],
+    )
+    return out.reshape(steps, rows_dev, NZ // cores * cols)
 
 
 def solution(mesh):

time: 127 us -> 118 us (0.929)
  waiting for transfers between devices: 55.7 us -> 41.9 us
  blocking collectives: 0 us -> 13.6 us
  starting transfers between devices: 49.1 us -> 37.3 us
  local copies, waits for them, and re-layouts: 3.99 us -> 7.78 us
    all_to_all x0 -> x1, blocking collectives: none -> 13.6 us  [on_device(): lax.all_to_all(sums, ('row', 'head'), split_axis=0, concat_axis=0, axis_i...]
    all_to_all x1 -> x0, waiting for transfers between devices: 6.52 us -> none  [on_device(): sums = lax.all_to_all(sums, 'head', split_axis=0, concat_axis=0, tiled=True)]
    ppermute x4 -> x1, starting transfers between devices: 9.92 us -> 3.6 us  [on_device(): taken = lax.ppermute(give, 'head', [(h, h ^ 1) for h in range(n_head)])]
    all_to_all x1 -> x0, starting transfers between devices: 5.44 us -> none  [on_device(): sums = lax.all_to_all(sums, 'head', split_axis=0, concat_axis=0, tiled=True)]
    unnamed x23 -> x27, local copies, waits for them, and re-layouts: 0.86 us -> 4.67 us
    ppermute x4 -> x1, waiting for transfers between devices: 4.6 us -> 0.86 us  [on_device(): taken = lax.ppermute(give, 'head', [(h, h ^ 1) for h in range(n_head)])]
    all_to_all x1, waiting for transfers between devices: 10.7 us -> 7.2 us  [on_device(): lax.all_to_all(head_out, 'row', split_axis=0, concat_axis=0, axis_index_g...]
    pallas_call x8 -> x10, Pallas kernels: 17.1 us -> 16 us  [call(): pl.pallas_call(body, out_shape=out_shape, in_specs=[HBM if i in in_hbm el...]
  transfers between devices with their start and end apart: 18 -> 14, of which waited for: 9 -> 8; matrix products, arithmetic and copies ran while one was open for 2% -> 2% of each run, Pallas kernels for 3% -> 4%
where the time goes in v6:
time: 118 us; the launch traced here: 117 us
  waiting for transfers between devices  41.9 us (36%)
  starting transfers between devices  37.3 us (32%)
  Pallas kernels  16 us (14%)
  blocking collectives  13.6 us (12%)
  local copies, waits for them, and re-layouts  7.78 us (7%)
    ppermute x4, waiting for transfers between devices, shift_x(): lax.ppermute(x, 'row', [(a * NZ + b, (a + k) % NX * NZ + b) for a in rang...  23.2 us
    pallas_call x10, Pallas kernels, call(): pl.pallas_call(body, out_shape=out_shape, in_specs=[HBM if i in in_hbm el...  16 us
    all_to_all x1, blocking collectives, on_device(): lax.all_to_all(sums, ('row', 'head'), split_axis=0, concat_axis=0, axis_i...  13.6 us
    all_to_all x1, starting transfers between devices, on_device(): got = lax.all_to_all(send, 'row', split_axis=0, concat_axis=0, tiled=True)  12.1 us
    ppermute x6, waiting for transfers between devices, shift_y(): lax.ppermute(x, 'head', [(h, (h + k * cores) % n_head) for h in range(n_h...  9.84 us
    ppermute x6, starting transfers between devices, shift_y(): lax.ppermute(x, 'head', [(h, (h + k * cores) % n_head) for h in range(n_h...  8.23 us
    all_to_all x1, waiting for transfers between devices, on_device(): lax.all_to_all(head_out, 'row', split_axis=0, concat_axis=0, axis_index_g...  7.2 us
    all_to_all x1, starting transfers between devices, on_device(): lax.all_to_all(head_out, 'row', split_axis=0, concat_axis=0, axis_index_g...  6.39 us
  transfers between devices with their start and end apart: 14, of which 8 were waited for; matrix products, arithmetic and copies ran while one was open for 2% of the time, Pallas kernels for 4%

profile of v6, /device:TPU:1, one launch (start us, length us, event | category | flops | bytes accessed | tf_op | source)
XLA Modules:
  0.0 117.1 jit_solution(12431042663108356673)
XLA Ops:
  0.0 4.8 %shard_map.128 = bf16[32,184,128]{2,1,0:T(8,128)(2,1)} custom-call(s32[1,80]{1,0:T(1,128)} %bitcast.22, s32[1,80]{1,0:T(1,128)} %bitcast.23, bf16[80,64,512]{2,1,0:T(8,128)(2,1)} %lat_hbm.1, bf16[80,4096]{1,0:T(8,128)(2,1)} %rope_hbm.1), custom_call_target="tpu_custom_call" | custom-call | flops 838860800 | bytes 2621440 | tf_op jit(solution)/shard_map/pallas_call | solution.py:26
  4.8 0.0 copy-start.9
  4.8 0.0 copy-start.10
  4.9 12.1 %all-to-all-start = ((bf16[32,184,128]{2,1,0:T(8,128)(2,1)}), bf16[32,184,128]{2,1,0:T(8,128)(2,1)}, u32[]{:S(2)}, u32[]{:S(2)}) async-start(bf16[32,184,128]{2,1,0:T(8,128)(2,1)} %shard_map.128), calls=%async_computation | async-start | bytes 3014656 | tf_op jit(solution)/shard_map/all_to_all | solution.py:458
  17.0 1.2 %collective-permute-start = (bf16[224,2048]{1,0:T(8,128)(2,1)}, bf16[224,2048]{1,0:T(8,128)(2,1)S(1)}, u32[]{:S(2)}, u32[]{:S(2)}) collective-permute-start(bf16[224,2048]{1,0:T(8,128)(2,1)} %bitcast.15), channel_id=1, source_target_pairs={{0,64},{8,72},{16,80},{24,88},{32,96},{40,104},{48,112},{56,120},{... | collective-permute-start | bytes 2752520 | tf_op jit(solution)/shard_map/ppermute | solution.py:399
  18.3 1.5 %collective-permute-start.1 = (bf16[224,2048]{1,0:T(8,128)(2,1)}, bf16[224,2048]{1,0:T(8,128)(2,1)}, u32[]{:S(2)}, u32[]{:S(2)}) collective-permute-start(bf16[224,2048]{1,0:T(8,128)(2,1)} %bitcast.16), channel_id=1, source_target_pairs={{0,192},{8,200},{16,208},{24,216},{32,224},{40,232},{48,240},{56,2... | collective-permute-start | bytes 2752520 | tf_op jit(solution)/shard_map/ppermute | solution.py:399
  19.8 0.1 pad.3.clone
  19.9 0.2 copy.32
  20.1 0.1 copy.35
  20.3 0.1 reshape.91
  20.4 0.1 pad.5.clone
  20.5 0.9 shard_map.127
  21.4 0.7 copy-done.5
  22.1 1.3 %collective-permute-start.2 = (bf16[640,128]{1,0:T(8,128)(2,1)S(1)}, bf16[640,128]{1,0:T(8,128)(2,1)S(1)}, u32[]{:S(2)}, u32[]{:S(2)}) collective-permute-start(bf16[640,128]{1,0:T(8,128)(2,1)S(1)} %get-tuple-element.27), channel_id=1, source_target_pairs={{0,2},{1,3},{2,4},{3,5},{4,6},{5,7},{6,0},{7,1},{8,10},{9,11},{10,... | collective-permute-start | bytes 491528 | tf_op jit(solution)/shard_map/ppermute | solution.py:395
  23.4 1.4 %collective-permute-start.4 = (bf16[640,128]{1,0:T(8,128)(2,1)S(1)}, bf16[640,128]{1,0:T(8,128)(2,1)S(1)}, u32[]{:S(2)}, u32[]{:S(2)}) collective-permute-start(bf16[640,128]{1,0:T(8,128)(2,1)S(1)} %get-tuple-element.27), channel_id=1, source_target_pairs={{0,6},{1,7},{2,0},{3,1},{4,2},{5,3},{6,4},{7,5},{8,14},{9,15},{10,... | collective-permute-start | bytes 491528 | tf_op jit(solution)/shard_map/ppermute | solution.py:395
  24.8 1.6 %collective-permute-start.3 = (bf16[640,128]{1,0:T(8,128)(2,1)S(1)}, bf16[640,128]{1,0:T(8,128)(2,1)S(1)}, u32[]{:S(2)}, u32[]{:S(2)}) collective-permute-start(bf16[640,128]{1,0:T(8,128)(2,1)S(1)} %get-tuple-element.29.refs_0_), channel_id=1, source_target_pairs={{0,4},{1,5},{2,6},{3,7},{4,0},{5,1},{6,2},{7,3},{8,12},{9,13},{10,... | collective-permute-start | bytes 491528 | tf_op jit(solution)/shard_map/ppermute | solution.py:395
  26.5 0.1 select_reduce_fusion
  26.6 0.1 subtract_subtract_fusion
  26.7 0.1 compare_select_fusion
  26.7 0.1 select_n.16.bias_ref
  26.9 1.1 collective-permute-done.2.refs_1_
  27.9 4.5 %collective-permute-done.3.refs_2_ = bf16[640,128]{1,0:T(8,128)(2,1)S(1)} collective-permute-done((bf16[640,128]{1,0:T(8,128)(2,1)S(1)}, bf16[640,128]{1,0:T(8,128)(2,1)S(1)}, u32[]{:S(2)}, u32[]{:S(2)}) %collective-permute-start.3) | collective-permute-done | bytes 163872 | tf_op jit(solution)/shard_map/ppermute | solution.py:395
  32.5 23.2 %collective-permute-done.near_hbm = bf16[224,2048]{1,0:T(8,128)(2,1)S(1)} collective-permute-done((bf16[224,2048]{1,0:T(8,128)(2,1)}, bf16[224,2048]{1,0:T(8,128)(2,1)S(1)}, u32[]{:S(2)}, u32[]{:S(2)}) %collective-permute-start) | collective-permute-done | bytes 917536 | tf_op jit(solution)/shard_map/ppermute | solution.py:399
  55.7 3.4 %shard_map.129.key_ref = bf16[2,320,640]{2,1,0:T(8,128)(2,1)S(1)} custom-call(bf16[32,184,128]{2,1,0:T(8,128)(2,1)} %all-to-all-done.block_hbm, f32[640,1]{1,0:T(8,128)S(1)} %select_n.16.bias_ref), custom_call_target="tpu_custom_call" | custom-call | flops 838860800 | bytes 1310720 | tf_op jit(solution)/shard_map/pallas_call | solution.py:26
  59.1 1.4 %collective-permute-start.5 = (bf16[2,320,640]{2,1,0:T(8,128)(2,1)S(1)}, bf16[2,320,640]{2,1,0:T(8,128)(2,1)S(1)}, u32[]{:S(2)}, u32[]{:S(2)}) collective-permute-start(bf16[2,320,640]{2,1,0:T(8,128)(2,1)S(1)} %shard_map.129.key_ref), channel_id=1, source_target_pairs={{0,1},{1,0},{2,3},{3,2},{4,5},{5,4},{6,7},{7,6},{8,9},{9,8},{10,11... | collective-permute-start | bytes 2457608 | tf_op jit(solution)/shard_map/ppermute | solution.py:528
  60.5 1.2 shard_map.130
  61.7 0.8 collective-permute-done.5.key_ref
  62.5 1.2 %shard_map.131 = (bf16[528,128]{1,0:T(8,128)(2,1)S(1)}, bf16[528,128]{1,0:T(8,128)(2,1)S(1)}, bf16[528,128]{1,0:T(8,128)(2,1)S(1)}, bf16[528,128]{1,0:T(8,128)(2,1)S(1)}) custom-call(bf16[2,320,640]{2,1,0:T(8,128)(2,1)S(1)} %collective-permute-done.5.key_ref, f32[2,512,256]{2,1,0:T(8,128)S(1)} %get-tuple-element.33.own_ref, ...), custom_call_target="tpu_custom_call" | custom-call | flops 377487360 | bytes 655360 | tf_op jit(solution)/shard_map/pallas_call | solution.py:26
  63.7 2.8 %collective-permute-start.6 = (bf16[528,128]{1,0:T(8,128)(2,1)S(1)}, bf16[528,128]{1,0:T(8,128)(2,1)S(1)}, u32[]{:S(2)}, u32[]{:S(2)}) collective-permute-start(bf16[528,128]{1,0:T(8,128)(2,1)S(1)} %get-tuple-element.36), channel_id=1, source_target_pairs={{0,6},{1,7},{2,0},{3,1},{4,2},{5,3},{6,4},{7,5},{8,14},{9,15},{10,... | collective-permute-start | bytes 405512 | tf_op jit(solution)/shard_map/ppermute | solution.py:395
  66.5 0.5 collective-permute-start.7
  66.9 0.6 collective-permute-start.8
  67.6 0.6 collective-permute-start.9
  68.2 1.8 %slice.11 = bf16[224,1024]{1,0:T(8,128)(2,1)} slice(bf16[224,2048]{1,0:T(8,128)(2,1)} %collective-permute-done.1.far_hbm), slice={[0:224], [1024:2048]} | slice | bytes 917504 | tf_op jit(solution)/shard_map/slice | solution.py:509
  70.0 2.1 %collective-permute-start.10 = (bf16[224,1024]{1,0:T(8,128)(2,1)}, bf16[224,1024]{1,0:T(8,128)(2,1)S(1)}, u32[]{:S(2)}, u32[]{:S(2)}) collective-permute-start(bf16[224,1024]{1,0:T(8,128)(2,1)} %slice.11), channel_id=1, source_target_pairs={{0,192},{8,200},{16,208},{24,216},{32,224},{40,232},{48,240},{56,2... | collective-permute-start | bytes 1376264 | tf_op jit(solution)/shard_map/ppermute | solution.py:399
  72.1 0.3 collective-permute-done.7.refs_2_
  72.5 3.9 %collective-permute-done.8.refs_3_ = bf16[528,128]{1,0:T(8,128)(2,1)S(1)} collective-permute-done((bf16[528,128]{1,0:T(8,128)(2,1)S(1)}, bf16[528,128]{1,0:T(8,128)(2,1)S(1)}, u32[]{:S(2)}, u32[]{:S(2)}) %collective-permute-start.8) | collective-permute-done | bytes 135200 | tf_op jit(solution)/shard_map/ppermute | solution.py:395
  76.4 1.5 %shard_map.132 = bf16[8,8,2048]{2,1,0:T(8,128)(2,1)} custom-call(f32[512,128]{1,0:T(8,128)S(1)} %copy-done.6, f32[8,128]{1,0:T(8,128)S(1)} %get-tuple-element.25.fresh_lse_ref, bf16[16,512,128]{2,1,0:T(8,128)(2,1)S(1)} %copy-done.2, bf16[528,128]{1,0:T(8,128)(2,1)S(1)} %get-tuple-element.35.refs_0_, bf16[528,128]{1,0:T(8,128)(2,1)S(1)} %collective-permute-done.6.refs_1_, ...), custom_call_target="tpu_custom_call" | custom-call | flops 16777216 | bytes 2097152 | tf_op jit(solution)/shard_map/pallas_call | solution.py:26
  77.9 6.4 %all-to-all-start.1 = ((bf16[8,8,2048]{2,1,0:T(8,128)(2,1)}), bf16[8,8,2048]{2,1,0:T(8,128)(2,1)S(1)}, u32[]{:S(2)}, u32[]{:S(2)}) async-start(bf16[8,8,2048]{2,1,0:T(8,128)(2,1)} %shard_map.132), calls=%async_computation.1 | async-start | bytes 524288 | tf_op jit(solution)/shard_map/all_to_all | solution.py:558
  84.3 1.7 %shard_map.133.w_ref = bf16[4,224,2048]{2,1,0:T(8,128)(2,1)S(1)} custom-call(bf16[224,2048]{1,0:T(8,128)(2,1)S(1)} %bitcast.17, bf16[224,2048]{1,0:T(8,128)(2,1)S(1)} %collective-permute-done.near_hbm, bf16[224,2048]{1,0:T(8,128)(2,1)} %collective-permute-done.1.far_hbm, bf16[224,1024]{1,0:T(8,128)(2,1)S(1)} %collective-permute-done.9.opp_a_hbm, ...), custom_call_target="tpu_custom_call" | custom-call | bytes 7340032 | tf_op jit(solution)/shard_map/pallas_call | solution.py:26
  86.1 1.8 %copy-done = bf16[4,224,2048]{2,1,0:T(8,128)(2,1)} copy-done((bf16[4,224,2048]{2,1,0:T(8,128)(2,1)}, bf16[4,224,2048]{2,1,0:T(8,128)(2,1)S(1)}, u32[]{:S(2)}) %copy-start) | copy-done | bytes 3670040
  87.8 7.2 %all-to-all-done.1 = bf16[8,8,2048]{2,1,0:T(8,128)(2,1)S(1)} async-done(((bf16[8,8,2048]{2,1,0:T(8,128)(2,1)}), bf16[8,8,2048]{2,1,0:T(8,128)(2,1)S(1)}, u32[]{:S(2)}, u32[]{:S(2)}) %all-to-all-start.1) | async-done | bytes 262176 | tf_op jit(solution)/shard_map/all_to_all | solution.py:558
  95.0 2.0 %copy-done.1 = bf16[4,224,2048]{2,1,0:T(8,128)(2,1)S(1)} copy-done((bf16[4,224,2048]{2,1,0:T(8,128)(2,1)S(1)}, bf16[4,224,2048]{2,1,0:T(8,128)(2,1)}, u32[]{:S(2)}) %copy-start.1) | copy-done | bytes 3670040
  97.1 1.3 %shard_map.134 = f32[32,8,224]{2,1,0:T(8,128)S(1)} custom-call(bf16[64,2048]{1,0:T(8,128)(2,1)S(1)} %bitcast.14, bf16[4,224,2048]{2,1,0:T(8,128)(2,1)S(1)} %copy-done.1), custom_call_target="tpu_custom_call" | custom-call | flops 234881024 | bytes 3670016 | tf_op jit(solution)/shard_map/pallas_call | solution.py:26
  98.3 13.6 %all_to_all.15.in_ref = f32[32,8,224]{2,1,0:T(8,128)S(1)} all-to-all(f32[32,8,224]{2,1,0:T(8,128)S(1)} %shard_map.134), channel_id=1, replica_groups={{0,2,4,6,8,10,12,14,16,18,20,22,24,26,28,30,32,34,36,38,40,42,44,46,48,..., dimensions={0} | all-to-all | bytes 458752 | tf_op jit(solution)/shard_map/all_to_all | solution.py:583
  111.9 3.6 %collective-permute-start.11 = (f32[4,8,224]{2,1,0:T(8,128)S(1)}, f32[4,8,224]{2,1,0:T(8,128)S(1)}, u32[]{:S(2)}, u32[]{:S(2)}) collective-permute-start(f32[4,8,224]{2,1,0:T(8,128)S(1)} %get-tuple-element.42), channel_id=1, source_target_pairs={{0,1},{1,0},{2,3},{3,2},{4,5},{5,4},{6,7},{7,6},{8,9},{9,8},{10,11... | collective-permute-start | bytes 86024 | tf_op jit(solution)/shard_map/ppermute | solution.py:593
  115.5 0.9 collective-permute-done.11.got_ref
  116.4 0.1 shard_map.136
  116.4 0.6 reshape.99
  (39 shorter events, 0.3 us)
Async XLA Ops:
  4.8 15.0 %copy-start.9 = (bf16[4,2,512]{2,1,0:T(2,128)(2,1)S(1)}, bf16[4,2,512]{2,1,0:T(2,128)(2,1)}, u32[]{:S(2)}) copy-start(bf16[4,2,512]{2,1,0:T(2,128)(2,1)} %param.15) | copy-start | bytes 24580
  4.8 15.1 %copy-start.10 = (bf16[4,2,64]{2,1,0:T(2,128)(2,1)S(1)}, bf16[4,2,64]{2,1,0:T(2,128)(2,1)}, u32[]{:S(2)}) copy-start(bf16[4,2,64]{2,1,0:T(2,128)(2,1)} %param.16) | copy-start | bytes 3076
  4.9 15.4 %copy-start.7 = (bf16[4,2,16,128]{3,2,1,0:T(8,128)(2,1)S(1)}, bf16[4,2,16,128]{3,2,1,0:T(8,128)(2,1)}, u32[]{:S(2)}) copy-start(bf16[4,2,16,128]{3,2,1,0:T(8,128)(2,1)} %param.13) | copy-start | bytes 98308
  4.9 15.4 %copy-start.8 = (bf16[4,2,1024]{2,1,0:T(2,128)(2,1)S(1)}, bf16[4,2,1024]{2,1,0:T(2,128)(2,1)}, u32[]{:S(2)}) copy-start(bf16[4,2,1024]{2,1,0:T(2,128)(2,1)} %param.14) | copy-start | bytes 49156
  4.9 15.6 %copy-start.3 = (bf16[16,128,512]{2,1,0:T(8,128)(2,1)S(1)}, bf16[16,128,512]{2,1,0:T(8,128)(2,1)}, u32[]{:S(2)}) copy-start(bf16[16,128,512]{2,1,0:T(8,128)(2,1)} %w_ref.2) | copy-start | bytes 6291460
  4.9 50.8 %all-to-all-start = ((bf16[32,184,128]{2,1,0:T(8,128)(2,1)}), bf16[32,184,128]{2,1,0:T(8,128)(2,1)}, u32[]{:S(2)}, u32[]{:S(2)}) async-start(bf16[32,184,128]{2,1,0:T(8,128)(2,1)} %shard_map.128), calls=%async_computation | async-start | bytes 3014656 | tf_op jit(solution)/shard_map/all_to_all | solution.py:458
  17.0 9.5 %copy-start.11 = (s32[2,40]{1,0:T(2,128)S(1)}, s32[2,40]{1,0:T(2,128)}, u32[]{:S(2)}) copy-start(s32[2,40]{1,0:T(2,128)} %param.21) | copy-start | bytes 964
  17.0 9.5 %copy-start.12 = (s32[2]{0:T(128)S(1)}, s32[2]{0:T(128)}, u32[]{:S(2)}) copy-start(s32[2]{0:T(128)} %param.22) | copy-start | bytes 28
  17.0 38.7 %collective-permute-start = (bf16[224,2048]{1,0:T(8,128)(2,1)}, bf16[224,2048]{1,0:T(8,128)(2,1)S(1)}, u32[]{:S(2)}, u32[]{:S(2)}) collective-permute-start(bf16[224,2048]{1,0:T(8,128)(2,1)} %bitcast.15), channel_id=1, source_target_pairs={{0,64},{8,72},{16,80},{24,88},{32,96},{40,104},{48,112},{56,120},{... | collective-permute-start | bytes 2752520 | tf_op jit(solution)/shard_map/ppermute | solution.py:399
  18.3 37.4 %collective-permute-start.1 = (bf16[224,2048]{1,0:T(8,128)(2,1)}, bf16[224,2048]{1,0:T(8,128)(2,1)}, u32[]{:S(2)}, u32[]{:S(2)}) collective-permute-start(bf16[224,2048]{1,0:T(8,128)(2,1)} %bitcast.16), channel_id=1, source_target_pairs={{0,192},{8,200},{16,208},{24,216},{32,224},{40,232},{48,240},{56,2... | collective-permute-start | bytes 2752520 | tf_op jit(solution)/shard_map/ppermute | solution.py:399
  21.4 0.7 copy-start.5
  22.1 5.8 %collective-permute-start.2 = (bf16[640,128]{1,0:T(8,128)(2,1)S(1)}, bf16[640,128]{1,0:T(8,128)(2,1)S(1)}, u32[]{:S(2)}, u32[]{:S(2)}) collective-permute-start(bf16[640,128]{1,0:T(8,128)(2,1)S(1)} %get-tuple-element.27), channel_id=1, source_target_pairs={{0,2},{1,3},{2,4},{3,5},{4,6},{5,7},{6,0},{7,1},{8,10},{9,11},{10,... | collective-permute-start | bytes 491528 | tf_op jit(solution)/shard_map/ppermute | solution.py:395
  23.4 9.1 %collective-permute-start.4 = (bf16[640,128]{1,0:T(8,128)(2,1)S(1)}, bf16[640,128]{1,0:T(8,128)(2,1)S(1)}, u32[]{:S(2)}, u32[]{:S(2)}) collective-permute-start(bf16[640,128]{1,0:T(8,128)(2,1)S(1)} %get-tuple-element.27), channel_id=1, source_target_pairs={{0,6},{1,7},{2,0},{3,1},{4,2},{5,3},{6,4},{7,5},{8,14},{9,15},{10,... | collective-permute-start | bytes 491528 | tf_op jit(solution)/shard_map/ppermute | solution.py:395
  24.8 7.6 %collective-permute-start.3 = (bf16[640,128]{1,0:T(8,128)(2,1)S(1)}, bf16[640,128]{1,0:T(8,128)(2,1)S(1)}, u32[]{:S(2)}, u32[]{:S(2)}) collective-permute-start(bf16[640,128]{1,0:T(8,128)(2,1)S(1)} %get-tuple-element.29.refs_0_), channel_id=1, source_target_pairs={{0,4},{1,5},{2,6},{3,7},{4,0},{5,1},{6,2},{7,3},{8,12},{9,13},{10,... | collective-permute-start | bytes 491528 | tf_op jit(solution)/shard_map/ppermute | solution.py:395
  59.1 3.4 %collective-permute-start.5 = (bf16[2,320,640]{2,1,0:T(8,128)(2,1)S(1)}, bf16[2,320,640]{2,1,0:T(8,128)(2,1)S(1)}, u32[]{:S(2)}, u32[]{:S(2)}) collective-permute-start(bf16[2,320,640]{2,1,0:T(8,128)(2,1)S(1)} %shard_map.129.key_ref), channel_id=1, source_target_pairs={{0,1},{1,0},{2,3},{3,2},{4,5},{5,4},{6,7},{7,6},{8,9},{9,8},{10,11... | collective-permute-start | bytes 2457608 | tf_op jit(solution)/shard_map/ppermute | solution.py:528
  62.5 13.9 %copy-start.2 = (bf16[16,512,128]{2,1,0:T(8,128)(2,1)S(1)}, bf16[16,512,128]{2,1,0:T(8,128)(2,1)}, u32[]{:S(2)}) copy-start(bf16[16,512,128]{2,1,0:T(8,128)(2,1)} %w_ref.3) | copy-start | bytes 6291460
  62.5 13.9 %copy-start.6 = (f32[512,128]{1,0:T(8,128)S(1)}, f32[512,128]{1,0:T(8,128)}, u32[]{:S(2)}) copy-start(f32[512,128]{1,0:T(8,128)} %copy-done.5) | copy-start | bytes 786436
  63.7 8.5 %collective-permute-start.6 = (bf16[528,128]{1,0:T(8,128)(2,1)S(1)}, bf16[528,128]{1,0:T(8,128)(2,1)S(1)}, u32[]{:S(2)}, u32[]{:S(2)}) collective-permute-start(bf16[528,128]{1,0:T(8,128)(2,1)S(1)} %get-tuple-element.36), channel_id=1, source_target_pairs={{0,6},{1,7},{2,0},{3,1},{4,2},{5,3},{6,4},{7,5},{8,14},{9,15},{10,... | collective-permute-start | bytes 405512 | tf_op jit(solution)/shard_map/ppermute | solution.py:395
  66.5 6.0 %collective-permute-start.7 = (bf16[528,128]{1,0:T(8,128)(2,1)S(1)}, bf16[528,128]{1,0:T(8,128)(2,1)S(1)}, u32[]{:S(2)}, u32[]{:S(2)}) collective-permute-start(bf16[528,128]{1,0:T(8,128)(2,1)S(1)} %get-tuple-element.37), channel_id=1, source_target_pairs={{0,4},{1,5},{2,6},{3,7},{4,0},{5,1},{6,2},{7,3},{8,12},{9,13},{10,... | collective-permute-start | bytes 405512 | tf_op jit(solution)/shard_map/ppermute | solution.py:395
  66.9 9.4 %collective-permute-start.8 = (bf16[528,128]{1,0:T(8,128)(2,1)S(1)}, bf16[528,128]{1,0:T(8,128)(2,1)S(1)}, u32[]{:S(2)}, u32[]{:S(2)}) collective-permute-start(bf16[528,128]{1,0:T(8,128)(2,1)S(1)} %get-tuple-element.38), channel_id=1, source_target_pairs={{0,2},{1,3},{2,4},{3,5},{4,6},{5,7},{6,0},{7,1},{8,10},{9,11},{10,... | collective-permute-start | bytes 405512 | tf_op jit(solution)/shard_map/ppermute | solution.py:395
  67.5 16.8 %copy-start.4 = (bf16[2048,224]{0,1:T(8,128)(2,1)S(1)}, bf16[2048,224]{0,1:T(8,128)(2,1)}, u32[]{:S(2)}) copy-start(bf16[2048,224]{0,1:T(8,128)(2,1)} %param.25) | copy-start | bytes 2752516
  67.6 16.8 %collective-permute-start.9 = (bf16[224,1024]{1,0:T(8,128)(2,1)S(1)}, bf16[224,1024]{1,0:T(8,128)(2,1)S(1)}, u32[]{:S(2)}, u32[]{:S(2)}) collective-permute-start(bf16[224,1024]{1,0:T(8,128)(2,1)S(1)} %slice.10), channel_id=1, source_target_pairs={{0,64},{8,72},{16,80},{24,88},{32,96},{40,104},{48,112},{56,120},{... | collective-permute-start | bytes 1376264 | tf_op jit(solution)/shard_map/ppermute | solution.py:399
  70.0 14.3 %collective-permute-start.10 = (bf16[224,1024]{1,0:T(8,128)(2,1)}, bf16[224,1024]{1,0:T(8,128)(2,1)S(1)}, u32[]{:S(2)}, u32[]{:S(2)}) collective-permute-start(bf16[224,1024]{1,0:T(8,128)(2,1)} %slice.11), channel_id=1, source_target_pairs={{0,192},{8,200},{16,208},{24,216},{32,224},{40,232},{48,240},{56,2... | collective-permute-start | bytes 1376264 | tf_op jit(solution)/shard_map/ppermute | solution.py:399
  77.9 17.1 %all-to-all-start.1 = ((bf16[8,8,2048]{2,1,0:T(8,128)(2,1)}), bf16[8,8,2048]{2,1,0:T(8,128)(2,1)S(1)}, u32[]{:S(2)}, u32[]{:S(2)}) async-start(bf16[8,8,2048]{2,1,0:T(8,128)(2,1)} %shard_map.132), calls=%async_computation.1 | async-start | bytes 524288 | tf_op jit(solution)/shard_map/all_to_all | solution.py:558
  86.1 1.8 %copy-start = (bf16[4,224,2048]{2,1,0:T(8,128)(2,1)}, bf16[4,224,2048]{2,1,0:T(8,128)(2,1)S(1)}, u32[]{:S(2)}) copy-start(bf16[4,224,2048]{2,1,0:T(8,128)(2,1)S(1)} %shard_map.133.w_ref) | copy-start | bytes 11010052
  95.0 2.0 %copy-start.1 = (bf16[4,224,2048]{2,1,0:T(8,128)(2,1)S(1)}, bf16[4,224,2048]{2,1,0:T(8,128)(2,1)}, u32[]{:S(2)}) copy-start(bf16[4,224,2048]{2,1,0:T(8,128)(2,1)} %copy-done) | copy-start | bytes 11010052
  111.9 4.5 %collective-permute-start.11 = (f32[4,8,224]{2,1,0:T(8,128)S(1)}, f32[4,8,224]{2,1,0:T(8,128)S(1)}, u32[]{:S(2)}, u32[]{:S(2)}) collective-permute-start(f32[4,8,224]{2,1,0:T(8,128)S(1)} %get-tuple-element.42), channel_id=1, source_target_pairs={{0,1},{1,0},{2,3},{3,2},{4,5},{5,4},{6,7},{7,6},{8,9},{9,8},{10,11... | collective-permute-start | bytes 86024 | tf_op jit(solution)/shard_map/ppermute | solution.py:593

commit v7 on v6

--- a/solution.py
+++ b/solution.py
@@ -57,11 +57,14 @@
     rows_dev,
     pages_row,
     per_pair,
-    rows_ref,
-    slots_ref,
+    rows_hbm,
+    slots_hbm,
     lat_hbm,
     rope_hbm,
     out_hbm,
+    rows_ref,
+    slots_ref,
+    lat_ref,
     lat_buf,
     rope_buf,
     buf_ref,
@@ -76,14 +79,29 @@
     rope_rows = rope_buf.shape[1] // TAIL
     lat_rows = per_pair * cuts * piece
     head = lax.axis_index("head")
-    first = pl.multiple_of(head // 2 * both, both)
-    lat_copy = pltpu.make_async_copy(lat_hbm.at[:, pl.ds(first, both), :], lat_buf, in_sem.at[0])
-    lat_copy.start()
+    lists = [
+        pltpu.make_async_copy(rows_hbm, rows_ref, in_sem.at[0]),
+        pltpu.make_async_copy(slots_hbm, slots_ref, in_sem.at[1]),
+    ]
+    for copy in lists:
+        copy.start()
     lane0 = pl.multiple_of(head * rope_buf.shape[1], rope_buf.shape[1])
     rope_copy = pltpu.make_async_copy(
-        rope_hbm.at[:, pl.ds(lane0, rope_buf.shape[1])], rope_buf, in_sem.at[1]
+        rope_hbm.at[:, pl.ds(lane0, rope_buf.shape[1])], rope_buf, in_sem.at[2]
     )
     rope_copy.start()
+    first = pl.multiple_of(head // 2 * both, both)
+    cut = pages // chunks
+    lat_copies = []
+    for i in range(chunks):
+        here = pl.ds(i * cut, cut)
+        copy = pltpu.make_async_copy(
+            lat_hbm.at[here, pl.ds(first, both), :], lat_buf.at[here], in_sem.at[3 + i]
+        )
+        copy.start()
+        lat_copies.append(copy)
+    for copy in lists:
+        copy.wait()
 
     dest = rows_ref[...] // rows_dev
     label = (rows_ref[...] % rows_dev * pages_row + slots_ref[...] + 1).astype(jnp.float32)
@@ -110,10 +128,12 @@
         tail = tail + dot(pick, rope_buf[:, j * TAIL : (j + 1) * TAIL])
     buf_ref[:, lat_rows:, :] = tail.reshape(count, rest, TAIL).astype(jnp.bfloat16)
 
-    lat_copy.wait()
-    lat = lat_buf[...].astype(jnp.float32).reshape(pages, 2, piece, lat_w)
-    lat = jnp.where(head % 2 == 1, lat[:, 1], lat[:, 0]).reshape(pages * piece, lat_w)
-    lat = lat.astype(jnp.bfloat16)
+    for i, copy in enumerate(lat_copies):
+        copy.wait()
+        lat = lat_buf[i * cut : (i + 1) * cut].astype(jnp.float32).reshape(cut, 2, piece, lat_w)
+        lat = jnp.where(head % 2 == 1, lat[:, 1], lat[:, 0]).reshape(cut * piece, lat_w)
+        lat_ref[i * cut * piece : (i + 1) * cut * piece, :] = lat.astype(jnp.bfloat16)
+    lat = lat_ref[...]
     step = count // chunks
     copies = []
     for i in range(chunks):
@@ -348,16 +368,10 @@
             out_ref[copy, :, head * value_w : (head + 1) * value_w] = value
 
 
-def stage_kernel(own_hbm, near_hbm, far_hbm, opp_a_hbm, opp_b_hbm, out_ref, sem_ref):
-    here = lax.axis_index("row") // NZ
-    depth = opp_a_hbm.shape[1]
-    near, far, opposite = [(here + k) % NX for k in (NX - 1, 1, 2)]
+def stage_kernel(own_hbm, near_hbm, far_hbm, out_ref, sem_ref):
     copies = [
-        pltpu.make_async_copy(own_hbm, out_ref.at[here], sem_ref.at[0]),
-        pltpu.make_async_copy(near_hbm, out_ref.at[near], sem_ref.at[1]),
-        pltpu.make_async_copy(far_hbm, out_ref.at[far], sem_ref.at[2]),
-        pltpu.make_async_copy(opp_a_hbm, out_ref.at[opposite, :, :depth], sem_ref.at[3]),
-        pltpu.make_async_copy(opp_b_hbm, out_ref.at[opposite, :, depth:], sem_ref.at[4]),
+        pltpu.make_async_copy(ref, out_ref.at[i], sem_ref.at[i])
+        for i, ref in enumerate((own_hbm, near_hbm, far_hbm))
     ]
     for copy in copies:
         copy.start()
@@ -365,12 +379,30 @@
         copy.wait()
 
 
-def project_kernel(width, x_ref, w_ref, out_ref):
-    x = x_ref[...]
-    for k in range(NX):
-        block = dot_t(x, w_ref[k])
+def project_kernel(
+    width, x_ref, w_ref, opp_a_hbm, opp_b_hbm, out_ref, opp_a_ref, opp_b_ref, sem_ref
+):
+    copies = [
+        pltpu.make_async_copy(opp_a_hbm, opp_a_ref, sem_ref.at[0]),
+        pltpu.make_async_copy(opp_b_hbm, opp_b_ref, sem_ref.at[1]),
+    ]
+    for copy in copies:
+        copy.start()
+    here = lax.axis_index("row") // NZ
+    depth = opp_a_hbm.shape[1]
+
+    def put(k, block):
+        owner = (here + k) % NX
         for z in range(NZ):
-            out_ref[z * NX + k] = block[z * width : (z + 1) * width]
+            rows = block[z * width : (z + 1) * width]
+            out_ref[z * NX + owner] = rows.astype(out_ref.dtype)
+
+    for i, k in enumerate((0, NX - 1, 1)):
+        put(k, dot_t(x_ref[...], w_ref[i]))
+    copies[0].wait()
+    opposite = dot_t(x_ref[:, :depth], opp_a_ref[...])
+    copies[1].wait()
+    put(2, opposite + dot_t(x_ref[:, depth:], opp_b_ref[...]))
 
 
 def sum_kernel(in_ref, keep_ref, send_ref):
@@ -379,13 +411,16 @@
     for i in range(per_core):
         for ref, half in ((keep_ref, core), (send_ref, 1 - core)):
             first = (half * per_core + i) * NX
-            ref[i] = functools.reduce(jnp.add, [in_ref[first + y] for y in range(NX)])
+            parts = [in_ref[first + y].astype(jnp.float32) for y in range(NX)]
+            ref[i] = functools.reduce(jnp.add, parts)
 
 
 def final_kernel(keep_ref, got_ref, out_ref):
-    count, width, _ = keep_ref.shape
-    value = [(keep_ref[i] + got_ref[i]).astype(jnp.bfloat16) for i in range(count)]
-    out_ref[...] = jnp.concatenate(value, axis=1)
+    value = [keep_ref[i] + got_ref[i] for i in range(keep_ref.shape[0])]
+    value = jnp.concatenate(value, axis=1)
+    rows = out_ref.shape[1]
+    for step in range(out_ref.shape[0]):
+        out_ref[step] = value[step * rows : (step + 1) * rows].astype(out_ref.dtype)
 
 
 def shift_y(x, n_head, k):
@@ -443,17 +478,20 @@
         jax.ShapeDtypeStruct((n_row, block, TAIL), bf16),
         [dest_rows[None, :], dest_slots[None, :], latent_pages, rope_pages],
         scratch=[
+            pltpu.VMEM((1, pages), jnp.int32),
+            pltpu.VMEM((1, pages), jnp.int32),
+            pltpu.VMEM((tokens, lat_w), bf16),
             pltpu.VMEM((pages, 2 * piece, lat_w), bf16),
             pltpu.VMEM((pages, piece * rope_w), bf16),
             pltpu.VMEM((n_row, block, TAIL), bf16),
-            pltpu.SemaphoreType.DMA((2,)),
+            pltpu.SemaphoreType.DMA((7,)),
             pltpu.SemaphoreType.DMA((4,)),
         ],
         flops=2 * slots * tokens * lat_w,
         nbytes=2 * (slots + 2 * tokens) * lat_w,
         mem=60,
         out_spec=HBM,
-        in_hbm=(2, 3),
+        in_hbm=(0, 1, 2, 3),
     )
     got = lax.all_to_all(send, "row", split_axis=0, concat_axis=0, tiled=True)
 
@@ -501,13 +539,7 @@
     bias = jnp.where(usable, 0.0, NEG).astype(f32).reshape(rows_dev * pages_row * piece, 1)
 
     got, w_near, w_far, all_queries = lax.optimization_barrier((got, w_near, w_far, all_queries))
-    w_cols = [
-        w_t,
-        w_near,
-        w_far,
-        shift_x(w_near[:, :depth], 1),
-        shift_x(w_far[:, depth:], -1),
-    ]
+    opposite = [shift_x(w_near[:, :depth], 1), shift_x(w_far[:, depth:], -1)]
     key = call(
         functools.partial(gather_kernel, piece, per_pair, rope_w, pages_row),
         jax.ShapeDtypeStruct((rows_dev, pages_row * piece, lat_w + TAIL), bf16),
@@ -562,18 +594,20 @@
     cores = n_head // NX
     w_ring = call(
         stage_kernel,
-        jax.ShapeDtypeStruct((NX,) + w_t.shape, bf16),
-        w_cols,
-        scratch=[pltpu.SemaphoreType.DMA((5,))],
-        nbytes=4 * NX * w_o.size,
-        in_hbm=(0, 1, 2, 3, 4),
+        jax.ShapeDtypeStruct((3,) + w_t.shape, bf16),
+        [w_t, w_near, w_far],
+        scratch=[pltpu.SemaphoreType.DMA((3,))],
+        nbytes=12 * w_o.size,
+        in_hbm=(0, 1, 2),
     )
     sums = call(
         functools.partial(project_kernel, width),
-        jax.ShapeDtypeStruct((NZ * NX, width, cols), f32),
-        [ring.reshape(NZ * width, heads * value_w), w_ring],
+        jax.ShapeDtypeStruct((NZ * NX, width, cols), bf16),
+        [ring.reshape(NZ * width, heads * value_w), w_ring] + opposite,
+        scratch=[pltpu.VMEM((cols, depth), bf16)] * 2 + [pltpu.SemaphoreType.DMA((2,))],
         flops=2 * NX * NZ * width * w_o.size,
         nbytes=2 * NX * w_o.size,
+        in_hbm=(2, 3),
     )
     planes = [
         [(x * NZ + z) * n_head + y * cores + core for z in range(NZ) for y in range(NX)]
@@ -591,12 +625,11 @@
     half = jax.ShapeDtypeStruct((NZ // cores, width, cols), f32)
     keep, give = call(sum_kernel, (half, half), [sums])
     taken = lax.ppermute(give, "head", [(h, h ^ 1) for h in range(n_head)])
-    out = call(
+    return call(
         final_kernel,
-        jax.ShapeDtypeStruct((width, NZ // cores * cols), bf16),
+        jax.ShapeDtypeStruct((steps, rows_dev, NZ // cores * cols), bf16),
         [keep, taken],
     )
-    return out.reshape(steps, rows_dev, NZ // cores * cols)
 
 
 def solution(mesh):

time: 118 us -> 115 us (0.975)
  waiting for transfers between devices: 41.9 us -> 40.2 us
  Pallas kernels: 16 us -> 17.3 us
  local copies, waits for them, and re-layouts: 7.78 us -> 6.53 us
  blocking collectives: 13.6 us -> 12.4 us
    unnamed x27, local copies, waits for them, and re-layouts: 4.67 us -> 3.22 us
    pallas_call x10, Pallas kernels: 16 us -> 17.3 us  [call(): pl.pallas_call(body, out_shape=out_shape, in_specs=[HBM if i in in_hbm el...]
  transfers between devices with their start and end apart: 14 -> 14, of which waited for: 8 -> 7; matrix products, arithmetic and copies ran while one was open for 2% -> 3% of each run, Pallas kernels for 4% -> 5%
where the time goes in v7:
time: 115 us; the launch traced here: 114 us
  waiting for transfers between devices  40.2 us (35%)
  starting transfers between devices  37 us (32%)
  Pallas kernels  17.3 us (15%)
  blocking collectives  12.4 us (11%)
  local copies, waits for them, and re-layouts  6.53 us (6%)
    ppermute x4, waiting for transfers between devices, shift_x(): lax.ppermute(x, 'row', [(a * NZ + b, (a + k) % NX * NZ + b) for a in rang...  22.7 us
    pallas_call x10, Pallas kernels, call(): pl.pallas_call(body, out_shape=out_shape, in_specs=[HBM if i in in_hbm el...  17.3 us
    all_to_all x1, blocking collectives, on_device(): lax.all_to_all(sums, ('row', 'head'), split_axis=0, concat_axis=0, axis_i...  12.4 us
    all_to_all x1, starting transfers between devices, on_device(): got = lax.all_to_all(send, 'row', split_axis=0, concat_axis=0, tiled=True)  12.1 us
    ppermute x6, waiting for transfers between devices, shift_y(): lax.ppermute(x, 'head', [(h, (h + k * cores) % n_head) for h in range(n_h...  9.19 us
    ppermute x6, starting transfers between devices, shift_y(): lax.ppermute(x, 'head', [(h, (h + k * cores) % n_head) for h in range(n_h...  8.23 us
    all_to_all x1, waiting for transfers between devices, on_device(): lax.all_to_all(head_out, 'row', split_axis=0, concat_axis=0, axis_index_g...  6.68 us
    all_to_all x1, starting transfers between devices, on_device(): lax.all_to_all(head_out, 'row', split_axis=0, concat_axis=0, axis_index_g...  6.39 us
  transfers between devices with their start and end apart: 14, of which 7 were waited for; matrix products, arithmetic and copies ran while one was open for 3% of the time, Pallas kernels for 5%

profile of v7, /device:TPU:1, one launch (start us, length us, event | category | flops | bytes accessed | tf_op | source)
XLA Modules:
  0.0 114.0 jit_solution(2964048349537128871)
XLA Ops:
  0.0 4.0 %shard_map.128 = bf16[32,184,128]{2,1,0:T(8,128)(2,1)} custom-call(s32[1,80]{1,0:T(1,128)} %bitcast.22, s32[1,80]{1,0:T(1,128)} %bitcast.23, bf16[80,64,512]{2,1,0:T(8,128)(2,1)} %lat_hbm.1, bf16[80,4096]{1,0:T(8,128)(2,1)} %rope_hbm.1), custom_call_target="tpu_custom_call" | custom-call | flops 838860800 | bytes 2621440 | tf_op jit(solution)/shard_map/pallas_call | solution.py:26
  4.1 0.0 copy-start.7
  4.1 0.0 copy-start.8
  4.1 12.1 %all-to-all-start = ((bf16[32,184,128]{2,1,0:T(8,128)(2,1)}), bf16[32,184,128]{2,1,0:T(8,128)(2,1)}, u32[]{:S(2)}, u32[]{:S(2)}) async-start(bf16[32,184,128]{2,1,0:T(8,128)(2,1)} %shard_map.128), calls=%async_computation | async-start | bytes 3014656 | tf_op jit(solution)/shard_map/all_to_all | solution.py:496
  16.2 0.0 copy-start.11
  16.3 1.2 %collective-permute-start = (bf16[224,2048]{1,0:T(8,128)(2,1)}, bf16[224,2048]{1,0:T(8,128)(2,1)S(1)}, u32[]{:S(2)}, u32[]{:S(2)}) collective-permute-start(bf16[224,2048]{1,0:T(8,128)(2,1)} %bitcast.15), channel_id=1, source_target_pairs={{0,64},{8,72},{16,80},{24,88},{32,96},{40,104},{48,112},{56,120},{... | collective-permute-start | bytes 2752520 | tf_op jit(solution)/shard_map/ppermute | solution.py:434
  17.5 1.5 %collective-permute-start.1 = (bf16[224,2048]{1,0:T(8,128)(2,1)}, bf16[224,2048]{1,0:T(8,128)(2,1)}, u32[]{:S(2)}, u32[]{:S(2)}) collective-permute-start(bf16[224,2048]{1,0:T(8,128)(2,1)} %bitcast.16), channel_id=1, source_target_pairs={{0,192},{8,200},{16,208},{24,216},{32,224},{40,232},{48,240},{56,2... | collective-permute-start | bytes 2752520 | tf_op jit(solution)/shard_map/ppermute | solution.py:434
  19.0 0.1 pad.3.clone
  19.1 0.2 copy.32
  19.4 0.1 copy.35
  19.5 0.1 reshape.88
  19.6 0.1 pad.5.clone
  19.7 1.3 %shard_map.127 = (bf16[640,128]{1,0:T(8,128)(2,1)S(1)}, bf16[640,128]{1,0:T(8,128)(2,1)}, f32[512,128]{1,0:T(8,128)S(1)}, f32[8,128]{1,0:T(8,128)S(1)}) custom-call(bf16[16,8,128]{2,1,0:T(8,128)(2,1)S(1)} %bitcast.18, bf16[128,128]{1,0:T(8,128)(2,1)S(1)} %pad_maximum_fusion.qtail_ref, bf16[16,128,512]{2,1,0:T(8,128)(2,1)S(1)} %copy-done.1, ...), custom_call_target="tpu_custom_call" | custom-call | flops 16777216 | bytes 2097152 | tf_op jit(solution)/shard_map/pallas_call | solution.py:26
  21.1 0.7 copy-done.5
  21.8 1.3 %collective-permute-start.2 = (bf16[640,128]{1,0:T(8,128)(2,1)}, bf16[640,128]{1,0:T(8,128)(2,1)S(1)}, u32[]{:S(2)}, u32[]{:S(2)}) collective-permute-start(bf16[640,128]{1,0:T(8,128)(2,1)} %get-tuple-element.27), channel_id=1, source_target_pairs={{0,2},{1,3},{2,4},{3,5},{4,6},{5,7},{6,0},{7,1},{8,10},{9,11},{10,... | collective-permute-start | bytes 491528 | tf_op jit(solution)/shard_map/ppermute | solution.py:430
  23.1 1.4 %collective-permute-start.4 = (bf16[640,128]{1,0:T(8,128)(2,1)}, bf16[640,128]{1,0:T(8,128)(2,1)S(1)}, u32[]{:S(2)}, u32[]{:S(2)}) collective-permute-start(bf16[640,128]{1,0:T(8,128)(2,1)} %get-tuple-element.27), channel_id=1, source_target_pairs={{0,6},{1,7},{2,0},{3,1},{4,2},{5,3},{6,4},{7,5},{8,14},{9,15},{10,... | collective-permute-start | bytes 491528 | tf_op jit(solution)/shard_map/ppermute | solution.py:430
  24.5 1.6 %collective-permute-start.3 = (bf16[640,128]{1,0:T(8,128)(2,1)S(1)}, bf16[640,128]{1,0:T(8,128)(2,1)S(1)}, u32[]{:S(2)}, u32[]{:S(2)}) collective-permute-start(bf16[640,128]{1,0:T(8,128)(2,1)S(1)} %get-tuple-element.29.refs_0_), channel_id=1, source_target_pairs={{0,4},{1,5},{2,6},{3,7},{4,0},{5,1},{6,2},{7,3},{8,12},{9,13},{10,... | collective-permute-start | bytes 491528 | tf_op jit(solution)/shard_map/ppermute | solution.py:430
  26.2 0.1 select_reduce_fusion
  26.3 0.1 subtract_subtract_fusion
  26.4 0.1 compare_select_fusion
  26.4 0.1 select_n.16.bias_ref
  26.6 1.3 %collective-permute-done.2.refs_1_ = bf16[640,128]{1,0:T(8,128)(2,1)S(1)} collective-permute-done((bf16[640,128]{1,0:T(8,128)(2,1)}, bf16[640,128]{1,0:T(8,128)(2,1)S(1)}, u32[]{:S(2)}, u32[]{:S(2)}) %collective-permute-start.2) | collective-permute-done | bytes 163872 | tf_op jit(solution)/shard_map/ppermute | solution.py:430
  27.8 4.4 %collective-permute-done.3.refs_2_ = bf16[640,128]{1,0:T(8,128)(2,1)S(1)} collective-permute-done((bf16[640,128]{1,0:T(8,128)(2,1)S(1)}, bf16[640,128]{1,0:T(8,128)(2,1)S(1)}, u32[]{:S(2)}, u32[]{:S(2)}) %collective-permute-start.3) | collective-permute-done | bytes 163872 | tf_op jit(solution)/shard_map/ppermute | solution.py:430
  32.2 22.7 %collective-permute-done.near_hbm = bf16[224,2048]{1,0:T(8,128)(2,1)S(1)} collective-permute-done((bf16[224,2048]{1,0:T(8,128)(2,1)}, bf16[224,2048]{1,0:T(8,128)(2,1)S(1)}, u32[]{:S(2)}, u32[]{:S(2)}) %collective-permute-start) | collective-permute-done | bytes 917536 | tf_op jit(solution)/shard_map/ppermute | solution.py:434
  54.9 3.7 %shard_map.129.key_ref = bf16[2,320,640]{2,1,0:T(8,128)(2,1)S(1)} custom-call(bf16[32,184,128]{2,1,0:T(8,128)(2,1)} %all-to-all-done.block_hbm, f32[640,1]{1,0:T(8,128)S(1)} %select_n.16.bias_ref), custom_call_target="tpu_custom_call" | custom-call | flops 838860800 | bytes 1310720 | tf_op jit(solution)/shard_map/pallas_call | solution.py:26
  58.6 1.5 %collective-permute-start.5 = (bf16[2,320,640]{2,1,0:T(8,128)(2,1)S(1)}, bf16[2,320,640]{2,1,0:T(8,128)(2,1)S(1)}, u32[]{:S(2)}, u32[]{:S(2)}) collective-permute-start(bf16[2,320,640]{2,1,0:T(8,128)(2,1)S(1)} %shard_map.129.key_ref), channel_id=1, source_target_pairs={{0,1},{1,0},{2,3},{3,2},{4,5},{5,4},{6,7},{7,6},{8,9},{9,8},{10,11... | collective-permute-start | bytes 2457608 | tf_op jit(solution)/shard_map/ppermute | solution.py:560
  60.1 1.1 %shard_map.130 = (f32[2,512,256]{2,1,0:T(8,128)S(1)}, f32[2,8,256]{2,1,0:T(8,128)S(1)}) custom-call(bf16[2,320,640]{2,1,0:T(8,128)(2,1)S(1)} %shard_map.129.key_ref, bf16[640,128]{1,0:T(8,128)(2,1)S(1)} %get-tuple-element.29.refs_0_, bf16[640,128]{1,0:T(8,128)(2,1)S(1)} %collective-permute-done.2.refs_1_, ...), custom_call_target="tpu_custom_call" | custom-call | flops 377487360 | bytes 655360 | tf_op jit(solution)/shard_map/pallas_call | solution.py:26
  61.2 0.8 collective-permute-done.5.key_ref
  62.0 1.2 %shard_map.131 = (bf16[528,128]{1,0:T(8,128)(2,1)S(1)}, bf16[528,128]{1,0:T(8,128)(2,1)S(1)}, bf16[528,128]{1,0:T(8,128)(2,1)S(1)}, bf16[528,128]{1,0:T(8,128)(2,1)S(1)}) custom-call(bf16[2,320,640]{2,1,0:T(8,128)(2,1)S(1)} %collective-permute-done.5.key_ref, f32[2,512,256]{2,1,0:T(8,128)S(1)} %get-tuple-element.33.own_ref, ...), custom_call_target="tpu_custom_call" | custom-call | flops 377487360 | bytes 655360 | tf_op jit(solution)/shard_map/pallas_call | solution.py:26
  63.2 2.8 %collective-permute-start.6 = (bf16[528,128]{1,0:T(8,128)(2,1)S(1)}, bf16[528,128]{1,0:T(8,128)(2,1)S(1)}, u32[]{:S(2)}, u32[]{:S(2)}) collective-permute-start(bf16[528,128]{1,0:T(8,128)(2,1)S(1)} %get-tuple-element.36), channel_id=1, source_target_pairs={{0,6},{1,7},{2,0},{3,1},{4,2},{5,3},{6,4},{7,5},{8,14},{9,15},{10,... | collective-permute-start | bytes 405512 | tf_op jit(solution)/shard_map/ppermute | solution.py:430
  66.0 0.5 collective-permute-start.7
  66.5 0.6 collective-permute-start.8
  67.1 0.8 slice.10
  67.9 0.2 collective-permute-start.9
  68.1 1.8 %slice.11 = bf16[224,1024]{1,0:T(8,128)(2,1)} slice(bf16[224,2048]{1,0:T(8,128)(2,1)} %collective-permute-done.1.far_hbm), slice={[0:224], [1024:2048]} | slice | bytes 917504 | tf_op jit(solution)/shard_map/slice | solution.py:542
  70.0 2.5 %collective-permute-start.10 = (bf16[224,1024]{1,0:T(8,128)(2,1)}, bf16[224,1024]{1,0:T(8,128)(2,1)}, u32[]{:S(2)}, u32[]{:S(2)}) collective-permute-start(bf16[224,1024]{1,0:T(8,128)(2,1)} %slice.11), channel_id=1, source_target_pairs={{0,192},{8,200},{16,208},{24,216},{32,224},{40,232},{48,240},{56,2... | collective-permute-start | bytes 1376264 | tf_op jit(solution)/shard_map/ppermute | solution.py:434
  72.4 3.5 %collective-permute-done.8.refs_3_ = bf16[528,128]{1,0:T(8,128)(2,1)S(1)} collective-permute-done((bf16[528,128]{1,0:T(8,128)(2,1)S(1)}, bf16[528,128]{1,0:T(8,128)(2,1)S(1)}, u32[]{:S(2)}, u32[]{:S(2)}) %collective-permute-start.8) | collective-permute-done | bytes 135200 | tf_op jit(solution)/shard_map/ppermute | solution.py:430
  75.9 1.5 %shard_map.132 = bf16[8,8,2048]{2,1,0:T(8,128)(2,1)} custom-call(f32[512,128]{1,0:T(8,128)S(1)} %copy-done.6, f32[8,128]{1,0:T(8,128)S(1)} %get-tuple-element.25.fresh_lse_ref, bf16[16,512,128]{2,1,0:T(8,128)(2,1)S(1)} %copy-done, bf16[528,128]{1,0:T(8,128)(2,1)S(1)} %get-tuple-element.35.refs_0_, bf16[528,128]{1,0:T(8,128)(2,1)S(1)} %collective-permute-done.6.refs_1_, ...), custom_call_target="tpu_custom_call" | custom-call | flops 16777216 | bytes 2097152 | tf_op jit(solution)/shard_map/pallas_call | solution.py:26
  77.5 6.4 %all-to-all-start.1 = ((bf16[8,8,2048]{2,1,0:T(8,128)(2,1)}), bf16[8,8,2048]{2,1,0:T(8,128)(2,1)S(1)}, u32[]{:S(2)}, u32[]{:S(2)}) async-start(bf16[8,8,2048]{2,1,0:T(8,128)(2,1)} %shard_map.132), calls=%async_computation.1 | async-start | bytes 524288 | tf_op jit(solution)/shard_map/all_to_all | solution.py:590
  83.9 1.2 %copy-done.3 = bf16[224,2048]{1,0:T(8,128)(2,1)S(1)} copy-done((bf16[224,2048]{1,0:T(8,128)(2,1)S(1)}, bf16[224,2048]{1,0:T(8,128)(2,1)}, u32[]{:S(2)}) %copy-start.3) | copy-done | bytes 917528
  85.0 1.2 %copy-done.4 = bf16[2048,224]{0,1:T(8,128)(2,1)S(1)} copy-done((bf16[2048,224]{0,1:T(8,128)(2,1)S(1)}, bf16[2048,224]{0,1:T(8,128)(2,1)}, u32[]{:S(2)}) %copy-start.4) | copy-done | bytes 917528
  86.2 1.6 %shard_map.133.w_ref = bf16[3,224,2048]{2,1,0:T(8,128)(2,1)S(1)} custom-call(bf16[224,2048]{1,0:T(8,128)(2,1)S(1)} %bitcast.17, bf16[224,2048]{1,0:T(8,128)(2,1)S(1)} %copy-done.3, bf16[224,2048]{1,0:T(8,128)(2,1)} %collective-permute-done.1.far_hbm), custom_call_target="tpu_custom_call" | custom-call | bytes 5505024 | tf_op jit(solution)/shard_map/pallas_call | solution.py:26
  87.9 6.7 %all-to-all-done.1 = bf16[8,8,2048]{2,1,0:T(8,128)(2,1)S(1)} async-done(((bf16[8,8,2048]{2,1,0:T(8,128)(2,1)}), bf16[8,8,2048]{2,1,0:T(8,128)(2,1)S(1)}, u32[]{:S(2)}, u32[]{:S(2)}) %all-to-all-start.1) | async-done | bytes 262176 | tf_op jit(solution)/shard_map/all_to_all | solution.py:590
  94.6 2.1 %shard_map.134 = bf16[32,8,224]{2,1,0:T(8,128)(2,1)S(1)} custom-call(bf16[64,2048]{1,0:T(8,128)(2,1)S(1)} %bitcast.14, bf16[3,224,2048]{2,1,0:T(8,128)(2,1)S(1)} %shard_map.133.w_ref, bf16[224,1024]{1,0:T(8,128)(2,1)S(1)} %collective-permute-done.9.opp_a_hbm, bf16[224,1024]{1,0:T(8,128)(2,1)} %collective-permute-done.10.opp_b_hbm), custom_call_target="tpu_custom_call" | custom-call | flops 234881024 | bytes 3670016 | tf_op jit(solution)/shard_map/pallas_call | solution.py:26
  96.7 12.4 %all_to_all.15.in_ref = bf16[32,8,224]{2,1,0:T(8,128)(2,1)S(1)} all-to-all(bf16[32,8,224]{2,1,0:T(8,128)(2,1)S(1)} %shard_map.134), channel_id=1, replica_groups={{0,2,4,6,8,10,12,14,16,18,20,22,24,26,28,30,32,34,36,38,40,42,44,46,48,..., dimensions={0} | all-to-all | bytes 229376 | tf_op jit(solution)/shard_map/all_to_all | solution.py:617
  109.1 3.4 %collective-permute-start.11 = (f32[4,8,224]{2,1,0:T(8,128)S(1)}, f32[4,8,224]{2,1,0:T(8,128)S(1)}, u32[]{:S(2)}, u32[]{:S(2)}) collective-permute-start(f32[4,8,224]{2,1,0:T(8,128)S(1)} %get-tuple-element.42), channel_id=1, source_target_pairs={{0,1},{1,0},{2,3},{3,2},{4,5},{5,4},{6,7},{7,6},{8,9},{9,8},{10,11... | collective-permute-start | bytes 86024 | tf_op jit(solution)/shard_map/ppermute | solution.py:627
  112.4 0.9 collective-permute-done.11.got_ref
  113.3 0.7 shard_map.136
  (38 shorter events, 0.2 us)
Async XLA Ops:
  4.0 15.0 %copy-start.9 = (bf16[4,2,512]{2,1,0:T(2,128)(2,1)S(1)}, bf16[4,2,512]{2,1,0:T(2,128)(2,1)}, u32[]{:S(2)}) copy-start(bf16[4,2,512]{2,1,0:T(2,128)(2,1)} %param.15) | copy-start | bytes 24580
  4.1 15.1 %copy-start.10 = (bf16[4,2,64]{2,1,0:T(2,128)(2,1)S(1)}, bf16[4,2,64]{2,1,0:T(2,128)(2,1)}, u32[]{:S(2)}) copy-start(bf16[4,2,64]{2,1,0:T(2,128)(2,1)} %param.16) | copy-start | bytes 3076
  4.1 15.4 %copy-start.7 = (bf16[4,2,16,128]{3,2,1,0:T(8,128)(2,1)S(1)}, bf16[4,2,16,128]{3,2,1,0:T(8,128)(2,1)}, u32[]{:S(2)}) copy-start(bf16[4,2,16,128]{3,2,1,0:T(8,128)(2,1)} %param.13) | copy-start | bytes 98308
  4.1 15.4 %copy-start.8 = (bf16[4,2,1024]{2,1,0:T(2,128)(2,1)S(1)}, bf16[4,2,1024]{2,1,0:T(2,128)(2,1)}, u32[]{:S(2)}) copy-start(bf16[4,2,1024]{2,1,0:T(2,128)(2,1)} %param.14) | copy-start | bytes 49156
  4.1 15.6 %copy-start.1 = (bf16[16,128,512]{2,1,0:T(8,128)(2,1)S(1)}, bf16[16,128,512]{2,1,0:T(8,128)(2,1)}, u32[]{:S(2)}) copy-start(bf16[16,128,512]{2,1,0:T(8,128)(2,1)} %w_ref.2) | copy-start | bytes 6291460
  4.1 50.8 %all-to-all-start = ((bf16[32,184,128]{2,1,0:T(8,128)(2,1)}), bf16[32,184,128]{2,1,0:T(8,128)(2,1)}, u32[]{:S(2)}, u32[]{:S(2)}) async-start(bf16[32,184,128]{2,1,0:T(8,128)(2,1)} %shard_map.128), calls=%async_computation | async-start | bytes 3014656 | tf_op jit(solution)/shard_map/all_to_all | solution.py:496
  16.2 9.9 %copy-start.11 = (s32[2,40]{1,0:T(2,128)S(1)}, s32[2,40]{1,0:T(2,128)}, u32[]{:S(2)}) copy-start(s32[2,40]{1,0:T(2,128)} %param.21) | copy-start | bytes 964
  16.2 10.0 %copy-start.12 = (s32[2]{0:T(128)S(1)}, s32[2]{0:T(128)}, u32[]{:S(2)}) copy-start(s32[2]{0:T(128)} %param.22) | copy-start | bytes 28
  16.3 38.7 %collective-permute-start = (bf16[224,2048]{1,0:T(8,128)(2,1)}, bf16[224,2048]{1,0:T(8,128)(2,1)S(1)}, u32[]{:S(2)}, u32[]{:S(2)}) collective-permute-start(bf16[224,2048]{1,0:T(8,128)(2,1)} %bitcast.15), channel_id=1, source_target_pairs={{0,64},{8,72},{16,80},{24,88},{32,96},{40,104},{48,112},{56,120},{... | collective-permute-start | bytes 2752520 | tf_op jit(solution)/shard_map/ppermute | solution.py:434
  17.5 37.4 %collective-permute-start.1 = (bf16[224,2048]{1,0:T(8,128)(2,1)}, bf16[224,2048]{1,0:T(8,128)(2,1)}, u32[]{:S(2)}, u32[]{:S(2)}) collective-permute-start(bf16[224,2048]{1,0:T(8,128)(2,1)} %bitcast.16), channel_id=1, source_target_pairs={{0,192},{8,200},{16,208},{24,216},{32,224},{40,232},{48,240},{56,2... | collective-permute-start | bytes 2752520 | tf_op jit(solution)/shard_map/ppermute | solution.py:434
  21.1 0.7 copy-start.5
  21.8 6.1 %collective-permute-start.2 = (bf16[640,128]{1,0:T(8,128)(2,1)}, bf16[640,128]{1,0:T(8,128)(2,1)S(1)}, u32[]{:S(2)}, u32[]{:S(2)}) collective-permute-start(bf16[640,128]{1,0:T(8,128)(2,1)} %get-tuple-element.27), channel_id=1, source_target_pairs={{0,2},{1,3},{2,4},{3,5},{4,6},{5,7},{6,0},{7,1},{8,10},{9,11},{10,... | collective-permute-start | bytes 491528 | tf_op jit(solution)/shard_map/ppermute | solution.py:430
  23.1 9.2 %collective-permute-start.4 = (bf16[640,128]{1,0:T(8,128)(2,1)}, bf16[640,128]{1,0:T(8,128)(2,1)S(1)}, u32[]{:S(2)}, u32[]{:S(2)}) collective-permute-start(bf16[640,128]{1,0:T(8,128)(2,1)} %get-tuple-element.27), channel_id=1, source_target_pairs={{0,6},{1,7},{2,0},{3,1},{4,2},{5,3},{6,4},{7,5},{8,14},{9,15},{10,... | collective-permute-start | bytes 491528 | tf_op jit(solution)/shard_map/ppermute | solution.py:430
  24.5 7.7 %collective-permute-start.3 = (bf16[640,128]{1,0:T(8,128)(2,1)S(1)}, bf16[640,128]{1,0:T(8,128)(2,1)S(1)}, u32[]{:S(2)}, u32[]{:S(2)}) collective-permute-start(bf16[640,128]{1,0:T(8,128)(2,1)S(1)} %get-tuple-element.29.refs_0_), channel_id=1, source_target_pairs={{0,4},{1,5},{2,6},{3,7},{4,0},{5,1},{6,2},{7,3},{8,12},{9,13},{10,... | collective-permute-start | bytes 491528 | tf_op jit(solution)/shard_map/ppermute | solution.py:430
  54.9 12.2 %copy-start.2 = (bf16[224,2048]{1,0:T(8,128)(2,1)}, bf16[224,2048]{1,0:T(8,128)(2,1)S(1)}, u32[]{:S(2)}) copy-start(bf16[224,2048]{1,0:T(8,128)(2,1)S(1)} %collective-permute-done.near_hbm) | copy-start | bytes 2752516
  58.6 3.4 %collective-permute-start.5 = (bf16[2,320,640]{2,1,0:T(8,128)(2,1)S(1)}, bf16[2,320,640]{2,1,0:T(8,128)(2,1)S(1)}, u32[]{:S(2)}, u32[]{:S(2)}) collective-permute-start(bf16[2,320,640]{2,1,0:T(8,128)(2,1)S(1)} %shard_map.129.key_ref), channel_id=1, source_target_pairs={{0,1},{1,0},{2,3},{3,2},{4,5},{5,4},{6,7},{7,6},{8,9},{9,8},{10,11... | collective-permute-start | bytes 2457608 | tf_op jit(solution)/shard_map/ppermute | solution.py:560
  62.0 13.9 %copy-start = (bf16[16,512,128]{2,1,0:T(8,128)(2,1)S(1)}, bf16[16,512,128]{2,1,0:T(8,128)(2,1)}, u32[]{:S(2)}) copy-start(bf16[16,512,128]{2,1,0:T(8,128)(2,1)} %w_ref.3) | copy-start | bytes 6291460
  62.0 13.9 %copy-start.6 = (f32[512,128]{1,0:T(8,128)S(1)}, f32[512,128]{1,0:T(8,128)}, u32[]{:S(2)}) copy-start(f32[512,128]{1,0:T(8,128)} %copy-done.5) | copy-start | bytes 786436
  63.2 9.2 %collective-permute-start.6 = (bf16[528,128]{1,0:T(8,128)(2,1)S(1)}, bf16[528,128]{1,0:T(8,128)(2,1)S(1)}, u32[]{:S(2)}, u32[]{:S(2)}) collective-permute-start(bf16[528,128]{1,0:T(8,128)(2,1)S(1)} %get-tuple-element.36), channel_id=1, source_target_pairs={{0,6},{1,7},{2,0},{3,1},{4,2},{5,3},{6,4},{7,5},{8,14},{9,15},{10,... | collective-permute-start | bytes 405512 | tf_op jit(solution)/shard_map/ppermute | solution.py:430
  66.0 6.4 %collective-permute-start.7 = (bf16[528,128]{1,0:T(8,128)(2,1)S(1)}, bf16[528,128]{1,0:T(8,128)(2,1)S(1)}, u32[]{:S(2)}, u32[]{:S(2)}) collective-permute-start(bf16[528,128]{1,0:T(8,128)(2,1)S(1)} %get-tuple-element.37), channel_id=1, source_target_pairs={{0,4},{1,5},{2,6},{3,7},{4,0},{5,1},{6,2},{7,3},{8,12},{9,13},{10,... | collective-permute-start | bytes 405512 | tf_op jit(solution)/shard_map/ppermute | solution.py:430
  66.5 9.4 %collective-permute-start.8 = (bf16[528,128]{1,0:T(8,128)(2,1)S(1)}, bf16[528,128]{1,0:T(8,128)(2,1)S(1)}, u32[]{:S(2)}, u32[]{:S(2)}) collective-permute-start(bf16[528,128]{1,0:T(8,128)(2,1)S(1)} %get-tuple-element.38), channel_id=1, source_target_pairs={{0,2},{1,3},{2,4},{3,5},{4,6},{5,7},{6,0},{7,1},{8,10},{9,11},{10,... | collective-permute-start | bytes 405512 | tf_op jit(solution)/shard_map/ppermute | solution.py:430
  67.9 20.0 %collective-permute-start.9 = (bf16[224,1024]{1,0:T(8,128)(2,1)}, bf16[224,1024]{1,0:T(8,128)(2,1)S(1)}, u32[]{:S(2)}, u32[]{:S(2)}) collective-permute-start(bf16[224,1024]{1,0:T(8,128)(2,1)} %slice.10), channel_id=1, source_target_pairs={{0,64},{8,72},{16,80},{24,88},{32,96},{40,104},{48,112},{56,120},{... | collective-permute-start | bytes 1376264 | tf_op jit(solution)/shard_map/ppermute | solution.py:434
  70.0 17.9 %collective-permute-start.10 = (bf16[224,1024]{1,0:T(8,128)(2,1)}, bf16[224,1024]{1,0:T(8,128)(2,1)}, u32[]{:S(2)}, u32[]{:S(2)}) collective-permute-start(bf16[224,1024]{1,0:T(8,128)(2,1)} %slice.11), channel_id=1, source_target_pairs={{0,192},{8,200},{16,208},{24,216},{32,224},{40,232},{48,240},{56,2... | collective-permute-start | bytes 1376264 | tf_op jit(solution)/shard_map/ppermute | solution.py:434
  77.5 17.1 %all-to-all-start.1 = ((bf16[8,8,2048]{2,1,0:T(8,128)(2,1)}), bf16[8,8,2048]{2,1,0:T(8,128)(2,1)S(1)}, u32[]{:S(2)}, u32[]{:S(2)}) async-start(bf16[8,8,2048]{2,1,0:T(8,128)(2,1)} %shard_map.132), calls=%async_computation.1 | async-start | bytes 524288 | tf_op jit(solution)/shard_map/all_to_all | solution.py:590
  83.9 1.2 %copy-start.3 = (bf16[224,2048]{1,0:T(8,128)(2,1)S(1)}, bf16[224,2048]{1,0:T(8,128)(2,1)}, u32[]{:S(2)}) copy-start(bf16[224,2048]{1,0:T(8,128)(2,1)} %copy-done.2) | copy-start | bytes 2752516
  85.0 1.2 %copy-start.4 = (bf16[2048,224]{0,1:T(8,128)(2,1)S(1)}, bf16[2048,224]{0,1:T(8,128)(2,1)}, u32[]{:S(2)}) copy-start(bf16[2048,224]{0,1:T(8,128)(2,1)} %param.25) | copy-start | bytes 2752516
  109.1 4.2 %collective-permute-start.11 = (f32[4,8,224]{2,1,0:T(8,128)S(1)}, f32[4,8,224]{2,1,0:T(8,128)S(1)}, u32[]{:S(2)}, u32[]{:S(2)}) collective-permute-start(f32[4,8,224]{2,1,0:T(8,128)S(1)} %get-tuple-element.42), channel_id=1, source_target_pairs={{0,1},{1,0},{2,3},{3,2},{4,5},{5,4},{6,7},{7,6},{8,9},{9,8},{10,11... | collective-permute-start | bytes 86024 | tf_op jit(solution)/shard_map/ppermute | solution.py:627

commit v8 on v7

--- a/solution.py
+++ b/solution.py
@@ -30,7 +30,9 @@
             HBM if i in in_hbm else SMEM if a.dtype == jnp.int32 and a.ndim == 1 else VMEM
             for i, a in enumerate(ins)
         ],
-        out_specs=jax.tree.map(lambda _: out_spec, out_shape),
+        out_specs=out_spec
+        if isinstance(out_spec, tuple)
+        else jax.tree.map(lambda _: out_spec, out_shape),
         scratch_shapes=list(scratch),
         compiler_params=pltpu.CompilerParams(vmem_limit_bytes=mem * 2**20),
         cost_estimate=pl.CostEstimate(flops=flops, bytes_accessed=nbytes, transcendentals=0),
@@ -225,6 +227,19 @@
         copy = pltpu.make_async_copy(block_hbm.at[here], block_ref.at[here], in_sem.at[i])
         copy.start()
         copies.append(copy)
+
+    def spread_over(columns, group, lane):
+        own = iota((count, columns), 0) == iota((1, columns), 1) // group
+        return ones_where(iota((TAIL, columns), 0) == lane), jnp.where(own, 1.0, 0.0)
+
+    lat_columns = count * pair_tokens
+    lat_inner = iota((1, lat_columns), 1) % pair_tokens
+    lat_spread = spread_over(lat_columns, pair_tokens, lat_inner)
+    rope_columns = count * rest
+    rope_inner = iota((1, rope_columns), 1) % rest
+    lane = jnp.where(rope_inner < per_pair * rope_rows, rope_inner // rope_rows * piece, TAIL)
+    rope_spread = spread_over(rope_columns, rest, lane)
+
     labels = []
     for i, copy in enumerate(copies):
         copy.wait()
@@ -243,25 +258,18 @@
             )
     labels = jnp.concatenate(labels, axis=0).astype(jnp.bfloat16)
 
-    def slot_of(columns, group, lane):
-        spread = ones_where(iota((TAIL, columns), 0) == lane)
-        wide = dot(labels, spread)
-        own = iota((count, columns), 0) == iota((1, columns), 1) // group
-        return jnp.sum(jnp.where(own, wide, 0.0), axis=0, keepdims=True).astype(jnp.int32) - 1
-
-    columns = count * pair_tokens
-    inner = iota((1, columns), 1) % pair_tokens
-    slot = slot_of(columns, pair_tokens, inner)
-    token = inner % piece
+    def slot_of(spread, own):
+        wide = dot(labels, spread) * own
+        return jnp.sum(wide, axis=0, keepdims=True).astype(jnp.int32) - 1
+
+    slot = slot_of(*lat_spread)
+    token = lat_inner % piece
     row = (slot >= pages_row).astype(jnp.int32)
     target = row * (per_row - pages_row * (piece // 2)) + token % 2 * half
     target = target + slot * (piece // 2) + token // 2
     target = jnp.where(slot >= 0, target, -1)
-    columns = count * rest
-    inner = iota((1, columns), 1) % rest
-    lane = jnp.where(inner < per_pair * rope_rows, inner // rope_rows * piece, TAIL)
-    slot = slot_of(columns, rest, lane)
-    rope_target = jnp.where(slot >= 0, slot * rope_rows + inner % rope_rows, -1)
+    slot = slot_of(*rope_spread)
+    rope_target = jnp.where(slot >= 0, slot * rope_rows + rope_inner % rope_rows, -1)
     copies = []
     for b in range(rows):
         pick = ones_where(iota((half, 1), 0) + b * half == rope_target)
@@ -298,12 +306,21 @@
     return jnp.concatenate(tiles, axis=1)
 
 
-def own_kernel(scale, key_ref, *refs):
-    q_refs, (part_ref, stat_ref) = refs[:-2], refs[-2:]
+def own_kernel(scale, key_ref, near_hbm, far_hbm, *refs):
+    q_refs, (part_ref, stat_ref, half_a, half_b, sem_ref) = refs[:-5], refs[-5:]
+    size = half_a.shape[0]
+    copies = [
+        pltpu.make_async_copy(near_hbm.at[pl.ds(0, size)], half_a, sem_ref.at[0]),
+        pltpu.make_async_copy(far_hbm.at[pl.ds(size, size)], half_b, sem_ref.at[1]),
+    ]
+    for copy in copies:
+        copy.start()
     for b in range(key_ref.shape[0]):
         high, total, part = attend(scale, key_ref[b], ask(q_refs, b), part_ref.shape[1])
         part_ref[b] = part
         stat_ref[b] = jnp.where(iota(stat_ref.shape[1:], 0) == 0, high, total)
+    for copy in copies:
+        copy.wait()
 
 
 def both_kernel(scale, key_ref, own_ref, stat_ref, *refs):
@@ -379,17 +396,15 @@
         copy.wait()
 
 
-def project_kernel(
-    width, x_ref, w_ref, opp_a_hbm, opp_b_hbm, out_ref, opp_a_ref, opp_b_ref, sem_ref
-):
+def project_kernel(width, x_ref, w_ref, opp_a_hbm, opp_b_hbm, out_ref, opp_ref, sem_ref):
+    size = opp_a_hbm.shape[0]
     copies = [
-        pltpu.make_async_copy(opp_a_hbm, opp_a_ref, sem_ref.at[0]),
-        pltpu.make_async_copy(opp_b_hbm, opp_b_ref, sem_ref.at[1]),
+        pltpu.make_async_copy(opp_a_hbm, opp_ref.at[pl.ds(0, size)], sem_ref.at[0]),
+        pltpu.make_async_copy(opp_b_hbm, opp_ref.at[pl.ds(size, size)], sem_ref.at[1]),
     ]
     for copy in copies:
         copy.start()
     here = lax.axis_index("row") // NZ
-    depth = opp_a_hbm.shape[1]
 
     def put(k, block):
         owner = (here + k) % NX
@@ -399,10 +414,9 @@
 
     for i, k in enumerate((0, NX - 1, 1)):
         put(k, dot_t(x_ref[...], w_ref[i]))
-    copies[0].wait()
-    opposite = dot_t(x_ref[:, :depth], opp_a_ref[...])
-    copies[1].wait()
-    put(2, opposite + dot_t(x_ref[:, depth:], opp_b_ref[...]))
+    for copy in copies:
+        copy.wait()
+    put(2, dot_t(x_ref[...], opp_ref[...]))
 
 
 def sum_kernel(in_ref, keep_ref, send_ref):
@@ -528,7 +542,6 @@
 
     w_t = w_o.T
     w_near, w_far = shift_x(w_t, 1), shift_x(w_t, -1)
-    depth = w_t.shape[1] // 2
 
     slot_ids = jnp.arange(pages_row, dtype=jnp.int32)
     holds = (page_table[:, :, None] == slot_ids[None, None, :]).astype(jnp.int32)
@@ -539,7 +552,6 @@
     bias = jnp.where(usable, 0.0, NEG).astype(f32).reshape(rows_dev * pages_row * piece, 1)
 
     got, w_near, w_far, all_queries = lax.optimization_barrier((got, w_near, w_far, all_queries))
-    opposite = [shift_x(w_near[:, :depth], 1), shift_x(w_far[:, depth:], -1)]
     key = call(
         functools.partial(gather_kernel, piece, per_pair, rope_w, pages_row),
         jax.ShapeDtypeStruct((rows_dev, pages_row * piece, lat_w + TAIL), bf16),
@@ -559,16 +571,23 @@
     )
     other = lax.ppermute(key, "head", [(h, h ^ 1) for h in range(n_head)])
     asked = NX * queries // rows_dev
-    own_part, own_stat = call(
+    half_w = jax.ShapeDtypeStruct((w_t.shape[0] // 2, w_t.shape[1]), bf16)
+    own_part, own_stat, half_a, half_b = call(
         functools.partial(own_kernel, scale),
         (
             jax.ShapeDtypeStruct((rows_dev, lat_w, asked), f32),
             jax.ShapeDtypeStruct((rows_dev, 8, asked), f32),
+            half_w,
+            half_w,
         ),
-        [key] + all_queries,
+        [key, w_near, w_far] + all_queries,
+        scratch=[pltpu.SemaphoreType.DMA((2,))],
         flops=2 * tokens * asked * (2 * lat_w + TAIL),
         nbytes=2 * tokens * lat_w,
-    )
+        out_spec=(VMEM, VMEM, HBM, HBM),
+        in_hbm=(1, 2),
+    )
+    opposite = [shift_x(half_a, 1), shift_x(half_b, -1)]
     parts = call(
         functools.partial(both_kernel, scale),
         tuple(jax.ShapeDtypeStruct((lat_w + INFO, queries), bf16) for _ in range(NX)),
@@ -604,7 +623,7 @@
         functools.partial(project_kernel, width),
         jax.ShapeDtypeStruct((NZ * NX, width, cols), bf16),
         [ring.reshape(NZ * width, heads * value_w), w_ring] + opposite,
-        scratch=[pltpu.VMEM((cols, depth), bf16)] * 2 + [pltpu.SemaphoreType.DMA((2,))],
+        scratch=[pltpu.VMEM(w_t.shape, bf16), pltpu.SemaphoreType.DMA((2,))],
         flops=2 * NX * NZ * width * w_o.size,
         nbytes=2 * NX * w_o.size,
         in_hbm=(2, 3),

time: 115 us -> 117 us (1.017)
  local copies, waits for them, and re-layouts: 6.53 us -> 11.3 us
  waiting for transfers between devices: 40.2 us -> 36.8 us
  Pallas kernels: 17.3 us -> 18.5 us
    ppermute x4, waiting for transfers between devices: 22.7 us -> 18.7 us  [shift_x(): lax.ppermute(x, 'row', [(a * NZ + b, (a + k) % NX * NZ + b) for a in rang...]
    unnamed x27 -> x29, local copies, waits for them, and re-layouts: 3.22 us -> 6.86 us
    slice x2 -> x0, local copies, waits for them, and re-layouts: 2.66 us -> none  [on_device(): opposite = [shift_x(w_near[:, :depth], 1), shift_x(w_far[:, depth:], -1)]]
    select_n x1, local copies, waits for them, and re-layouts: 0.13 us -> 1.76 us  [on_device(): jnp.where(usable, 0.0, NEG).astype(f32)]
    pallas_call x10, Pallas kernels: 17.3 us -> 18.5 us  [call(): pl.pallas_call(body, out_shape=out_shape, in_specs=[HBM if i in in_hbm el...]
  transfers between devices with their start and end apart: 14 -> 14, of which waited for: 7 -> 9; matrix products, arithmetic and copies ran while one was open for 3% -> 5% of each run, Pallas kernels for 5% -> 5%
where the time goes in v8:
time: 117 us; the launch traced here: 116 us
  waiting for transfers between devices  36.8 us (31%)
  starting transfers between devices  36.2 us (31%)
  Pallas kernels  18.5 us (16%)
  blocking collectives  12.4 us (11%)
  local copies, waits for them, and re-layouts  11.3 us (10%)
    ppermute x4, waiting for transfers between devices, shift_x(): lax.ppermute(x, 'row', [(a * NZ + b, (a + k) % NX * NZ + b) for a in rang...  18.7 us
    pallas_call x10, Pallas kernels, call(): pl.pallas_call(body, out_shape=out_shape, in_specs=[HBM if i in in_hbm el...  18.5 us
    all_to_all x1, blocking collectives, on_device(): lax.all_to_all(sums, ('row', 'head'), split_axis=0, concat_axis=0, axis_i...  12.4 us
    all_to_all x1, starting transfers between devices, on_device(): got = lax.all_to_all(send, 'row', split_axis=0, concat_axis=0, tiled=True)  11.9 us
    ppermute x6, waiting for transfers between devices, shift_y(): lax.ppermute(x, 'head', [(h, (h + k * cores) % n_head) for h in range(n_h...  10.1 us
    ppermute x6, starting transfers between devices, shift_y(): lax.ppermute(x, 'head', [(h, (h + k * cores) % n_head) for h in range(n_h...  8.41 us
    all_to_all x1, waiting for transfers between devices, on_device(): lax.all_to_all(head_out, 'row', split_axis=0, concat_axis=0, axis_index_g...  7.12 us
    unnamed x29, local copies, waits for them, and re-layouts  6.86 us
  transfers between devices with their start and end apart: 14, of which 9 were waited for; matrix products, arithmetic and copies ran while one was open for 5% of the time, Pallas kernels for 5%

profile of v8, /device:TPU:1, one launch (start us, length us, event | category | flops | bytes accessed | tf_op | source)
XLA Modules:
  0.0 116.4 jit_solution(2078852592757517696)
XLA Ops:
  0.0 4.0 %shard_map.128 = bf16[32,184,128]{2,1,0:T(8,128)(2,1)} custom-call(s32[1,80]{1,0:T(1,128)} %bitcast.19, s32[1,80]{1,0:T(1,128)} %bitcast.20, bf16[80,64,512]{2,1,0:T(8,128)(2,1)} %lat_hbm.1, bf16[80,4096]{1,0:T(8,128)(2,1)} %rope_hbm.1), custom_call_target="tpu_custom_call" | custom-call | flops 838860800 | bytes 2621440 | tf_op jit(solution)/shard_map/pallas_call | solution.py:26
  4.1 0.0 copy-start.11
  4.1 11.9 %all-to-all-start = ((bf16[32,184,128]{2,1,0:T(8,128)(2,1)}), bf16[32,184,128]{2,1,0:T(8,128)(2,1)S(1)}, u32[]{:S(2)}, u32[]{:S(2)}) async-start(bf16[32,184,128]{2,1,0:T(8,128)(2,1)} %shard_map.128), calls=%async_computation | async-start | bytes 3014656 | tf_op jit(solution)/shard_map/all_to_all | solution.py:510
  16.0 2.6 %collective-permute-start.1 = (bf16[224,2048]{1,0:T(8,128)(2,1)}, bf16[224,2048]{1,0:T(8,128)(2,1)S(1)}, u32[]{:S(2)}, u32[]{:S(2)}) collective-permute-start(bf16[224,2048]{1,0:T(8,128)(2,1)} %bitcast.8.own_hbm), channel_id=1, source_target_pairs={{0,192},{8,200},{16,208},{24,216},{32,224},{40,232},{48,240},{56,2... | collective-permute-start | bytes 2752520 | tf_op jit(solution)/shard_map/ppermute | solution.py:448
  18.6 0.1 pad.3.clone
  18.7 0.2 copy.32
  18.8 0.7 slice_bitcast_fusion.fresh_t_ref
  19.5 0.1 copy.35
  19.6 0.1 pad.5.clone
  19.7 0.8 copy.30
  20.5 0.8 reshape.88
  21.4 1.6 %copy-done.5 = bf16[16,128,512]{2,1,0:T(8,128)(2,1)S(1)} copy-done((bf16[16,128,512]{2,1,0:T(8,128)(2,1)S(1)}, bf16[16,128,512]{2,1,0:T(8,128)(2,1)}, u32[]{:S(2)}) %copy-start.5) | copy-done | bytes 2097176
  23.0 0.9 copy-done.6
  23.9 1.3 %shard_map.127 = (bf16[640,128]{1,0:T(8,128)(2,1)S(1)}, bf16[640,128]{1,0:T(8,128)(2,1)}, f32[512,128]{1,0:T(8,128)S(1)}, f32[8,128]{1,0:T(8,128)S(1)}) custom-call(bf16[16,8,128]{2,1,0:T(8,128)(2,1)S(1)} %bitcast.15, bf16[128,128]{1,0:T(8,128)(2,1)S(1)} %pad_maximum_fusion.qtail_ref, bf16[16,128,512]{2,1,0:T(8,128)(2,1)S(1)} %copy-done.5, ...), custom_call_target="tpu_custom_call" | custom-call | flops 16777216 | bytes 2097152 | tf_op jit(solution)/shard_map/pallas_call | solution.py:26
  25.2 0.7 copy-done.8
  25.9 2.7 %collective-permute-start.4 = (bf16[640,128]{1,0:T(8,128)(2,1)}, bf16[640,128]{1,0:T(8,128)(2,1)}, u32[]{:S(2)}, u32[]{:S(2)}) collective-permute-start(bf16[640,128]{1,0:T(8,128)(2,1)} %get-tuple-element.29), channel_id=1, source_target_pairs={{0,6},{1,7},{2,0},{3,1},{4,2},{5,3},{6,4},{7,5},{8,14},{9,15},{10,... | collective-permute-start | bytes 491528 | tf_op jit(solution)/shard_map/ppermute | solution.py:444
  28.6 1.6 %collective-permute-start.3 = (bf16[640,128]{1,0:T(8,128)(2,1)S(1)}, bf16[640,128]{1,0:T(8,128)(2,1)}, u32[]{:S(2)}, u32[]{:S(2)}) collective-permute-start(bf16[640,128]{1,0:T(8,128)(2,1)S(1)} %get-tuple-element.33.refs_0_), channel_id=1, source_target_pairs={{0,4},{1,5},{2,6},{3,7},{4,0},{5,1},{6,2},{7,3},{8,12},{9,13},{10,... | collective-permute-start | bytes 491528 | tf_op jit(solution)/shard_map/ppermute | solution.py:444
  30.3 0.1 select_reduce_fusion
  30.4 0.1 subtract_subtract_fusion
  30.5 0.7 compare_select_fusion
  31.2 1.8 %select_n.16.bias_ref = f32[640,1]{1,0:T(8,128)} reshape(f32[2,2,40,4]{3,2,1,0:T(8,128)} %compare_select_fusion) | data formatting | bytes 5120 | tf_op jit(solution)/shard_map/jit(_where)/select_n | solution.py:552
  32.9 3.5 %collective-permute-done.3.refs_2_ = bf16[640,128]{1,0:T(8,128)(2,1)} collective-permute-done((bf16[640,128]{1,0:T(8,128)(2,1)S(1)}, bf16[640,128]{1,0:T(8,128)(2,1)}, u32[]{:S(2)}, u32[]{:S(2)}) %collective-permute-start.3) | collective-permute-done | bytes 163872 | tf_op jit(solution)/shard_map/ppermute | solution.py:444
  36.4 0.4 collective-permute-done.2.refs_1_
  36.8 16.0 %collective-permute-done.1.far_hbm = bf16[224,2048]{1,0:T(8,128)(2,1)S(1)} collective-permute-done((bf16[224,2048]{1,0:T(8,128)(2,1)}, bf16[224,2048]{1,0:T(8,128)(2,1)S(1)}, u32[]{:S(2)}, u32[]{:S(2)}) %collective-permute-start.1) | collective-permute-done | bytes 917536 | tf_op jit(solution)/shard_map/ppermute | solution.py:448
  52.9 2.7 %collective-permute-done.near_hbm = bf16[224,2048]{1,0:T(8,128)(2,1)S(1)} collective-permute-done((bf16[224,2048]{1,0:T(8,128)(2,1)}, bf16[224,2048]{1,0:T(8,128)(2,1)S(1)}, u32[]{:S(2)}, u32[]{:S(2)}) %collective-permute-start) | collective-permute-done | bytes 917536 | tf_op jit(solution)/shard_map/ppermute | solution.py:448
  55.5 1.2 %copy-done.7 = f32[640,1]{1,0:T(8,128)S(1)} copy-done((f32[640,1]{1,0:T(8,128)S(1)}, f32[640,1]{1,0:T(8,128)}, u32[]{:S(2)}) %copy-start.7) | copy-done | bytes 2584
  56.7 3.0 %shard_map.129.key_ref = bf16[2,320,640]{2,1,0:T(8,128)(2,1)S(1)} custom-call(bf16[32,184,128]{2,1,0:T(8,128)(2,1)S(1)} %all-to-all-done.block_hbm, f32[640,1]{1,0:T(8,128)S(1)} %copy-done.7), custom_call_target="tpu_custom_call" | custom-call | flops 838860800 | bytes 1310720 | tf_op jit(solution)/shard_map/pallas_call | solution.py:26
  59.8 1.5 %collective-permute-start.5 = (bf16[2,320,640]{2,1,0:T(8,128)(2,1)S(1)}, bf16[2,320,640]{2,1,0:T(8,128)(2,1)S(1)}, u32[]{:S(2)}, u32[]{:S(2)}) collective-permute-start(bf16[2,320,640]{2,1,0:T(8,128)(2,1)S(1)} %shard_map.129.key_ref), channel_id=1, source_target_pairs={{0,1},{1,0},{2,3},{3,2},{4,5},{5,4},{6,7},{7,6},{8,9},{9,8},{10,11... | collective-permute-start | bytes 2457608 | tf_op jit(solution)/shard_map/ppermute | solution.py:572
  61.3 2.3 %shard_map.130 = (f32[2,512,256]{2,1,0:T(8,128)S(1)}, f32[2,8,256]{2,1,0:T(8,128)S(1)}, bf16[112,2048]{1,0:T(8,128)(2,1)}, bf16[112,2048]{1,0:T(8,128)(2,1)}) custom-call(bf16[2,320,640]{2,1,0:T(8,128)(2,1)S(1)} %shard_map.129.key_ref, bf16[224,2048]{1,0:T(8,128)(2,1)S(1)} %collective-permute-done.near_hbm, ...), custom_call_target="tpu_custom_call" | custom-call | flops 377487360 | bytes 655360 | tf_op jit(solution)/shard_map/pallas_call | solution.py:26
  63.6 2.4 %shard_map.131 = (bf16[528,128]{1,0:T(8,128)(2,1)S(1)}, bf16[528,128]{1,0:T(8,128)(2,1)S(1)}, bf16[528,128]{1,0:T(8,128)(2,1)S(1)}, bf16[528,128]{1,0:T(8,128)(2,1)S(1)}) custom-call(bf16[2,320,640]{2,1,0:T(8,128)(2,1)S(1)} %collective-permute-done.5.key_ref, f32[2,512,256]{2,1,0:T(8,128)S(1)} %get-tuple-element.37.own_ref, ...), custom_call_target="tpu_custom_call" | custom-call | flops 377487360 | bytes 655360 | tf_op jit(solution)/shard_map/pallas_call | solution.py:26
  66.0 3.0 %collective-permute-start.6 = (bf16[528,128]{1,0:T(8,128)(2,1)S(1)}, bf16[528,128]{1,0:T(8,128)(2,1)S(1)}, u32[]{:S(2)}, u32[]{:S(2)}) collective-permute-start(bf16[528,128]{1,0:T(8,128)(2,1)S(1)} %get-tuple-element.40), channel_id=1, source_target_pairs={{0,6},{1,7},{2,0},{3,1},{4,2},{5,3},{6,4},{7,5},{8,14},{9,15},{10,... | collective-permute-start | bytes 405512 | tf_op jit(solution)/shard_map/ppermute | solution.py:444
  69.0 0.3 collective-permute-start.7
  69.3 0.7 collective-permute-start.8
  70.0 2.7 %collective-permute-start.10 = (bf16[112,2048]{1,0:T(8,128)(2,1)}, bf16[112,2048]{1,0:T(8,128)(2,1)}, u32[]{:S(2)}, u32[]{:S(2)}) collective-permute-start(bf16[112,2048]{1,0:T(8,128)(2,1)} %get-tuple-element.44), channel_id=1, source_target_pairs={{0,192},{8,200},{16,208},{24,216},{32,224},{40,232},{48,240},{56,2... | collective-permute-start | bytes 1376264 | tf_op jit(solution)/shard_map/ppermute | solution.py:448
  72.7 2.0 %collective-permute-done.6.refs_1_ = bf16[528,128]{1,0:T(8,128)(2,1)S(1)} collective-permute-done((bf16[528,128]{1,0:T(8,128)(2,1)S(1)}, bf16[528,128]{1,0:T(8,128)(2,1)S(1)}, u32[]{:S(2)}, u32[]{:S(2)}) %collective-permute-start.6) | collective-permute-done | bytes 135200 | tf_op jit(solution)/shard_map/ppermute | solution.py:444
  74.7 0.7 collective-permute-done.7.refs_2_
  75.4 3.5 %collective-permute-done.8.refs_3_ = bf16[528,128]{1,0:T(8,128)(2,1)S(1)} collective-permute-done((bf16[528,128]{1,0:T(8,128)(2,1)S(1)}, bf16[528,128]{1,0:T(8,128)(2,1)S(1)}, u32[]{:S(2)}, u32[]{:S(2)}) %collective-permute-start.8) | collective-permute-done | bytes 135200 | tf_op jit(solution)/shard_map/ppermute | solution.py:444
  78.9 1.5 %shard_map.132 = bf16[8,8,2048]{2,1,0:T(8,128)(2,1)} custom-call(f32[512,128]{1,0:T(8,128)S(1)} %copy-done.9, f32[8,128]{1,0:T(8,128)S(1)} %get-tuple-element.27.fresh_lse_ref, bf16[16,512,128]{2,1,0:T(8,128)(2,1)S(1)} %copy-done.4, bf16[528,128]{1,0:T(8,128)(2,1)S(1)} %get-tuple-element.39.refs_0_, bf16[528,128]{1,0:T(8,128)(2,1)S(1)} %collective-permute-done.6.refs_1_, ...), custom_call_target="tpu_custom_call" | custom-call | flops 16777216 | bytes 2097152 | tf_op jit(solution)/shard_map/pallas_call | solution.py:26
  80.4 5.8 %all-to-all-start.1 = ((bf16[8,8,2048]{2,1,0:T(8,128)(2,1)}), bf16[8,8,2048]{2,1,0:T(8,128)(2,1)S(1)}, u32[]{:S(2)}, u32[]{:S(2)}) async-start(bf16[8,8,2048]{2,1,0:T(8,128)(2,1)} %shard_map.132), calls=%async_computation.1 | async-start | bytes 524288 | tf_op jit(solution)/shard_map/all_to_all | solution.py:609
  86.2 1.2 %copy-done.1 = bf16[224,2048]{1,0:T(8,128)(2,1)S(1)} copy-done((bf16[224,2048]{1,0:T(8,128)(2,1)S(1)}, bf16[224,2048]{1,0:T(8,128)(2,1)}, u32[]{:S(2)}) %copy-start.1) | copy-done | bytes 917528
  87.4 1.2 %copy-done.3 = bf16[224,2048]{1,0:T(8,128)(2,1)S(1)} copy-done((bf16[224,2048]{1,0:T(8,128)(2,1)S(1)}, bf16[224,2048]{1,0:T(8,128)(2,1)}, u32[]{:S(2)}) %copy-start.3) | copy-done | bytes 917528
  88.6 1.2 %shard_map.133.w_ref = bf16[3,224,2048]{2,1,0:T(8,128)(2,1)S(1)} custom-call(bf16[224,2048]{1,0:T(8,128)(2,1)} %bitcast.8.own_hbm, bf16[224,2048]{1,0:T(8,128)(2,1)S(1)} %copy-done.3, bf16[224,2048]{1,0:T(8,128)(2,1)S(1)} %copy-done.1), custom_call_target="tpu_custom_call" | custom-call | bytes 5505024 | tf_op jit(solution)/shard_map/pallas_call | solution.py:26
  89.8 7.1 %all-to-all-done.1 = bf16[8,8,2048]{2,1,0:T(8,128)(2,1)S(1)} async-done(((bf16[8,8,2048]{2,1,0:T(8,128)(2,1)}), bf16[8,8,2048]{2,1,0:T(8,128)(2,1)S(1)}, u32[]{:S(2)}, u32[]{:S(2)}) %all-to-all-start.1) | async-done | bytes 262176 | tf_op jit(solution)/shard_map/all_to_all | solution.py:609
  97.0 2.1 %shard_map.134 = bf16[32,8,224]{2,1,0:T(8,128)(2,1)S(1)} custom-call(bf16[64,2048]{1,0:T(8,128)(2,1)S(1)} %bitcast.14, bf16[3,224,2048]{2,1,0:T(8,128)(2,1)S(1)} %shard_map.133.w_ref, bf16[112,2048]{1,0:T(8,128)(2,1)S(1)} %collective-permute-done.9.opp_a_hbm, bf16[112,2048]{1,0:T(8,128)(2,1)} %collective-permute-done.10.opp_b_hbm), custom_call_target="tpu_custom_call" | custom-call | flops 234881024 | bytes 3670016 | tf_op jit(solution)/shard_map/pallas_call | solution.py:26
  99.0 12.4 %all_to_all.15.in_ref = bf16[32,8,224]{2,1,0:T(8,128)(2,1)S(1)} all-to-all(bf16[32,8,224]{2,1,0:T(8,128)(2,1)S(1)} %shard_map.134), channel_id=1, replica_groups={{0,2,4,6,8,10,12,14,16,18,20,22,24,26,28,30,32,34,36,38,40,42,44,46,48,..., dimensions={0} | all-to-all | bytes 229376 | tf_op jit(solution)/shard_map/all_to_all | solution.py:636
  111.4 3.4 %collective-permute-start.11 = (f32[4,8,224]{2,1,0:T(8,128)S(1)}, f32[4,8,224]{2,1,0:T(8,128)S(1)}, u32[]{:S(2)}, u32[]{:S(2)}) collective-permute-start(f32[4,8,224]{2,1,0:T(8,128)S(1)} %get-tuple-element.46), channel_id=1, source_target_pairs={{0,1},{1,0},{2,3},{3,2},{4,5},{5,4},{6,7},{7,6},{8,9},{9,8},{10,11... | collective-permute-start | bytes 86024 | tf_op jit(solution)/shard_map/ppermute | solution.py:646
  114.8 0.9 collective-permute-done.11.got_ref
  115.7 0.7 shard_map.136
  (38 shorter events, 0.2 us)
Async XLA Ops:
  4.0 14.5 %copy-start.10 = (bf16[4,2,512]{2,1,0:T(2,128)(2,1)S(1)}, bf16[4,2,512]{2,1,0:T(2,128)(2,1)}, u32[]{:S(2)}) copy-start(bf16[4,2,512]{2,1,0:T(2,128)(2,1)} %param.15) | copy-start | bytes 24580
  4.1 14.6 %copy-start.11 = (bf16[4,2,64]{2,1,0:T(2,128)(2,1)S(1)}, bf16[4,2,64]{2,1,0:T(2,128)(2,1)}, u32[]{:S(2)}) copy-start(bf16[4,2,64]{2,1,0:T(2,128)(2,1)} %param.16) | copy-start | bytes 3076
  4.1 51.5 %all-to-all-start = ((bf16[32,184,128]{2,1,0:T(8,128)(2,1)}), bf16[32,184,128]{2,1,0:T(8,128)(2,1)S(1)}, u32[]{:S(2)}, u32[]{:S(2)}) async-start(bf16[32,184,128]{2,1,0:T(8,128)(2,1)} %shard_map.128), calls=%async_computation | async-start | bytes 3014656 | tf_op jit(solution)/shard_map/all_to_all | solution.py:510
  16.0 14.3 %copy-start.12 = (s32[2,40]{1,0:T(2,128)S(1)}, s32[2,40]{1,0:T(2,128)}, u32[]{:S(2)}) copy-start(s32[2,40]{1,0:T(2,128)} %param.21) | copy-start | bytes 964
  16.0 14.4 %copy-start.13 = (s32[2]{0:T(128)S(1)}, s32[2]{0:T(128)}, u32[]{:S(2)}) copy-start(s32[2]{0:T(128)} %param.22) | copy-start | bytes 28
  16.0 36.9 %collective-permute-start.1 = (bf16[224,2048]{1,0:T(8,128)(2,1)}, bf16[224,2048]{1,0:T(8,128)(2,1)S(1)}, u32[]{:S(2)}, u32[]{:S(2)}) collective-permute-start(bf16[224,2048]{1,0:T(8,128)(2,1)} %bitcast.8.own_hbm), channel_id=1, source_target_pairs={{0,192},{8,200},{16,208},{24,216},{32,224},{40,232},{48,240},{56,2... | collective-permute-start | bytes 2752520 | tf_op jit(solution)/shard_map/ppermute | solution.py:448
  18.5 37.0 %collective-permute-start = (bf16[224,2048]{1,0:T(8,128)(2,1)}, bf16[224,2048]{1,0:T(8,128)(2,1)S(1)}, u32[]{:S(2)}, u32[]{:S(2)}) collective-permute-start(bf16[224,2048]{1,0:T(8,128)(2,1)} %bitcast.8.own_hbm), channel_id=1, source_target_pairs={{0,64},{8,72},{16,80},{24,88},{32,96},{40,104},{48,112},{56,120},{... | collective-permute-start | bytes 2752520 | tf_op jit(solution)/shard_map/ppermute | solution.py:448
  21.4 1.6 %copy-start.5 = (bf16[16,128,512]{2,1,0:T(8,128)(2,1)S(1)}, bf16[16,128,512]{2,1,0:T(8,128)(2,1)}, u32[]{:S(2)}) copy-start(bf16[16,128,512]{2,1,0:T(8,128)(2,1)} %w_ref.2) | copy-start | bytes 6291460
  23.0 0.9 copy-start.6
  25.2 0.7 copy-start.8
  25.9 10.5 %collective-permute-start.4 = (bf16[640,128]{1,0:T(8,128)(2,1)}, bf16[640,128]{1,0:T(8,128)(2,1)}, u32[]{:S(2)}, u32[]{:S(2)}) collective-permute-start(bf16[640,128]{1,0:T(8,128)(2,1)} %get-tuple-element.29), channel_id=1, source_target_pairs={{0,6},{1,7},{2,0},{3,1},{4,2},{5,3},{6,4},{7,5},{8,14},{9,15},{10,... | collective-permute-start | bytes 491528 | tf_op jit(solution)/shard_map/ppermute | solution.py:444
  28.6 8.2 %collective-permute-start.2 = (bf16[640,128]{1,0:T(8,128)(2,1)}, bf16[640,128]{1,0:T(8,128)(2,1)}, u32[]{:S(2)}, u32[]{:S(2)}) collective-permute-start(bf16[640,128]{1,0:T(8,128)(2,1)} %get-tuple-element.29), channel_id=1, source_target_pairs={{0,2},{1,3},{2,4},{3,5},{4,6},{5,7},{6,0},{7,1},{8,10},{9,11},{10,... | collective-permute-start | bytes 491528 | tf_op jit(solution)/shard_map/ppermute | solution.py:444
  28.6 7.8 %collective-permute-start.3 = (bf16[640,128]{1,0:T(8,128)(2,1)S(1)}, bf16[640,128]{1,0:T(8,128)(2,1)}, u32[]{:S(2)}, u32[]{:S(2)}) collective-permute-start(bf16[640,128]{1,0:T(8,128)(2,1)S(1)} %get-tuple-element.33.refs_0_), channel_id=1, source_target_pairs={{0,4},{1,5},{2,6},{3,7},{4,0},{5,1},{6,2},{7,3},{8,12},{9,13},{10,... | collective-permute-start | bytes 491528 | tf_op jit(solution)/shard_map/ppermute | solution.py:444
  52.9 10.7 %copy-start = (bf16[224,2048]{1,0:T(8,128)(2,1)}, bf16[224,2048]{1,0:T(8,128)(2,1)S(1)}, u32[]{:S(2)}) copy-start(bf16[224,2048]{1,0:T(8,128)(2,1)S(1)} %collective-permute-done.1.far_hbm) | copy-start | bytes 2752516
  55.5 8.0 %copy-start.2 = (bf16[224,2048]{1,0:T(8,128)(2,1)}, bf16[224,2048]{1,0:T(8,128)(2,1)S(1)}, u32[]{:S(2)}) copy-start(bf16[224,2048]{1,0:T(8,128)(2,1)S(1)} %collective-permute-done.near_hbm) | copy-start | bytes 2752516
  55.5 1.2 %copy-start.7 = (f32[640,1]{1,0:T(8,128)S(1)}, f32[640,1]{1,0:T(8,128)}, u32[]{:S(2)}) copy-start(f32[640,1]{1,0:T(8,128)} %select_n.16.bias_ref) | copy-start | bytes 7684
  59.8 3.8 %collective-permute-start.5 = (bf16[2,320,640]{2,1,0:T(8,128)(2,1)S(1)}, bf16[2,320,640]{2,1,0:T(8,128)(2,1)S(1)}, u32[]{:S(2)}, u32[]{:S(2)}) collective-permute-start(bf16[2,320,640]{2,1,0:T(8,128)(2,1)S(1)} %shard_map.129.key_ref), channel_id=1, source_target_pairs={{0,1},{1,0},{2,3},{3,2},{4,5},{5,4},{6,7},{7,6},{8,9},{9,8},{10,11... | collective-permute-start | bytes 2457608 | tf_op jit(solution)/shard_map/ppermute | solution.py:572
  63.6 15.3 %copy-start.4 = (bf16[16,512,128]{2,1,0:T(8,128)(2,1)S(1)}, bf16[16,512,128]{2,1,0:T(8,128)(2,1)}, u32[]{:S(2)}) copy-start(bf16[16,512,128]{2,1,0:T(8,128)(2,1)} %w_ref.3) | copy-start | bytes 6291460
  63.6 15.3 %copy-start.9 = (f32[512,128]{1,0:T(8,128)S(1)}, f32[512,128]{1,0:T(8,128)}, u32[]{:S(2)}) copy-start(f32[512,128]{1,0:T(8,128)} %copy-done.8) | copy-start | bytes 786436
  66.0 8.7 %collective-permute-start.6 = (bf16[528,128]{1,0:T(8,128)(2,1)S(1)}, bf16[528,128]{1,0:T(8,128)(2,1)S(1)}, u32[]{:S(2)}, u32[]{:S(2)}) collective-permute-start(bf16[528,128]{1,0:T(8,128)(2,1)S(1)} %get-tuple-element.40), channel_id=1, source_target_pairs={{0,6},{1,7},{2,0},{3,1},{4,2},{5,3},{6,4},{7,5},{8,14},{9,15},{10,... | collective-permute-start | bytes 405512 | tf_op jit(solution)/shard_map/ppermute | solution.py:444
  69.0 6.4 %collective-permute-start.7 = (bf16[528,128]{1,0:T(8,128)(2,1)S(1)}, bf16[528,128]{1,0:T(8,128)(2,1)S(1)}, u32[]{:S(2)}, u32[]{:S(2)}) collective-permute-start(bf16[528,128]{1,0:T(8,128)(2,1)S(1)} %get-tuple-element.41), channel_id=1, source_target_pairs={{0,4},{1,5},{2,6},{3,7},{4,0},{5,1},{6,2},{7,3},{8,12},{9,13},{10,... | collective-permute-start | bytes 405512 | tf_op jit(solution)/shard_map/ppermute | solution.py:444
  69.3 9.6 %collective-permute-start.8 = (bf16[528,128]{1,0:T(8,128)(2,1)S(1)}, bf16[528,128]{1,0:T(8,128)(2,1)S(1)}, u32[]{:S(2)}, u32[]{:S(2)}) collective-permute-start(bf16[528,128]{1,0:T(8,128)(2,1)S(1)} %get-tuple-element.42), channel_id=1, source_target_pairs={{0,2},{1,3},{2,4},{3,5},{4,6},{5,7},{6,0},{7,1},{8,10},{9,11},{10,... | collective-permute-start | bytes 405512 | tf_op jit(solution)/shard_map/ppermute | solution.py:444
  70.0 19.8 %collective-permute-start.9 = (bf16[112,2048]{1,0:T(8,128)(2,1)}, bf16[112,2048]{1,0:T(8,128)(2,1)S(1)}, u32[]{:S(2)}, u32[]{:S(2)}) collective-permute-start(bf16[112,2048]{1,0:T(8,128)(2,1)} %get-tuple-element.43), channel_id=1, source_target_pairs={{0,64},{8,72},{16,80},{24,88},{32,96},{40,104},{48,112},{56,120},{... | collective-permute-start | bytes 1376264 | tf_op jit(solution)/shard_map/ppermute | solution.py:448
  70.0 19.8 %collective-permute-start.10 = (bf16[112,2048]{1,0:T(8,128)(2,1)}, bf16[112,2048]{1,0:T(8,128)(2,1)}, u32[]{:S(2)}, u32[]{:S(2)}) collective-permute-start(bf16[112,2048]{1,0:T(8,128)(2,1)} %get-tuple-element.44), channel_id=1, source_target_pairs={{0,192},{8,200},{16,208},{24,216},{32,224},{40,232},{48,240},{56,2... | collective-permute-start | bytes 1376264 | tf_op jit(solution)/shard_map/ppermute | solution.py:448
  80.4 16.5 %all-to-all-start.1 = ((bf16[8,8,2048]{2,1,0:T(8,128)(2,1)}), bf16[8,8,2048]{2,1,0:T(8,128)(2,1)S(1)}, u32[]{:S(2)}, u32[]{:S(2)}) async-start(bf16[8,8,2048]{2,1,0:T(8,128)(2,1)} %shard_map.132), calls=%async_computation.1 | async-start | bytes 524288 | tf_op jit(solution)/shard_map/all_to_all | solution.py:609
  86.2 1.2 %copy-start.1 = (bf16[224,2048]{1,0:T(8,128)(2,1)S(1)}, bf16[224,2048]{1,0:T(8,128)(2,1)}, u32[]{:S(2)}) copy-start(bf16[224,2048]{1,0:T(8,128)(2,1)} %copy-done) | copy-start | bytes 2752516
  87.4 1.2 %copy-start.3 = (bf16[224,2048]{1,0:T(8,128)(2,1)S(1)}, bf16[224,2048]{1,0:T(8,128)(2,1)}, u32[]{:S(2)}) copy-start(bf16[224,2048]{1,0:T(8,128)(2,1)} %copy-done.2) | copy-start | bytes 2752516
  111.4 4.3 %collective-permute-start.11 = (f32[4,8,224]{2,1,0:T(8,128)S(1)}, f32[4,8,224]{2,1,0:T(8,128)S(1)}, u32[]{:S(2)}, u32[]{:S(2)}) collective-permute-start(f32[4,8,224]{2,1,0:T(8,128)S(1)} %get-tuple-element.46), channel_id=1, source_target_pairs={{0,1},{1,0},{2,3},{3,2},{4,5},{5,4},{6,7},{7,6},{8,9},{9,8},{10,11... | collective-permute-start | bytes 86024 | tf_op jit(solution)/shard_map/ppermute | solution.py:646

commit v9 on v8

--- a/solution.py
+++ b/solution.py
@@ -306,21 +306,12 @@
     return jnp.concatenate(tiles, axis=1)
 
 
-def own_kernel(scale, key_ref, near_hbm, far_hbm, *refs):
-    q_refs, (part_ref, stat_ref, half_a, half_b, sem_ref) = refs[:-5], refs[-5:]
-    size = half_a.shape[0]
-    copies = [
-        pltpu.make_async_copy(near_hbm.at[pl.ds(0, size)], half_a, sem_ref.at[0]),
-        pltpu.make_async_copy(far_hbm.at[pl.ds(size, size)], half_b, sem_ref.at[1]),
-    ]
-    for copy in copies:
-        copy.start()
+def own_kernel(scale, key_ref, *refs):
+    q_refs, (part_ref, stat_ref) = refs[:-2], refs[-2:]
     for b in range(key_ref.shape[0]):
         high, total, part = attend(scale, key_ref[b], ask(q_refs, b), part_ref.shape[1])
         part_ref[b] = part
         stat_ref[b] = jnp.where(iota(stat_ref.shape[1:], 0) == 0, high, total)
-    for copy in copies:
-        copy.wait()
 
 
 def both_kernel(scale, key_ref, own_ref, stat_ref, *refs):
@@ -571,23 +562,18 @@
     )
     other = lax.ppermute(key, "head", [(h, h ^ 1) for h in range(n_head)])
     asked = NX * queries // rows_dev
-    half_w = jax.ShapeDtypeStruct((w_t.shape[0] // 2, w_t.shape[1]), bf16)
-    own_part, own_stat, half_a, half_b = call(
+    own_part, own_stat = call(
         functools.partial(own_kernel, scale),
         (
             jax.ShapeDtypeStruct((rows_dev, lat_w, asked), f32),
             jax.ShapeDtypeStruct((rows_dev, 8, asked), f32),
-            half_w,
-            half_w,
         ),
-        [key, w_near, w_far] + all_queries,
-        scratch=[pltpu.SemaphoreType.DMA((2,))],
+        [key] + all_queries,
         flops=2 * tokens * asked * (2 * lat_w + TAIL),
         nbytes=2 * tokens * lat_w,
-        out_spec=(VMEM, VMEM, HBM, HBM),
-        in_hbm=(1, 2),
-    )
-    opposite = [shift_x(half_a, 1), shift_x(half_b, -1)]
+    )
+    size = w_t.shape[0] // 2
+    opposite = [shift_x(w_near[:size], 1), shift_x(w_far[size:], -1)]
     parts = call(
         functools.partial(both_kernel, scale),
         tuple(jax.ShapeDtypeStruct((lat_w + INFO, queries), bf16) for _ in range(NX)),

time: 117 us -> 114 us (0.974)
  local copies, waits for them, and re-layouts: 11.3 us -> 6.53 us
  waiting for transfers between devices: 36.8 us -> 40.2 us
  Pallas kernels: 18.5 us -> 17.3 us
    ppermute x4, waiting for transfers between devices: 18.7 us -> 22.7 us  [shift_x(): lax.ppermute(x, 'row', [(a * NZ + b, (a + k) % NX * NZ + b) for a in rang...]
    unnamed x29 -> x27, local copies, waits for them, and re-layouts: 6.86 us -> 3.22 us
    slice x0 -> x2, local copies, waits for them, and re-layouts: none -> 2.66 us  [on_device(): opposite = [shift_x(w_near[:size], 1), shift_x(w_far[size:], -1)]]
    select_n x1, local copies, waits for them, and re-layouts: 1.76 us -> 0.13 us  [on_device(): jnp.where(usable, 0.0, NEG).astype(f32)]
    pallas_call x10, Pallas kernels: 18.5 us -> 17.3 us  [call(): pl.pallas_call(body, out_shape=out_shape, in_specs=[HBM if i in in_hbm el...]
  transfers between devices with their start and end apart: 14 -> 14, of which waited for: 9 -> 7; matrix products, arithmetic and copies ran while one was open for 5% -> 3% of each run, Pallas kernels for 5% -> 5%
where the time goes in v9:
time: 114 us
  waiting for transfers between devices  40.2 us (35%)
  starting transfers between devices  37 us (32%)
  Pallas kernels  17.3 us (15%)
  blocking collectives  12.4 us (11%)
  local copies, waits for them, and re-layouts  6.53 us (6%)
    ppermute x4, waiting for transfers between devices, shift_x(): lax.ppermute(x, 'row', [(a * NZ + b, (a + k) % NX * NZ + b) for a in rang...  22.7 us
    pallas_call x10, Pallas kernels, call(): pl.pallas_call(body, out_shape=out_shape, in_specs=[HBM if i in in_hbm el...  17.3 us
    all_to_all x1, blocking collectives, on_device(): lax.all_to_all(sums, ('row', 'head'), split_axis=0, concat_axis=0, axis_i...  12.4 us
    all_to_all x1, starting transfers between devices, on_device(): got = lax.all_to_all(send, 'row', split_axis=0, concat_axis=0, tiled=True)  12.1 us
    ppermute x6, waiting for transfers between devices, shift_y(): lax.ppermute(x, 'head', [(h, (h + k * cores) % n_head) for h in range(n_h...  9.19 us
    ppermute x6, starting transfers between devices, shift_y(): lax.ppermute(x, 'head', [(h, (h + k * cores) % n_head) for h in range(n_h...  8.23 us
    all_to_all x1, waiting for transfers between devices, on_device(): lax.all_to_all(head_out, 'row', split_axis=0, concat_axis=0, axis_index_g...  6.68 us
    all_to_all x1, starting transfers between devices, on_device(): lax.all_to_all(head_out, 'row', split_axis=0, concat_axis=0, axis_index_g...  6.39 us
  transfers between devices with their start and end apart: 14, of which 7 were waited for; matrix products, arithmetic and copies ran while one was open for 3% of the time, Pallas kernels for 5%

profile of v9, /device:TPU:1, one launch (start us, length us, event | category | flops | bytes accessed | tf_op | source)
XLA Modules:
  0.0 113.9 jit_solution(642548988068751349)
XLA Ops:
  0.0 4.0 %shard_map.128 = bf16[32,184,128]{2,1,0:T(8,128)(2,1)} custom-call(s32[1,80]{1,0:T(1,128)} %bitcast.22, s32[1,80]{1,0:T(1,128)} %bitcast.23, bf16[80,64,512]{2,1,0:T(8,128)(2,1)} %lat_hbm.1, bf16[80,4096]{1,0:T(8,128)(2,1)} %rope_hbm.1), custom_call_target="tpu_custom_call" | custom-call | flops 838860800 | bytes 2621440 | tf_op jit(solution)/shard_map/pallas_call | solution.py:26
  4.1 0.0 copy-start.7
  4.1 0.0 copy-start.8
  4.1 12.1 %all-to-all-start = ((bf16[32,184,128]{2,1,0:T(8,128)(2,1)}), bf16[32,184,128]{2,1,0:T(8,128)(2,1)}, u32[]{:S(2)}, u32[]{:S(2)}) async-start(bf16[32,184,128]{2,1,0:T(8,128)(2,1)} %shard_map.128), calls=%async_computation | async-start | bytes 3014656 | tf_op jit(solution)/shard_map/all_to_all | solution.py:501
  16.2 0.0 copy-start.11
  16.3 1.2 %collective-permute-start = (bf16[224,2048]{1,0:T(8,128)(2,1)}, bf16[224,2048]{1,0:T(8,128)(2,1)S(1)}, u32[]{:S(2)}, u32[]{:S(2)}) collective-permute-start(bf16[224,2048]{1,0:T(8,128)(2,1)} %bitcast.15), channel_id=1, source_target_pairs={{0,64},{8,72},{16,80},{24,88},{32,96},{40,104},{48,112},{56,120},{... | collective-permute-start | bytes 2752520 | tf_op jit(solution)/shard_map/ppermute | solution.py:439
  17.5 1.5 %collective-permute-start.1 = (bf16[224,2048]{1,0:T(8,128)(2,1)}, bf16[224,2048]{1,0:T(8,128)(2,1)}, u32[]{:S(2)}, u32[]{:S(2)}) collective-permute-start(bf16[224,2048]{1,0:T(8,128)(2,1)} %bitcast.16), channel_id=1, source_target_pairs={{0,192},{8,200},{16,208},{24,216},{32,224},{40,232},{48,240},{56,2... | collective-permute-start | bytes 2752520 | tf_op jit(solution)/shard_map/ppermute | solution.py:439
  19.0 0.1 pad.3.clone
  19.1 0.2 copy.32
  19.4 0.1 copy.35
  19.5 0.1 reshape.88
  19.6 0.1 pad.5.clone
  19.7 1.3 %shard_map.127 = (bf16[640,128]{1,0:T(8,128)(2,1)S(1)}, bf16[640,128]{1,0:T(8,128)(2,1)}, f32[512,128]{1,0:T(8,128)S(1)}, f32[8,128]{1,0:T(8,128)S(1)}) custom-call(bf16[16,8,128]{2,1,0:T(8,128)(2,1)S(1)} %bitcast.18, bf16[128,128]{1,0:T(8,128)(2,1)S(1)} %pad_maximum_fusion.qtail_ref, bf16[16,128,512]{2,1,0:T(8,128)(2,1)S(1)} %copy-done.1, ...), custom_call_target="tpu_custom_call" | custom-call | flops 16777216 | bytes 2097152 | tf_op jit(solution)/shard_map/pallas_call | solution.py:26
  21.1 0.7 copy-done.5
  21.8 1.3 %collective-permute-start.2 = (bf16[640,128]{1,0:T(8,128)(2,1)}, bf16[640,128]{1,0:T(8,128)(2,1)S(1)}, u32[]{:S(2)}, u32[]{:S(2)}) collective-permute-start(bf16[640,128]{1,0:T(8,128)(2,1)} %get-tuple-element.27), channel_id=1, source_target_pairs={{0,2},{1,3},{2,4},{3,5},{4,6},{5,7},{6,0},{7,1},{8,10},{9,11},{10,... | collective-permute-start | bytes 491528 | tf_op jit(solution)/shard_map/ppermute | solution.py:435
  23.1 1.4 %collective-permute-start.4 = (bf16[640,128]{1,0:T(8,128)(2,1)}, bf16[640,128]{1,0:T(8,128)(2,1)S(1)}, u32[]{:S(2)}, u32[]{:S(2)}) collective-permute-start(bf16[640,128]{1,0:T(8,128)(2,1)} %get-tuple-element.27), channel_id=1, source_target_pairs={{0,6},{1,7},{2,0},{3,1},{4,2},{5,3},{6,4},{7,5},{8,14},{9,15},{10,... | collective-permute-start | bytes 491528 | tf_op jit(solution)/shard_map/ppermute | solution.py:435
  24.5 1.6 %collective-permute-start.3 = (bf16[640,128]{1,0:T(8,128)(2,1)S(1)}, bf16[640,128]{1,0:T(8,128)(2,1)S(1)}, u32[]{:S(2)}, u32[]{:S(2)}) collective-permute-start(bf16[640,128]{1,0:T(8,128)(2,1)S(1)} %get-tuple-element.29.refs_0_), channel_id=1, source_target_pairs={{0,4},{1,5},{2,6},{3,7},{4,0},{5,1},{6,2},{7,3},{8,12},{9,13},{10,... | collective-permute-start | bytes 491528 | tf_op jit(solution)/shard_map/ppermute | solution.py:435
  26.2 0.1 select_reduce_fusion
  26.3 0.1 subtract_subtract_fusion
  26.4 0.1 compare_select_fusion
  26.4 0.1 select_n.16.bias_ref
  26.6 1.3 %collective-permute-done.2.refs_1_ = bf16[640,128]{1,0:T(8,128)(2,1)S(1)} collective-permute-done((bf16[640,128]{1,0:T(8,128)(2,1)}, bf16[640,128]{1,0:T(8,128)(2,1)S(1)}, u32[]{:S(2)}, u32[]{:S(2)}) %collective-permute-start.2) | collective-permute-done | bytes 163872 | tf_op jit(solution)/shard_map/ppermute | solution.py:435
  27.8 4.4 %collective-permute-done.3.refs_2_ = bf16[640,128]{1,0:T(8,128)(2,1)S(1)} collective-permute-done((bf16[640,128]{1,0:T(8,128)(2,1)S(1)}, bf16[640,128]{1,0:T(8,128)(2,1)S(1)}, u32[]{:S(2)}, u32[]{:S(2)}) %collective-permute-start.3) | collective-permute-done | bytes 163872 | tf_op jit(solution)/shard_map/ppermute | solution.py:435
  32.2 22.7 %collective-permute-done.near_hbm = bf16[224,2048]{1,0:T(8,128)(2,1)S(1)} collective-permute-done((bf16[224,2048]{1,0:T(8,128)(2,1)}, bf16[224,2048]{1,0:T(8,128)(2,1)S(1)}, u32[]{:S(2)}, u32[]{:S(2)}) %collective-permute-start) | collective-permute-done | bytes 917536 | tf_op jit(solution)/shard_map/ppermute | solution.py:439
  54.9 3.6 %shard_map.129.key_ref = bf16[2,320,640]{2,1,0:T(8,128)(2,1)S(1)} custom-call(bf16[32,184,128]{2,1,0:T(8,128)(2,1)} %all-to-all-done.block_hbm, f32[640,1]{1,0:T(8,128)S(1)} %select_n.16.bias_ref), custom_call_target="tpu_custom_call" | custom-call | flops 838860800 | bytes 1310720 | tf_op jit(solution)/shard_map/pallas_call | solution.py:26
  58.6 1.5 %collective-permute-start.5 = (bf16[2,320,640]{2,1,0:T(8,128)(2,1)S(1)}, bf16[2,320,640]{2,1,0:T(8,128)(2,1)S(1)}, u32[]{:S(2)}, u32[]{:S(2)}) collective-permute-start(bf16[2,320,640]{2,1,0:T(8,128)(2,1)S(1)} %shard_map.129.key_ref), channel_id=1, source_target_pairs={{0,1},{1,0},{2,3},{3,2},{4,5},{5,4},{6,7},{7,6},{8,9},{9,8},{10,11... | collective-permute-start | bytes 2457608 | tf_op jit(solution)/shard_map/ppermute | solution.py:563
  60.0 1.1 %shard_map.130 = (f32[2,512,256]{2,1,0:T(8,128)S(1)}, f32[2,8,256]{2,1,0:T(8,128)S(1)}) custom-call(bf16[2,320,640]{2,1,0:T(8,128)(2,1)S(1)} %shard_map.129.key_ref, bf16[640,128]{1,0:T(8,128)(2,1)S(1)} %get-tuple-element.29.refs_0_, bf16[640,128]{1,0:T(8,128)(2,1)S(1)} %collective-permute-done.2.refs_1_, ...), custom_call_target="tpu_custom_call" | custom-call | flops 377487360 | bytes 655360 | tf_op jit(solution)/shard_map/pallas_call | solution.py:26
  61.2 0.8 collective-permute-done.5.key_ref
  62.0 1.2 %shard_map.131 = (bf16[528,128]{1,0:T(8,128)(2,1)S(1)}, bf16[528,128]{1,0:T(8,128)(2,1)S(1)}, bf16[528,128]{1,0:T(8,128)(2,1)S(1)}, bf16[528,128]{1,0:T(8,128)(2,1)S(1)}) custom-call(bf16[2,320,640]{2,1,0:T(8,128)(2,1)S(1)} %collective-permute-done.5.key_ref, f32[2,512,256]{2,1,0:T(8,128)S(1)} %get-tuple-element.33.own_ref, ...), custom_call_target="tpu_custom_call" | custom-call | flops 377487360 | bytes 655360 | tf_op jit(solution)/shard_map/pallas_call | solution.py:26
  63.2 2.8 %collective-permute-start.6 = (bf16[528,128]{1,0:T(8,128)(2,1)S(1)}, bf16[528,128]{1,0:T(8,128)(2,1)S(1)}, u32[]{:S(2)}, u32[]{:S(2)}) collective-permute-start(bf16[528,128]{1,0:T(8,128)(2,1)S(1)} %get-tuple-element.36), channel_id=1, source_target_pairs={{0,6},{1,7},{2,0},{3,1},{4,2},{5,3},{6,4},{7,5},{8,14},{9,15},{10,... | collective-permute-start | bytes 405512 | tf_op jit(solution)/shard_map/ppermute | solution.py:435
  66.0 0.5 collective-permute-start.7
  66.4 0.6 collective-permute-start.8
  67.0 0.8 slice.10
  67.8 0.2 collective-permute-start.9
  68.1 1.8 %slice.11 = bf16[112,2048]{1,0:T(8,128)(2,1)} slice(bf16[224,2048]{1,0:T(8,128)(2,1)} %collective-permute-done.1.far_hbm), slice={[112:224], [0:2048]} | slice | bytes 917504 | tf_op jit(solution)/shard_map/slice | solution.py:576
  69.9 2.5 %collective-permute-start.10 = (bf16[112,2048]{1,0:T(8,128)(2,1)}, bf16[112,2048]{1,0:T(8,128)(2,1)}, u32[]{:S(2)}, u32[]{:S(2)}) collective-permute-start(bf16[112,2048]{1,0:T(8,128)(2,1)} %slice.11), channel_id=1, source_target_pairs={{0,192},{8,200},{16,208},{24,216},{32,224},{40,232},{48,240},{56,2... | collective-permute-start | bytes 1376264 | tf_op jit(solution)/shard_map/ppermute | solution.py:439
  72.4 3.5 %collective-permute-done.8.refs_3_ = bf16[528,128]{1,0:T(8,128)(2,1)S(1)} collective-permute-done((bf16[528,128]{1,0:T(8,128)(2,1)S(1)}, bf16[528,128]{1,0:T(8,128)(2,1)S(1)}, u32[]{:S(2)}, u32[]{:S(2)}) %collective-permute-start.8) | collective-permute-done | bytes 135200 | tf_op jit(solution)/shard_map/ppermute | solution.py:435
  75.9 1.5 %shard_map.132 = bf16[8,8,2048]{2,1,0:T(8,128)(2,1)} custom-call(f32[512,128]{1,0:T(8,128)S(1)} %copy-done.6, f32[8,128]{1,0:T(8,128)S(1)} %get-tuple-element.25.fresh_lse_ref, bf16[16,512,128]{2,1,0:T(8,128)(2,1)S(1)} %copy-done, bf16[528,128]{1,0:T(8,128)(2,1)S(1)} %get-tuple-element.35.refs_0_, bf16[528,128]{1,0:T(8,128)(2,1)S(1)} %collective-permute-done.6.refs_1_, ...), custom_call_target="tpu_custom_call" | custom-call | flops 16777216 | bytes 2097152 | tf_op jit(solution)/shard_map/pallas_call | solution.py:26
  77.4 6.4 %all-to-all-start.1 = ((bf16[8,8,2048]{2,1,0:T(8,128)(2,1)}), bf16[8,8,2048]{2,1,0:T(8,128)(2,1)S(1)}, u32[]{:S(2)}, u32[]{:S(2)}) async-start(bf16[8,8,2048]{2,1,0:T(8,128)(2,1)} %shard_map.132), calls=%async_computation.1 | async-start | bytes 524288 | tf_op jit(solution)/shard_map/all_to_all | solution.py:595
  83.8 1.2 %copy-done.3 = bf16[224,2048]{1,0:T(8,128)(2,1)S(1)} copy-done((bf16[224,2048]{1,0:T(8,128)(2,1)S(1)}, bf16[224,2048]{1,0:T(8,128)(2,1)}, u32[]{:S(2)}) %copy-start.3) | copy-done | bytes 917528
  85.0 1.2 %copy-done.4 = bf16[2048,224]{0,1:T(8,128)(2,1)S(1)} copy-done((bf16[2048,224]{0,1:T(8,128)(2,1)S(1)}, bf16[2048,224]{0,1:T(8,128)(2,1)}, u32[]{:S(2)}) %copy-start.4) | copy-done | bytes 917528
  86.2 1.6 %shard_map.133.w_ref = bf16[3,224,2048]{2,1,0:T(8,128)(2,1)S(1)} custom-call(bf16[224,2048]{1,0:T(8,128)(2,1)S(1)} %bitcast.17, bf16[224,2048]{1,0:T(8,128)(2,1)S(1)} %copy-done.3, bf16[224,2048]{1,0:T(8,128)(2,1)} %collective-permute-done.1.far_hbm), custom_call_target="tpu_custom_call" | custom-call | bytes 5505024 | tf_op jit(solution)/shard_map/pallas_call | solution.py:26
  87.9 6.7 %all-to-all-done.1 = bf16[8,8,2048]{2,1,0:T(8,128)(2,1)S(1)} async-done(((bf16[8,8,2048]{2,1,0:T(8,128)(2,1)}), bf16[8,8,2048]{2,1,0:T(8,128)(2,1)S(1)}, u32[]{:S(2)}, u32[]{:S(2)}) %all-to-all-start.1) | async-done | bytes 262176 | tf_op jit(solution)/shard_map/all_to_all | solution.py:595
  94.5 2.1 %shard_map.134 = bf16[32,8,224]{2,1,0:T(8,128)(2,1)S(1)} custom-call(bf16[64,2048]{1,0:T(8,128)(2,1)S(1)} %bitcast.14, bf16[3,224,2048]{2,1,0:T(8,128)(2,1)S(1)} %shard_map.133.w_ref, bf16[112,2048]{1,0:T(8,128)(2,1)S(1)} %collective-permute-done.9.opp_a_hbm, bf16[112,2048]{1,0:T(8,128)(2,1)} %collective-permute-done.10.opp_b_hbm), custom_call_target="tpu_custom_call" | custom-call | flops 234881024 | bytes 3670016 | tf_op jit(solution)/shard_map/pallas_call | solution.py:26
  96.6 12.4 %all_to_all.15.in_ref = bf16[32,8,224]{2,1,0:T(8,128)(2,1)S(1)} all-to-all(bf16[32,8,224]{2,1,0:T(8,128)(2,1)S(1)} %shard_map.134), channel_id=1, replica_groups={{0,2,4,6,8,10,12,14,16,18,20,22,24,26,28,30,32,34,36,38,40,42,44,46,48,..., dimensions={0} | all-to-all | bytes 229376 | tf_op jit(solution)/shard_map/all_to_all | solution.py:622
  109.0 3.4 %collective-permute-start.11 = (f32[4,8,224]{2,1,0:T(8,128)S(1)}, f32[4,8,224]{2,1,0:T(8,128)S(1)}, u32[]{:S(2)}, u32[]{:S(2)}) collective-permute-start(f32[4,8,224]{2,1,0:T(8,128)S(1)} %get-tuple-element.42), channel_id=1, source_target_pairs={{0,1},{1,0},{2,3},{3,2},{4,5},{5,4},{6,7},{7,6},{8,9},{9,8},{10,11... | collective-permute-start | bytes 86024 | tf_op jit(solution)/shard_map/ppermute | solution.py:632
  112.4 0.9 collective-permute-done.11.got_ref
  113.2 0.7 shard_map.136
  (38 shorter events, 0.2 us)
Async XLA Ops:
  4.0 15.0 %copy-start.9 = (bf16[4,2,512]{2,1,0:T(2,128)(2,1)S(1)}, bf16[4,2,512]{2,1,0:T(2,128)(2,1)}, u32[]{:S(2)}) copy-start(bf16[4,2,512]{2,1,0:T(2,128)(2,1)} %param.15) | copy-start | bytes 24580
  4.1 15.1 %copy-start.10 = (bf16[4,2,64]{2,1,0:T(2,128)(2,1)S(1)}, bf16[4,2,64]{2,1,0:T(2,128)(2,1)}, u32[]{:S(2)}) copy-start(bf16[4,2,64]{2,1,0:T(2,128)(2,1)} %param.16) | copy-start | bytes 3076
  4.1 15.4 %copy-start.7 = (bf16[4,2,16,128]{3,2,1,0:T(8,128)(2,1)S(1)}, bf16[4,2,16,128]{3,2,1,0:T(8,128)(2,1)}, u32[]{:S(2)}) copy-start(bf16[4,2,16,128]{3,2,1,0:T(8,128)(2,1)} %param.13) | copy-start | bytes 98308
  4.1 15.4 %copy-start.8 = (bf16[4,2,1024]{2,1,0:T(2,128)(2,1)S(1)}, bf16[4,2,1024]{2,1,0:T(2,128)(2,1)}, u32[]{:S(2)}) copy-start(bf16[4,2,1024]{2,1,0:T(2,128)(2,1)} %param.14) | copy-start | bytes 49156
  4.1 15.6 %copy-start.1 = (bf16[16,128,512]{2,1,0:T(8,128)(2,1)S(1)}, bf16[16,128,512]{2,1,0:T(8,128)(2,1)}, u32[]{:S(2)}) copy-start(bf16[16,128,512]{2,1,0:T(8,128)(2,1)} %w_ref.2) | copy-start | bytes 6291460
  4.1 50.8 %all-to-all-start = ((bf16[32,184,128]{2,1,0:T(8,128)(2,1)}), bf16[32,184,128]{2,1,0:T(8,128)(2,1)}, u32[]{:S(2)}, u32[]{:S(2)}) async-start(bf16[32,184,128]{2,1,0:T(8,128)(2,1)} %shard_map.128), calls=%async_computation | async-start | bytes 3014656 | tf_op jit(solution)/shard_map/all_to_all | solution.py:501
  16.2 9.9 %copy-start.11 = (s32[2,40]{1,0:T(2,128)S(1)}, s32[2,40]{1,0:T(2,128)}, u32[]{:S(2)}) copy-start(s32[2,40]{1,0:T(2,128)} %param.21) | copy-start | bytes 964
  16.2 10.0 %copy-start.12 = (s32[2]{0:T(128)S(1)}, s32[2]{0:T(128)}, u32[]{:S(2)}) copy-start(s32[2]{0:T(128)} %param.22) | copy-start | bytes 28
  16.3 38.7 %collective-permute-start = (bf16[224,2048]{1,0:T(8,128)(2,1)}, bf16[224,2048]{1,0:T(8,128)(2,1)S(1)}, u32[]{:S(2)}, u32[]{:S(2)}) collective-permute-start(bf16[224,2048]{1,0:T(8,128)(2,1)} %bitcast.15), channel_id=1, source_target_pairs={{0,64},{8,72},{16,80},{24,88},{32,96},{40,104},{48,112},{56,120},{... | collective-permute-start | bytes 2752520 | tf_op jit(solution)/shard_map/ppermute | solution.py:439
  17.5 37.4 %collective-permute-start.1 = (bf16[224,2048]{1,0:T(8,128)(2,1)}, bf16[224,2048]{1,0:T(8,128)(2,1)}, u32[]{:S(2)}, u32[]{:S(2)}) collective-permute-start(bf16[224,2048]{1,0:T(8,128)(2,1)} %bitcast.16), channel_id=1, source_target_pairs={{0,192},{8,200},{16,208},{24,216},{32,224},{40,232},{48,240},{56,2... | collective-permute-start | bytes 2752520 | tf_op jit(solution)/shard_map/ppermute | solution.py:439
  21.1 0.7 copy-start.5
  21.8 6.1 %collective-permute-start.2 = (bf16[640,128]{1,0:T(8,128)(2,1)}, bf16[640,128]{1,0:T(8,128)(2,1)S(1)}, u32[]{:S(2)}, u32[]{:S(2)}) collective-permute-start(bf16[640,128]{1,0:T(8,128)(2,1)} %get-tuple-element.27), channel_id=1, source_target_pairs={{0,2},{1,3},{2,4},{3,5},{4,6},{5,7},{6,0},{7,1},{8,10},{9,11},{10,... | collective-permute-start | bytes 491528 | tf_op jit(solution)/shard_map/ppermute | solution.py:435
  23.1 9.2 %collective-permute-start.4 = (bf16[640,128]{1,0:T(8,128)(2,1)}, bf16[640,128]{1,0:T(8,128)(2,1)S(1)}, u32[]{:S(2)}, u32[]{:S(2)}) collective-permute-start(bf16[640,128]{1,0:T(8,128)(2,1)} %get-tuple-element.27), channel_id=1, source_target_pairs={{0,6},{1,7},{2,0},{3,1},{4,2},{5,3},{6,4},{7,5},{8,14},{9,15},{10,... | collective-permute-start | bytes 491528 | tf_op jit(solution)/shard_map/ppermute | solution.py:435
  24.5 7.7 %collective-permute-start.3 = (bf16[640,128]{1,0:T(8,128)(2,1)S(1)}, bf16[640,128]{1,0:T(8,128)(2,1)S(1)}, u32[]{:S(2)}, u32[]{:S(2)}) collective-permute-start(bf16[640,128]{1,0:T(8,128)(2,1)S(1)} %get-tuple-element.29.refs_0_), channel_id=1, source_target_pairs={{0,4},{1,5},{2,6},{3,7},{4,0},{5,1},{6,2},{7,3},{8,12},{9,13},{10,... | collective-permute-start | bytes 491528 | tf_op jit(solution)/shard_map/ppermute | solution.py:435
  54.9 12.1 %copy-start.2 = (bf16[224,2048]{1,0:T(8,128)(2,1)}, bf16[224,2048]{1,0:T(8,128)(2,1)S(1)}, u32[]{:S(2)}) copy-start(bf16[224,2048]{1,0:T(8,128)(2,1)S(1)} %collective-permute-done.near_hbm) | copy-start | bytes 2752516
  58.6 3.4 %collective-permute-start.5 = (bf16[2,320,640]{2,1,0:T(8,128)(2,1)S(1)}, bf16[2,320,640]{2,1,0:T(8,128)(2,1)S(1)}, u32[]{:S(2)}, u32[]{:S(2)}) collective-permute-start(bf16[2,320,640]{2,1,0:T(8,128)(2,1)S(1)} %shard_map.129.key_ref), channel_id=1, source_target_pairs={{0,1},{1,0},{2,3},{3,2},{4,5},{5,4},{6,7},{7,6},{8,9},{9,8},{10,11... | collective-permute-start | bytes 2457608 | tf_op jit(solution)/shard_map/ppermute | solution.py:563
  62.0 13.9 %copy-start = (bf16[16,512,128]{2,1,0:T(8,128)(2,1)S(1)}, bf16[16,512,128]{2,1,0:T(8,128)(2,1)}, u32[]{:S(2)}) copy-start(bf16[16,512,128]{2,1,0:T(8,128)(2,1)} %w_ref.3) | copy-start | bytes 6291460
  62.0 13.9 %copy-start.6 = (f32[512,128]{1,0:T(8,128)S(1)}, f32[512,128]{1,0:T(8,128)}, u32[]{:S(2)}) copy-start(f32[512,128]{1,0:T(8,128)} %copy-done.5) | copy-start | bytes 786436
  63.2 9.2 %collective-permute-start.6 = (bf16[528,128]{1,0:T(8,128)(2,1)S(1)}, bf16[528,128]{1,0:T(8,128)(2,1)S(1)}, u32[]{:S(2)}, u32[]{:S(2)}) collective-permute-start(bf16[528,128]{1,0:T(8,128)(2,1)S(1)} %get-tuple-element.36), channel_id=1, source_target_pairs={{0,6},{1,7},{2,0},{3,1},{4,2},{5,3},{6,4},{7,5},{8,14},{9,15},{10,... | collective-permute-start | bytes 405512 | tf_op jit(solution)/shard_map/ppermute | solution.py:435
  66.0 6.4 %collective-permute-start.7 = (bf16[528,128]{1,0:T(8,128)(2,1)S(1)}, bf16[528,128]{1,0:T(8,128)(2,1)S(1)}, u32[]{:S(2)}, u32[]{:S(2)}) collective-permute-start(bf16[528,128]{1,0:T(8,128)(2,1)S(1)} %get-tuple-element.37), channel_id=1, source_target_pairs={{0,4},{1,5},{2,6},{3,7},{4,0},{5,1},{6,2},{7,3},{8,12},{9,13},{10,... | collective-permute-start | bytes 405512 | tf_op jit(solution)/shard_map/ppermute | solution.py:435
  66.4 9.4 %collective-permute-start.8 = (bf16[528,128]{1,0:T(8,128)(2,1)S(1)}, bf16[528,128]{1,0:T(8,128)(2,1)S(1)}, u32[]{:S(2)}, u32[]{:S(2)}) collective-permute-start(bf16[528,128]{1,0:T(8,128)(2,1)S(1)} %get-tuple-element.38), channel_id=1, source_target_pairs={{0,2},{1,3},{2,4},{3,5},{4,6},{5,7},{6,0},{7,1},{8,10},{9,11},{10,... | collective-permute-start | bytes 405512 | tf_op jit(solution)/shard_map/ppermute | solution.py:435
  67.8 20.0 %collective-permute-start.9 = (bf16[112,2048]{1,0:T(8,128)(2,1)}, bf16[112,2048]{1,0:T(8,128)(2,1)S(1)}, u32[]{:S(2)}, u32[]{:S(2)}) collective-permute-start(bf16[112,2048]{1,0:T(8,128)(2,1)} %slice.10), channel_id=1, source_target_pairs={{0,64},{8,72},{16,80},{24,88},{32,96},{40,104},{48,112},{56,120},{... | collective-permute-start | bytes 1376264 | tf_op jit(solution)/shard_map/ppermute | solution.py:439
  69.9 17.9 %collective-permute-start.10 = (bf16[112,2048]{1,0:T(8,128)(2,1)}, bf16[112,2048]{1,0:T(8,128)(2,1)}, u32[]{:S(2)}, u32[]{:S(2)}) collective-permute-start(bf16[112,2048]{1,0:T(8,128)(2,1)} %slice.11), channel_id=1, source_target_pairs={{0,192},{8,200},{16,208},{24,216},{32,224},{40,232},{48,240},{56,2... | collective-permute-start | bytes 1376264 | tf_op jit(solution)/shard_map/ppermute | solution.py:439
  77.4 17.1 %all-to-all-start.1 = ((bf16[8,8,2048]{2,1,0:T(8,128)(2,1)}), bf16[8,8,2048]{2,1,0:T(8,128)(2,1)S(1)}, u32[]{:S(2)}, u32[]{:S(2)}) async-start(bf16[8,8,2048]{2,1,0:T(8,128)(2,1)} %shard_map.132), calls=%async_computation.1 | async-start | bytes 524288 | tf_op jit(solution)/shard_map/all_to_all | solution.py:595
  83.8 1.2 %copy-start.3 = (bf16[224,2048]{1,0:T(8,128)(2,1)S(1)}, bf16[224,2048]{1,0:T(8,128)(2,1)}, u32[]{:S(2)}) copy-start(bf16[224,2048]{1,0:T(8,128)(2,1)} %copy-done.2) | copy-start | bytes 2752516
  85.0 1.2 %copy-start.4 = (bf16[2048,224]{0,1:T(8,128)(2,1)S(1)}, bf16[2048,224]{0,1:T(8,128)(2,1)}, u32[]{:S(2)}) copy-start(bf16[2048,224]{0,1:T(8,128)(2,1)} %param.25) | copy-start | bytes 2752516
  109.0 4.2 %collective-permute-start.11 = (f32[4,8,224]{2,1,0:T(8,128)S(1)}, f32[4,8,224]{2,1,0:T(8,128)S(1)}, u32[]{:S(2)}, u32[]{:S(2)}) collective-permute-start(f32[4,8,224]{2,1,0:T(8,128)S(1)} %get-tuple-element.42), channel_id=1, source_target_pairs={{0,1},{1,0},{2,3},{3,2},{4,5},{5,4},{6,7},{7,6},{8,9},{9,8},{10,11... | collective-permute-start | bytes 86024 | tf_op jit(solution)/shard_map/ppermute | solution.py:632

commit v10 on v9

--- a/solution.py
+++ b/solution.py
@@ -376,10 +376,10 @@
             out_ref[copy, :, head * value_w : (head + 1) * value_w] = value
 
 
-def stage_kernel(own_hbm, near_hbm, far_hbm, out_ref, sem_ref):
+def stage_kernel(own_hbm, near_hbm, out_ref, sem_ref):
     copies = [
-        pltpu.make_async_copy(ref, out_ref.at[i], sem_ref.at[i])
-        for i, ref in enumerate((own_hbm, near_hbm, far_hbm))
+        pltpu.make_async_copy(own_hbm, out_ref.at[0], sem_ref.at[0]),
+        pltpu.make_async_copy(near_hbm, out_ref.at[1], sem_ref.at[1]),
     ]
     for copy in copies:
         copy.start()
@@ -387,11 +387,10 @@
         copy.wait()
 
 
-def project_kernel(width, x_ref, w_ref, opp_a_hbm, opp_b_hbm, out_ref, opp_ref, sem_ref):
-    size = opp_a_hbm.shape[0]
+def project_kernel(width, x_ref, w_ref, far_hbm, opposite_hbm, out_ref, late_ref, sem_ref):
     copies = [
-        pltpu.make_async_copy(opp_a_hbm, opp_ref.at[pl.ds(0, size)], sem_ref.at[0]),
-        pltpu.make_async_copy(opp_b_hbm, opp_ref.at[pl.ds(size, size)], sem_ref.at[1]),
+        pltpu.make_async_copy(far_hbm, late_ref.at[0], sem_ref.at[0]),
+        pltpu.make_async_copy(opposite_hbm, late_ref.at[1], sem_ref.at[1]),
     ]
     for copy in copies:
         copy.start()
@@ -403,11 +402,11 @@
             rows = block[z * width : (z + 1) * width]
             out_ref[z * NX + owner] = rows.astype(out_ref.dtype)
 
-    for i, k in enumerate((0, NX - 1, 1)):
-        put(k, dot_t(x_ref[...], w_ref[i]))
-    for copy in copies:
+    put(0, dot_t(x_ref[...], w_ref[0]))
+    put(NX - 1, dot_t(x_ref[...], w_ref[1]))
+    for i, copy in enumerate(copies):
         copy.wait()
-    put(2, dot_t(x_ref[...], opp_ref[...]))
+        put(1 + i, dot_t(x_ref[...], late_ref[i]))
 
 
 def sum_kernel(in_ref, keep_ref, send_ref):
@@ -542,7 +541,7 @@
     usable = within[None, :, None, :] < limit[:, None, :, None]
     bias = jnp.where(usable, 0.0, NEG).astype(f32).reshape(rows_dev * pages_row * piece, 1)
 
-    got, w_near, w_far, all_queries = lax.optimization_barrier((got, w_near, w_far, all_queries))
+    got, w_near, all_queries = lax.optimization_barrier((got, w_near, all_queries))
     key = call(
         functools.partial(gather_kernel, piece, per_pair, rope_w, pages_row),
         jax.ShapeDtypeStruct((rows_dev, pages_row * piece, lat_w + TAIL), bf16),
@@ -572,8 +571,7 @@
         flops=2 * tokens * asked * (2 * lat_w + TAIL),
         nbytes=2 * tokens * lat_w,
     )
-    size = w_t.shape[0] // 2
-    opposite = [shift_x(w_near[:size], 1), shift_x(w_far[size:], -1)]
+    w_opposite = shift_x(w_near, 1)
     parts = call(
         functools.partial(both_kernel, scale),
         tuple(jax.ShapeDtypeStruct((lat_w + INFO, queries), bf16) for _ in range(NX)),
@@ -599,17 +597,17 @@
     cores = n_head // NX
     w_ring = call(
         stage_kernel,
-        jax.ShapeDtypeStruct((3,) + w_t.shape, bf16),
-        [w_t, w_near, w_far],
-        scratch=[pltpu.SemaphoreType.DMA((3,))],
-        nbytes=12 * w_o.size,
-        in_hbm=(0, 1, 2),
+        jax.ShapeDtypeStruct((2,) + w_t.shape, bf16),
+        [w_t, w_near],
+        scratch=[pltpu.SemaphoreType.DMA((2,))],
+        nbytes=8 * w_o.size,
+        in_hbm=(0, 1),
     )
     sums = call(
         functools.partial(project_kernel, width),
         jax.ShapeDtypeStruct((NZ * NX, width, cols), bf16),
-        [ring.reshape(NZ * width, heads * value_w), w_ring] + opposite,
-        scratch=[pltpu.VMEM(w_t.shape, bf16), pltpu.SemaphoreType.DMA((2,))],
+        [ring.reshape(NZ * width, heads * value_w), w_ring, w_far, w_opposite],
+        scratch=[pltpu.VMEM((2,) + w_t.shape, bf16), pltpu.SemaphoreType.DMA((2,))],
         flops=2 * NX * NZ * width * w_o.size,
         nbytes=2 * NX * w_o.size,
         in_hbm=(2, 3),

time: 114 us -> 116 us (1.018)
  waiting for transfers between devices: 40.2 us -> 49.7 us
  local copies, waits for them, and re-layouts: 6.53 us -> 1.5 us
  starting transfers between devices: 37 us -> 34.4 us
    ppermute x6, waiting for transfers between devices: 9.19 us -> 14.5 us  [shift_y(): lax.ppermute(x, 'head', [(h, (h + k * cores) % n_head) for h in range(n_h...]
    all_to_all x1, waiting for transfers between devices: 6.68 us -> 9.42 us  [on_device(): lax.all_to_all(head_out, 'row', split_axis=0, concat_axis=0, axis_index_g...]
    ppermute x4 -> x3, starting transfers between devices: 5.43 us -> 2.73 us  [shift_x(): lax.ppermute(x, 'row', [(a * NZ + b, (a + k) % NX * NZ + b) for a in rang...]
    slice x2 -> x0, local copies, waits for them, and re-layouts: 2.66 us -> none  [on_device(): opposite = [shift_x(w_near[:size], 1), shift_x(w_far[size:], -1)]]
    unnamed x27 -> x23, local copies, waits for them, and re-layouts: 3.22 us -> 0.85 us
    ppermute x4 -> x3, waiting for transfers between devices: 22.7 us -> 24.8 us  [shift_x(): lax.ppermute(x, 'row', [(a * NZ + b, (a + k) % NX * NZ + b) for a in rang...]
  transfers between devices with their start and end apart: 14 -> 13, of which waited for: 7 -> 8; matrix products, arithmetic and copies ran while one was open for 3% -> 1% of each run, Pallas kernels for 5% -> 5%
where the time goes in v10:
time: 116 us; the launch traced here: 115 us
  waiting for transfers between devices  49.7 us (43%)
  starting transfers between devices  34.4 us (30%)
  Pallas kernels  16.6 us (14%)
  blocking collectives  12.4 us (11%)
  local copies, waits for them, and re-layouts  1.5 us (1%)
    ppermute x3, waiting for transfers between devices, shift_x(): lax.ppermute(x, 'row', [(a * NZ + b, (a + k) % NX * NZ + b) for a in rang...  24.8 us
    pallas_call x10, Pallas kernels, call(): pl.pallas_call(body, out_shape=out_shape, in_specs=[HBM if i in in_hbm el...  16.6 us
    ppermute x6, waiting for transfers between devices, shift_y(): lax.ppermute(x, 'head', [(h, (h + k * cores) % n_head) for h in range(n_h...  14.5 us
    all_to_all x1, blocking collectives, on_device(): lax.all_to_all(sums, ('row', 'head'), split_axis=0, concat_axis=0, axis_i...  12.4 us
    all_to_all x1, starting transfers between devices, on_device(): got = lax.all_to_all(send, 'row', split_axis=0, concat_axis=0, tiled=True)  12.3 us
    all_to_all x1, waiting for transfers between devices, on_device(): lax.all_to_all(head_out, 'row', split_axis=0, concat_axis=0, axis_index_g...  9.42 us
    ppermute x6, starting transfers between devices, shift_y(): lax.ppermute(x, 'head', [(h, (h + k * cores) % n_head) for h in range(n_h...  8.41 us
    all_to_all x1, starting transfers between devices, on_device(): lax.all_to_all(head_out, 'row', split_axis=0, concat_axis=0, axis_index_g...  6.38 us
  transfers between devices with their start and end apart: 13, of which 8 were waited for; matrix products, arithmetic and copies ran while one was open for 1% of the time, Pallas kernels for 5%

profile of v10, /device:TPU:1, one launch (start us, length us, event | category | flops | bytes accessed | tf_op | source)
XLA Modules:
  0.0 115.1 jit_solution(5337691157359085765)
XLA Ops:
  0.0 4.1 %shard_map.128 = bf16[32,184,128]{2,1,0:T(8,128)(2,1)} custom-call(s32[1,80]{1,0:T(1,128)} %bitcast.22, s32[1,80]{1,0:T(1,128)} %bitcast.23, bf16[80,64,512]{2,1,0:T(8,128)(2,1)} %lat_hbm.1, bf16[80,4096]{1,0:T(8,128)(2,1)} %rope_hbm.1), custom_call_target="tpu_custom_call" | custom-call | flops 838860800 | bytes 2621440 | tf_op jit(solution)/shard_map/pallas_call | solution.py:26
  4.1 0.0 copy-start.2
  4.1 0.0 copy-start.5
  4.1 0.0 copy-start.6
  4.1 0.0 copy-start.1
  4.1 12.3 %all-to-all-start = ((bf16[32,184,128]{2,1,0:T(8,128)(2,1)}), bf16[32,184,128]{2,1,0:T(8,128)(2,1)}, u32[]{:S(2)}, u32[]{:S(2)}) async-start(bf16[32,184,128]{2,1,0:T(8,128)(2,1)} %shard_map.128), calls=%async_computation | async-start | bytes 3014656 | tf_op jit(solution)/shard_map/all_to_all | solution.py:500
  16.4 0.0 copy-start.9
  16.4 0.0 copy-start.10
  16.4 1.2 %collective-permute-start = (bf16[224,2048]{1,0:T(8,128)(2,1)S(1)}, bf16[224,2048]{1,0:T(8,128)(2,1)}, u32[]{:S(2)}, u32[]{:S(2)}) collective-permute-start(bf16[224,2048]{1,0:T(8,128)(2,1)S(1)} %bitcast.15), channel_id=1, source_target_pairs={{0,64},{8,72},{16,80},{24,88},{32,96},{40,104},{48,112},{56,120},{... | collective-permute-start | bytes 2752520 | tf_op jit(solution)/shard_map/ppermute | solution.py:438
  17.7 0.1 pad.3.clone
  17.8 0.2 copy.32
  18.0 0.1 copy.35
  18.2 0.1 reshape.88
  18.3 0.1 pad.5.clone
  18.4 0.9 shard_map.127
  19.3 0.7 copy-done.3
  20.0 1.3 %collective-permute-start.1 = (bf16[640,128]{1,0:T(8,128)(2,1)S(1)}, bf16[640,128]{1,0:T(8,128)(2,1)S(1)}, u32[]{:S(2)}, u32[]{:S(2)}) collective-permute-start(bf16[640,128]{1,0:T(8,128)(2,1)S(1)} %get-tuple-element.26), channel_id=1, source_target_pairs={{0,2},{1,3},{2,4},{3,5},{4,6},{5,7},{6,0},{7,1},{8,10},{9,11},{10,... | collective-permute-start | bytes 491528 | tf_op jit(solution)/shard_map/ppermute | solution.py:434
  21.3 1.4 %collective-permute-start.3 = (bf16[640,128]{1,0:T(8,128)(2,1)S(1)}, bf16[640,128]{1,0:T(8,128)(2,1)S(1)}, u32[]{:S(2)}, u32[]{:S(2)}) collective-permute-start(bf16[640,128]{1,0:T(8,128)(2,1)S(1)} %get-tuple-element.26), channel_id=1, source_target_pairs={{0,6},{1,7},{2,0},{3,1},{4,2},{5,3},{6,4},{7,5},{8,14},{9,15},{10,... | collective-permute-start | bytes 491528 | tf_op jit(solution)/shard_map/ppermute | solution.py:434
  22.7 1.6 %collective-permute-start.2 = (bf16[640,128]{1,0:T(8,128)(2,1)S(1)}, bf16[640,128]{1,0:T(8,128)(2,1)S(1)}, u32[]{:S(2)}, u32[]{:S(2)}) collective-permute-start(bf16[640,128]{1,0:T(8,128)(2,1)S(1)} %get-tuple-element.28.refs_0_), channel_id=1, source_target_pairs={{0,4},{1,5},{2,6},{3,7},{4,0},{5,1},{6,2},{7,3},{8,12},{9,13},{10,... | collective-permute-start | bytes 491528 | tf_op jit(solution)/shard_map/ppermute | solution.py:434
  24.4 0.1 select_reduce_fusion
  24.5 0.1 subtract_subtract_fusion
  24.5 0.1 compare_select_fusion
  24.6 0.1 select_n.16.bias_ref
  24.8 1.1 collective-permute-done.1.refs_1_
  25.8 4.5 %collective-permute-done.2.refs_2_ = bf16[640,128]{1,0:T(8,128)(2,1)S(1)} collective-permute-done((bf16[640,128]{1,0:T(8,128)(2,1)S(1)}, bf16[640,128]{1,0:T(8,128)(2,1)S(1)}, u32[]{:S(2)}, u32[]{:S(2)}) %collective-permute-start.2) | collective-permute-done | bytes 163872 | tf_op jit(solution)/shard_map/ppermute | solution.py:434
  30.4 24.8 %collective-permute-done.near_hbm = bf16[224,2048]{1,0:T(8,128)(2,1)} collective-permute-done((bf16[224,2048]{1,0:T(8,128)(2,1)S(1)}, bf16[224,2048]{1,0:T(8,128)(2,1)}, u32[]{:S(2)}, u32[]{:S(2)}) %collective-permute-start) | collective-permute-done | bytes 917536 | tf_op jit(solution)/shard_map/ppermute | solution.py:438
  55.2 3.3 %shard_map.129.key_ref = bf16[2,320,640]{2,1,0:T(8,128)(2,1)S(1)} custom-call(bf16[32,184,128]{2,1,0:T(8,128)(2,1)} %all-to-all-done.block_hbm, f32[640,1]{1,0:T(8,128)S(1)} %select_n.16.bias_ref), custom_call_target="tpu_custom_call" | custom-call | flops 838860800 | bytes 1310720 | tf_op jit(solution)/shard_map/pallas_call | solution.py:26
  58.5 0.0 copy-start
  58.5 1.5 %collective-permute-start.4 = (bf16[2,320,640]{2,1,0:T(8,128)(2,1)S(1)}, bf16[2,320,640]{2,1,0:T(8,128)(2,1)S(1)}, u32[]{:S(2)}, u32[]{:S(2)}) collective-permute-start(bf16[2,320,640]{2,1,0:T(8,128)(2,1)S(1)} %shard_map.129.key_ref), channel_id=1, source_target_pairs={{0,1},{1,0},{2,3},{3,2},{4,5},{5,4},{6,7},{7,6},{8,9},{9,8},{10,11... | collective-permute-start | bytes 2457608 | tf_op jit(solution)/shard_map/ppermute | solution.py:562
  60.0 0.6 collective-permute-start.8
  60.5 0.9 collective-permute-start.9
  61.5 1.2 %shard_map.130 = (f32[2,512,256]{2,1,0:T(8,128)S(1)}, f32[2,8,256]{2,1,0:T(8,128)S(1)}) custom-call(bf16[2,320,640]{2,1,0:T(8,128)(2,1)S(1)} %shard_map.129.key_ref, bf16[640,128]{1,0:T(8,128)(2,1)S(1)} %get-tuple-element.28.refs_0_, bf16[640,128]{1,0:T(8,128)(2,1)S(1)} %collective-permute-done.1.refs_1_, ...), custom_call_target="tpu_custom_call" | custom-call | flops 377487360 | bytes 655360 | tf_op jit(solution)/shard_map/pallas_call | solution.py:26
  62.6 1.2 %shard_map.131 = (bf16[528,128]{1,0:T(8,128)(2,1)S(1)}, bf16[528,128]{1,0:T(8,128)(2,1)S(1)}, bf16[528,128]{1,0:T(8,128)(2,1)S(1)}, bf16[528,128]{1,0:T(8,128)(2,1)S(1)}) custom-call(bf16[2,320,640]{2,1,0:T(8,128)(2,1)S(1)} %collective-permute-done.4.key_ref, f32[2,512,256]{2,1,0:T(8,128)S(1)} %get-tuple-element.32.own_ref, ...), custom_call_target="tpu_custom_call" | custom-call | flops 377487360 | bytes 655360 | tf_op jit(solution)/shard_map/pallas_call | solution.py:26
  63.8 3.0 %collective-permute-start.5 = (bf16[528,128]{1,0:T(8,128)(2,1)S(1)}, bf16[528,128]{1,0:T(8,128)(2,1)S(1)}, u32[]{:S(2)}, u32[]{:S(2)}) collective-permute-start(bf16[528,128]{1,0:T(8,128)(2,1)S(1)} %get-tuple-element.35), channel_id=1, source_target_pairs={{0,6},{1,7},{2,0},{3,1},{4,2},{5,3},{6,4},{7,5},{8,14},{9,15},{10,... | collective-permute-start | bytes 405512 | tf_op jit(solution)/shard_map/ppermute | solution.py:434
  66.8 0.3 collective-permute-start.6
  67.2 0.7 collective-permute-start.7
  67.9 4.2 %collective-permute-done.5.refs_1_ = bf16[528,128]{1,0:T(8,128)(2,1)S(1)} collective-permute-done((bf16[528,128]{1,0:T(8,128)(2,1)S(1)}, bf16[528,128]{1,0:T(8,128)(2,1)S(1)}, u32[]{:S(2)}, u32[]{:S(2)}) %collective-permute-start.5) | collective-permute-done | bytes 135200 | tf_op jit(solution)/shard_map/ppermute | solution.py:434
  72.0 0.5 collective-permute-done.6.refs_2_
  72.5 4.3 %collective-permute-done.7.refs_3_ = bf16[528,128]{1,0:T(8,128)(2,1)S(1)} collective-permute-done((bf16[528,128]{1,0:T(8,128)(2,1)S(1)}, bf16[528,128]{1,0:T(8,128)(2,1)S(1)}, u32[]{:S(2)}, u32[]{:S(2)}) %collective-permute-start.7) | collective-permute-done | bytes 135200 | tf_op jit(solution)/shard_map/ppermute | solution.py:434
  76.8 1.5 %shard_map.132 = bf16[8,8,2048]{2,1,0:T(8,128)(2,1)} custom-call(f32[512,128]{1,0:T(8,128)S(1)} %copy-done.4, f32[8,128]{1,0:T(8,128)S(1)} %get-tuple-element.24.fresh_lse_ref, bf16[16,512,128]{2,1,0:T(8,128)(2,1)S(1)} %copy-done, bf16[528,128]{1,0:T(8,128)(2,1)S(1)} %get-tuple-element.34.refs_0_, bf16[528,128]{1,0:T(8,128)(2,1)S(1)} %collective-permute-done.5.refs_1_, ...), custom_call_target="tpu_custom_call" | custom-call | flops 16777216 | bytes 2097152 | tf_op jit(solution)/shard_map/pallas_call | solution.py:26
  78.3 6.4 %all-to-all-start.1 = ((bf16[8,8,2048]{2,1,0:T(8,128)(2,1)}), bf16[8,8,2048]{2,1,0:T(8,128)(2,1)S(1)}, u32[]{:S(2)}, u32[]{:S(2)}) async-start(bf16[8,8,2048]{2,1,0:T(8,128)(2,1)} %shard_map.132), calls=%async_computation.1 | async-start | bytes 524288 | tf_op jit(solution)/shard_map/all_to_all | solution.py:593
  84.7 1.4 %shard_map.133.w_ref = bf16[2,224,2048]{2,1,0:T(8,128)(2,1)S(1)} custom-call(bf16[224,2048]{1,0:T(8,128)(2,1)S(1)} %bitcast.17, bf16[224,2048]{1,0:T(8,128)(2,1)} %collective-permute-done.near_hbm), custom_call_target="tpu_custom_call" | custom-call | bytes 3670016 | tf_op jit(solution)/shard_map/pallas_call | solution.py:26
  86.2 9.4 %all-to-all-done.1 = bf16[8,8,2048]{2,1,0:T(8,128)(2,1)S(1)} async-done(((bf16[8,8,2048]{2,1,0:T(8,128)(2,1)}), bf16[8,8,2048]{2,1,0:T(8,128)(2,1)S(1)}, u32[]{:S(2)}, u32[]{:S(2)}) %all-to-all-start.1) | async-done | bytes 262176 | tf_op jit(solution)/shard_map/all_to_all | solution.py:593
  95.6 2.4 %shard_map.134 = bf16[32,8,224]{2,1,0:T(8,128)(2,1)S(1)} custom-call(bf16[64,2048]{1,0:T(8,128)(2,1)S(1)} %bitcast.14, bf16[2,224,2048]{2,1,0:T(8,128)(2,1)S(1)} %shard_map.133.w_ref, bf16[224,2048]{1,0:T(8,128)(2,1)} %collective-permute-done.8.far_hbm, bf16[224,2048]{1,0:T(8,128)(2,1)} %collective-permute-done.9.opposite_hbm), custom_call_target="tpu_custom_call" | custom-call | flops 234881024 | bytes 3670016 | tf_op jit(solution)/shard_map/pallas_call | solution.py:26
  98.0 12.4 %all_to_all.15.in_ref = bf16[32,8,224]{2,1,0:T(8,128)(2,1)S(1)} all-to-all(bf16[32,8,224]{2,1,0:T(8,128)(2,1)S(1)} %shard_map.134), channel_id=1, replica_groups={{0,2,4,6,8,10,12,14,16,18,20,22,24,26,28,30,32,34,36,38,40,42,44,46,48,..., dimensions={0} | all-to-all | bytes 229376 | tf_op jit(solution)/shard_map/all_to_all | solution.py:620
  110.4 3.1 %collective-permute-start.10 = (f32[4,8,224]{2,1,0:T(8,128)S(1)}, f32[4,8,224]{2,1,0:T(8,128)S(1)}, u32[]{:S(2)}, u32[]{:S(2)}) collective-permute-start(f32[4,8,224]{2,1,0:T(8,128)S(1)} %get-tuple-element.40), channel_id=1, source_target_pairs={{0,1},{1,0},{2,3},{3,2},{4,5},{5,4},{6,7},{7,6},{8,9},{9,8},{10,11... | collective-permute-start | bytes 86024 | tf_op jit(solution)/shard_map/ppermute | solution.py:630
  113.6 0.9 collective-permute-done.10.got_ref
  114.4 0.7 shard_map.136
  (30 shorter events, 0.2 us)
Async XLA Ops:
  0.0 17.7 %copy-start.7 = (bf16[4,2,512]{2,1,0:T(2,128)(2,1)S(1)}, bf16[4,2,512]{2,1,0:T(2,128)(2,1)}, u32[]{:S(2)}) copy-start(bf16[4,2,512]{2,1,0:T(2,128)(2,1)} %param.15) | copy-start | bytes 24580
  0.0 17.8 %copy-start.8 = (bf16[4,2,64]{2,1,0:T(2,128)(2,1)S(1)}, bf16[4,2,64]{2,1,0:T(2,128)(2,1)}, u32[]{:S(2)}) copy-start(bf16[4,2,64]{2,1,0:T(2,128)(2,1)} %param.16) | copy-start | bytes 3076
  4.1 12.3 %copy-start.2 = (bf16[2048,224]{0,1:T(8,128)(2,1)S(1)}, bf16[2048,224]{0,1:T(8,128)(2,1)}, u32[]{:S(2)}) copy-start(bf16[2048,224]{0,1:T(8,128)(2,1)} %param.25) | copy-start | bytes 2752516
  4.1 14.0 %copy-start.5 = (bf16[4,2,16,128]{3,2,1,0:T(8,128)(2,1)S(1)}, bf16[4,2,16,128]{3,2,1,0:T(8,128)(2,1)}, u32[]{:S(2)}) copy-start(bf16[4,2,16,128]{3,2,1,0:T(8,128)(2,1)} %param.13) | copy-start | bytes 98308
  4.1 14.0 %copy-start.6 = (bf16[4,2,1024]{2,1,0:T(2,128)(2,1)S(1)}, bf16[4,2,1024]{2,1,0:T(2,128)(2,1)}, u32[]{:S(2)}) copy-start(bf16[4,2,1024]{2,1,0:T(2,128)(2,1)} %param.14) | copy-start | bytes 49156
  4.1 14.3 %copy-start.1 = (bf16[16,128,512]{2,1,0:T(8,128)(2,1)S(1)}, bf16[16,128,512]{2,1,0:T(8,128)(2,1)}, u32[]{:S(2)}) copy-start(bf16[16,128,512]{2,1,0:T(8,128)(2,1)} %w_ref.2) | copy-start | bytes 6291460
  4.1 51.0 %all-to-all-start = ((bf16[32,184,128]{2,1,0:T(8,128)(2,1)}), bf16[32,184,128]{2,1,0:T(8,128)(2,1)}, u32[]{:S(2)}, u32[]{:S(2)}) async-start(bf16[32,184,128]{2,1,0:T(8,128)(2,1)} %shard_map.128), calls=%async_computation | async-start | bytes 3014656 | tf_op jit(solution)/shard_map/all_to_all | solution.py:500
  16.4 8.0 %copy-start.9 = (s32[2,40]{1,0:T(2,128)S(1)}, s32[2,40]{1,0:T(2,128)}, u32[]{:S(2)}) copy-start(s32[2,40]{1,0:T(2,128)} %param.21) | copy-start | bytes 964
  16.4 8.0 %copy-start.10 = (s32[2]{0:T(128)S(1)}, s32[2]{0:T(128)}, u32[]{:S(2)}) copy-start(s32[2]{0:T(128)} %param.22) | copy-start | bytes 28
  16.4 38.7 %collective-permute-start = (bf16[224,2048]{1,0:T(8,128)(2,1)S(1)}, bf16[224,2048]{1,0:T(8,128)(2,1)}, u32[]{:S(2)}, u32[]{:S(2)}) collective-permute-start(bf16[224,2048]{1,0:T(8,128)(2,1)S(1)} %bitcast.15), channel_id=1, source_target_pairs={{0,64},{8,72},{16,80},{24,88},{32,96},{40,104},{48,112},{56,120},{... | collective-permute-start | bytes 2752520 | tf_op jit(solution)/shard_map/ppermute | solution.py:438
  19.3 0.7 copy-start.3
  20.0 5.8 %collective-permute-start.1 = (bf16[640,128]{1,0:T(8,128)(2,1)S(1)}, bf16[640,128]{1,0:T(8,128)(2,1)S(1)}, u32[]{:S(2)}, u32[]{:S(2)}) collective-permute-start(bf16[640,128]{1,0:T(8,128)(2,1)S(1)} %get-tuple-element.26), channel_id=1, source_target_pairs={{0,2},{1,3},{2,4},{3,5},{4,6},{5,7},{6,0},{7,1},{8,10},{9,11},{10,... | collective-permute-start | bytes 491528 | tf_op jit(solution)/shard_map/ppermute | solution.py:434
  21.3 9.1 %collective-permute-start.3 = (bf16[640,128]{1,0:T(8,128)(2,1)S(1)}, bf16[640,128]{1,0:T(8,128)(2,1)S(1)}, u32[]{:S(2)}, u32[]{:S(2)}) collective-permute-start(bf16[640,128]{1,0:T(8,128)(2,1)S(1)} %get-tuple-element.26), channel_id=1, source_target_pairs={{0,6},{1,7},{2,0},{3,1},{4,2},{5,3},{6,4},{7,5},{8,14},{9,15},{10,... | collective-permute-start | bytes 491528 | tf_op jit(solution)/shard_map/ppermute | solution.py:434
  22.7 7.6 %collective-permute-start.2 = (bf16[640,128]{1,0:T(8,128)(2,1)S(1)}, bf16[640,128]{1,0:T(8,128)(2,1)S(1)}, u32[]{:S(2)}, u32[]{:S(2)}) collective-permute-start(bf16[640,128]{1,0:T(8,128)(2,1)S(1)} %get-tuple-element.28.refs_0_), channel_id=1, source_target_pairs={{0,4},{1,5},{2,6},{3,7},{4,0},{5,1},{6,2},{7,3},{8,12},{9,13},{10,... | collective-permute-start | bytes 491528 | tf_op jit(solution)/shard_map/ppermute | solution.py:434
  58.5 18.3 %copy-start = (bf16[16,512,128]{2,1,0:T(8,128)(2,1)S(1)}, bf16[16,512,128]{2,1,0:T(8,128)(2,1)}, u32[]{:S(2)}) copy-start(bf16[16,512,128]{2,1,0:T(8,128)(2,1)} %w_ref.3) | copy-start | bytes 6291460
  58.5 18.3 %copy-start.4 = (f32[512,128]{1,0:T(8,128)S(1)}, f32[512,128]{1,0:T(8,128)}, u32[]{:S(2)}) copy-start(f32[512,128]{1,0:T(8,128)} %copy-done.3) | copy-start | bytes 786436
  58.5 4.1 %collective-permute-start.4 = (bf16[2,320,640]{2,1,0:T(8,128)(2,1)S(1)}, bf16[2,320,640]{2,1,0:T(8,128)(2,1)S(1)}, u32[]{:S(2)}, u32[]{:S(2)}) collective-permute-start(bf16[2,320,640]{2,1,0:T(8,128)(2,1)S(1)} %shard_map.129.key_ref), channel_id=1, source_target_pairs={{0,1},{1,0},{2,3},{3,2},{4,5},{5,4},{6,7},{7,6},{8,9},{9,8},{10,11... | collective-permute-start | bytes 2457608 | tf_op jit(solution)/shard_map/ppermute | solution.py:562
  60.0 26.2 %collective-permute-start.8 = (bf16[224,2048]{1,0:T(8,128)(2,1)S(1)}, bf16[224,2048]{1,0:T(8,128)(2,1)}, u32[]{:S(2)}, u32[]{:S(2)}) collective-permute-start(bf16[224,2048]{1,0:T(8,128)(2,1)S(1)} %bitcast.16), channel_id=1, source_target_pairs={{0,192},{8,200},{16,208},{24,216},{32,224},{40,232},{48,240},{56,2... | collective-permute-start | bytes 2752520 | tf_op jit(solution)/shard_map/ppermute | solution.py:438
  60.5 25.6 %collective-permute-start.9 = (bf16[224,2048]{1,0:T(8,128)(2,1)}, bf16[224,2048]{1,0:T(8,128)(2,1)}, u32[]{:S(2)}, u32[]{:S(2)}) collective-permute-start(bf16[224,2048]{1,0:T(8,128)(2,1)} %collective-permute-done.near_hbm), channel_id=1, source_target_pairs={{0,64},{8,72},{16,80},{24,88},{32,96},{40,104},{48,112},{56,120},{... | collective-permute-start | bytes 2752520 | tf_op jit(solution)/shard_map/ppermute | solution.py:438
  63.8 8.2 %collective-permute-start.5 = (bf16[528,128]{1,0:T(8,128)(2,1)S(1)}, bf16[528,128]{1,0:T(8,128)(2,1)S(1)}, u32[]{:S(2)}, u32[]{:S(2)}) collective-permute-start(bf16[528,128]{1,0:T(8,128)(2,1)S(1)} %get-tuple-element.35), channel_id=1, source_target_pairs={{0,6},{1,7},{2,0},{3,1},{4,2},{5,3},{6,4},{7,5},{8,14},{9,15},{10,... | collective-permute-start | bytes 405512 | tf_op jit(solution)/shard_map/ppermute | solution.py:434
  66.8 5.7 %collective-permute-start.6 = (bf16[528,128]{1,0:T(8,128)(2,1)S(1)}, bf16[528,128]{1,0:T(8,128)(2,1)S(1)}, u32[]{:S(2)}, u32[]{:S(2)}) collective-permute-start(bf16[528,128]{1,0:T(8,128)(2,1)S(1)} %get-tuple-element.36), channel_id=1, source_target_pairs={{0,4},{1,5},{2,6},{3,7},{4,0},{5,1},{6,2},{7,3},{8,12},{9,13},{10,... | collective-permute-start | bytes 405512 | tf_op jit(solution)/shard_map/ppermute | solution.py:434
  67.2 9.6 %collective-permute-start.7 = (bf16[528,128]{1,0:T(8,128)(2,1)S(1)}, bf16[528,128]{1,0:T(8,128)(2,1)S(1)}, u32[]{:S(2)}, u32[]{:S(2)}) collective-permute-start(bf16[528,128]{1,0:T(8,128)(2,1)S(1)} %get-tuple-element.37), channel_id=1, source_target_pairs={{0,2},{1,3},{2,4},{3,5},{4,6},{5,7},{6,0},{7,1},{8,10},{9,11},{10,... | collective-permute-start | bytes 405512 | tf_op jit(solution)/shard_map/ppermute | solution.py:434
  78.3 17.2 %all-to-all-start.1 = ((bf16[8,8,2048]{2,1,0:T(8,128)(2,1)}), bf16[8,8,2048]{2,1,0:T(8,128)(2,1)S(1)}, u32[]{:S(2)}, u32[]{:S(2)}) async-start(bf16[8,8,2048]{2,1,0:T(8,128)(2,1)} %shard_map.132), calls=%async_computation.1 | async-start | bytes 524288 | tf_op jit(solution)/shard_map/all_to_all | solution.py:593
  110.4 4.0 %collective-permute-start.10 = (f32[4,8,224]{2,1,0:T(8,128)S(1)}, f32[4,8,224]{2,1,0:T(8,128)S(1)}, u32[]{:S(2)}, u32[]{:S(2)}) collective-permute-start(f32[4,8,224]{2,1,0:T(8,128)S(1)} %get-tuple-element.40), channel_id=1, source_target_pairs={{0,1},{1,0},{2,3},{3,2},{4,5},{5,4},{6,7},{7,6},{8,9},{9,8},{10,11... | collective-permute-start | bytes 86024 | tf_op jit(solution)/shard_map/ppermute | solution.py:630

commit v11 on v9

--- a/solution.py
+++ b/solution.py
@@ -102,8 +102,16 @@
         )
         copy.start()
         lat_copies.append(copy)
+    def unpack(i):
+        lat_copies[i].wait()
+        lat = lat_buf[i * cut : (i + 1) * cut].astype(jnp.float32).reshape(cut, 2, piece, lat_w)
+        lat = jnp.where(head % 2 == 1, lat[:, 1], lat[:, 0]).reshape(cut * piece, lat_w)
+        lat_ref[i * cut * piece : (i + 1) * cut * piece, :] = lat.astype(jnp.bfloat16)
+
     for copy in lists:
         copy.wait()
+    for i in range(chunks // 2):
+        unpack(i)
 
     dest = rows_ref[...] // rows_dev
     label = (rows_ref[...] % rows_dev * pages_row + slots_ref[...] + 1).astype(jnp.float32)
@@ -128,13 +136,10 @@
     for j in range(rope_rows):
         pick = ones_where(row == dest * rest + rank * rope_rows + j)
         tail = tail + dot(pick, rope_buf[:, j * TAIL : (j + 1) * TAIL])
-    buf_ref[:, lat_rows:, :] = tail.reshape(count, rest, TAIL).astype(jnp.bfloat16)
-
-    for i, copy in enumerate(lat_copies):
-        copy.wait()
-        lat = lat_buf[i * cut : (i + 1) * cut].astype(jnp.float32).reshape(cut, 2, piece, lat_w)
-        lat = jnp.where(head % 2 == 1, lat[:, 1], lat[:, 0]).reshape(cut * piece, lat_w)
-        lat_ref[i * cut * piece : (i + 1) * cut * piece, :] = lat.astype(jnp.bfloat16)
+    tail = tail.reshape(count, rest, TAIL)
+
+    for i in range(chunks // 2, chunks):
+        unpack(i)
     lat = lat_ref[...]
     step = count // chunks
     copies = []
@@ -147,7 +152,8 @@
         ]
         value = jnp.concatenate(value, axis=1).reshape(step, lat_rows, TAIL)
         here = pl.ds(i * step, step)
-        buf_ref[here, :lat_rows, :] = value.astype(jnp.bfloat16)
+        value = jnp.concatenate([tail[i * step : (i + 1) * step], value], axis=1)
+        buf_ref[here] = value.astype(jnp.bfloat16)
         copy = pltpu.make_async_copy(buf_ref.at[here], out_hbm.at[here], out_sem.at[i])
         copy.start()
         copies.append(copy)
@@ -203,8 +209,8 @@
     bias_ref,
     key_hbm,
     block_ref,
+    early_ref,
     lat_ref,
-    tail_ref,
     key_ref,
     in_sem,
     out_sem,
@@ -219,9 +225,13 @@
     rope_rows = piece * rope_w // TAIL
     half = per_row // 2
 
-    chunks = in_sem.shape[0]
+    chunks = in_sem.shape[0] - 1
     step = count // chunks
     copies = []
+    early = pltpu.make_async_copy(
+        block_hbm.at[:, pl.ds(0, early_ref.shape[1]), :], early_ref, in_sem.at[chunks]
+    )
+    early.start()
     for i in range(chunks):
         here = pl.ds(i * step, step)
         copy = pltpu.make_async_copy(block_hbm.at[here], block_ref.at[here], in_sem.at[i])
@@ -240,23 +250,11 @@
     lane = jnp.where(rope_inner < per_pair * rope_rows, rope_inner // rope_rows * piece, TAIL)
     rope_spread = spread_over(rope_columns, rest, lane)
 
-    labels = []
-    for i, copy in enumerate(copies):
-        copy.wait()
-        here = slice(i * step, (i + 1) * step)
-        tail = block_ref[here, lat_rows:, :].astype(jnp.float32)
-        marked = iota(tail.shape, 1) == per_pair * rope_rows
-        labels.append(jnp.sum(jnp.where(marked, tail, 0.0), axis=1))
-        tail_ref[i * step * rest : (i + 1) * step * rest, :] = tail.reshape(
-            step * rest, TAIL
-        ).astype(jnp.bfloat16)
-        lat = block_ref[here, :lat_rows, :].astype(jnp.float32)
-        lat = lat.reshape(step * per_pair, cuts, piece, TAIL)
-        for c in range(cuts):
-            lat_ref[i * step * pair_tokens : (i + 1) * step * pair_tokens, pl.ds(c * TAIL, TAIL)] = (
-                lat[:, c].reshape(step * pair_tokens, TAIL).astype(jnp.bfloat16)
-            )
-    labels = jnp.concatenate(labels, axis=0).astype(jnp.bfloat16)
+    early.wait()
+    tail = early_ref[...].astype(jnp.float32)[:, :rest]
+    marked = iota(tail.shape, 1) == per_pair * rope_rows
+    labels = jnp.sum(jnp.where(marked, tail, 0.0), axis=1).astype(jnp.bfloat16)
+    tail = tail.reshape(rope_columns, TAIL).astype(jnp.bfloat16)
 
     def slot_of(spread, own):
         wide = dot(labels, spread) * own
@@ -270,15 +268,24 @@
     target = jnp.where(slot >= 0, target, -1)
     slot = slot_of(*rope_spread)
     rope_target = jnp.where(slot >= 0, slot * rope_rows + rope_inner % rope_rows, -1)
-    copies = []
     for b in range(rows):
         pick = ones_where(iota((half, 1), 0) + b * half == rope_target)
-        rope_b = dot(pick, tail_ref[...])
+        rope_b = dot(pick, tail)
         rope_b = jnp.concatenate([rope_b, pltpu.roll(rope_b, TAIL - rope_w, 1)], axis=0)
         lane = iota(rope_b.shape, 1)
         bias = bias_ref[b * per_row : (b + 1) * per_row]
         rope_b = jnp.where(lane < rope_w, rope_b, jnp.where(lane == rope_w, bias, 0.0))
         key_ref[b, :, lat_w:] = rope_b.astype(jnp.bfloat16)
+    for i, copy in enumerate(copies):
+        copy.wait()
+        lat = block_ref[i * step : (i + 1) * step].astype(jnp.float32)[:, rest:]
+        lat = lat.reshape(step * per_pair, cuts, piece, TAIL)
+        for c in range(cuts):
+            lat_ref[i * step * pair_tokens : (i + 1) * step * pair_tokens, pl.ds(c * TAIL, TAIL)] = (
+                lat[:, c].reshape(step * pair_tokens, TAIL).astype(jnp.bfloat16)
+            )
+    copies = []
+    for b in range(rows):
         pick = ones_where(iota((per_row, 1), 0) + b * per_row == target)
         key_ref[b, :, :lat_w] = dot(pick, lat_ref[...]).astype(jnp.bfloat16)
         copy = pltpu.make_async_copy(key_ref.at[b], key_hbm.at[b], out_sem.at[b])
@@ -315,10 +322,11 @@
 
 
 def both_kernel(scale, key_ref, own_ref, stat_ref, *refs):
-    count = len(refs) // 2
-    q_refs, out_refs = refs[:count], refs[count:]
+    q_refs, out_ref = refs[:-1], refs[-1]
+    count = len(q_refs)
     lat_w = own_ref.shape[1]
     queries = q_refs[0].shape[1]
+    here = lax.axis_index("head") // 2
     parts = []
     for b in range(key_ref.shape[0]):
         high, total, part = attend(scale, key_ref[b], ask(q_refs, b), lat_w)
@@ -337,12 +345,13 @@
     for k in range(0, count, 2):
         lanes = slice(k * queries // 2, (k + 2) * queries // 2)
         one, two = parts[0][:, lanes], parts[1][:, lanes]
-        out_refs[k][...] = jnp.where(left, one, two).astype(jnp.bfloat16)
-        out_refs[k + 1][...] = jnp.where(left, two, one).astype(jnp.bfloat16)
-
-
-def merge_kernel(rows_dev, fresh_ref, fresh_lse_ref, w_ref, *refs):
-    part_refs, out_ref, lat_ref = refs[:-2], refs[-2], refs[-1]
+        out_ref[(here - k + count) % count] = jnp.where(left, one, two).astype(jnp.bfloat16)
+        out_ref[(here - k - 1 + count) % count] = jnp.where(left, two, one).astype(jnp.bfloat16)
+
+
+def merge_kernel(rows_dev, fresh_ref, fresh_lse_ref, w_ref, in_ref, out_ref, lat_ref):
+    here = lax.axis_index("head") // 2
+    part_refs = [in_ref.at[(here + k) % NX] for k in range(NX)]
     heads, lat_w, value_w = w_ref.shape
     width = out_ref.shape[1]
     steps = width // rows_dev
@@ -549,10 +558,10 @@
         [got, bias],
         scratch=[
             pltpu.VMEM(got.shape, bf16),
+            pltpu.VMEM((n_row, 32, TAIL), bf16),
             pltpu.VMEM((slots, lat_w), bf16),
-            pltpu.VMEM((n_row * (block - lat_rows), TAIL), bf16),
             pltpu.VMEM((rows_dev, pages_row * piece, lat_w + TAIL), bf16),
-            pltpu.SemaphoreType.DMA((4,)),
+            pltpu.SemaphoreType.DMA((5,)),
             pltpu.SemaphoreType.DMA((rows_dev,)),
         ],
         flops=2 * slots * tokens * lat_w,
@@ -576,16 +585,19 @@
     opposite = [shift_x(w_near[:size], 1), shift_x(w_far[size:], -1)]
     parts = call(
         functools.partial(both_kernel, scale),
-        tuple(jax.ShapeDtypeStruct((lat_w + INFO, queries), bf16) for _ in range(NX)),
+        jax.ShapeDtypeStruct((NX, lat_w + INFO, queries), bf16),
         [other, own_part, own_stat] + all_queries,
         flops=2 * tokens * asked * (2 * lat_w + TAIL),
         nbytes=2 * tokens * lat_w,
     )
-    parts = [shift_y(part, n_head, -k) for k, part in enumerate(parts)]
+    kinds = [list(range(core, n_head, 2)) for core in range(2)]
+    parts = lax.all_to_all(
+        parts, "head", split_axis=0, concat_axis=0, axis_index_groups=kinds, tiled=True
+    )
     head_out = call(
         functools.partial(merge_kernel, rows_dev),
         jax.ShapeDtypeStruct((NZ, width, heads * value_w), bf16),
-        [fresh_part, fresh_lse, w_uv] + parts,
+        [fresh_part, fresh_lse, w_uv, parts],
         scratch=[pltpu.VMEM((queries, lat_w), f32)],
         flops=2 * queries * lat_w * value_w,
         nbytes=2 * heads * lat_w * value_w,

time: 114 us -> 118 us (1.035)
  local copies, waits for them, and re-layouts: 6.53 us -> 8.76 us
  waiting for transfers between devices: 40.2 us -> 38.6 us
  Pallas kernels: 17.3 us -> 18.5 us
    all_to_all x0 -> x1, starting transfers between devices: none -> 4.32 us  [on_device(): lax.all_to_all(parts, 'head', split_axis=0, concat_axis=0, axis_index_gro...]
    ppermute x6 -> x3, starting transfers between devices: 8.23 us -> 4.38 us  [shift_y(): lax.ppermute(x, 'head', [(h, (h + k * cores) % n_head) for h in range(n_h...]
    all_to_all x0 -> x1, waiting for transfers between devices: none -> 3.75 us  [on_device(): lax.all_to_all(parts, 'head', split_axis=0, concat_axis=0, axis_index_gro...]
    ppermute x6 -> x3, waiting for transfers between devices: 9.19 us -> 5.67 us  [shift_y(): lax.ppermute(x, 'head', [(h, (h + k * cores) % n_head) for h in range(n_h...]
    unnamed x27 -> x31, local copies, waits for them, and re-layouts: 3.22 us -> 5.44 us
    all_to_all x1, waiting for transfers between devices: 6.68 us -> 5.45 us  [on_device(): lax.all_to_all(head_out, 'row', split_axis=0, concat_axis=0, axis_index_g...]
    pallas_call x10, Pallas kernels: 17.3 us -> 18.5 us  [call(): pl.pallas_call(body, out_shape=out_shape, in_specs=[HBM if i in in_hbm el...]
  transfers between devices with their start and end apart: 14 -> 12, of which waited for: 7 -> 7; matrix products, arithmetic and copies ran while one was open for 3% -> 3% of each run, Pallas kernels for 5% -> 5%
where the time goes in v11:
time: 118 us; the launch traced here: 117 us
  waiting for transfers between devices  38.6 us (33%)
  starting transfers between devices  37.8 us (32%)
  Pallas kernels  18.5 us (16%)
  blocking collectives  13.3 us (11%)
  local copies, waits for them, and re-layouts  8.76 us (7%)
    ppermute x4, waiting for transfers between devices, shift_x(): lax.ppermute(x, 'row', [(a * NZ + b, (a + k) % NX * NZ + b) for a in rang...  22.1 us
    pallas_call x10, Pallas kernels, call(): pl.pallas_call(body, out_shape=out_shape, in_specs=[HBM if i in in_hbm el...  18.5 us
    all_to_all x1, blocking collectives, on_device(): lax.all_to_all(sums, ('row', 'head'), split_axis=0, concat_axis=0, axis_i...  13.3 us
    all_to_all x1, starting transfers between devices, on_device(): got = lax.all_to_all(send, 'row', split_axis=0, concat_axis=0, tiled=True)  12.1 us
    all_to_all x1, starting transfers between devices, on_device(): lax.all_to_all(head_out, 'row', split_axis=0, concat_axis=0, axis_index_g...  6.38 us
    ppermute x3, waiting for transfers between devices, shift_y(): lax.ppermute(x, 'head', [(h, (h + k * cores) % n_head) for h in range(n_h...  5.67 us
    all_to_all x1, waiting for transfers between devices, on_device(): lax.all_to_all(head_out, 'row', split_axis=0, concat_axis=0, axis_index_g...  5.45 us
    unnamed x31, local copies, waits for them, and re-layouts  5.44 us
  transfers between devices with their start and end apart: 12, of which 7 were waited for; matrix products, arithmetic and copies ran while one was open for 3% of the time, Pallas kernels for 5%

profile of v11, /device:TPU:1, one launch (start us, length us, event | category | flops | bytes accessed | tf_op | source)
XLA Modules:
  0.0 117.4 jit_solution(14091237463452604330)
XLA Ops:
  0.0 4.5 %shard_map.128 = bf16[32,184,128]{2,1,0:T(8,128)(2,1)} custom-call(s32[1,80]{1,0:T(1,128)} %bitcast.22, s32[1,80]{1,0:T(1,128)} %bitcast.23, bf16[80,64,512]{2,1,0:T(8,128)(2,1)} %lat_hbm.1, bf16[80,4096]{1,0:T(8,128)(2,1)} %rope_hbm.1), custom_call_target="tpu_custom_call" | custom-call | flops 838860800 | bytes 2621440 | tf_op jit(solution)/shard_map/pallas_call | solution.py:26
  4.5 0.0 copy-start.11
  4.5 0.0 copy-start.12
  4.5 12.1 %all-to-all-start = ((bf16[32,184,128]{2,1,0:T(8,128)(2,1)}), bf16[32,184,128]{2,1,0:T(8,128)(2,1)}, u32[]{:S(2)}, u32[]{:S(2)}) async-start(bf16[32,184,128]{2,1,0:T(8,128)(2,1)} %shard_map.128), calls=%async_computation | async-start | bytes 3014656 | tf_op jit(solution)/shard_map/all_to_all | solution.py:510
  16.7 1.2 %collective-permute-start = (bf16[224,2048]{1,0:T(8,128)(2,1)}, bf16[224,2048]{1,0:T(8,128)(2,1)S(1)}, u32[]{:S(2)}, u32[]{:S(2)}) collective-permute-start(bf16[224,2048]{1,0:T(8,128)(2,1)} %bitcast.15), channel_id=1, source_target_pairs={{0,64},{8,72},{16,80},{24,88},{32,96},{40,104},{48,112},{56,120},{... | collective-permute-start | bytes 2752520 | tf_op jit(solution)/shard_map/ppermute | solution.py:448
  17.9 1.5 %collective-permute-start.1 = (bf16[224,2048]{1,0:T(8,128)(2,1)}, bf16[224,2048]{1,0:T(8,128)(2,1)}, u32[]{:S(2)}, u32[]{:S(2)}) collective-permute-start(bf16[224,2048]{1,0:T(8,128)(2,1)} %bitcast.16), channel_id=1, source_target_pairs={{0,192},{8,200},{16,208},{24,216},{32,224},{40,232},{48,240},{56,2... | collective-permute-start | bytes 2752520 | tf_op jit(solution)/shard_map/ppermute | solution.py:448
  19.5 0.1 pad.3.clone
  19.6 0.2 copy.32
  19.8 0.1 copy.35
  19.9 0.1 reshape.88
  20.1 0.1 pad.5.clone
  20.2 1.3 %shard_map.127 = (bf16[640,128]{1,0:T(8,128)(2,1)S(1)}, bf16[640,128]{1,0:T(8,128)(2,1)}, f32[512,128]{1,0:T(8,128)S(1)}, f32[8,128]{1,0:T(8,128)S(1)}) custom-call(bf16[16,8,128]{2,1,0:T(8,128)(2,1)S(1)} %bitcast.18, bf16[128,128]{1,0:T(8,128)(2,1)S(1)} %pad_maximum_fusion.qtail_ref, bf16[16,128,512]{2,1,0:T(8,128)(2,1)S(1)} %copy-done.1, ...), custom_call_target="tpu_custom_call" | custom-call | flops 16777216 | bytes 2097152 | tf_op jit(solution)/shard_map/pallas_call | solution.py:26
  21.5 0.7 copy-done.5
  22.2 0.6 copy-done.7
  22.8 1.3 %collective-permute-start.2 = (bf16[640,128]{1,0:T(8,128)(2,1)}, bf16[640,128]{1,0:T(8,128)(2,1)S(1)}, u32[]{:S(2)}, u32[]{:S(2)}) collective-permute-start(bf16[640,128]{1,0:T(8,128)(2,1)} %get-tuple-element.23), channel_id=1, source_target_pairs={{0,2},{1,3},{2,4},{3,5},{4,6},{5,7},{6,0},{7,1},{8,10},{9,11},{10,... | collective-permute-start | bytes 491528 | tf_op jit(solution)/shard_map/ppermute | solution.py:444
  24.1 1.4 %collective-permute-start.4 = (bf16[640,128]{1,0:T(8,128)(2,1)}, bf16[640,128]{1,0:T(8,128)(2,1)S(1)}, u32[]{:S(2)}, u32[]{:S(2)}) collective-permute-start(bf16[640,128]{1,0:T(8,128)(2,1)} %get-tuple-element.23), channel_id=1, source_target_pairs={{0,6},{1,7},{2,0},{3,1},{4,2},{5,3},{6,4},{7,5},{8,14},{9,15},{10,... | collective-permute-start | bytes 491528 | tf_op jit(solution)/shard_map/ppermute | solution.py:444
  25.5 1.6 %collective-permute-start.3 = (bf16[640,128]{1,0:T(8,128)(2,1)S(1)}, bf16[640,128]{1,0:T(8,128)(2,1)S(1)}, u32[]{:S(2)}, u32[]{:S(2)}) collective-permute-start(bf16[640,128]{1,0:T(8,128)(2,1)S(1)} %get-tuple-element.25.refs_0_), channel_id=1, source_target_pairs={{0,4},{1,5},{2,6},{3,7},{4,0},{5,1},{6,2},{7,3},{8,12},{9,13},{10,... | collective-permute-start | bytes 491528 | tf_op jit(solution)/shard_map/ppermute | solution.py:444
  27.2 0.1 select_reduce_fusion
  27.3 0.1 subtract_subtract_fusion
  27.4 0.1 compare_select_fusion
  27.5 0.1 select_n.16.bias_ref
  27.6 1.3 %collective-permute-done.2.refs_1_ = bf16[640,128]{1,0:T(8,128)(2,1)S(1)} collective-permute-done((bf16[640,128]{1,0:T(8,128)(2,1)}, bf16[640,128]{1,0:T(8,128)(2,1)S(1)}, u32[]{:S(2)}, u32[]{:S(2)}) %collective-permute-start.2) | collective-permute-done | bytes 163872 | tf_op jit(solution)/shard_map/ppermute | solution.py:444
  28.9 4.4 %collective-permute-done.3.refs_2_ = bf16[640,128]{1,0:T(8,128)(2,1)S(1)} collective-permute-done((bf16[640,128]{1,0:T(8,128)(2,1)S(1)}, bf16[640,128]{1,0:T(8,128)(2,1)S(1)}, u32[]{:S(2)}, u32[]{:S(2)}) %collective-permute-start.3) | collective-permute-done | bytes 163872 | tf_op jit(solution)/shard_map/ppermute | solution.py:444
  33.3 22.1 %collective-permute-done.near_hbm = bf16[224,2048]{1,0:T(8,128)(2,1)S(1)} collective-permute-done((bf16[224,2048]{1,0:T(8,128)(2,1)}, bf16[224,2048]{1,0:T(8,128)(2,1)S(1)}, u32[]{:S(2)}, u32[]{:S(2)}) %collective-permute-start) | collective-permute-done | bytes 917536 | tf_op jit(solution)/shard_map/ppermute | solution.py:448
  55.3 3.6 %shard_map.129.key_ref = bf16[2,320,640]{2,1,0:T(8,128)(2,1)S(1)} custom-call(bf16[32,184,128]{2,1,0:T(8,128)(2,1)} %all-to-all-done.block_hbm, f32[640,1]{1,0:T(8,128)S(1)} %select_n.16.bias_ref), custom_call_target="tpu_custom_call" | custom-call | flops 838860800 | bytes 1310720 | tf_op jit(solution)/shard_map/pallas_call | solution.py:26
  58.9 1.4 %collective-permute-start.5 = (bf16[2,320,640]{2,1,0:T(8,128)(2,1)S(1)}, bf16[2,320,640]{2,1,0:T(8,128)(2,1)S(1)}, u32[]{:S(2)}, u32[]{:S(2)}) collective-permute-start(bf16[2,320,640]{2,1,0:T(8,128)(2,1)S(1)} %shard_map.129.key_ref), channel_id=1, source_target_pairs={{0,1},{1,0},{2,3},{3,2},{4,5},{5,4},{6,7},{7,6},{8,9},{9,8},{10,11... | collective-permute-start | bytes 2457608 | tf_op jit(solution)/shard_map/ppermute | solution.py:572
  60.4 1.1 shard_map.130
  61.5 0.8 collective-permute-done.5.key_ref
  62.3 2.0 %shard_map.131 = bf16[4,528,128]{2,1,0:T(8,128)(2,1)} custom-call(bf16[2,320,640]{2,1,0:T(8,128)(2,1)S(1)} %collective-permute-done.5.key_ref, f32[2,512,256]{2,1,0:T(8,128)S(1)} %get-tuple-element.29.own_ref, f32[2,8,256]{2,1,0:T(8,128)S(1)} %get-tuple-element.30.stat_ref, bf16[640,128]{1,0:T(8,128)(2,1)S(1)} %get-tuple-element.25.refs_0_, ...), custom_call_target="tpu_custom_call" | custom-call | flops 377487360 | bytes 655360 | tf_op jit(solution)/shard_map/pallas_call | solution.py:26
  64.3 4.3 %all-to-all-start.1 = ((bf16[4,528,128]{2,1,0:T(8,128)(2,1)}), bf16[4,528,128]{2,1,0:T(8,128)(2,1)S(1)}, u32[]{:S(2)}, u32[]{:S(2)}) async-start(bf16[4,528,128]{2,1,0:T(8,128)(2,1)} %shard_map.131), calls=%async_computation.1 | async-start | bytes 1081344 | tf_op jit(solution)/shard_map/all_to_all | solution.py:594
  68.7 0.8 slice.10
  69.5 0.4 collective-permute-start.6
  69.8 1.9 %slice.11 = bf16[112,2048]{1,0:T(8,128)(2,1)} slice(bf16[224,2048]{1,0:T(8,128)(2,1)} %collective-permute-done.1.far_hbm), slice={[112:224], [0:2048]} | slice | bytes 917504 | tf_op jit(solution)/shard_map/slice | solution.py:585
  71.7 2.3 %collective-permute-start.7 = (bf16[112,2048]{1,0:T(8,128)(2,1)}, bf16[112,2048]{1,0:T(8,128)(2,1)}, u32[]{:S(2)}, u32[]{:S(2)}) collective-permute-start(bf16[112,2048]{1,0:T(8,128)(2,1)} %slice.11), channel_id=1, source_target_pairs={{0,192},{8,200},{16,208},{24,216},{32,224},{40,232},{48,240},{56,2... | collective-permute-start | bytes 1376264 | tf_op jit(solution)/shard_map/ppermute | solution.py:448
  74.0 3.7 %all-to-all-done.1.in_ref = bf16[4,528,128]{2,1,0:T(8,128)(2,1)S(1)} async-done(((bf16[4,528,128]{2,1,0:T(8,128)(2,1)}), bf16[4,528,128]{2,1,0:T(8,128)(2,1)S(1)}, u32[]{:S(2)}, u32[]{:S(2)}) %all-to-all-start.1) | async-done | bytes 540704 | tf_op jit(solution)/shard_map/all_to_all | solution.py:594
  77.8 0.9 copy-done.6
  78.7 0.7 copy-done.8
  79.4 1.5 %shard_map.132 = bf16[8,8,2048]{2,1,0:T(8,128)(2,1)} custom-call(f32[512,128]{1,0:T(8,128)S(1)} %copy-done.6, f32[8,128]{1,0:T(8,128)S(1)} %copy-done.8, bf16[16,512,128]{2,1,0:T(8,128)(2,1)S(1)} %copy-done, bf16[4,528,128]{2,1,0:T(8,128)(2,1)S(1)} %all-to-all-done.1.in_ref), custom_call_target="tpu_custom_call" | custom-call | flops 16777216 | bytes 2097152 | tf_op jit(solution)/shard_map/pallas_call | solution.py:26
  80.9 6.4 %all-to-all-start.2 = ((bf16[8,8,2048]{2,1,0:T(8,128)(2,1)}), bf16[8,8,2048]{2,1,0:T(8,128)(2,1)S(1)}, u32[]{:S(2)}, u32[]{:S(2)}) async-start(bf16[8,8,2048]{2,1,0:T(8,128)(2,1)} %shard_map.132), calls=%async_computation.2 | async-start | bytes 524288 | tf_op jit(solution)/shard_map/all_to_all | solution.py:607
  87.3 1.2 %copy-done.3 = bf16[224,2048]{1,0:T(8,128)(2,1)S(1)} copy-done((bf16[224,2048]{1,0:T(8,128)(2,1)S(1)}, bf16[224,2048]{1,0:T(8,128)(2,1)}, u32[]{:S(2)}) %copy-start.3) | copy-done | bytes 917528
  88.5 1.2 %copy-done.4 = bf16[2048,224]{0,1:T(8,128)(2,1)S(1)} copy-done((bf16[2048,224]{0,1:T(8,128)(2,1)S(1)}, bf16[2048,224]{0,1:T(8,128)(2,1)}, u32[]{:S(2)}) %copy-start.4) | copy-done | bytes 917528
  89.7 1.6 %shard_map.133.w_ref = bf16[3,224,2048]{2,1,0:T(8,128)(2,1)S(1)} custom-call(bf16[224,2048]{1,0:T(8,128)(2,1)S(1)} %bitcast.17, bf16[224,2048]{1,0:T(8,128)(2,1)S(1)} %copy-done.3, bf16[224,2048]{1,0:T(8,128)(2,1)} %collective-permute-done.1.far_hbm), custom_call_target="tpu_custom_call" | custom-call | bytes 5505024 | tf_op jit(solution)/shard_map/pallas_call | solution.py:26
  91.4 5.5 %all-to-all-done.2 = bf16[8,8,2048]{2,1,0:T(8,128)(2,1)S(1)} async-done(((bf16[8,8,2048]{2,1,0:T(8,128)(2,1)}), bf16[8,8,2048]{2,1,0:T(8,128)(2,1)S(1)}, u32[]{:S(2)}, u32[]{:S(2)}) %all-to-all-start.2) | async-done | bytes 262176 | tf_op jit(solution)/shard_map/all_to_all | solution.py:607
  96.8 2.1 %shard_map.134 = bf16[32,8,224]{2,1,0:T(8,128)(2,1)S(1)} custom-call(bf16[64,2048]{1,0:T(8,128)(2,1)S(1)} %bitcast.14, bf16[3,224,2048]{2,1,0:T(8,128)(2,1)S(1)} %shard_map.133.w_ref, bf16[112,2048]{1,0:T(8,128)(2,1)S(1)} %collective-permute-done.6.opp_a_hbm, bf16[112,2048]{1,0:T(8,128)(2,1)} %collective-permute-done.7.opp_b_hbm), custom_call_target="tpu_custom_call" | custom-call | flops 234881024 | bytes 3670016 | tf_op jit(solution)/shard_map/pallas_call | solution.py:26
  98.9 13.3 %all_to_all.20.in_ref = bf16[32,8,224]{2,1,0:T(8,128)(2,1)S(1)} all-to-all(bf16[32,8,224]{2,1,0:T(8,128)(2,1)S(1)} %shard_map.134), channel_id=1, replica_groups={{0,2,4,6,8,10,12,14,16,18,20,22,24,26,28,30,32,34,36,38,40,42,44,46,48,..., dimensions={0} | all-to-all | bytes 229376 | tf_op jit(solution)/shard_map/all_to_all | solution.py:634
  112.2 3.7 %collective-permute-start.8 = (f32[4,8,224]{2,1,0:T(8,128)S(1)}, f32[4,8,224]{2,1,0:T(8,128)S(1)}, u32[]{:S(2)}, u32[]{:S(2)}) collective-permute-start(f32[4,8,224]{2,1,0:T(8,128)S(1)} %get-tuple-element.34), channel_id=1, source_target_pairs={{0,1},{1,0},{2,3},{3,2},{4,5},{5,4},{6,7},{7,6},{8,9},{9,8},{10,11... | collective-permute-start | bytes 86024 | tf_op jit(solution)/shard_map/ppermute | solution.py:644
  115.9 0.9 collective-permute-done.8.got_ref
  116.7 0.7 shard_map.136
  (38 shorter events, 0.2 us)
Async XLA Ops:
  4.5 15.0 %copy-start.11 = (bf16[4,2,512]{2,1,0:T(2,128)(2,1)S(1)}, bf16[4,2,512]{2,1,0:T(2,128)(2,1)}, u32[]{:S(2)}) copy-start(bf16[4,2,512]{2,1,0:T(2,128)(2,1)} %param.15) | copy-start | bytes 24580
  4.5 15.1 %copy-start.12 = (bf16[4,2,64]{2,1,0:T(2,128)(2,1)S(1)}, bf16[4,2,64]{2,1,0:T(2,128)(2,1)}, u32[]{:S(2)}) copy-start(bf16[4,2,64]{2,1,0:T(2,128)(2,1)} %param.16) | copy-start | bytes 3076
  4.5 15.4 %copy-start.9 = (bf16[4,2,16,128]{3,2,1,0:T(8,128)(2,1)S(1)}, bf16[4,2,16,128]{3,2,1,0:T(8,128)(2,1)}, u32[]{:S(2)}) copy-start(bf16[4,2,16,128]{3,2,1,0:T(8,128)(2,1)} %param.13) | copy-start | bytes 98308
  4.5 15.4 %copy-start.10 = (bf16[4,2,1024]{2,1,0:T(2,128)(2,1)S(1)}, bf16[4,2,1024]{2,1,0:T(2,128)(2,1)}, u32[]{:S(2)}) copy-start(bf16[4,2,1024]{2,1,0:T(2,128)(2,1)} %param.14) | copy-start | bytes 49156
  4.5 15.6 %copy-start.1 = (bf16[16,128,512]{2,1,0:T(8,128)(2,1)S(1)}, bf16[16,128,512]{2,1,0:T(8,128)(2,1)}, u32[]{:S(2)}) copy-start(bf16[16,128,512]{2,1,0:T(8,128)(2,1)} %w_ref.2) | copy-start | bytes 6291460
  4.5 50.8 %all-to-all-start = ((bf16[32,184,128]{2,1,0:T(8,128)(2,1)}), bf16[32,184,128]{2,1,0:T(8,128)(2,1)}, u32[]{:S(2)}, u32[]{:S(2)}) async-start(bf16[32,184,128]{2,1,0:T(8,128)(2,1)} %shard_map.128), calls=%async_computation | async-start | bytes 3014656 | tf_op jit(solution)/shard_map/all_to_all | solution.py:510
  16.7 10.5 %copy-start.13 = (s32[2,40]{1,0:T(2,128)S(1)}, s32[2,40]{1,0:T(2,128)}, u32[]{:S(2)}) copy-start(s32[2,40]{1,0:T(2,128)} %param.21) | copy-start | bytes 964
  16.7 10.6 %copy-start.14 = (s32[2]{0:T(128)S(1)}, s32[2]{0:T(128)}, u32[]{:S(2)}) copy-start(s32[2]{0:T(128)} %param.22) | copy-start | bytes 28
  16.7 38.7 %collective-permute-start = (bf16[224,2048]{1,0:T(8,128)(2,1)}, bf16[224,2048]{1,0:T(8,128)(2,1)S(1)}, u32[]{:S(2)}, u32[]{:S(2)}) collective-permute-start(bf16[224,2048]{1,0:T(8,128)(2,1)} %bitcast.15), channel_id=1, source_target_pairs={{0,64},{8,72},{16,80},{24,88},{32,96},{40,104},{48,112},{56,120},{... | collective-permute-start | bytes 2752520 | tf_op jit(solution)/shard_map/ppermute | solution.py:448
  17.9 37.4 %collective-permute-start.1 = (bf16[224,2048]{1,0:T(8,128)(2,1)}, bf16[224,2048]{1,0:T(8,128)(2,1)}, u32[]{:S(2)}, u32[]{:S(2)}) collective-permute-start(bf16[224,2048]{1,0:T(8,128)(2,1)} %bitcast.16), channel_id=1, source_target_pairs={{0,192},{8,200},{16,208},{24,216},{32,224},{40,232},{48,240},{56,2... | collective-permute-start | bytes 2752520 | tf_op jit(solution)/shard_map/ppermute | solution.py:448
  21.5 0.7 copy-start.5
  22.2 0.6 copy-start.7
  22.8 6.1 %collective-permute-start.2 = (bf16[640,128]{1,0:T(8,128)(2,1)}, bf16[640,128]{1,0:T(8,128)(2,1)S(1)}, u32[]{:S(2)}, u32[]{:S(2)}) collective-permute-start(bf16[640,128]{1,0:T(8,128)(2,1)} %get-tuple-element.23), channel_id=1, source_target_pairs={{0,2},{1,3},{2,4},{3,5},{4,6},{5,7},{6,0},{7,1},{8,10},{9,11},{10,... | collective-permute-start | bytes 491528 | tf_op jit(solution)/shard_map/ppermute | solution.py:444
  24.1 9.2 %collective-permute-start.4 = (bf16[640,128]{1,0:T(8,128)(2,1)}, bf16[640,128]{1,0:T(8,128)(2,1)S(1)}, u32[]{:S(2)}, u32[]{:S(2)}) collective-permute-start(bf16[640,128]{1,0:T(8,128)(2,1)} %get-tuple-element.23), channel_id=1, source_target_pairs={{0,6},{1,7},{2,0},{3,1},{4,2},{5,3},{6,4},{7,5},{8,14},{9,15},{10,... | collective-permute-start | bytes 491528 | tf_op jit(solution)/shard_map/ppermute | solution.py:444
  25.5 7.7 %collective-permute-start.3 = (bf16[640,128]{1,0:T(8,128)(2,1)S(1)}, bf16[640,128]{1,0:T(8,128)(2,1)S(1)}, u32[]{:S(2)}, u32[]{:S(2)}) collective-permute-start(bf16[640,128]{1,0:T(8,128)(2,1)S(1)} %get-tuple-element.25.refs_0_), channel_id=1, source_target_pairs={{0,4},{1,5},{2,6},{3,7},{4,0},{5,1},{6,2},{7,3},{8,12},{9,13},{10,... | collective-permute-start | bytes 491528 | tf_op jit(solution)/shard_map/ppermute | solution.py:444
  55.3 13.3 %copy-start.2 = (bf16[224,2048]{1,0:T(8,128)(2,1)}, bf16[224,2048]{1,0:T(8,128)(2,1)S(1)}, u32[]{:S(2)}) copy-start(bf16[224,2048]{1,0:T(8,128)(2,1)S(1)} %collective-permute-done.near_hbm) | copy-start | bytes 2752516
  58.9 3.4 %collective-permute-start.5 = (bf16[2,320,640]{2,1,0:T(8,128)(2,1)S(1)}, bf16[2,320,640]{2,1,0:T(8,128)(2,1)S(1)}, u32[]{:S(2)}, u32[]{:S(2)}) collective-permute-start(bf16[2,320,640]{2,1,0:T(8,128)(2,1)S(1)} %shard_map.129.key_ref), channel_id=1, source_target_pairs={{0,1},{1,0},{2,3},{3,2},{4,5},{5,4},{6,7},{7,6},{8,9},{9,8},{10,11... | collective-permute-start | bytes 2457608 | tf_op jit(solution)/shard_map/ppermute | solution.py:572
  64.3 13.4 %copy-start = (bf16[16,512,128]{2,1,0:T(8,128)(2,1)S(1)}, bf16[16,512,128]{2,1,0:T(8,128)(2,1)}, u32[]{:S(2)}) copy-start(bf16[16,512,128]{2,1,0:T(8,128)(2,1)} %w_ref.3) | copy-start | bytes 6291460
  64.3 13.4 %all-to-all-start.1 = ((bf16[4,528,128]{2,1,0:T(8,128)(2,1)}), bf16[4,528,128]{2,1,0:T(8,128)(2,1)S(1)}, u32[]{:S(2)}, u32[]{:S(2)}) async-start(bf16[4,528,128]{2,1,0:T(8,128)(2,1)} %shard_map.131), calls=%async_computation.1 | async-start | bytes 1081344 | tf_op jit(solution)/shard_map/all_to_all | solution.py:594
  69.5 21.9 %collective-permute-start.6 = (bf16[112,2048]{1,0:T(8,128)(2,1)}, bf16[112,2048]{1,0:T(8,128)(2,1)S(1)}, u32[]{:S(2)}, u32[]{:S(2)}) collective-permute-start(bf16[112,2048]{1,0:T(8,128)(2,1)} %slice.10), channel_id=1, source_target_pairs={{0,64},{8,72},{16,80},{24,88},{32,96},{40,104},{48,112},{56,120},{... | collective-permute-start | bytes 1376264 | tf_op jit(solution)/shard_map/ppermute | solution.py:448
  71.7 19.7 %collective-permute-start.7 = (bf16[112,2048]{1,0:T(8,128)(2,1)}, bf16[112,2048]{1,0:T(8,128)(2,1)}, u32[]{:S(2)}, u32[]{:S(2)}) collective-permute-start(bf16[112,2048]{1,0:T(8,128)(2,1)} %slice.11), channel_id=1, source_target_pairs={{0,192},{8,200},{16,208},{24,216},{32,224},{40,232},{48,240},{56,2... | collective-permute-start | bytes 1376264 | tf_op jit(solution)/shard_map/ppermute | solution.py:448
  77.8 1.0 copy-start.6
  78.7 0.7 copy-start.8
  80.9 15.9 %all-to-all-start.2 = ((bf16[8,8,2048]{2,1,0:T(8,128)(2,1)}), bf16[8,8,2048]{2,1,0:T(8,128)(2,1)S(1)}, u32[]{:S(2)}, u32[]{:S(2)}) async-start(bf16[8,8,2048]{2,1,0:T(8,128)(2,1)} %shard_map.132), calls=%async_computation.2 | async-start | bytes 524288 | tf_op jit(solution)/shard_map/all_to_all | solution.py:607
  87.3 1.2 %copy-start.3 = (bf16[224,2048]{1,0:T(8,128)(2,1)S(1)}, bf16[224,2048]{1,0:T(8,128)(2,1)}, u32[]{:S(2)}) copy-start(bf16[224,2048]{1,0:T(8,128)(2,1)} %copy-done.2) | copy-start | bytes 2752516
  88.5 1.2 %copy-start.4 = (bf16[2048,224]{0,1:T(8,128)(2,1)S(1)}, bf16[2048,224]{0,1:T(8,128)(2,1)}, u32[]{:S(2)}) copy-start(bf16[2048,224]{0,1:T(8,128)(2,1)} %param.25) | copy-start | bytes 2752516
  112.2 4.5 %collective-permute-start.8 = (f32[4,8,224]{2,1,0:T(8,128)S(1)}, f32[4,8,224]{2,1,0:T(8,128)S(1)}, u32[]{:S(2)}, u32[]{:S(2)}) collective-permute-start(f32[4,8,224]{2,1,0:T(8,128)S(1)} %get-tuple-element.34), channel_id=1, source_target_pairs={{0,1},{1,0},{2,3},{3,2},{4,5},{5,4},{6,7},{7,6},{8,9},{9,8},{10,11... | collective-permute-start | bytes 86024 | tf_op jit(solution)/shard_map/ppermute | solution.py:644

commit v12 on v9

--- a/solution.py
+++ b/solution.py
@@ -387,14 +387,9 @@
         copy.wait()
 
 
-def project_kernel(width, x_ref, w_ref, opp_a_hbm, opp_b_hbm, out_ref, opp_ref, sem_ref):
-    size = opp_a_hbm.shape[0]
-    copies = [
-        pltpu.make_async_copy(opp_a_hbm, opp_ref.at[pl.ds(0, size)], sem_ref.at[0]),
-        pltpu.make_async_copy(opp_b_hbm, opp_ref.at[pl.ds(size, size)], sem_ref.at[1]),
-    ]
-    for copy in copies:
-        copy.start()
+def project_kernel(width, x_ref, w_ref, opposite_hbm, out_ref, opposite_ref, sem_ref):
+    copy = pltpu.make_async_copy(opposite_hbm, opposite_ref, sem_ref.at[0])
+    copy.start()
     here = lax.axis_index("row") // NZ
 
     def put(k, block):
@@ -405,9 +400,8 @@
 
     for i, k in enumerate((0, NX - 1, 1)):
         put(k, dot_t(x_ref[...], w_ref[i]))
-    for copy in copies:
-        copy.wait()
-    put(2, dot_t(x_ref[...], opp_ref[...]))
+    copy.wait()
+    put(2, dot_t(x_ref[...], opposite_ref[...]))
 
 
 def sum_kernel(in_ref, keep_ref, send_ref):
@@ -532,7 +526,7 @@
     all_queries = [shift_y((query, swapped)[k % 2], n_head, k) for k in range(NX)]
 
     w_t = w_o.T
-    w_near, w_far = shift_x(w_t, 1), shift_x(w_t, -1)
+    w_near, w_far, w_opposite = shift_x(w_t, 1), shift_x(w_t, -1), shift_x(w_t, 2)
 
     slot_ids = jnp.arange(pages_row, dtype=jnp.int32)
     holds = (page_table[:, :, None] == slot_ids[None, None, :]).astype(jnp.int32)
@@ -572,8 +566,6 @@
         flops=2 * tokens * asked * (2 * lat_w + TAIL),
         nbytes=2 * tokens * lat_w,
     )
-    size = w_t.shape[0] // 2
-    opposite = [shift_x(w_near[:size], 1), shift_x(w_far[size:], -1)]
     parts = call(
         functools.partial(both_kernel, scale),
         tuple(jax.ShapeDtypeStruct((lat_w + INFO, queries), bf16) for _ in range(NX)),
@@ -608,11 +600,11 @@
     sums = call(
         functools.partial(project_kernel, width),
         jax.ShapeDtypeStruct((NZ * NX, width, cols), bf16),
-        [ring.reshape(NZ * width, heads * value_w), w_ring] + opposite,
-        scratch=[pltpu.VMEM(w_t.shape, bf16), pltpu.SemaphoreType.DMA((2,))],
+        [ring.reshape(NZ * width, heads * value_w), w_ring, w_opposite],
+        scratch=[pltpu.VMEM(w_t.shape, bf16), pltpu.SemaphoreType.DMA((1,))],
         flops=2 * NX * NZ * width * w_o.size,
         nbytes=2 * NX * w_o.size,
-        in_hbm=(2, 3),
+        in_hbm=(2,),
     )
     planes = [
         [(x * NZ + z) * n_head + y * cores + core for z in range(NZ) for y in range(NX)]

time: 114 us -> 115 us (level)
  waiting for transfers between devices: 40.2 us -> 46.9 us
  local copies, waits for them, and re-layouts: 6.53 us -> 2.66 us
  starting transfers between devices: 37 us -> 35.4 us
    ppermute x6, waiting for transfers between devices: 9.19 us -> 14.6 us  [shift_y(): lax.ppermute(x, 'head', [(h, (h + k * cores) % n_head) for h in range(n_h...]
    slice x2 -> x0, local copies, waits for them, and re-layouts: 2.66 us -> none  [on_device(): opposite = [shift_x(w_near[:size], 1), shift_x(w_far[size:], -1)]]
    all_to_all x1, waiting for transfers between devices: 6.68 us -> 8.27 us  [on_device(): lax.all_to_all(head_out, 'row', split_axis=0, concat_axis=0, axis_index_g...]
    ppermute x4 -> x3, starting transfers between devices: 5.43 us -> 4.01 us  [shift_x(): lax.ppermute(x, 'row', [(a * NZ + b, (a + k) % NX * NZ + b) for a in rang...]
    unnamed x27 -> x25, local copies, waits for them, and re-layouts: 3.22 us -> 2.02 us
    ppermute x4 -> x3, waiting for transfers between devices: 22.7 us -> 23.2 us  [shift_x(): lax.ppermute(x, 'row', [(a * NZ + b, (a + k) % NX * NZ + b) for a in rang...]
  transfers between devices with their start and end apart: 14 -> 13, of which waited for: 7 -> 8; matrix products, arithmetic and copies ran while one was open for 3% -> 1% of each run, Pallas kernels for 5% -> 6%
where the time goes in v12:
time: 115 us; the launch traced here: 114 us
  waiting for transfers between devices  46.9 us (41%)
  starting transfers between devices  35.4 us (31%)
  Pallas kernels  16.5 us (14%)
  blocking collectives  12.4 us (11%)
  local copies, waits for them, and re-layouts  2.66 us (2%)
    ppermute x3, waiting for transfers between devices, shift_x(): lax.ppermute(x, 'row', [(a * NZ + b, (a + k) % NX * NZ + b) for a in rang...  23.2 us
    pallas_call x10, Pallas kernels, call(): pl.pallas_call(body, out_shape=out_shape, in_specs=[HBM if i in in_hbm el...  16.5 us
    ppermute x6, waiting for transfers between devices, shift_y(): lax.ppermute(x, 'head', [(h, (h + k * cores) % n_head) for h in range(n_h...  14.6 us
    all_to_all x1, blocking collectives, on_device(): lax.all_to_all(sums, ('row', 'head'), split_axis=0, concat_axis=0, axis_i...  12.4 us
    all_to_all x1, starting transfers between devices, on_device(): got = lax.all_to_all(send, 'row', split_axis=0, concat_axis=0, tiled=True)  12.1 us
    ppermute x6, starting transfers between devices, shift_y(): lax.ppermute(x, 'head', [(h, (h + k * cores) % n_head) for h in range(n_h...  8.42 us
    all_to_all x1, waiting for transfers between devices, on_device(): lax.all_to_all(head_out, 'row', split_axis=0, concat_axis=0, axis_index_g...  8.27 us
    all_to_all x1, starting transfers between devices, on_device(): lax.all_to_all(head_out, 'row', split_axis=0, concat_axis=0, axis_index_g...  6.39 us
  transfers between devices with their start and end apart: 13, of which 8 were waited for; matrix products, arithmetic and copies ran while one was open for 1% of the time, Pallas kernels for 6%

profile of v12, /device:TPU:1, one launch (start us, length us, event | category | flops | bytes accessed | tf_op | source)
XLA Modules:
  0.0 114.5 jit_solution(14268669199074800804)
XLA Ops:
  0.0 4.0 %shard_map.128 = bf16[32,184,128]{2,1,0:T(8,128)(2,1)} custom-call(s32[1,80]{1,0:T(1,128)} %bitcast.19, s32[1,80]{1,0:T(1,128)} %bitcast.20, bf16[80,64,512]{2,1,0:T(8,128)(2,1)} %lat_hbm.1, bf16[80,4096]{1,0:T(8,128)(2,1)} %rope_hbm.1), custom_call_target="tpu_custom_call" | custom-call | flops 838860800 | bytes 2621440 | tf_op jit(solution)/shard_map/pallas_call | solution.py:26
  4.0 0.0 copy-start.8
  4.1 0.0 copy-start.9
  4.1 0.0 copy-start.6
  4.1 0.0 copy-start.7
  4.1 0.0 copy-start.1
  4.1 12.1 %all-to-all-start = ((bf16[32,184,128]{2,1,0:T(8,128)(2,1)}), bf16[32,184,128]{2,1,0:T(8,128)(2,1)}, u32[]{:S(2)}, u32[]{:S(2)}) async-start(bf16[32,184,128]{2,1,0:T(8,128)(2,1)} %shard_map.128), calls=%async_computation | async-start | bytes 3014656 | tf_op jit(solution)/shard_map/all_to_all | solution.py:495
  16.3 1.2 %collective-permute-start = (bf16[224,2048]{1,0:T(8,128)(2,1)}, bf16[224,2048]{1,0:T(8,128)(2,1)S(1)}, u32[]{:S(2)}, u32[]{:S(2)}) collective-permute-start(bf16[224,2048]{1,0:T(8,128)(2,1)} %bitcast.8.own_hbm), channel_id=1, source_target_pairs={{0,64},{8,72},{16,80},{24,88},{32,96},{40,104},{48,112},{56,120},{... | collective-permute-start | bytes 2752520 | tf_op jit(solution)/shard_map/ppermute | solution.py:433
  17.5 1.5 %collective-permute-start.1 = (bf16[224,2048]{1,0:T(8,128)(2,1)}, bf16[224,2048]{1,0:T(8,128)(2,1)}, u32[]{:S(2)}, u32[]{:S(2)}) collective-permute-start(bf16[224,2048]{1,0:T(8,128)(2,1)} %bitcast.8.own_hbm), channel_id=1, source_target_pairs={{0,192},{8,200},{16,208},{24,216},{32,224},{40,232},{48,240},{56,2... | collective-permute-start | bytes 2752520 | tf_op jit(solution)/shard_map/ppermute | solution.py:433
  19.0 0.1 pad.3.clone
  19.1 0.2 copy.32
  19.3 0.1 copy.35
  19.5 0.1 reshape.88
  19.6 0.1 pad.5.clone
  19.7 0.9 shard_map.127
  20.6 0.7 copy-done.4
  21.3 1.3 %collective-permute-start.2 = (bf16[640,128]{1,0:T(8,128)(2,1)S(1)}, bf16[640,128]{1,0:T(8,128)(2,1)S(1)}, u32[]{:S(2)}, u32[]{:S(2)}) collective-permute-start(bf16[640,128]{1,0:T(8,128)(2,1)S(1)} %get-tuple-element.27), channel_id=1, source_target_pairs={{0,2},{1,3},{2,4},{3,5},{4,6},{5,7},{6,0},{7,1},{8,10},{9,11},{10,... | collective-permute-start | bytes 491528 | tf_op jit(solution)/shard_map/ppermute | solution.py:429
  22.6 1.4 %collective-permute-start.4 = (bf16[640,128]{1,0:T(8,128)(2,1)S(1)}, bf16[640,128]{1,0:T(8,128)(2,1)S(1)}, u32[]{:S(2)}, u32[]{:S(2)}) collective-permute-start(bf16[640,128]{1,0:T(8,128)(2,1)S(1)} %get-tuple-element.27), channel_id=1, source_target_pairs={{0,6},{1,7},{2,0},{3,1},{4,2},{5,3},{6,4},{7,5},{8,14},{9,15},{10,... | collective-permute-start | bytes 491528 | tf_op jit(solution)/shard_map/ppermute | solution.py:429
  24.0 1.6 %collective-permute-start.3 = (bf16[640,128]{1,0:T(8,128)(2,1)S(1)}, bf16[640,128]{1,0:T(8,128)(2,1)S(1)}, u32[]{:S(2)}, u32[]{:S(2)}) collective-permute-start(bf16[640,128]{1,0:T(8,128)(2,1)S(1)} %get-tuple-element.29.refs_0_), channel_id=1, source_target_pairs={{0,4},{1,5},{2,6},{3,7},{4,0},{5,1},{6,2},{7,3},{8,12},{9,13},{10,... | collective-permute-start | bytes 491528 | tf_op jit(solution)/shard_map/ppermute | solution.py:429
  25.7 0.1 select_reduce_fusion
  25.8 0.1 subtract_subtract_fusion
  25.8 0.1 compare_select_fusion
  25.9 0.1 select_n.16.bias_ref
  26.1 1.1 collective-permute-done.2.refs_1_
  27.1 4.5 %collective-permute-done.3.refs_2_ = bf16[640,128]{1,0:T(8,128)(2,1)S(1)} collective-permute-done((bf16[640,128]{1,0:T(8,128)(2,1)S(1)}, bf16[640,128]{1,0:T(8,128)(2,1)S(1)}, u32[]{:S(2)}, u32[]{:S(2)}) %collective-permute-start.3) | collective-permute-done | bytes 163872 | tf_op jit(solution)/shard_map/ppermute | solution.py:429
  31.7 23.2 %collective-permute-done.near_hbm = bf16[224,2048]{1,0:T(8,128)(2,1)S(1)} collective-permute-done((bf16[224,2048]{1,0:T(8,128)(2,1)}, bf16[224,2048]{1,0:T(8,128)(2,1)S(1)}, u32[]{:S(2)}, u32[]{:S(2)}) %collective-permute-start) | collective-permute-done | bytes 917536 | tf_op jit(solution)/shard_map/ppermute | solution.py:433
  54.9 3.7 %shard_map.129.key_ref = bf16[2,320,640]{2,1,0:T(8,128)(2,1)S(1)} custom-call(bf16[32,184,128]{2,1,0:T(8,128)(2,1)} %all-to-all-done.block_hbm, f32[640,1]{1,0:T(8,128)S(1)} %select_n.16.bias_ref), custom_call_target="tpu_custom_call" | custom-call | flops 838860800 | bytes 1310720 | tf_op jit(solution)/shard_map/pallas_call | solution.py:26
  58.6 0.0 copy-start
  58.6 1.4 %collective-permute-start.5 = (bf16[2,320,640]{2,1,0:T(8,128)(2,1)S(1)}, bf16[2,320,640]{2,1,0:T(8,128)(2,1)S(1)}, u32[]{:S(2)}, u32[]{:S(2)}) collective-permute-start(bf16[2,320,640]{2,1,0:T(8,128)(2,1)S(1)} %shard_map.129.key_ref), channel_id=1, source_target_pairs={{0,1},{1,0},{2,3},{3,2},{4,5},{5,4},{6,7},{7,6},{8,9},{9,8},{10,11... | collective-permute-start | bytes 2457608 | tf_op jit(solution)/shard_map/ppermute | solution.py:557
  60.0 1.3 %collective-permute-start.9 = (bf16[224,2048]{1,0:T(8,128)(2,1)}, bf16[224,2048]{1,0:T(8,128)(2,1)}, u32[]{:S(2)}, u32[]{:S(2)}) collective-permute-start(bf16[224,2048]{1,0:T(8,128)(2,1)} %bitcast.8.own_hbm), channel_id=1, source_target_pairs={{0,128},{8,136},{16,144},{24,152},{32,160},{40,168},{48,176},{56,1... | collective-permute-start | bytes 2752520 | tf_op jit(solution)/shard_map/ppermute | solution.py:433
  61.3 1.2 %shard_map.130 = (f32[2,512,256]{2,1,0:T(8,128)S(1)}, f32[2,8,256]{2,1,0:T(8,128)S(1)}) custom-call(bf16[2,320,640]{2,1,0:T(8,128)(2,1)S(1)} %shard_map.129.key_ref, bf16[640,128]{1,0:T(8,128)(2,1)S(1)} %get-tuple-element.29.refs_0_, bf16[640,128]{1,0:T(8,128)(2,1)S(1)} %collective-permute-done.2.refs_1_, ...), custom_call_target="tpu_custom_call" | custom-call | flops 377487360 | bytes 655360 | tf_op jit(solution)/shard_map/pallas_call | solution.py:26
  62.5 1.2 %shard_map.131 = (bf16[528,128]{1,0:T(8,128)(2,1)S(1)}, bf16[528,128]{1,0:T(8,128)(2,1)S(1)}, bf16[528,128]{1,0:T(8,128)(2,1)S(1)}, bf16[528,128]{1,0:T(8,128)(2,1)S(1)}) custom-call(bf16[2,320,640]{2,1,0:T(8,128)(2,1)S(1)} %collective-permute-done.5.key_ref, f32[2,512,256]{2,1,0:T(8,128)S(1)} %get-tuple-element.33.own_ref, ...), custom_call_target="tpu_custom_call" | custom-call | flops 377487360 | bytes 655360 | tf_op jit(solution)/shard_map/pallas_call | solution.py:26
  63.7 3.0 %collective-permute-start.6 = (bf16[528,128]{1,0:T(8,128)(2,1)S(1)}, bf16[528,128]{1,0:T(8,128)(2,1)S(1)}, u32[]{:S(2)}, u32[]{:S(2)}) collective-permute-start(bf16[528,128]{1,0:T(8,128)(2,1)S(1)} %get-tuple-element.36), channel_id=1, source_target_pairs={{0,6},{1,7},{2,0},{3,1},{4,2},{5,3},{6,4},{7,5},{8,14},{9,15},{10,... | collective-permute-start | bytes 405512 | tf_op jit(solution)/shard_map/ppermute | solution.py:429
  66.7 0.3 collective-permute-start.7
  67.0 0.7 collective-permute-start.8
  67.7 4.3 %collective-permute-done.6.refs_1_ = bf16[528,128]{1,0:T(8,128)(2,1)S(1)} collective-permute-done((bf16[528,128]{1,0:T(8,128)(2,1)S(1)}, bf16[528,128]{1,0:T(8,128)(2,1)S(1)}, u32[]{:S(2)}, u32[]{:S(2)}) %collective-permute-start.6) | collective-permute-done | bytes 135200 | tf_op jit(solution)/shard_map/ppermute | solution.py:429
  72.0 0.8 collective-permute-done.7.refs_2_
  72.8 3.9 %collective-permute-done.8.refs_3_ = bf16[528,128]{1,0:T(8,128)(2,1)S(1)} collective-permute-done((bf16[528,128]{1,0:T(8,128)(2,1)S(1)}, bf16[528,128]{1,0:T(8,128)(2,1)S(1)}, u32[]{:S(2)}, u32[]{:S(2)}) %collective-permute-start.8) | collective-permute-done | bytes 135200 | tf_op jit(solution)/shard_map/ppermute | solution.py:429
  76.7 1.6 %shard_map.132 = bf16[8,8,2048]{2,1,0:T(8,128)(2,1)} custom-call(f32[512,128]{1,0:T(8,128)S(1)} %copy-done.5, f32[8,128]{1,0:T(8,128)S(1)} %get-tuple-element.25.fresh_lse_ref, bf16[16,512,128]{2,1,0:T(8,128)(2,1)S(1)} %copy-done, bf16[528,128]{1,0:T(8,128)(2,1)S(1)} %get-tuple-element.35.refs_0_, bf16[528,128]{1,0:T(8,128)(2,1)S(1)} %collective-permute-done.6.refs_1_, ...), custom_call_target="tpu_custom_call" | custom-call | flops 16777216 | bytes 2097152 | tf_op jit(solution)/shard_map/pallas_call | solution.py:26
  78.3 6.4 %all-to-all-start.1 = ((bf16[8,8,2048]{2,1,0:T(8,128)(2,1)}), bf16[8,8,2048]{2,1,0:T(8,128)(2,1)S(1)}, u32[]{:S(2)}, u32[]{:S(2)}) async-start(bf16[8,8,2048]{2,1,0:T(8,128)(2,1)} %shard_map.132), calls=%async_computation.1 | async-start | bytes 524288 | tf_op jit(solution)/shard_map/all_to_all | solution.py:587
  84.6 1.2 %copy-done.3 = bf16[224,2048]{1,0:T(8,128)(2,1)S(1)} copy-done((bf16[224,2048]{1,0:T(8,128)(2,1)S(1)}, bf16[224,2048]{1,0:T(8,128)(2,1)}, u32[]{:S(2)}) %copy-start.3) | copy-done | bytes 917528
  85.8 1.5 %shard_map.133.w_ref = bf16[3,224,2048]{2,1,0:T(8,128)(2,1)S(1)} custom-call(bf16[224,2048]{1,0:T(8,128)(2,1)} %bitcast.8.own_hbm, bf16[224,2048]{1,0:T(8,128)(2,1)S(1)} %copy-done.3, bf16[224,2048]{1,0:T(8,128)(2,1)} %collective-permute-done.1.far_hbm), custom_call_target="tpu_custom_call" | custom-call | bytes 5505024 | tf_op jit(solution)/shard_map/pallas_call | solution.py:26
  87.4 8.3 %all-to-all-done.1 = bf16[8,8,2048]{2,1,0:T(8,128)(2,1)S(1)} async-done(((bf16[8,8,2048]{2,1,0:T(8,128)(2,1)}), bf16[8,8,2048]{2,1,0:T(8,128)(2,1)S(1)}, u32[]{:S(2)}, u32[]{:S(2)}) %all-to-all-start.1) | async-done | bytes 262176 | tf_op jit(solution)/shard_map/all_to_all | solution.py:587
  95.6 1.8 %shard_map.134 = bf16[32,8,224]{2,1,0:T(8,128)(2,1)S(1)} custom-call(bf16[64,2048]{1,0:T(8,128)(2,1)S(1)} %bitcast.14, bf16[3,224,2048]{2,1,0:T(8,128)(2,1)S(1)} %shard_map.133.w_ref, bf16[224,2048]{1,0:T(8,128)(2,1)} %collective-permute-done.9.opposite_hbm), custom_call_target="tpu_custom_call" | custom-call | flops 234881024 | bytes 3670016 | tf_op jit(solution)/shard_map/pallas_call | solution.py:26
  97.5 12.4 %all_to_all.15.in_ref = bf16[32,8,224]{2,1,0:T(8,128)(2,1)S(1)} all-to-all(bf16[32,8,224]{2,1,0:T(8,128)(2,1)S(1)} %shard_map.134), channel_id=1, replica_groups={{0,2,4,6,8,10,12,14,16,18,20,22,24,26,28,30,32,34,36,38,40,42,44,46,48,..., dimensions={0} | all-to-all | bytes 229376 | tf_op jit(solution)/shard_map/all_to_all | solution.py:614
  109.9 3.1 %collective-permute-start.10 = (f32[4,8,224]{2,1,0:T(8,128)S(1)}, f32[4,8,224]{2,1,0:T(8,128)S(1)}, u32[]{:S(2)}, u32[]{:S(2)}) collective-permute-start(f32[4,8,224]{2,1,0:T(8,128)S(1)} %get-tuple-element.42), channel_id=1, source_target_pairs={{0,1},{1,0},{2,3},{3,2},{4,5},{5,4},{6,7},{7,6},{8,9},{9,8},{10,11... | collective-permute-start | bytes 86024 | tf_op jit(solution)/shard_map/ppermute | solution.py:624
  112.9 0.9 collective-permute-done.10.got_ref
  113.8 0.7 shard_map.136
  (32 shorter events, 0.2 us)
Async XLA Ops:
  4.0 15.0 %copy-start.8 = (bf16[4,2,512]{2,1,0:T(2,128)(2,1)S(1)}, bf16[4,2,512]{2,1,0:T(2,128)(2,1)}, u32[]{:S(2)}) copy-start(bf16[4,2,512]{2,1,0:T(2,128)(2,1)} %param.15) | copy-start | bytes 24580
  4.1 15.1 %copy-start.9 = (bf16[4,2,64]{2,1,0:T(2,128)(2,1)S(1)}, bf16[4,2,64]{2,1,0:T(2,128)(2,1)}, u32[]{:S(2)}) copy-start(bf16[4,2,64]{2,1,0:T(2,128)(2,1)} %param.16) | copy-start | bytes 3076
  4.1 15.4 %copy-start.6 = (bf16[4,2,16,128]{3,2,1,0:T(8,128)(2,1)S(1)}, bf16[4,2,16,128]{3,2,1,0:T(8,128)(2,1)}, u32[]{:S(2)}) copy-start(bf16[4,2,16,128]{3,2,1,0:T(8,128)(2,1)} %param.13) | copy-start | bytes 98308
  4.1 15.4 %copy-start.7 = (bf16[4,2,1024]{2,1,0:T(2,128)(2,1)S(1)}, bf16[4,2,1024]{2,1,0:T(2,128)(2,1)}, u32[]{:S(2)}) copy-start(bf16[4,2,1024]{2,1,0:T(2,128)(2,1)} %param.14) | copy-start | bytes 49156
  4.1 15.6 %copy-start.1 = (bf16[16,128,512]{2,1,0:T(8,128)(2,1)S(1)}, bf16[16,128,512]{2,1,0:T(8,128)(2,1)}, u32[]{:S(2)}) copy-start(bf16[16,128,512]{2,1,0:T(8,128)(2,1)} %w_ref.2) | copy-start | bytes 6291460
  4.1 50.8 %all-to-all-start = ((bf16[32,184,128]{2,1,0:T(8,128)(2,1)}), bf16[32,184,128]{2,1,0:T(8,128)(2,1)}, u32[]{:S(2)}, u32[]{:S(2)}) async-start(bf16[32,184,128]{2,1,0:T(8,128)(2,1)} %shard_map.128), calls=%async_computation | async-start | bytes 3014656 | tf_op jit(solution)/shard_map/all_to_all | solution.py:495
  16.2 9.4 %copy-start.10 = (s32[2,40]{1,0:T(2,128)S(1)}, s32[2,40]{1,0:T(2,128)}, u32[]{:S(2)}) copy-start(s32[2,40]{1,0:T(2,128)} %param.21) | copy-start | bytes 964
  16.2 9.5 %copy-start.11 = (s32[2]{0:T(128)S(1)}, s32[2]{0:T(128)}, u32[]{:S(2)}) copy-start(s32[2]{0:T(128)} %param.22) | copy-start | bytes 28
  16.3 38.7 %collective-permute-start = (bf16[224,2048]{1,0:T(8,128)(2,1)}, bf16[224,2048]{1,0:T(8,128)(2,1)S(1)}, u32[]{:S(2)}, u32[]{:S(2)}) collective-permute-start(bf16[224,2048]{1,0:T(8,128)(2,1)} %bitcast.8.own_hbm), channel_id=1, source_target_pairs={{0,64},{8,72},{16,80},{24,88},{32,96},{40,104},{48,112},{56,120},{... | collective-permute-start | bytes 2752520 | tf_op jit(solution)/shard_map/ppermute | solution.py:433
  17.5 37.4 %collective-permute-start.1 = (bf16[224,2048]{1,0:T(8,128)(2,1)}, bf16[224,2048]{1,0:T(8,128)(2,1)}, u32[]{:S(2)}, u32[]{:S(2)}) collective-permute-start(bf16[224,2048]{1,0:T(8,128)(2,1)} %bitcast.8.own_hbm), channel_id=1, source_target_pairs={{0,192},{8,200},{16,208},{24,216},{32,224},{40,232},{48,240},{56,2... | collective-permute-start | bytes 2752520 | tf_op jit(solution)/shard_map/ppermute | solution.py:433
  20.6 0.7 copy-start.4
  21.3 5.8 %collective-permute-start.2 = (bf16[640,128]{1,0:T(8,128)(2,1)S(1)}, bf16[640,128]{1,0:T(8,128)(2,1)S(1)}, u32[]{:S(2)}, u32[]{:S(2)}) collective-permute-start(bf16[640,128]{1,0:T(8,128)(2,1)S(1)} %get-tuple-element.27), channel_id=1, source_target_pairs={{0,2},{1,3},{2,4},{3,5},{4,6},{5,7},{6,0},{7,1},{8,10},{9,11},{10,... | collective-permute-start | bytes 491528 | tf_op jit(solution)/shard_map/ppermute | solution.py:429
  22.6 9.1 %collective-permute-start.4 = (bf16[640,128]{1,0:T(8,128)(2,1)S(1)}, bf16[640,128]{1,0:T(8,128)(2,1)S(1)}, u32[]{:S(2)}, u32[]{:S(2)}) collective-permute-start(bf16[640,128]{1,0:T(8,128)(2,1)S(1)} %get-tuple-element.27), channel_id=1, source_target_pairs={{0,6},{1,7},{2,0},{3,1},{4,2},{5,3},{6,4},{7,5},{8,14},{9,15},{10,... | collective-permute-start | bytes 491528 | tf_op jit(solution)/shard_map/ppermute | solution.py:429
  24.0 7.6 %collective-permute-start.3 = (bf16[640,128]{1,0:T(8,128)(2,1)S(1)}, bf16[640,128]{1,0:T(8,128)(2,1)S(1)}, u32[]{:S(2)}, u32[]{:S(2)}) collective-permute-start(bf16[640,128]{1,0:T(8,128)(2,1)S(1)} %get-tuple-element.29.refs_0_), channel_id=1, source_target_pairs={{0,4},{1,5},{2,6},{3,7},{4,0},{5,1},{6,2},{7,3},{8,12},{9,13},{10,... | collective-permute-start | bytes 491528 | tf_op jit(solution)/shard_map/ppermute | solution.py:429
  54.9 7.6 %copy-start.2 = (bf16[224,2048]{1,0:T(8,128)(2,1)}, bf16[224,2048]{1,0:T(8,128)(2,1)S(1)}, u32[]{:S(2)}) copy-start(bf16[224,2048]{1,0:T(8,128)(2,1)S(1)} %collective-permute-done.near_hbm) | copy-start | bytes 2752516
  58.6 18.1 %copy-start = (bf16[16,512,128]{2,1,0:T(8,128)(2,1)S(1)}, bf16[16,512,128]{2,1,0:T(8,128)(2,1)}, u32[]{:S(2)}) copy-start(bf16[16,512,128]{2,1,0:T(8,128)(2,1)} %w_ref.3) | copy-start | bytes 6291460
  58.6 18.1 %copy-start.5 = (f32[512,128]{1,0:T(8,128)S(1)}, f32[512,128]{1,0:T(8,128)}, u32[]{:S(2)}) copy-start(f32[512,128]{1,0:T(8,128)} %copy-done.4) | copy-start | bytes 786436
  58.6 3.9 %collective-permute-start.5 = (bf16[2,320,640]{2,1,0:T(8,128)(2,1)S(1)}, bf16[2,320,640]{2,1,0:T(8,128)(2,1)S(1)}, u32[]{:S(2)}, u32[]{:S(2)}) collective-permute-start(bf16[2,320,640]{2,1,0:T(8,128)(2,1)S(1)} %shard_map.129.key_ref), channel_id=1, source_target_pairs={{0,1},{1,0},{2,3},{3,2},{4,5},{5,4},{6,7},{7,6},{8,9},{9,8},{10,11... | collective-permute-start | bytes 2457608 | tf_op jit(solution)/shard_map/ppermute | solution.py:557
  60.0 27.3 %collective-permute-start.9 = (bf16[224,2048]{1,0:T(8,128)(2,1)}, bf16[224,2048]{1,0:T(8,128)(2,1)}, u32[]{:S(2)}, u32[]{:S(2)}) collective-permute-start(bf16[224,2048]{1,0:T(8,128)(2,1)} %bitcast.8.own_hbm), channel_id=1, source_target_pairs={{0,128},{8,136},{16,144},{24,152},{32,160},{40,168},{48,176},{56,1... | collective-permute-start | bytes 2752520 | tf_op jit(solution)/shard_map/ppermute | solution.py:433
  63.7 8.4 %collective-permute-start.6 = (bf16[528,128]{1,0:T(8,128)(2,1)S(1)}, bf16[528,128]{1,0:T(8,128)(2,1)S(1)}, u32[]{:S(2)}, u32[]{:S(2)}) collective-permute-start(bf16[528,128]{1,0:T(8,128)(2,1)S(1)} %get-tuple-element.36), channel_id=1, source_target_pairs={{0,6},{1,7},{2,0},{3,1},{4,2},{5,3},{6,4},{7,5},{8,14},{9,15},{10,... | collective-permute-start | bytes 405512 | tf_op jit(solution)/shard_map/ppermute | solution.py:429
  66.7 6.1 %collective-permute-start.7 = (bf16[528,128]{1,0:T(8,128)(2,1)S(1)}, bf16[528,128]{1,0:T(8,128)(2,1)S(1)}, u32[]{:S(2)}, u32[]{:S(2)}) collective-permute-start(bf16[528,128]{1,0:T(8,128)(2,1)S(1)} %get-tuple-element.37), channel_id=1, source_target_pairs={{0,4},{1,5},{2,6},{3,7},{4,0},{5,1},{6,2},{7,3},{8,12},{9,13},{10,... | collective-permute-start | bytes 405512 | tf_op jit(solution)/shard_map/ppermute | solution.py:429
  67.0 9.7 %collective-permute-start.8 = (bf16[528,128]{1,0:T(8,128)(2,1)S(1)}, bf16[528,128]{1,0:T(8,128)(2,1)S(1)}, u32[]{:S(2)}, u32[]{:S(2)}) collective-permute-start(bf16[528,128]{1,0:T(8,128)(2,1)S(1)} %get-tuple-element.38), channel_id=1, source_target_pairs={{0,2},{1,3},{2,4},{3,5},{4,6},{5,7},{6,0},{7,1},{8,10},{9,11},{10,... | collective-permute-start | bytes 405512 | tf_op jit(solution)/shard_map/ppermute | solution.py:429
  78.3 17.4 %all-to-all-start.1 = ((bf16[8,8,2048]{2,1,0:T(8,128)(2,1)}), bf16[8,8,2048]{2,1,0:T(8,128)(2,1)S(1)}, u32[]{:S(2)}, u32[]{:S(2)}) async-start(bf16[8,8,2048]{2,1,0:T(8,128)(2,1)} %shard_map.132), calls=%async_computation.1 | async-start | bytes 524288 | tf_op jit(solution)/shard_map/all_to_all | solution.py:587
  84.6 1.2 %copy-start.3 = (bf16[224,2048]{1,0:T(8,128)(2,1)S(1)}, bf16[224,2048]{1,0:T(8,128)(2,1)}, u32[]{:S(2)}) copy-start(bf16[224,2048]{1,0:T(8,128)(2,1)} %copy-done.2) | copy-start | bytes 2752516
  109.9 3.9 %collective-permute-start.10 = (f32[4,8,224]{2,1,0:T(8,128)S(1)}, f32[4,8,224]{2,1,0:T(8,128)S(1)}, u32[]{:S(2)}, u32[]{:S(2)}) collective-permute-start(f32[4,8,224]{2,1,0:T(8,128)S(1)} %get-tuple-element.42), channel_id=1, source_target_pairs={{0,1},{1,0},{2,3},{3,2},{4,5},{5,4},{6,7},{7,6},{8,9},{9,8},{10,11... | collective-permute-start | bytes 86024 | tf_op jit(solution)/shard_map/ppermute | solution.py:624

commit v13 on v9

--- a/solution.py
+++ b/solution.py
@@ -199,14 +199,10 @@
     per_pair,
     rope_w,
     pages_row,
-    block_hbm,
+    block_ref,
     bias_ref,
     key_hbm,
-    block_ref,
-    lat_ref,
-    tail_ref,
     key_ref,
-    in_sem,
     out_sem,
 ):
     rows, per_row, key_w = key_ref.shape
@@ -219,15 +215,6 @@
     rope_rows = piece * rope_w // TAIL
     half = per_row // 2
 
-    chunks = in_sem.shape[0]
-    step = count // chunks
-    copies = []
-    for i in range(chunks):
-        here = pl.ds(i * step, step)
-        copy = pltpu.make_async_copy(block_hbm.at[here], block_ref.at[here], in_sem.at[i])
-        copy.start()
-        copies.append(copy)
-
     def spread_over(columns, group, lane):
         own = iota((count, columns), 0) == iota((1, columns), 1) // group
         return ones_where(iota((TAIL, columns), 0) == lane), jnp.where(own, 1.0, 0.0)
@@ -240,23 +227,15 @@
     lane = jnp.where(rope_inner < per_pair * rope_rows, rope_inner // rope_rows * piece, TAIL)
     rope_spread = spread_over(rope_columns, rest, lane)
 
-    labels = []
-    for i, copy in enumerate(copies):
-        copy.wait()
-        here = slice(i * step, (i + 1) * step)
-        tail = block_ref[here, lat_rows:, :].astype(jnp.float32)
-        marked = iota(tail.shape, 1) == per_pair * rope_rows
-        labels.append(jnp.sum(jnp.where(marked, tail, 0.0), axis=1))
-        tail_ref[i * step * rest : (i + 1) * step * rest, :] = tail.reshape(
-            step * rest, TAIL
-        ).astype(jnp.bfloat16)
-        lat = block_ref[here, :lat_rows, :].astype(jnp.float32)
-        lat = lat.reshape(step * per_pair, cuts, piece, TAIL)
-        for c in range(cuts):
-            lat_ref[i * step * pair_tokens : (i + 1) * step * pair_tokens, pl.ds(c * TAIL, TAIL)] = (
-                lat[:, c].reshape(step * pair_tokens, TAIL).astype(jnp.bfloat16)
-            )
-    labels = jnp.concatenate(labels, axis=0).astype(jnp.bfloat16)
+    tail = block_ref[:, lat_rows:, :].astype(jnp.float32)
+    marked = iota(tail.shape, 1) == per_pair * rope_rows
+    labels = jnp.sum(jnp.where(marked, tail, 0.0), axis=1).astype(jnp.bfloat16)
+    tail = tail.reshape(rope_columns, TAIL).astype(jnp.bfloat16)
+    lat = block_ref[:, :lat_rows, :].astype(jnp.float32)
+    lat = lat.reshape(count * per_pair, cuts, piece, TAIL)
+    lat = [lat[:, c].reshape(lat_columns, TAIL).astype(jnp.bfloat16) for c in range(cuts)]
+    lat = jnp.concatenate(lat, axis=1)
+    bias_all = bias_ref[...].T
 
     def slot_of(spread, own):
         wide = dot(labels, spread) * own
@@ -273,14 +252,14 @@
     copies = []
     for b in range(rows):
         pick = ones_where(iota((half, 1), 0) + b * half == rope_target)
-        rope_b = dot(pick, tail_ref[...])
+        rope_b = dot(pick, tail)
         rope_b = jnp.concatenate([rope_b, pltpu.roll(rope_b, TAIL - rope_w, 1)], axis=0)
         lane = iota(rope_b.shape, 1)
-        bias = bias_ref[b * per_row : (b + 1) * per_row]
+        bias = bias_all[b * per_row : (b + 1) * per_row, :1]
         rope_b = jnp.where(lane < rope_w, rope_b, jnp.where(lane == rope_w, bias, 0.0))
         key_ref[b, :, lat_w:] = rope_b.astype(jnp.bfloat16)
         pick = ones_where(iota((per_row, 1), 0) + b * per_row == target)
-        key_ref[b, :, :lat_w] = dot(pick, lat_ref[...]).astype(jnp.bfloat16)
+        key_ref[b, :, :lat_w] = dot(pick, lat).astype(jnp.bfloat16)
         copy = pltpu.make_async_copy(key_ref.at[b], key_hbm.at[b], out_sem.at[b])
         copy.start()
         copies.append(copy)
@@ -540,7 +519,8 @@
     limit = lengths[:, None] - logical * page_len - head * piece
     within = jnp.arange(piece, dtype=jnp.int32).reshape(piece // 2, 2).T
     usable = within[None, :, None, :] < limit[:, None, :, None]
-    bias = jnp.where(usable, 0.0, NEG).astype(f32).reshape(rows_dev * pages_row * piece, 1)
+    bias = jnp.where(usable, 0.0, NEG).astype(f32).reshape(1, rows_dev * pages_row * piece)
+    bias = jnp.broadcast_to(bias, (8, bias.shape[1]))
 
     got, w_near, w_far, all_queries = lax.optimization_barrier((got, w_near, w_far, all_queries))
     key = call(
@@ -548,17 +528,12 @@
         jax.ShapeDtypeStruct((rows_dev, pages_row * piece, lat_w + TAIL), bf16),
         [got, bias],
         scratch=[
-            pltpu.VMEM(got.shape, bf16),
-            pltpu.VMEM((slots, lat_w), bf16),
-            pltpu.VMEM((n_row * (block - lat_rows), TAIL), bf16),
             pltpu.VMEM((rows_dev, pages_row * piece, lat_w + TAIL), bf16),
-            pltpu.SemaphoreType.DMA((4,)),
             pltpu.SemaphoreType.DMA((rows_dev,)),
         ],
         flops=2 * slots * tokens * lat_w,
         nbytes=2 * slots * lat_w,
         out_spec=HBM,
-        in_hbm=(0,),
     )
     other = lax.ppermute(key, "head", [(h, h ^ 1) for h in range(n_head)])
     asked = NX * queries // rows_dev

time: 114 us -> 115 us (level)
  no operation moved by 1% of the time
where the time goes in v13:
time: 115 us; the launch traced here: 114 us
  waiting for transfers between devices  40.2 us (35%)
  starting transfers between devices  37 us (32%)
  Pallas kernels  17.4 us (15%)
  blocking collectives  12.4 us (11%)
  local copies, waits for them, and re-layouts  6.51 us (6%)
    ppermute x4, waiting for transfers between devices, shift_x(): lax.ppermute(x, 'row', [(a * NZ + b, (a + k) % NX * NZ + b) for a in rang...  22.7 us
    pallas_call x10, Pallas kernels, call(): pl.pallas_call(body, out_shape=out_shape, in_specs=[HBM if i in in_hbm el...  17.4 us
    all_to_all x1, blocking collectives, on_device(): lax.all_to_all(sums, ('row', 'head'), split_axis=0, concat_axis=0, axis_i...  12.4 us
    all_to_all x1, starting transfers between devices, on_device(): got = lax.all_to_all(send, 'row', split_axis=0, concat_axis=0, tiled=True)  12.1 us
    ppermute x6, waiting for transfers between devices, shift_y(): lax.ppermute(x, 'head', [(h, (h + k * cores) % n_head) for h in range(n_h...  9.22 us
    ppermute x6, starting transfers between devices, shift_y(): lax.ppermute(x, 'head', [(h, (h + k * cores) % n_head) for h in range(n_h...  8.23 us
    all_to_all x1, waiting for transfers between devices, on_device(): lax.all_to_all(head_out, 'row', split_axis=0, concat_axis=0, axis_index_g...  6.68 us
    all_to_all x1, starting transfers between devices, on_device(): lax.all_to_all(head_out, 'row', split_axis=0, concat_axis=0, axis_index_g...  6.39 us
  transfers between devices with their start and end apart: 14, of which 7 were waited for; matrix products, arithmetic and copies ran while one was open for 3% of the time, Pallas kernels for 5%

profile of v13, /device:TPU:1, one launch (start us, length us, event | category | flops | bytes accessed | tf_op | source)
XLA Modules:
  0.0 114.0 jit_solution(16334587320255454445)
XLA Ops:
  0.0 4.0 %shard_map.128 = bf16[32,184,128]{2,1,0:T(8,128)(2,1)} custom-call(s32[1,80]{1,0:T(1,128)} %bitcast.22, s32[1,80]{1,0:T(1,128)} %bitcast.23, bf16[80,64,512]{2,1,0:T(8,128)(2,1)} %lat_hbm.1, bf16[80,4096]{1,0:T(8,128)(2,1)} %rope_hbm.1), custom_call_target="tpu_custom_call" | custom-call | flops 838860800 | bytes 2621440 | tf_op jit(solution)/shard_map/pallas_call | solution.py:26
  4.1 0.0 copy-start.7
  4.1 0.0 copy-start.8
  4.1 12.1 %all-to-all-start = ((bf16[32,184,128]{2,1,0:T(8,128)(2,1)}), bf16[32,184,128]{2,1,0:T(8,128)(2,1)}, u32[]{:S(2)}, u32[]{:S(2)}) async-start(bf16[32,184,128]{2,1,0:T(8,128)(2,1)} %shard_map.128), calls=%async_computation | async-start | bytes 3014656 | tf_op jit(solution)/shard_map/all_to_all | solution.py:480
  16.2 0.0 copy-start.11
  16.3 1.2 %collective-permute-start = (bf16[224,2048]{1,0:T(8,128)(2,1)}, bf16[224,2048]{1,0:T(8,128)(2,1)S(1)}, u32[]{:S(2)}, u32[]{:S(2)}) collective-permute-start(bf16[224,2048]{1,0:T(8,128)(2,1)} %bitcast.15), channel_id=1, source_target_pairs={{0,64},{8,72},{16,80},{24,88},{32,96},{40,104},{48,112},{56,120},{... | collective-permute-start | bytes 2752520 | tf_op jit(solution)/shard_map/ppermute | solution.py:418
  17.5 1.5 %collective-permute-start.1 = (bf16[224,2048]{1,0:T(8,128)(2,1)}, bf16[224,2048]{1,0:T(8,128)(2,1)}, u32[]{:S(2)}, u32[]{:S(2)}) collective-permute-start(bf16[224,2048]{1,0:T(8,128)(2,1)} %bitcast.16), channel_id=1, source_target_pairs={{0,192},{8,200},{16,208},{24,216},{32,224},{40,232},{48,240},{56,2... | collective-permute-start | bytes 2752520 | tf_op jit(solution)/shard_map/ppermute | solution.py:418
  19.0 0.1 pad.3.clone
  19.1 0.2 copy.30
  19.4 0.1 copy.32
  19.5 0.1 reshape.78
  19.6 0.1 pad.5.clone
  19.7 1.3 %shard_map.127 = (bf16[640,128]{1,0:T(8,128)(2,1)S(1)}, bf16[640,128]{1,0:T(8,128)(2,1)}, f32[512,128]{1,0:T(8,128)S(1)}, f32[8,128]{1,0:T(8,128)S(1)}) custom-call(bf16[16,8,128]{2,1,0:T(8,128)(2,1)S(1)} %bitcast.18, bf16[128,128]{1,0:T(8,128)(2,1)S(1)} %pad_maximum_fusion.qtail_ref, bf16[16,128,512]{2,1,0:T(8,128)(2,1)S(1)} %copy-done.1, ...), custom_call_target="tpu_custom_call" | custom-call | flops 16777216 | bytes 2097152 | tf_op jit(solution)/shard_map/pallas_call | solution.py:26
  21.1 0.7 copy-done.5
  21.8 1.3 %collective-permute-start.2 = (bf16[640,128]{1,0:T(8,128)(2,1)}, bf16[640,128]{1,0:T(8,128)(2,1)S(1)}, u32[]{:S(2)}, u32[]{:S(2)}) collective-permute-start(bf16[640,128]{1,0:T(8,128)(2,1)} %get-tuple-element.27), channel_id=1, source_target_pairs={{0,2},{1,3},{2,4},{3,5},{4,6},{5,7},{6,0},{7,1},{8,10},{9,11},{10,... | collective-permute-start | bytes 491528 | tf_op jit(solution)/shard_map/ppermute | solution.py:414
  23.1 1.4 %collective-permute-start.4 = (bf16[640,128]{1,0:T(8,128)(2,1)}, bf16[640,128]{1,0:T(8,128)(2,1)S(1)}, u32[]{:S(2)}, u32[]{:S(2)}) collective-permute-start(bf16[640,128]{1,0:T(8,128)(2,1)} %get-tuple-element.27), channel_id=1, source_target_pairs={{0,6},{1,7},{2,0},{3,1},{4,2},{5,3},{6,4},{7,5},{8,14},{9,15},{10,... | collective-permute-start | bytes 491528 | tf_op jit(solution)/shard_map/ppermute | solution.py:414
  24.5 1.6 %collective-permute-start.3 = (bf16[640,128]{1,0:T(8,128)(2,1)S(1)}, bf16[640,128]{1,0:T(8,128)(2,1)S(1)}, u32[]{:S(2)}, u32[]{:S(2)}) collective-permute-start(bf16[640,128]{1,0:T(8,128)(2,1)S(1)} %get-tuple-element.29.refs_0_), channel_id=1, source_target_pairs={{0,4},{1,5},{2,6},{3,7},{4,0},{5,1},{6,2},{7,3},{8,12},{9,13},{10,... | collective-permute-start | bytes 491528 | tf_op jit(solution)/shard_map/ppermute | solution.py:414
  26.2 0.1 select_reduce_fusion
  26.3 0.1 subtract_subtract_fusion
  26.4 0.1 compare_select_fusion
  26.4 0.1 select_n.12
  26.6 1.3 %collective-permute-done.2.refs_1_ = bf16[640,128]{1,0:T(8,128)(2,1)S(1)} collective-permute-done((bf16[640,128]{1,0:T(8,128)(2,1)}, bf16[640,128]{1,0:T(8,128)(2,1)S(1)}, u32[]{:S(2)}, u32[]{:S(2)}) %collective-permute-start.2) | collective-permute-done | bytes 163872 | tf_op jit(solution)/shard_map/ppermute | solution.py:414
  27.8 4.4 %collective-permute-done.3.refs_2_ = bf16[640,128]{1,0:T(8,128)(2,1)S(1)} collective-permute-done((bf16[640,128]{1,0:T(8,128)(2,1)S(1)}, bf16[640,128]{1,0:T(8,128)(2,1)S(1)}, u32[]{:S(2)}, u32[]{:S(2)}) %collective-permute-start.3) | collective-permute-done | bytes 163872 | tf_op jit(solution)/shard_map/ppermute | solution.py:414
  32.2 22.7 %collective-permute-done.near_hbm = bf16[224,2048]{1,0:T(8,128)(2,1)S(1)} collective-permute-done((bf16[224,2048]{1,0:T(8,128)(2,1)}, bf16[224,2048]{1,0:T(8,128)(2,1)S(1)}, u32[]{:S(2)}, u32[]{:S(2)}) %collective-permute-start) | collective-permute-done | bytes 917536 | tf_op jit(solution)/shard_map/ppermute | solution.py:418
  54.9 3.8 %shard_map.129.key_ref = bf16[2,320,640]{2,1,0:T(8,128)(2,1)S(1)} custom-call(bf16[32,184,128]{2,1,0:T(8,128)(2,1)} %all-to-all-done.block_ref, f32[8,640]{1,0:T(8,128)S(1)} %broadcast_in_dim.41.bias_ref), custom_call_target="tpu_custom_call" | custom-call | flops 838860800 | bytes 1310720 | tf_op jit(solution)/shard_map/pallas_call | solution.py:26
  58.7 1.4 %collective-permute-start.5 = (bf16[2,320,640]{2,1,0:T(8,128)(2,1)S(1)}, bf16[2,320,640]{2,1,0:T(8,128)(2,1)S(1)}, u32[]{:S(2)}, u32[]{:S(2)}) collective-permute-start(bf16[2,320,640]{2,1,0:T(8,128)(2,1)S(1)} %shard_map.129.key_ref), channel_id=1, source_target_pairs={{0,1},{1,0},{2,3},{3,2},{4,5},{5,4},{6,7},{7,6},{8,9},{9,8},{10,11... | collective-permute-start | bytes 2457608 | tf_op jit(solution)/shard_map/ppermute | solution.py:538
  60.1 1.2 %shard_map.130 = (f32[2,512,256]{2,1,0:T(8,128)S(1)}, f32[2,8,256]{2,1,0:T(8,128)S(1)}) custom-call(bf16[2,320,640]{2,1,0:T(8,128)(2,1)S(1)} %shard_map.129.key_ref, bf16[640,128]{1,0:T(8,128)(2,1)S(1)} %get-tuple-element.29.refs_0_, bf16[640,128]{1,0:T(8,128)(2,1)S(1)} %collective-permute-done.2.refs_1_, ...), custom_call_target="tpu_custom_call" | custom-call | flops 377487360 | bytes 655360 | tf_op jit(solution)/shard_map/pallas_call | solution.py:26
  61.3 0.8 collective-permute-done.5.key_ref
  62.1 1.2 %shard_map.131 = (bf16[528,128]{1,0:T(8,128)(2,1)S(1)}, bf16[528,128]{1,0:T(8,128)(2,1)S(1)}, bf16[528,128]{1,0:T(8,128)(2,1)S(1)}, bf16[528,128]{1,0:T(8,128)(2,1)S(1)}) custom-call(bf16[2,320,640]{2,1,0:T(8,128)(2,1)S(1)} %collective-permute-done.5.key_ref, f32[2,512,256]{2,1,0:T(8,128)S(1)} %get-tuple-element.33.own_ref, ...), custom_call_target="tpu_custom_call" | custom-call | flops 377487360 | bytes 655360 | tf_op jit(solution)/shard_map/pallas_call | solution.py:26
  63.3 2.8 %collective-permute-start.6 = (bf16[528,128]{1,0:T(8,128)(2,1)S(1)}, bf16[528,128]{1,0:T(8,128)(2,1)S(1)}, u32[]{:S(2)}, u32[]{:S(2)}) collective-permute-start(bf16[528,128]{1,0:T(8,128)(2,1)S(1)} %get-tuple-element.36), channel_id=1, source_target_pairs={{0,6},{1,7},{2,0},{3,1},{4,2},{5,3},{6,4},{7,5},{8,14},{9,15},{10,... | collective-permute-start | bytes 405512 | tf_op jit(solution)/shard_map/ppermute | solution.py:414
  66.1 0.5 collective-permute-start.7
  66.6 0.6 collective-permute-start.8
  67.2 0.8 slice.10
  68.0 0.2 collective-permute-start.9
  68.2 1.8 %slice.11 = bf16[112,2048]{1,0:T(8,128)(2,1)} slice(bf16[224,2048]{1,0:T(8,128)(2,1)} %collective-permute-done.1.far_hbm), slice={[112:224], [0:2048]} | slice | bytes 917504 | tf_op jit(solution)/shard_map/slice | solution.py:551
  70.0 2.5 %collective-permute-start.10 = (bf16[112,2048]{1,0:T(8,128)(2,1)}, bf16[112,2048]{1,0:T(8,128)(2,1)}, u32[]{:S(2)}, u32[]{:S(2)}) collective-permute-start(bf16[112,2048]{1,0:T(8,128)(2,1)} %slice.11), channel_id=1, source_target_pairs={{0,192},{8,200},{16,208},{24,216},{32,224},{40,232},{48,240},{56,2... | collective-permute-start | bytes 1376264 | tf_op jit(solution)/shard_map/ppermute | solution.py:418
  72.5 3.5 %collective-permute-done.8.refs_3_ = bf16[528,128]{1,0:T(8,128)(2,1)S(1)} collective-permute-done((bf16[528,128]{1,0:T(8,128)(2,1)S(1)}, bf16[528,128]{1,0:T(8,128)(2,1)S(1)}, u32[]{:S(2)}, u32[]{:S(2)}) %collective-permute-start.8) | collective-permute-done | bytes 135200 | tf_op jit(solution)/shard_map/ppermute | solution.py:414
  76.0 1.5 %shard_map.132 = bf16[8,8,2048]{2,1,0:T(8,128)(2,1)} custom-call(f32[512,128]{1,0:T(8,128)S(1)} %copy-done.6, f32[8,128]{1,0:T(8,128)S(1)} %get-tuple-element.25.fresh_lse_ref, bf16[16,512,128]{2,1,0:T(8,128)(2,1)S(1)} %copy-done, bf16[528,128]{1,0:T(8,128)(2,1)S(1)} %get-tuple-element.35.refs_0_, bf16[528,128]{1,0:T(8,128)(2,1)S(1)} %collective-permute-done.6.refs_1_, ...), custom_call_target="tpu_custom_call" | custom-call | flops 16777216 | bytes 2097152 | tf_op jit(solution)/shard_map/pallas_call | solution.py:26
  77.6 6.4 %all-to-all-start.1 = ((bf16[8,8,2048]{2,1,0:T(8,128)(2,1)}), bf16[8,8,2048]{2,1,0:T(8,128)(2,1)S(1)}, u32[]{:S(2)}, u32[]{:S(2)}) async-start(bf16[8,8,2048]{2,1,0:T(8,128)(2,1)} %shard_map.132), calls=%async_computation.1 | async-start | bytes 524288 | tf_op jit(solution)/shard_map/all_to_all | solution.py:570
  84.0 1.2 %copy-done.3 = bf16[224,2048]{1,0:T(8,128)(2,1)S(1)} copy-done((bf16[224,2048]{1,0:T(8,128)(2,1)S(1)}, bf16[224,2048]{1,0:T(8,128)(2,1)}, u32[]{:S(2)}) %copy-start.3) | copy-done | bytes 917528
  85.1 1.2 %copy-done.4 = bf16[2048,224]{0,1:T(8,128)(2,1)S(1)} copy-done((bf16[2048,224]{0,1:T(8,128)(2,1)S(1)}, bf16[2048,224]{0,1:T(8,128)(2,1)}, u32[]{:S(2)}) %copy-start.4) | copy-done | bytes 917528
  86.3 1.6 %shard_map.133.w_ref = bf16[3,224,2048]{2,1,0:T(8,128)(2,1)S(1)} custom-call(bf16[224,2048]{1,0:T(8,128)(2,1)S(1)} %bitcast.17, bf16[224,2048]{1,0:T(8,128)(2,1)S(1)} %copy-done.3, bf16[224,2048]{1,0:T(8,128)(2,1)} %collective-permute-done.1.far_hbm), custom_call_target="tpu_custom_call" | custom-call | bytes 5505024 | tf_op jit(solution)/shard_map/pallas_call | solution.py:26
  88.0 6.7 %all-to-all-done.1 = bf16[8,8,2048]{2,1,0:T(8,128)(2,1)S(1)} async-done(((bf16[8,8,2048]{2,1,0:T(8,128)(2,1)}), bf16[8,8,2048]{2,1,0:T(8,128)(2,1)S(1)}, u32[]{:S(2)}, u32[]{:S(2)}) %all-to-all-start.1) | async-done | bytes 262176 | tf_op jit(solution)/shard_map/all_to_all | solution.py:570
  94.7 2.1 %shard_map.134 = bf16[32,8,224]{2,1,0:T(8,128)(2,1)S(1)} custom-call(bf16[64,2048]{1,0:T(8,128)(2,1)S(1)} %bitcast.14, bf16[3,224,2048]{2,1,0:T(8,128)(2,1)S(1)} %shard_map.133.w_ref, bf16[112,2048]{1,0:T(8,128)(2,1)S(1)} %collective-permute-done.9.opp_a_hbm, bf16[112,2048]{1,0:T(8,128)(2,1)} %collective-permute-done.10.opp_b_hbm), custom_call_target="tpu_custom_call" | custom-call | flops 234881024 | bytes 3670016 | tf_op jit(solution)/shard_map/pallas_call | solution.py:26
  96.7 12.4 %all_to_all.15.in_ref = bf16[32,8,224]{2,1,0:T(8,128)(2,1)S(1)} all-to-all(bf16[32,8,224]{2,1,0:T(8,128)(2,1)S(1)} %shard_map.134), channel_id=1, replica_groups={{0,2,4,6,8,10,12,14,16,18,20,22,24,26,28,30,32,34,36,38,40,42,44,46,48,..., dimensions={0} | all-to-all | bytes 229376 | tf_op jit(solution)/shard_map/all_to_all | solution.py:597
  109.1 3.4 %collective-permute-start.11 = (f32[4,8,224]{2,1,0:T(8,128)S(1)}, f32[4,8,224]{2,1,0:T(8,128)S(1)}, u32[]{:S(2)}, u32[]{:S(2)}) collective-permute-start(f32[4,8,224]{2,1,0:T(8,128)S(1)} %get-tuple-element.42), channel_id=1, source_target_pairs={{0,1},{1,0},{2,3},{3,2},{4,5},{5,4},{6,7},{7,6},{8,9},{9,8},{10,11... | collective-permute-start | bytes 86024 | tf_op jit(solution)/shard_map/ppermute | solution.py:607
  112.5 0.9 collective-permute-done.11.got_ref
  113.3 0.7 shard_map.136
  (39 shorter events, 0.2 us)
Async XLA Ops:
  4.0 15.0 %copy-start.9 = (bf16[4,2,512]{2,1,0:T(2,128)(2,1)S(1)}, bf16[4,2,512]{2,1,0:T(2,128)(2,1)}, u32[]{:S(2)}) copy-start(bf16[4,2,512]{2,1,0:T(2,128)(2,1)} %param.15) | copy-start | bytes 24580
  4.1 15.1 %copy-start.10 = (bf16[4,2,64]{2,1,0:T(2,128)(2,1)S(1)}, bf16[4,2,64]{2,1,0:T(2,128)(2,1)}, u32[]{:S(2)}) copy-start(bf16[4,2,64]{2,1,0:T(2,128)(2,1)} %param.16) | copy-start | bytes 3076
  4.1 15.4 %copy-start.7 = (bf16[4,2,16,128]{3,2,1,0:T(8,128)(2,1)S(1)}, bf16[4,2,16,128]{3,2,1,0:T(8,128)(2,1)}, u32[]{:S(2)}) copy-start(bf16[4,2,16,128]{3,2,1,0:T(8,128)(2,1)} %param.13) | copy-start | bytes 98308
  4.1 15.4 %copy-start.8 = (bf16[4,2,1024]{2,1,0:T(2,128)(2,1)S(1)}, bf16[4,2,1024]{2,1,0:T(2,128)(2,1)}, u32[]{:S(2)}) copy-start(bf16[4,2,1024]{2,1,0:T(2,128)(2,1)} %param.14) | copy-start | bytes 49156
  4.1 15.6 %copy-start.1 = (bf16[16,128,512]{2,1,0:T(8,128)(2,1)S(1)}, bf16[16,128,512]{2,1,0:T(8,128)(2,1)}, u32[]{:S(2)}) copy-start(bf16[16,128,512]{2,1,0:T(8,128)(2,1)} %w_ref.2) | copy-start | bytes 6291460
  4.1 50.8 %all-to-all-start = ((bf16[32,184,128]{2,1,0:T(8,128)(2,1)}), bf16[32,184,128]{2,1,0:T(8,128)(2,1)}, u32[]{:S(2)}, u32[]{:S(2)}) async-start(bf16[32,184,128]{2,1,0:T(8,128)(2,1)} %shard_map.128), calls=%async_computation | async-start | bytes 3014656 | tf_op jit(solution)/shard_map/all_to_all | solution.py:480
  16.2 9.9 %copy-start.11 = (s32[2,40]{1,0:T(2,128)S(1)}, s32[2,40]{1,0:T(2,128)}, u32[]{:S(2)}) copy-start(s32[2,40]{1,0:T(2,128)} %param.21) | copy-start | bytes 964
  16.2 10.0 %copy-start.12 = (s32[2]{0:T(128)S(1)}, s32[2]{0:T(128)}, u32[]{:S(2)}) copy-start(s32[2]{0:T(128)} %param.22) | copy-start | bytes 28
  16.3 38.7 %collective-permute-start = (bf16[224,2048]{1,0:T(8,128)(2,1)}, bf16[224,2048]{1,0:T(8,128)(2,1)S(1)}, u32[]{:S(2)}, u32[]{:S(2)}) collective-permute-start(bf16[224,2048]{1,0:T(8,128)(2,1)} %bitcast.15), channel_id=1, source_target_pairs={{0,64},{8,72},{16,80},{24,88},{32,96},{40,104},{48,112},{56,120},{... | collective-permute-start | bytes 2752520 | tf_op jit(solution)/shard_map/ppermute | solution.py:418
  17.5 37.4 %collective-permute-start.1 = (bf16[224,2048]{1,0:T(8,128)(2,1)}, bf16[224,2048]{1,0:T(8,128)(2,1)}, u32[]{:S(2)}, u32[]{:S(2)}) collective-permute-start(bf16[224,2048]{1,0:T(8,128)(2,1)} %bitcast.16), channel_id=1, source_target_pairs={{0,192},{8,200},{16,208},{24,216},{32,224},{40,232},{48,240},{56,2... | collective-permute-start | bytes 2752520 | tf_op jit(solution)/shard_map/ppermute | solution.py:418
  21.1 0.7 copy-start.5
  21.8 6.1 %collective-permute-start.2 = (bf16[640,128]{1,0:T(8,128)(2,1)}, bf16[640,128]{1,0:T(8,128)(2,1)S(1)}, u32[]{:S(2)}, u32[]{:S(2)}) collective-permute-start(bf16[640,128]{1,0:T(8,128)(2,1)} %get-tuple-element.27), channel_id=1, source_target_pairs={{0,2},{1,3},{2,4},{3,5},{4,6},{5,7},{6,0},{7,1},{8,10},{9,11},{10,... | collective-permute-start | bytes 491528 | tf_op jit(solution)/shard_map/ppermute | solution.py:414
  23.1 9.2 %collective-permute-start.4 = (bf16[640,128]{1,0:T(8,128)(2,1)}, bf16[640,128]{1,0:T(8,128)(2,1)S(1)}, u32[]{:S(2)}, u32[]{:S(2)}) collective-permute-start(bf16[640,128]{1,0:T(8,128)(2,1)} %get-tuple-element.27), channel_id=1, source_target_pairs={{0,6},{1,7},{2,0},{3,1},{4,2},{5,3},{6,4},{7,5},{8,14},{9,15},{10,... | collective-permute-start | bytes 491528 | tf_op jit(solution)/shard_map/ppermute | solution.py:414
  24.5 7.7 %collective-permute-start.3 = (bf16[640,128]{1,0:T(8,128)(2,1)S(1)}, bf16[640,128]{1,0:T(8,128)(2,1)S(1)}, u32[]{:S(2)}, u32[]{:S(2)}) collective-permute-start(bf16[640,128]{1,0:T(8,128)(2,1)S(1)} %get-tuple-element.29.refs_0_), channel_id=1, source_target_pairs={{0,4},{1,5},{2,6},{3,7},{4,0},{5,1},{6,2},{7,3},{8,12},{9,13},{10,... | collective-permute-start | bytes 491528 | tf_op jit(solution)/shard_map/ppermute | solution.py:414
  54.9 12.2 %copy-start.2 = (bf16[224,2048]{1,0:T(8,128)(2,1)}, bf16[224,2048]{1,0:T(8,128)(2,1)S(1)}, u32[]{:S(2)}) copy-start(bf16[224,2048]{1,0:T(8,128)(2,1)S(1)} %collective-permute-done.near_hbm) | copy-start | bytes 2752516
  58.7 3.4 %collective-permute-start.5 = (bf16[2,320,640]{2,1,0:T(8,128)(2,1)S(1)}, bf16[2,320,640]{2,1,0:T(8,128)(2,1)S(1)}, u32[]{:S(2)}, u32[]{:S(2)}) collective-permute-start(bf16[2,320,640]{2,1,0:T(8,128)(2,1)S(1)} %shard_map.129.key_ref), channel_id=1, source_target_pairs={{0,1},{1,0},{2,3},{3,2},{4,5},{5,4},{6,7},{7,6},{8,9},{9,8},{10,11... | collective-permute-start | bytes 2457608 | tf_op jit(solution)/shard_map/ppermute | solution.py:538
  62.1 13.9 %copy-start = (bf16[16,512,128]{2,1,0:T(8,128)(2,1)S(1)}, bf16[16,512,128]{2,1,0:T(8,128)(2,1)}, u32[]{:S(2)}) copy-start(bf16[16,512,128]{2,1,0:T(8,128)(2,1)} %w_ref.3) | copy-start | bytes 6291460
  62.1 13.9 %copy-start.6 = (f32[512,128]{1,0:T(8,128)S(1)}, f32[512,128]{1,0:T(8,128)}, u32[]{:S(2)}) copy-start(f32[512,128]{1,0:T(8,128)} %copy-done.5) | copy-start | bytes 786436
  63.3 9.2 %collective-permute-start.6 = (bf16[528,128]{1,0:T(8,128)(2,1)S(1)}, bf16[528,128]{1,0:T(8,128)(2,1)S(1)}, u32[]{:S(2)}, u32[]{:S(2)}) collective-permute-start(bf16[528,128]{1,0:T(8,128)(2,1)S(1)} %get-tuple-element.36), channel_id=1, source_target_pairs={{0,6},{1,7},{2,0},{3,1},{4,2},{5,3},{6,4},{7,5},{8,14},{9,15},{10,... | collective-permute-start | bytes 405512 | tf_op jit(solution)/shard_map/ppermute | solution.py:414
  66.1 6.4 %collective-permute-start.7 = (bf16[528,128]{1,0:T(8,128)(2,1)S(1)}, bf16[528,128]{1,0:T(8,128)(2,1)S(1)}, u32[]{:S(2)}, u32[]{:S(2)}) collective-permute-start(bf16[528,128]{1,0:T(8,128)(2,1)S(1)} %get-tuple-element.37), channel_id=1, source_target_pairs={{0,4},{1,5},{2,6},{3,7},{4,0},{5,1},{6,2},{7,3},{8,12},{9,13},{10,... | collective-permute-start | bytes 405512 | tf_op jit(solution)/shard_map/ppermute | solution.py:414
  66.6 9.4 %collective-permute-start.8 = (bf16[528,128]{1,0:T(8,128)(2,1)S(1)}, bf16[528,128]{1,0:T(8,128)(2,1)S(1)}, u32[]{:S(2)}, u32[]{:S(2)}) collective-permute-start(bf16[528,128]{1,0:T(8,128)(2,1)S(1)} %get-tuple-element.38), channel_id=1, source_target_pairs={{0,2},{1,3},{2,4},{3,5},{4,6},{5,7},{6,0},{7,1},{8,10},{9,11},{10,... | collective-permute-start | bytes 405512 | tf_op jit(solution)/shard_map/ppermute | solution.py:414
  68.0 20.0 %collective-permute-start.9 = (bf16[112,2048]{1,0:T(8,128)(2,1)}, bf16[112,2048]{1,0:T(8,128)(2,1)S(1)}, u32[]{:S(2)}, u32[]{:S(2)}) collective-permute-start(bf16[112,2048]{1,0:T(8,128)(2,1)} %slice.10), channel_id=1, source_target_pairs={{0,64},{8,72},{16,80},{24,88},{32,96},{40,104},{48,112},{56,120},{... | collective-permute-start | bytes 1376264 | tf_op jit(solution)/shard_map/ppermute | solution.py:418
  70.0 17.9 %collective-permute-start.10 = (bf16[112,2048]{1,0:T(8,128)(2,1)}, bf16[112,2048]{1,0:T(8,128)(2,1)}, u32[]{:S(2)}, u32[]{:S(2)}) collective-permute-start(bf16[112,2048]{1,0:T(8,128)(2,1)} %slice.11), channel_id=1, source_target_pairs={{0,192},{8,200},{16,208},{24,216},{32,224},{40,232},{48,240},{56,2... | collective-permute-start | bytes 1376264 | tf_op jit(solution)/shard_map/ppermute | solution.py:418
  77.6 17.1 %all-to-all-start.1 = ((bf16[8,8,2048]{2,1,0:T(8,128)(2,1)}), bf16[8,8,2048]{2,1,0:T(8,128)(2,1)S(1)}, u32[]{:S(2)}, u32[]{:S(2)}) async-start(bf16[8,8,2048]{2,1,0:T(8,128)(2,1)} %shard_map.132), calls=%async_computation.1 | async-start | bytes 524288 | tf_op jit(solution)/shard_map/all_to_all | solution.py:570
  83.9 1.2 %copy-start.3 = (bf16[224,2048]{1,0:T(8,128)(2,1)S(1)}, bf16[224,2048]{1,0:T(8,128)(2,1)}, u32[]{:S(2)}) copy-start(bf16[224,2048]{1,0:T(8,128)(2,1)} %copy-done.2) | copy-start | bytes 2752516
  85.1 1.2 %copy-start.4 = (bf16[2048,224]{0,1:T(8,128)(2,1)S(1)}, bf16[2048,224]{0,1:T(8,128)(2,1)}, u32[]{:S(2)}) copy-start(bf16[2048,224]{0,1:T(8,128)(2,1)} %param.25) | copy-start | bytes 2752516
  109.1 4.2 %collective-permute-start.11 = (f32[4,8,224]{2,1,0:T(8,128)S(1)}, f32[4,8,224]{2,1,0:T(8,128)S(1)}, u32[]{:S(2)}, u32[]{:S(2)}) collective-permute-start(f32[4,8,224]{2,1,0:T(8,128)S(1)} %get-tuple-element.42), channel_id=1, source_target_pairs={{0,1},{1,0},{2,3},{3,2},{4,5},{5,4},{6,7},{7,6},{8,9},{9,8},{10,11... | collective-permute-start | bytes 86024 | tf_op jit(solution)/shard_map/ppermute | solution.py:607
